TPU v7x, 32 devices: a whole 2x2x4 slice. The times are simulated.
32 devices in a mesh: mid: 8 (over y, x, core), sub: 4 (over z).
Axes of the slice: x: 2, y: 2, z: 4, core: 2. Of those that a mesh axis runs over, the one named last changes fastest.
Arguments:
- signal: bfloat16 [24576, 1152], P(('mid', 'sub')), may hold values from -6 to 6
- col_basis: bfloat16 [24576, 256], P(('mid', 'sub')), may hold values from -0.21875 to 0.21875
- right_coupling: bfloat16 [32, 2, 256, 256], P(('mid', 'sub')), may hold values from -0.375 to 0.375
- middle_coupling: bfloat16 [32, 256, 256], P(('mid', 'sub')), may hold values from -0.375 to 0.375
- left_coupling: bfloat16 [32, 2, 256, 256], P(('mid', 'sub')), may hold values from -0.375 to 0.375
- row_basis: bfloat16 [24576, 256], P(('mid', 'sub')), may hold values from -0.375 to 0.375
- node_order: int32 [8], replicated, may hold values from 0 to 7, each once
Outputs:
- product: bfloat16 [24576, 1152], P(('mid', 'sub'))
Inputs may be any that keep to these rules, and one draw needn't show every extreme that they name: node_order holds each of 0 to 7 exactly once.
All inputs are finite; a program needn't handle non-finite values.
Results may differ from a plain program's by a relative error of at most 0.013.
Values may be sent and summed in bfloat16 or wider, within the bound.
No kernel may reach another device: no remote copies, remote signals or barrier semaphores. Data moves between devices by JAX's collectives and lax.ppermute only.
A program may use at most 64 MiB of HBM per device.

v0:
```python
import jax
import jax.numpy as jnp
from jax import lax
from jax.sharding import PartitionSpec as P


def from_partner(block, axis, distance):
    count = lax.axis_size(axis)
    route = []
    for low in range(count):
        high = low | 1 << distance
        if high != low and high < count:
            route += [(low, high), (high, low)]
    return lax.ppermute(block, axis, route)


def stack_halves(coeffs, received, bitval):
    half = coeffs.shape[0] // 2
    keep = jnp.where(bitval == 1, coeffs[half:], coeffs[:half])
    return jnp.where(
        bitval == 1,
        jnp.concatenate([received, keep], axis=0),
        jnp.concatenate([keep, received], axis=0),
    )


def outgoing(coeffs, bitval):
    half = coeffs.shape[0] // 2
    return jnp.where(bitval == 1, coeffs[:half], coeffs[half:])


def chain(
    signal_blk, col_basis, right_coupling, middle_coupling, left_coupling, row_basis, node_order
):
    position = lax.axis_index("sub")
    width = col_basis.shape[1]
    groups = lax.axis_size("mid")
    coeffs = lax.dot_general(
        col_basis, signal_blk, (((0,), (0,)), ((), ())), preferred_element_type=jnp.float32
    ).astype(jnp.bfloat16)
    for level, bit in ((0, 0), (1, 1)):
        bitval = position >> bit & 1
        received = from_partner(outgoing(coeffs, bitval), "sub", bit)
        stacked = stack_halves(coeffs, received, bitval)
        coeffs = jnp.dot(
            right_coupling[0, level], stacked, preferred_element_type=jnp.float32
        ).astype(jnp.bfloat16)
    pieces = coeffs.reshape(groups, width // groups, coeffs.shape[1])
    ordered = jnp.take(pieces, node_order, axis=0)
    arrived = lax.all_to_all(ordered, "mid", split_axis=0, concat_axis=0, tiled=True)
    flat = arrived.reshape(width, arrived.shape[2])
    coeffs = jnp.dot(middle_coupling[0], flat, preferred_element_type=jnp.float32).astype(
        jnp.bfloat16
    )
    for level, bit in ((0, 1), (1, 0)):
        bitval = position >> bit & 1
        received = from_partner(outgoing(coeffs, bitval), "sub", bit)
        stacked = stack_halves(coeffs, received, bitval)
        coeffs = jnp.dot(
            left_coupling[0, level], stacked, preferred_element_type=jnp.float32
        ).astype(jnp.bfloat16)
    return jnp.dot(row_basis, coeffs, preferred_element_type=jnp.float32).astype(jnp.bfloat16)


def local(signal, col_basis, right_coupling, middle_coupling, left_coupling, row_basis, node_order):
    return chain(
        signal, col_basis, right_coupling, middle_coupling, left_coupling, row_basis, node_order
    )


def solution(mesh):
    return jax.shard_map(
        local,
        mesh=mesh,
        in_specs=(
            P(("mid", "sub"), None),
            P(("mid", "sub"), None),
            P(("mid", "sub"), None, None, None),
            P(("mid", "sub"), None, None),
            P(("mid", "sub"), None, None, None),
            P(("mid", "sub"), None),
            P(),
        ),
        out_specs=P(("mid", "sub"), None),
        check_vma=False,
    )
```

profile of v0, /device:TPU:0, one launch (start us, length us, event | category | flops | bytes accessed | tf_op | source)
XLA Modules:
  0.0 75.1 jit_solution(15184483438032055309)
XLA Ops:
  0.0 1.5 %copy-done = bf16[768,1152]{1,0:T(8,128)(2,1)S(1)} copy-done((bf16[768,1152]{1,0:T(8,128)(2,1)S(1)}, bf16[768,1152]{1,0:T(8,128)(2,1)}, u32[]{:S(2)}) %copy-start) | copy-done | bytes 1769496
  1.5 1.7 %convolution_convert_fusion.6 = bf16[256,1152]{1,0:T(8,128)(2,1)S(1)} fusion(bf16[768,256]{1,0:T(8,128)(2,1)} %param.8, bf16[768,1152]{1,0:T(8,128)(2,1)S(1)} %copy-done), kind=kOutput, calls=%fused_computation.8 | convolution fusion | flops 453279744 | bytes 2752512 | tf_op jit(solution)/shard_map/dot_general | solution.py:38
  3.2 0.0 copy-start.5
  3.2 0.1 broadcast_select_fusion.8
  3.3 3.1 %collective-permute-start = (bf16[128,1152]{1,0:T(8,128)(2,1)S(1)}, bf16[128,1152]{1,0:T(8,128)(2,1)S(1)}, u32[]{:S(2)}, u32[]{:S(2)}) collective-permute-start(bf16[128,1152]{1,0:T(8,128)(2,1)S(1)} %get-tuple-element.11), channel_id=1, source_target_pairs={{0,1},{1,0},{2,3},{3,2},{4,5},{5,4},{6,7},{7,6},{8,9},{9,8},{10,11... | collective-permute-start | bytes 884744 | tf_op jit(solution)/shard_map/ppermute | solution.py:14
  6.4 7.0 %collective-permute-done = bf16[128,1152]{1,0:T(8,128)(2,1)S(1)} collective-permute-done((bf16[128,1152]{1,0:T(8,128)(2,1)S(1)}, bf16[128,1152]{1,0:T(8,128)(2,1)S(1)}, u32[]{:S(2)}, u32[]{:S(2)}) %collective-permute-start) | collective-permute-done | bytes 294944 | tf_op jit(solution)/shard_map/ppermute | solution.py:14
  13.4 0.4 fusion.1
  13.7 0.1 broadcast_select_fusion.4
  13.8 2.8 %collective-permute-start.1 = (bf16[128,1152]{1,0:T(8,128)(2,1)S(1)}, bf16[128,1152]{1,0:T(8,128)(2,1)S(1)}, u32[]{:S(2)}, u32[]{:S(2)}) collective-permute-start(bf16[128,1152]{1,0:T(8,128)(2,1)S(1)} %get-tuple-element.9), channel_id=1, source_target_pairs={{0,2},{2,0},{1,3},{3,1},{4,6},{6,4},{5,7},{7,5},{8,10},{10,8},{9,1... | collective-permute-start | bytes 884744 | tf_op jit(solution)/shard_map/ppermute | solution.py:14
  16.7 12.6 %collective-permute-done.1 = bf16[128,1152]{1,0:T(8,128)(2,1)S(1)} collective-permute-done((bf16[128,1152]{1,0:T(8,128)(2,1)S(1)}, bf16[128,1152]{1,0:T(8,128)(2,1)S(1)}, u32[]{:S(2)}, u32[]{:S(2)}) %collective-permute-start.1) | collective-permute-done | bytes 294944 | tf_op jit(solution)/shard_map/ppermute | solution.py:14
  29.3 0.4 convolution_convert_fusion.3
  29.7 0.6 gather_fusion
  30.3 0.1 broadcast_select_fusion
  30.5 13.8 %all_to_all.5 = bf16[8,32,1152]{2,1,0:T(8,128)(2,1)S(1)} all-to-all(bf16[8,32,1152]{2,1,0:T(8,128)(2,1)S(1)} %broadcast_select_fusion), channel_id=1, replica_groups=mesh['mid'=8,'sub'=4] {'mid'}, dimensions={0} | all-to-all | bytes 1179648 | tf_op jit(solution)/shard_map/all_to_all | solution.py:50
  44.3 0.3 fusion.2
  44.6 0.1 broadcast_select_fusion.2
  44.7 0.1 collective-permute-start.2
  44.8 15.9 %collective-permute-done.2 = bf16[128,1152]{1,0:T(8,128)(2,1)S(1)} collective-permute-done((bf16[128,1152]{1,0:T(8,128)(2,1)S(1)}, bf16[128,1152]{1,0:T(8,128)(2,1)S(1)}, u32[]{:S(2)}, u32[]{:S(2)}) %collective-permute-start.2) | collective-permute-done | bytes 294944 | tf_op jit(solution)/shard_map/ppermute | solution.py:14
  60.7 0.4 fusion.3
  61.1 0.8 %broadcast_select_fusion.6 = (bf16[128,1152]{1,0:T(8,128)(2,1)S(1)}, bf16[128,1152]{1,0:T(8,128)(2,1)}) fusion(pred[]{:T(512)S(6)} %eq.4, bf16[256,1152]{1,0:T(8,128)(2,1)S(1)} %fusion.3), kind=kLoop, calls=%fused_computation.46 | loop fusion | flops 294912 | bytes 1179649 | tf_op jit(solution)/shard_map/jit(_where)/select_n | solution.py:29
  61.8 8.1 %collective-permute-done.3 = bf16[128,1152]{1,0:T(8,128)(2,1)S(1)} collective-permute-done((bf16[128,1152]{1,0:T(8,128)(2,1)S(1)}, bf16[128,1152]{1,0:T(8,128)(2,1)S(1)}, u32[]{:S(2)}, u32[]{:S(2)}) %collective-permute-start.3) | collective-permute-done | bytes 294944 | tf_op jit(solution)/shard_map/ppermute | solution.py:14
  69.9 0.7 copy-done.2
  70.6 2.3 %fusion = bf16[768,1152]{0,1:T(8,128)(2,1)S(1)} fusion(bf16[768,256]{1,0:T(8,128)(2,1)} %param.12, bf16[128,1152]{1,0:T(8,128)(2,1)} %get-tuple-element.6, bf16[128,1152]{1,0:T(8,128)(2,1)} %copy-done.2, pred[]{:T(512)S(6)} %eq.4, bf16[1,2,256,256]{3,2,1,0:T(8,128)(2,1)} %param.11), kind=kOutput, calls=%fused_computation.2 | convolution fusion | flops 607813632 | bytes 2883585 | tf_op jit(solution)/shard_map/dot_general | solution.py:62
  72.9 2.2 %copy.8 = bf16[768,1152]{1,0:T(8,128)(2,1)} copy(bf16[768,1152]{0,1:T(8,128)(2,1)S(1)} %fusion) | data formatting | bytes 3538944 | tf_op jit(solution)/shard_map/convert_element_type | solution.py:62
  (13 shorter events, 0.0 us)
Async XLA Ops:
  0.0 1.5 %copy-start = (bf16[768,1152]{1,0:T(8,128)(2,1)S(1)}, bf16[768,1152]{1,0:T(8,128)(2,1)}, u32[]{:S(2)}) copy-start(bf16[768,1152]{1,0:T(8,128)(2,1)} %param.7) | copy-start | bytes 5308420
  3.2 3.2 %copy-start.5 = (s32[8]{0:T(128)S(1)}, s32[8]{0:T(128)}, u32[]{:S(2)}) copy-start(s32[8]{0:T(128)} %param.13) | copy-start | bytes 100
  3.2 10.2 %copy-start.3 = (bf16[1,2,256,256]{3,2,1,0:T(8,128)(2,1)S(1)}, bf16[1,2,256,256]{3,2,1,0:T(8,128)(2,1)}, u32[]{:S(2)}) copy-start(bf16[1,2,256,256]{3,2,1,0:T(8,128)(2,1)} %param.9) | copy-start | bytes 786436
  3.3 10.1 %collective-permute-start = (bf16[128,1152]{1,0:T(8,128)(2,1)S(1)}, bf16[128,1152]{1,0:T(8,128)(2,1)S(1)}, u32[]{:S(2)}, u32[]{:S(2)}) collective-permute-start(bf16[128,1152]{1,0:T(8,128)(2,1)S(1)} %get-tuple-element.11), channel_id=1, source_target_pairs={{0,1},{1,0},{2,3},{3,2},{4,5},{5,4},{6,7},{7,6},{8,9},{9,8},{10,11... | collective-permute-start | bytes 884744 | tf_op jit(solution)/shard_map/ppermute | solution.py:14
  13.8 15.5 %collective-permute-start.1 = (bf16[128,1152]{1,0:T(8,128)(2,1)S(1)}, bf16[128,1152]{1,0:T(8,128)(2,1)S(1)}, u32[]{:S(2)}, u32[]{:S(2)}) collective-permute-start(bf16[128,1152]{1,0:T(8,128)(2,1)S(1)} %get-tuple-element.9), channel_id=1, source_target_pairs={{0,2},{2,0},{1,3},{3,1},{4,6},{6,4},{5,7},{7,5},{8,10},{10,8},{9,1... | collective-permute-start | bytes 884744 | tf_op jit(solution)/shard_map/ppermute | solution.py:14
  30.3 14.0 %copy-start.1 = (bf16[1,256,256]{2,1,0:T(8,128)(2,1)S(1)}, bf16[1,256,256]{2,1,0:T(8,128)(2,1)}, u32[]{:S(2)}) copy-start(bf16[1,256,256]{2,1,0:T(8,128)(2,1)} %param.10) | copy-start | bytes 393220
  44.3 16.4 %copy-start.4 = (bf16[1,2,256,256]{3,2,1,0:T(8,128)(2,1)S(1)}, bf16[1,2,256,256]{3,2,1,0:T(8,128)(2,1)}, u32[]{:S(2)}) copy-start(bf16[1,2,256,256]{3,2,1,0:T(8,128)(2,1)} %param.11) | copy-start | bytes 786436
  44.7 16.0 %collective-permute-start.2 = (bf16[128,1152]{1,0:T(8,128)(2,1)S(1)}, bf16[128,1152]{1,0:T(8,128)(2,1)S(1)}, u32[]{:S(2)}, u32[]{:S(2)}) collective-permute-start(bf16[128,1152]{1,0:T(8,128)(2,1)S(1)} %get-tuple-element.7), channel_id=1, source_target_pairs={{0,2},{2,0},{1,3},{3,1},{4,6},{6,4},{5,7},{7,5},{8,10},{10,8},{9,1... | collective-permute-start | bytes 884744 | tf_op jit(solution)/shard_map/ppermute | solution.py:14
  61.8 8.1 %collective-permute-start.3 = (bf16[128,1152]{1,0:T(8,128)(2,1)S(1)}, bf16[128,1152]{1,0:T(8,128)(2,1)S(1)}, u32[]{:S(2)}, u32[]{:S(2)}) collective-permute-start(bf16[128,1152]{1,0:T(8,128)(2,1)S(1)} %get-tuple-element.5), channel_id=1, source_target_pairs={{0,1},{1,0},{2,3},{3,2},{4,5},{5,4},{6,7},{7,6},{8,9},{9,8},{10,11... | collective-permute-start | bytes 884744 | tf_op jit(solution)/shard_map/ppermute | solution.py:14
  69.9 0.7 copy-start.2
where the time goes:
time: 75.4 us; the launch traced here: 75.1 us
  waiting for transfers between devices  43.6 us (58%)
  blocking collectives  13.8 us (18%)
  starting transfers between devices  5.98 us (8%)
  matrix products  5.46 us (7%)
  local copies, waits for them, and re-layouts  5.06 us (7%)
  other arithmetic  1.1 us (1%)
    ppermute x4, waiting for transfers between devices, from_partner(): return lax.ppermute(block, axis, route)  43.6 us
    all_to_all x1, blocking collectives, chain(): lax.all_to_all(ordered, 'mid', split_axis=0, concat_axis=0, tiled=True)  13.8 us
    ppermute x4, starting transfers between devices, from_partner(): return lax.ppermute(block, axis, route)  5.98 us
    dot_general x1, matrix products, chain(): jnp.dot(row_basis, coeffs, preferred_element_type=jnp.float32)  2.31 us
    unnamed x12, local copies, waits for them, and re-layouts  2.21 us
    convert_element_type x1, local copies, waits for them, and re-layouts, chain(): jnp.dot(row_basis, coeffs, preferred_element_type=jnp.float32)  2.21 us
    dot_general x1, matrix products, chain(): lax.dot_general(col_basis, signal_blk, (((0,), (0,)), ((), ())), preferre...  1.7 us
  transfers between devices with their start and end apart: 4, of which 4 were waited for; matrix products, arithmetic and copies ran while one was open for 0% of the time, Pallas kernels for 0%

commit v1 on v0

v1 whole, which is shorter than its diff:
```python
import jax
import jax.numpy as jnp
from jax import lax
from jax.sharding import PartitionSpec as P

LANES = 128
CHUNKS = 3


def cuts(columns):
    tiles = max(columns // LANES, 1)
    count = min(CHUNKS, tiles)
    edges = [tiles * i // count * LANES for i in range(count)] + [columns]
    return list(zip(edges[:-1], edges[1:]))


def swap(block, axis, distance):
    count = lax.axis_size(axis)
    return lax.ppermute(block, axis, [(i, i ^ distance) for i in range(count)])


def relative_rows(matrix, order):
    blocks = matrix.reshape((order.shape[0], -1) + matrix.shape[1:])
    return jnp.take(blocks, order, axis=0, mode="clip").reshape(matrix.shape)


def relative_columns(matrix, order):
    rows = matrix.shape[0]
    blocks = matrix.reshape(rows, order.shape[0], -1)
    return jnp.take(blocks, order, axis=1, mode="clip").reshape(matrix.shape)


def halves(matrix, axis, bitval):
    low, high = jnp.split(matrix, 2, axis=axis)
    return jnp.where(bitval == 1, jnp.concatenate([high, low], axis=axis), matrix)


def product(left, right):
    return jnp.dot(left, right, preferred_element_type=jnp.float32).astype(jnp.bfloat16)


def exchange(coeffs, axis, distance, block):
    rows, columns = coeffs.shape
    slots = coeffs.reshape(-1, 2, block, columns)
    keep, send = slots[:, 0], slots[:, 1]
    got = swap(send, axis, distance)
    return jnp.stack([keep, got], axis=1).reshape(rows, columns)


def local(signal, col_basis, right_coupling, middle_coupling, left_coupling, row_basis, node_order):
    place = lax.axis_index("sub")
    group = lax.axis_index("mid")
    groups = lax.axis_size("mid")
    width = col_basis.shape[1]
    bit0 = place & 1
    bit1 = place >> 1 & 1
    order = jnp.arange(groups, dtype=jnp.int32) ^ group

    first = halves(col_basis, 1, bit0)
    right0 = halves(halves(right_coupling[0, 0], 1, bit0), 0, bit1)
    right1 = relative_rows(halves(right_coupling[0, 1], 1, bit1), node_order[order])
    middle = halves(relative_columns(middle_coupling[0], order), 0, bit1)
    left0 = halves(halves(left_coupling[0, 0], 1, bit1), 0, bit0)
    left1 = halves(left_coupling[0, 1], 1, bit0)

    outs = []
    for low, high in cuts(signal.shape[1]):
        coeffs = lax.dot_general(
            first, signal[:, low:high], (((0,), (0,)), ((), ())), preferred_element_type=jnp.float32
        ).astype(jnp.bfloat16)
        coeffs = product(right0, exchange(coeffs, "sub", 1, width // 2))
        coeffs = product(right1, exchange(coeffs, "sub", 2, width // 2))
        distance = groups // 2
        while distance:
            coeffs = exchange(coeffs, "mid", distance, width // groups * distance)
            distance //= 2
        coeffs = product(middle, coeffs)
        coeffs = product(left0, exchange(coeffs, "sub", 2, width // 2))
        coeffs = product(left1, exchange(coeffs, "sub", 1, width // 2))
        outs.append(product(row_basis, coeffs))
    return jnp.concatenate(outs, axis=1)


def solution(mesh):
    return jax.shard_map(
        local,
        mesh=mesh,
        in_specs=(
            P(("mid", "sub"), None),
            P(("mid", "sub"), None),
            P(("mid", "sub"), None, None, None),
            P(("mid", "sub"), None, None),
            P(("mid", "sub"), None, None, None),
            P(("mid", "sub"), None),
            P(),
        ),
        out_specs=P(("mid", "sub"), None),
        check_vma=False,
    )
```

time: 75.4 us -> 67.9 us (0.901)
  starting transfers between devices: 5.98 us -> 22.8 us
  waiting for transfers between devices: 43.6 us -> 27.6 us
  blocking collectives: 13.8 us -> 0 us
  other arithmetic: 1.1 us -> 3.18 us
  matrix products: 5.46 us -> 7.49 us
  local copies, waits for them, and re-layouts: 5.06 us -> 5.92 us
    ppermute x4 -> x21, starting transfers between devices: 5.98 us -> 22.8 us  [swap(): return lax.ppermute(block, axis, [(i, i ^ distance) for i in range(count)])]
    ppermute x4 -> x21, waiting for transfers between devices: 43.6 us -> 27.6 us  [swap(): return lax.ppermute(block, axis, [(i, i ^ distance) for i in range(count)])]
    all_to_all x1 -> x0, blocking collectives: 13.8 us -> none  [chain(): lax.all_to_all(ordered, 'mid', split_axis=0, concat_axis=0, tiled=True)]
    concatenate x0 -> x6, local copies, waits for them, and re-layouts: none -> 2.32 us  [the longest x1 2.21 us: local(): return jnp.concatenate(outs, axis=1)]
    convert_element_type x1 -> x0, local copies, waits for them, and re-layouts: 2.21 us -> none  [chain(): jnp.dot(row_basis, coeffs, preferred_element_type=jnp.float32)]
    dot_general x6 -> x18, matrix products: 5.46 us -> 7.49 us  [the longest x15 5.25 us: product(): jnp.dot(left, right, preferred_element_type=jnp.float32)]
    unnamed x12 -> x16, local copies, waits for them, and re-layouts: 2.21 us -> 0.2 us
    split x0 -> x3, local copies, waits for them, and re-layouts: none -> 1.23 us  [halves(): low, high = jnp.split(matrix, 2, axis=axis)]
  transfers between devices with their start and end apart: 4 -> 21, of which waited for: 4 -> 12; matrix products, arithmetic and copies ran while one was open for 0% -> 12% of each run, Pallas kernels for 0% -> 0%
where the time goes in v1:
time: 67.9 us; the launch traced here: 67.7 us
  waiting for transfers between devices  27.6 us (41%)
  starting transfers between devices  22.8 us (34%)
  matrix products  7.49 us (11%)
  local copies, waits for them, and re-layouts  5.92 us (9%)
  other arithmetic  3.18 us (5%)
  between operations  0.68 us (1%)
    ppermute x21, waiting for transfers between devices, swap(): return lax.ppermute(block, axis, [(i, i ^ distance) for i in range(count)])  27.6 us
    ppermute x21, starting transfers between devices, swap(): return lax.ppermute(block, axis, [(i, i ^ distance) for i in range(count)])  22.8 us
    dot_general x15, matrix products, product(): jnp.dot(left, right, preferred_element_type=jnp.float32)  5.25 us
    dot_general x3, matrix products, local(): lax.dot_general(first, signal[:, low:high], (((0,), (0,)), ((), ())), pre...  2.24 us
    concatenate x1, local copies, waits for them, and re-layouts, local(): return jnp.concatenate(outs, axis=1)  2.21 us
    select_n x8, other arithmetic, halves(): jnp.where(bitval == 1, jnp.concatenate([high, low], axis=axis), matrix)  1.43 us
  transfers between devices with their start and end apart: 21, of which 12 were waited for; matrix products, arithmetic and copies ran while one was open for 12% of the time, Pallas kernels for 0%

profile of v1, /device:TPU:0, one launch (start us, length us, event | category | flops | bytes accessed | tf_op | source)
XLA Modules:
  0.0 67.7 jit_solution(2962310933954504320)
XLA Ops:
  0.0 1.2 %fusion.20 = (bf16[768,128]{1,0:T(8,128)(2,1)S(1)}, bf16[768,128]{1,0:T(8,128)(2,1)S(1)}) fusion(bf16[768,256]{1,0:T(8,128)(2,1)} %param.8), kind=kLoop, calls=%fused_computation.122 | loop fusion | bytes 786432 | tf_op jit(solution)/shard_map/split | solution.py:34
  1.2 1.1 %maximum_select_fusion = bf16[768,256]{1,0:T(8,128)(2,1)S(1)} fusion(bf16[768,256]{1,0:T(8,128)(2,1)} %param.8, bf16[768,128]{1,0:T(8,128)(2,1)S(1)} %get-tuple-element.6, bf16[768,128]{1,0:T(8,128)(2,1)S(1)} %get-tuple-element.5, pred[]{:T(512)S(6)} %eq.4), kind=kLoop, calls=%fused_computation.31 | loop fusion | flops 983040 | bytes 1179649 | tf_op jit(solution)/shard_map/jit(_where)/select_n | solution.py:35
  2.3 1.5 %convolution_convert_fusion.18 = bf16[256,384]{1,0:T(8,128)(2,1)S(1)} fusion(bf16[768,256]{1,0:T(8,128)(2,1)S(1)} %maximum_select_fusion, bf16[768,1152]{1,0:T(8,128)(2,1)} %param.7), kind=kOutput, calls=%fused_computation.25 | convolution fusion | flops 151093248 | bytes 1179648 | tf_op jit(solution)/shard_map/dot_general | solution.py:68
  3.9 2.1 %collective-permute-start.14 = (bf16[1,128,384]{2,1,0:T(8,128)(2,1)S(1)}, bf16[1,128,384]{2,1,0:T(8,128)(2,1)S(1)}, u32[]{:S(2)}, u32[]{:S(2)}) collective-permute-start(bf16[1,128,384]{2,1,0:T(8,128)(2,1)S(1)} %get-tuple-element.53), channel_id=1, source_target_pairs={{0,1},{1,0},{2,3},{3,2},{4,5},{5,4},{6,7},{7,6},{8,9},{9,8},{10,11... | collective-permute-start | bytes 294920 | tf_op jit(solution)/shard_map/ppermute | solution.py:19
  6.9 2.1 %collective-permute-start.7 = (bf16[1,128,384]{2,1,0:T(8,128)(2,1)S(1)}, bf16[1,128,384]{2,1,0:T(8,128)(2,1)S(1)}, u32[]{:S(2)}, u32[]{:S(2)}) collective-permute-start(bf16[1,128,384]{2,1,0:T(8,128)(2,1)S(1)} %get-tuple-element.39), channel_id=1, source_target_pairs={{0,1},{1,0},{2,3},{3,2},{4,5},{5,4},{6,7},{7,6},{8,9},{9,8},{10,11... | collective-permute-start | bytes 294920 | tf_op jit(solution)/shard_map/ppermute | solution.py:19
  11.8 2.6 %collective-permute-start.15 = (bf16[1,128,384]{2,1,0:T(8,128)(2,1)S(1)}, bf16[1,128,384]{2,1,0:T(8,128)(2,1)S(1)}, u32[]{:S(2)}, u32[]{:S(2)}) collective-permute-start(bf16[1,128,384]{2,1,0:T(8,128)(2,1)S(1)} %get-tuple-element.51), channel_id=1, source_target_pairs={{0,2},{1,3},{2,0},{3,1},{4,6},{5,7},{6,4},{7,5},{8,10},{9,11},{10,... | collective-permute-start | bytes 294920 | tf_op jit(solution)/shard_map/ppermute | solution.py:19
  14.8 1.2 %collective-permute-start.1 = (bf16[1,128,384]{2,1,0:T(8,128)(2,1)S(1)}, bf16[1,128,384]{2,1,0:T(8,128)(2,1)S(1)}, u32[]{:S(2)}, u32[]{:S(2)}) collective-permute-start(bf16[1,128,384]{2,1,0:T(8,128)(2,1)S(1)} %get-tuple-element.23), channel_id=1, source_target_pairs={{0,2},{1,3},{2,0},{3,1},{4,6},{5,7},{6,4},{7,5},{8,10},{9,11},{10,... | collective-permute-start | bytes 294920 | tf_op jit(solution)/shard_map/ppermute | solution.py:19
  16.3 1.8 %collective-permute-start.8 = (bf16[1,128,384]{2,1,0:T(8,128)(2,1)S(1)}, bf16[1,128,384]{2,1,0:T(8,128)(2,1)S(1)}, u32[]{:S(2)}, u32[]{:S(2)}) collective-permute-start(bf16[1,128,384]{2,1,0:T(8,128)(2,1)S(1)} %get-tuple-element.37), channel_id=1, source_target_pairs={{0,2},{1,3},{2,0},{3,1},{4,6},{5,7},{6,4},{7,5},{8,10},{9,11},{10,... | collective-permute-start | bytes 294920 | tf_op jit(solution)/shard_map/ppermute | solution.py:19
  18.1 5.8 %collective-permute-done.15 = bf16[1,128,384]{2,1,0:T(8,128)(2,1)S(1)} collective-permute-done((bf16[1,128,384]{2,1,0:T(8,128)(2,1)S(1)}, bf16[1,128,384]{2,1,0:T(8,128)(2,1)S(1)}, u32[]{:S(2)}, u32[]{:S(2)}) %collective-permute-start.15) | collective-permute-done | bytes 98336 | tf_op jit(solution)/shard_map/ppermute | solution.py:19
  24.2 1.6 %collective-permute-start.16 = (bf16[1,128,384]{2,1,0:T(8,128)(2,1)S(1)}, bf16[1,128,384]{2,1,0:T(8,128)(2,1)S(1)}, u32[]{:S(2)}, u32[]{:S(2)}) collective-permute-start(bf16[1,128,384]{2,1,0:T(8,128)(2,1)S(1)} %get-tuple-element.49), channel_id=1, source_target_pairs={{0,16},{4,20},{8,24},{12,28},{16,0},{20,4},{24,8},{28,12},{1,17},{... | collective-permute-start | bytes 294920 | tf_op jit(solution)/shard_map/ppermute | solution.py:19
  26.3 1.6 %collective-permute-start.2 = (bf16[1,128,384]{2,1,0:T(8,128)(2,1)S(1)}, bf16[1,128,384]{2,1,0:T(8,128)(2,1)S(1)}, u32[]{:S(2)}, u32[]{:S(2)}) collective-permute-start(bf16[1,128,384]{2,1,0:T(8,128)(2,1)S(1)} %get-tuple-element.21), channel_id=1, source_target_pairs={{0,16},{4,20},{8,24},{12,28},{16,0},{20,4},{24,8},{28,12},{1,17},{... | collective-permute-start | bytes 294920 | tf_op jit(solution)/shard_map/ppermute | solution.py:19
  29.8 1.6 %collective-permute-start.17 = (bf16[2,64,384]{2,1,0:T(8,128)(2,1)S(1)}, bf16[2,64,384]{2,1,0:T(8,128)(2,1)S(1)}, u32[]{:S(2)}, u32[]{:S(2)}) collective-permute-start(bf16[2,64,384]{2,1,0:T(8,128)(2,1)S(1)} %get-tuple-element.47), channel_id=1, source_target_pairs={{0,8},{4,12},{8,0},{12,4},{16,24},{20,28},{24,16},{28,20},{1,9},{5... | collective-permute-start | bytes 294920 | tf_op jit(solution)/shard_map/ppermute | solution.py:19
  31.9 1.6 %collective-permute-start.3 = (bf16[2,64,384]{2,1,0:T(8,128)(2,1)S(1)}, bf16[2,64,384]{2,1,0:T(8,128)(2,1)S(1)}, u32[]{:S(2)}, u32[]{:S(2)}) collective-permute-start(bf16[2,64,384]{2,1,0:T(8,128)(2,1)S(1)} %get-tuple-element.19), channel_id=1, source_target_pairs={{0,8},{4,12},{8,0},{12,4},{16,24},{20,28},{24,16},{28,20},{1,9},{5... | collective-permute-start | bytes 294920 | tf_op jit(solution)/shard_map/ppermute | solution.py:19
  34.8 1.8 %collective-permute-done.3 = bf16[2,64,384]{2,1,0:T(8,128)(2,1)S(1)} collective-permute-done((bf16[2,64,384]{2,1,0:T(8,128)(2,1)S(1)}, bf16[2,64,384]{2,1,0:T(8,128)(2,1)S(1)}, u32[]{:S(2)}, u32[]{:S(2)}) %collective-permute-start.3) | collective-permute-done | bytes 98336 | tf_op jit(solution)/shard_map/ppermute | solution.py:19
  36.8 1.4 %collective-permute-done.10 = bf16[2,64,384]{2,1,0:T(8,128)(2,1)S(1)} collective-permute-done((bf16[2,64,384]{2,1,0:T(8,128)(2,1)S(1)}, bf16[2,64,384]{2,1,0:T(8,128)(2,1)S(1)}, u32[]{:S(2)}, u32[]{:S(2)}) %collective-permute-start.10) | collective-permute-done | bytes 98336 | tf_op jit(solution)/shard_map/ppermute | solution.py:19
  39.1 3.0 %collective-permute-start.5 = (bf16[1,128,384]{2,1,0:T(8,128)(2,1)S(1)}, bf16[1,128,384]{2,1,0:T(8,128)(2,1)S(1)}, u32[]{:S(2)}, u32[]{:S(2)}) collective-permute-start(bf16[1,128,384]{2,1,0:T(8,128)(2,1)S(1)} %get-tuple-element.15), channel_id=1, source_target_pairs={{0,2},{1,3},{2,0},{3,1},{4,6},{5,7},{6,4},{7,5},{8,10},{9,11},{10,... | collective-permute-start | bytes 294920 | tf_op jit(solution)/shard_map/ppermute | solution.py:19
  42.5 9.0 %collective-permute-done.19 = bf16[1,128,384]{2,1,0:T(8,128)(2,1)S(1)} collective-permute-done((bf16[1,128,384]{2,1,0:T(8,128)(2,1)S(1)}, bf16[1,128,384]{2,1,0:T(8,128)(2,1)S(1)}, u32[]{:S(2)}, u32[]{:S(2)}) %collective-permute-start.19) | collective-permute-done | bytes 98336 | tf_op jit(solution)/shard_map/ppermute | solution.py:19
  51.9 1.7 %collective-permute-done.5 = bf16[1,128,384]{2,1,0:T(8,128)(2,1)S(1)} collective-permute-done((bf16[1,128,384]{2,1,0:T(8,128)(2,1)S(1)}, bf16[1,128,384]{2,1,0:T(8,128)(2,1)S(1)}, u32[]{:S(2)}, u32[]{:S(2)}) %collective-permute-start.5) | collective-permute-done | bytes 98336 | tf_op jit(solution)/shard_map/ppermute | solution.py:19
  54.3 1.2 %collective-permute-done.12 = bf16[1,128,384]{2,1,0:T(8,128)(2,1)S(1)} collective-permute-done((bf16[1,128,384]{2,1,0:T(8,128)(2,1)S(1)}, bf16[1,128,384]{2,1,0:T(8,128)(2,1)S(1)}, u32[]{:S(2)}, u32[]{:S(2)}) %collective-permute-start.12) | collective-permute-done | bytes 98336 | tf_op jit(solution)/shard_map/ppermute | solution.py:19
  56.4 3.3 %collective-permute-done.6 = bf16[1,128,384]{2,1,0:T(8,128)(2,1)S(1)} collective-permute-done((bf16[1,128,384]{2,1,0:T(8,128)(2,1)S(1)}, bf16[1,128,384]{2,1,0:T(8,128)(2,1)S(1)}, u32[]{:S(2)}, u32[]{:S(2)}) %collective-permute-start.6) | collective-permute-done | bytes 98336 | tf_op jit(solution)/shard_map/ppermute | solution.py:19
  59.7 2.0 %collective-permute-done.13 = bf16[1,128,384]{2,1,0:T(8,128)(2,1)S(1)} collective-permute-done((bf16[1,128,384]{2,1,0:T(8,128)(2,1)S(1)}, bf16[1,128,384]{2,1,0:T(8,128)(2,1)S(1)}, u32[]{:S(2)}, u32[]{:S(2)}) %collective-permute-start.13) | collective-permute-done | bytes 98336 | tf_op jit(solution)/shard_map/ppermute | solution.py:19
  62.9 1.4 %fusion.2 = bf16[768,384]{0,1:T(8,128)(2,1)} fusion(bf16[768,256]{1,0:T(8,128)(2,1)S(1)} %copy-done, bf16[256,256]{1,0:T(8,128)(2,1)S(1)} %fusion.6, bf16[256,384]{1,0:T(8,128)(2,1)S(1)} %bitcast.212), kind=kOutput, calls=%fused_computation.9 | convolution fusion | flops 201719808 | bytes 1310720 | tf_op jit(solution)/shard_map/dot_general | solution.py:39
  64.3 1.2 %pad_maximum_fusion = bf16[768,1152]{0,1:T(8,128)(2,1)S(1)} fusion(bf16[768,384]{0,1:T(8,128)(2,1)} %fusion.2, bf16[768,384]{0,1:T(8,128)(2,1)S(1)} %fusion.1, bf16[768,384]{0,1:T(8,128)(2,1)S(1)} %fusion), kind=kLoop, calls=%fused_computation.3 | loop fusion | flops 5308416 | bytes 3538944 | tf_op jit(solution)/shard_map/concatenate | solution.py:81
  65.5 2.2 %copy.25 = bf16[768,1152]{1,0:T(8,128)(2,1)} copy(bf16[768,1152]{0,1:T(8,128)(2,1)S(1)} %pad_maximum_fusion) | data formatting | bytes 3538944 | tf_op jit(solution)/shard_map/concatenate | solution.py:81
  (118 shorter events, 13.0 us)
Async XLA Ops:
  0.0 61.7 %copy-start = (bf16[768,256]{1,0:T(8,128)(2,1)S(1)}, bf16[768,256]{1,0:T(8,128)(2,1)}, u32[]{:S(2)}) copy-start(bf16[768,256]{1,0:T(8,128)(2,1)} %param.12) | copy-start | bytes 1179652
  0.0 5.9 %copy-start.5 = (bf16[768,1152]{1,0:T(8,128)(2,1)S(1)}, bf16[768,1152]{1,0:T(8,128)(2,1)}, u32[]{:S(2)}) copy-start(bf16[768,1152]{1,0:T(8,128)(2,1)} %param.7) | copy-start | bytes 5308420
  3.8 5.3 %copy-start.3 = (bf16[1,2,256,256]{3,2,1,0:T(8,128)(2,1)S(1)}, bf16[1,2,256,256]{3,2,1,0:T(8,128)(2,1)}, u32[]{:S(2)}) copy-start(bf16[1,2,256,256]{3,2,1,0:T(8,128)(2,1)} %param.9) | copy-start | bytes 786436
  3.9 7.7 %collective-permute-start.14 = (bf16[1,128,384]{2,1,0:T(8,128)(2,1)S(1)}, bf16[1,128,384]{2,1,0:T(8,128)(2,1)S(1)}, u32[]{:S(2)}, u32[]{:S(2)}) collective-permute-start(bf16[1,128,384]{2,1,0:T(8,128)(2,1)S(1)} %get-tuple-element.53), channel_id=1, source_target_pairs={{0,1},{1,0},{2,3},{3,2},{4,5},{5,4},{6,7},{7,6},{8,9},{9,8},{10,11... | collective-permute-start | bytes 294920 | tf_op jit(solution)/shard_map/ppermute | solution.py:19
  6.4 8.1 %collective-permute-start = (bf16[1,128,384]{2,1,0:T(8,128)(2,1)S(1)}, bf16[1,128,384]{2,1,0:T(8,128)(2,1)S(1)}, u32[]{:S(2)}, u32[]{:S(2)}) collective-permute-start(bf16[1,128,384]{2,1,0:T(8,128)(2,1)S(1)} %get-tuple-element.25), channel_id=1, source_target_pairs={{0,1},{1,0},{2,3},{3,2},{4,5},{5,4},{6,7},{7,6},{8,9},{9,8},{10,11... | collective-permute-start | bytes 294920 | tf_op jit(solution)/shard_map/ppermute | solution.py:19
  6.9 9.1 %collective-permute-start.7 = (bf16[1,128,384]{2,1,0:T(8,128)(2,1)S(1)}, bf16[1,128,384]{2,1,0:T(8,128)(2,1)S(1)}, u32[]{:S(2)}, u32[]{:S(2)}) collective-permute-start(bf16[1,128,384]{2,1,0:T(8,128)(2,1)S(1)} %get-tuple-element.39), channel_id=1, source_target_pairs={{0,1},{1,0},{2,3},{3,2},{4,5},{5,4},{6,7},{7,6},{8,9},{9,8},{10,11... | collective-permute-start | bytes 294920 | tf_op jit(solution)/shard_map/ppermute | solution.py:19
  11.8 12.1 %collective-permute-start.15 = (bf16[1,128,384]{2,1,0:T(8,128)(2,1)S(1)}, bf16[1,128,384]{2,1,0:T(8,128)(2,1)S(1)}, u32[]{:S(2)}, u32[]{:S(2)}) collective-permute-start(bf16[1,128,384]{2,1,0:T(8,128)(2,1)S(1)} %get-tuple-element.51), channel_id=1, source_target_pairs={{0,2},{1,3},{2,0},{3,1},{4,6},{5,7},{6,4},{7,5},{8,10},{9,11},{10,... | collective-permute-start | bytes 294920 | tf_op jit(solution)/shard_map/ppermute | solution.py:19
  14.8 11.3 %collective-permute-start.1 = (bf16[1,128,384]{2,1,0:T(8,128)(2,1)S(1)}, bf16[1,128,384]{2,1,0:T(8,128)(2,1)S(1)}, u32[]{:S(2)}, u32[]{:S(2)}) collective-permute-start(bf16[1,128,384]{2,1,0:T(8,128)(2,1)S(1)} %get-tuple-element.23), channel_id=1, source_target_pairs={{0,2},{1,3},{2,0},{3,1},{4,6},{5,7},{6,4},{7,5},{8,10},{9,11},{10,... | collective-permute-start | bytes 294920 | tf_op jit(solution)/shard_map/ppermute | solution.py:19
  16.3 11.6 %collective-permute-start.8 = (bf16[1,128,384]{2,1,0:T(8,128)(2,1)S(1)}, bf16[1,128,384]{2,1,0:T(8,128)(2,1)S(1)}, u32[]{:S(2)}, u32[]{:S(2)}) collective-permute-start(bf16[1,128,384]{2,1,0:T(8,128)(2,1)S(1)} %get-tuple-element.37), channel_id=1, source_target_pairs={{0,2},{1,3},{2,0},{3,1},{4,6},{5,7},{6,4},{7,5},{8,10},{9,11},{10,... | collective-permute-start | bytes 294920 | tf_op jit(solution)/shard_map/ppermute | solution.py:19
  24.2 5.5 %collective-permute-start.16 = (bf16[1,128,384]{2,1,0:T(8,128)(2,1)S(1)}, bf16[1,128,384]{2,1,0:T(8,128)(2,1)S(1)}, u32[]{:S(2)}, u32[]{:S(2)}) collective-permute-start(bf16[1,128,384]{2,1,0:T(8,128)(2,1)S(1)} %get-tuple-element.49), channel_id=1, source_target_pairs={{0,16},{4,20},{8,24},{12,28},{16,0},{20,4},{24,8},{28,12},{1,17},{... | collective-permute-start | bytes 294920 | tf_op jit(solution)/shard_map/ppermute | solution.py:19
  26.3 5.5 %collective-permute-start.2 = (bf16[1,128,384]{2,1,0:T(8,128)(2,1)S(1)}, bf16[1,128,384]{2,1,0:T(8,128)(2,1)S(1)}, u32[]{:S(2)}, u32[]{:S(2)}) collective-permute-start(bf16[1,128,384]{2,1,0:T(8,128)(2,1)S(1)} %get-tuple-element.21), channel_id=1, source_target_pairs={{0,16},{4,20},{8,24},{12,28},{16,0},{20,4},{24,8},{28,12},{1,17},{... | collective-permute-start | bytes 294920 | tf_op jit(solution)/shard_map/ppermute | solution.py:19
  28.2 5.3 %collective-permute-start.9 = (bf16[1,128,384]{2,1,0:T(8,128)(2,1)S(1)}, bf16[1,128,384]{2,1,0:T(8,128)(2,1)S(1)}, u32[]{:S(2)}, u32[]{:S(2)}) collective-permute-start(bf16[1,128,384]{2,1,0:T(8,128)(2,1)S(1)} %get-tuple-element.35), channel_id=1, source_target_pairs={{0,16},{4,20},{8,24},{12,28},{16,0},{20,4},{24,8},{28,12},{1,17},{... | collective-permute-start | bytes 294920 | tf_op jit(solution)/shard_map/ppermute | solution.py:19
  29.8 4.9 %collective-permute-start.17 = (bf16[2,64,384]{2,1,0:T(8,128)(2,1)S(1)}, bf16[2,64,384]{2,1,0:T(8,128)(2,1)S(1)}, u32[]{:S(2)}, u32[]{:S(2)}) collective-permute-start(bf16[2,64,384]{2,1,0:T(8,128)(2,1)S(1)} %get-tuple-element.47), channel_id=1, source_target_pairs={{0,8},{4,12},{8,0},{12,4},{16,24},{20,28},{24,16},{28,20},{1,9},{5... | collective-permute-start | bytes 294920 | tf_op jit(solution)/shard_map/ppermute | solution.py:19
  31.9 4.8 %collective-permute-start.3 = (bf16[2,64,384]{2,1,0:T(8,128)(2,1)S(1)}, bf16[2,64,384]{2,1,0:T(8,128)(2,1)S(1)}, u32[]{:S(2)}, u32[]{:S(2)}) collective-permute-start(bf16[2,64,384]{2,1,0:T(8,128)(2,1)S(1)} %get-tuple-element.19), channel_id=1, source_target_pairs={{0,8},{4,12},{8,0},{12,4},{16,24},{20,28},{24,16},{28,20},{1,9},{5... | collective-permute-start | bytes 294920 | tf_op jit(solution)/shard_map/ppermute | solution.py:19
  33.5 4.7 %collective-permute-start.10 = (bf16[2,64,384]{2,1,0:T(8,128)(2,1)S(1)}, bf16[2,64,384]{2,1,0:T(8,128)(2,1)S(1)}, u32[]{:S(2)}, u32[]{:S(2)}) collective-permute-start(bf16[2,64,384]{2,1,0:T(8,128)(2,1)S(1)} %get-tuple-element.33), channel_id=1, source_target_pairs={{0,8},{4,12},{8,0},{12,4},{16,24},{20,28},{24,16},{28,20},{1,9},{5... | collective-permute-start | bytes 294920 | tf_op jit(solution)/shard_map/ppermute | solution.py:19
  34.7 3.6 %collective-permute-start.18 = (bf16[4,32,384]{2,1,0:T(8,128)(2,1)S(1)}, bf16[4,32,384]{2,1,0:T(8,128)(2,1)S(1)}, u32[]{:S(2)}, u32[]{:S(2)}) collective-permute-start(bf16[4,32,384]{2,1,0:T(8,128)(2,1)S(1)} %get-tuple-element.45), channel_id=1, source_target_pairs={{0,4},{4,0},{8,12},{12,8},{16,20},{20,16},{24,28},{28,24},{1,5},{5... | collective-permute-start | bytes 294920 | tf_op jit(solution)/shard_map/ppermute | solution.py:19
  36.7 2.1 %collective-permute-start.4 = (bf16[4,32,384]{2,1,0:T(8,128)(2,1)S(1)}, bf16[4,32,384]{2,1,0:T(8,128)(2,1)S(1)}, u32[]{:S(2)}, u32[]{:S(2)}) collective-permute-start(bf16[4,32,384]{2,1,0:T(8,128)(2,1)S(1)} %get-tuple-element.17), channel_id=1, source_target_pairs={{0,4},{4,0},{8,12},{12,8},{16,20},{20,16},{24,28},{28,24},{1,5},{5... | collective-permute-start | bytes 294920 | tf_op jit(solution)/shard_map/ppermute | solution.py:19
  38.2 3.9 %collective-permute-start.11 = (bf16[4,32,384]{2,1,0:T(8,128)(2,1)S(1)}, bf16[4,32,384]{2,1,0:T(8,128)(2,1)S(1)}, u32[]{:S(2)}, u32[]{:S(2)}) collective-permute-start(bf16[4,32,384]{2,1,0:T(8,128)(2,1)S(1)} %get-tuple-element.31), channel_id=1, source_target_pairs={{0,4},{4,0},{8,12},{12,8},{16,20},{20,16},{24,28},{28,24},{1,5},{5... | collective-permute-start | bytes 294920 | tf_op jit(solution)/shard_map/ppermute | solution.py:19
  38.7 12.9 %collective-permute-start.19 = (bf16[1,128,384]{2,1,0:T(8,128)(2,1)S(1)}, bf16[1,128,384]{2,1,0:T(8,128)(2,1)S(1)}, u32[]{:S(2)}, u32[]{:S(2)}) collective-permute-start(bf16[1,128,384]{2,1,0:T(8,128)(2,1)S(1)} %get-tuple-element.43), channel_id=1, source_target_pairs={{0,2},{1,3},{2,0},{3,1},{4,6},{5,7},{6,4},{7,5},{8,10},{9,11},{10,... | collective-permute-start | bytes 294920 | tf_op jit(solution)/shard_map/ppermute | solution.py:19
  39.1 14.5 %collective-permute-start.5 = (bf16[1,128,384]{2,1,0:T(8,128)(2,1)S(1)}, bf16[1,128,384]{2,1,0:T(8,128)(2,1)S(1)}, u32[]{:S(2)}, u32[]{:S(2)}) collective-permute-start(bf16[1,128,384]{2,1,0:T(8,128)(2,1)S(1)} %get-tuple-element.15), channel_id=1, source_target_pairs={{0,2},{1,3},{2,0},{3,1},{4,6},{5,7},{6,4},{7,5},{8,10},{9,11},{10,... | collective-permute-start | bytes 294920 | tf_op jit(solution)/shard_map/ppermute | solution.py:19
  42.4 13.0 %collective-permute-start.12 = (bf16[1,128,384]{2,1,0:T(8,128)(2,1)S(1)}, bf16[1,128,384]{2,1,0:T(8,128)(2,1)S(1)}, u32[]{:S(2)}, u32[]{:S(2)}) collective-permute-start(bf16[1,128,384]{2,1,0:T(8,128)(2,1)S(1)} %get-tuple-element.29), channel_id=1, source_target_pairs={{0,2},{1,3},{2,0},{3,1},{4,6},{5,7},{6,4},{7,5},{8,10},{9,11},{10,... | collective-permute-start | bytes 294920 | tf_op jit(solution)/shard_map/ppermute | solution.py:19
  51.8 11.0 %collective-permute-start.20 = (bf16[1,128,384]{2,1,0:T(8,128)(2,1)S(1)}, bf16[1,128,384]{2,1,0:T(8,128)(2,1)S(1)}, u32[]{:S(2)}, u32[]{:S(2)}) collective-permute-start(bf16[1,128,384]{2,1,0:T(8,128)(2,1)S(1)} %get-tuple-element.41), channel_id=1, source_target_pairs={{0,1},{1,0},{2,3},{3,2},{4,5},{5,4},{6,7},{7,6},{8,9},{9,8},{10,11... | collective-permute-start | bytes 294920 | tf_op jit(solution)/shard_map/ppermute | solution.py:19
  53.9 5.7 %collective-permute-start.6 = (bf16[1,128,384]{2,1,0:T(8,128)(2,1)S(1)}, bf16[1,128,384]{2,1,0:T(8,128)(2,1)S(1)}, u32[]{:S(2)}, u32[]{:S(2)}) collective-permute-start(bf16[1,128,384]{2,1,0:T(8,128)(2,1)S(1)} %get-tuple-element.13), channel_id=1, source_target_pairs={{0,1},{1,0},{2,3},{3,2},{4,5},{5,4},{6,7},{7,6},{8,9},{9,8},{10,11... | collective-permute-start | bytes 294920 | tf_op jit(solution)/shard_map/ppermute | solution.py:19
  55.8 5.9 %collective-permute-start.13 = (bf16[1,128,384]{2,1,0:T(8,128)(2,1)S(1)}, bf16[1,128,384]{2,1,0:T(8,128)(2,1)S(1)}, u32[]{:S(2)}, u32[]{:S(2)}) collective-permute-start(bf16[1,128,384]{2,1,0:T(8,128)(2,1)S(1)} %get-tuple-element.27), channel_id=1, source_target_pairs={{0,1},{1,0},{2,3},{3,2},{4,5},{5,4},{6,7},{7,6},{8,9},{9,8},{10,11... | collective-permute-start | bytes 294920 | tf_op jit(solution)/shard_map/ppermute | solution.py:19
  (3 other events, 8.8 us)

commit v2 on v1

--- a/solution.py
+++ b/solution.py
@@ -17,6 +17,14 @@
 def swap(block, axis, distance):
     count = lax.axis_size(axis)
     return lax.ppermute(block, axis, [(i, i ^ distance) for i in range(count)])
+
+
+def gathered(block, axis, distance):
+    count = lax.axis_size(axis)
+    pairs = [[i, i ^ distance] for i in range(count) if not i & distance]
+    both = lax.all_gather(block, axis, axis_index_groups=pairs)
+    upper = lax.axis_index(axis) & distance
+    return jnp.where(upper != 0, both[0], both[1])
 
 
 def relative_rows(matrix, order):
@@ -43,7 +51,7 @@
     rows, columns = coeffs.shape
     slots = coeffs.reshape(-1, 2, block, columns)
     keep, send = slots[:, 0], slots[:, 1]
-    got = swap(send, axis, distance)
+    got = swap(send, axis, distance) if axis == "sub" else gathered(send, axis, distance)
     return jnp.stack([keep, got], axis=1).reshape(rows, columns)
 
 

time: 67.9 us -> 86.1 us (1.27)
  blocking collectives: 0 us -> 37.8 us
  waiting for transfers between devices: 27.6 us -> 14.5 us
  starting transfers between devices: 22.8 us -> 16.1 us
    all_gather x0 -> x9, blocking collectives: none -> 37.8 us  [gathered(): both = lax.all_gather(block, axis, axis_index_groups=pairs)]
    ppermute x21 -> x12, waiting for transfers between devices: 27.6 us -> 14.5 us  [swap(): return lax.ppermute(block, axis, [(i, i ^ distance) for i in range(count)])]
    ppermute x21 -> x12, starting transfers between devices: 22.8 us -> 16.1 us  [swap(): return lax.ppermute(block, axis, [(i, i ^ distance) for i in range(count)])]
  transfers between devices with their start and end apart: 21 -> 12, of which waited for: 12 -> 4; matrix products, arithmetic and copies ran while one was open for 12% -> 9% of each run, Pallas kernels for 0% -> 0%
where the time goes in v2:
time: 86.1 us; the launch traced here: 85.8 us
  blocking collectives  37.8 us (44%)
  starting transfers between devices  16.1 us (19%)
  waiting for transfers between devices  14.5 us (17%)
  matrix products  7.49 us (9%)
  local copies, waits for them, and re-layouts  5.86 us (7%)
  other arithmetic  3.33 us (4%)
    all_gather x9, blocking collectives, gathered(): both = lax.all_gather(block, axis, axis_index_groups=pairs)  37.8 us
    ppermute x12, starting transfers between devices, swap(): return lax.ppermute(block, axis, [(i, i ^ distance) for i in range(count)])  16.1 us
    ppermute x12, waiting for transfers between devices, swap(): return lax.ppermute(block, axis, [(i, i ^ distance) for i in range(count)])  14.5 us
    dot_general x15, matrix products, product(): jnp.dot(left, right, preferred_element_type=jnp.float32)  5.25 us
    dot_general x3, matrix products, local(): lax.dot_general(first, signal[:, low:high], (((0,), (0,)), ((), ())), pre...  2.24 us
    concatenate x1, local copies, waits for them, and re-layouts, local(): return jnp.concatenate(outs, axis=1)  2.21 us
  transfers between devices with their start and end apart: 12, of which 4 were waited for; matrix products, arithmetic and copies ran while one was open for 9% of the time, Pallas kernels for 0%

profile of v2, /device:TPU:0, one launch (start us, length us, event | category | flops | bytes accessed | tf_op | source)
XLA Modules:
  0.0 85.8 jit_solution(8403028864345990525)
XLA Ops:
  0.0 1.2 %fusion.14 = (bf16[768,128]{1,0:T(8,128)(2,1)S(1)}, bf16[768,128]{1,0:T(8,128)(2,1)S(1)}) fusion(bf16[768,256]{1,0:T(8,128)(2,1)} %param.8), kind=kLoop, calls=%fused_computation.116 | loop fusion | bytes 786432 | tf_op jit(solution)/shard_map/split | solution.py:42
  2.3 1.5 %convolution_convert_fusion.18 = bf16[256,384]{1,0:T(8,128)(2,1)S(1)} fusion(bf16[768,256]{1,0:T(8,128)(2,1)S(1)} %maximum_select_fusion, bf16[768,1152]{1,0:T(8,128)(2,1)} %param.7), kind=kOutput, calls=%fused_computation.25 | convolution fusion | flops 151093248 | bytes 1179648 | tf_op jit(solution)/shard_map/dot_general | solution.py:76
  3.9 2.1 %collective-permute-start.8 = (bf16[1,128,384]{2,1,0:T(8,128)(2,1)S(1)}, bf16[1,128,384]{2,1,0:T(8,128)(2,1)S(1)}, u32[]{:S(2)}, u32[]{:S(2)}) collective-permute-start(bf16[1,128,384]{2,1,0:T(8,128)(2,1)S(1)} %get-tuple-element.53), channel_id=1, source_target_pairs={{0,1},{1,0},{2,3},{3,2},{4,5},{5,4},{6,7},{7,6},{8,9},{9,8},{10,11... | collective-permute-start | bytes 294920 | tf_op jit(solution)/shard_map/ppermute | solution.py:19
  6.9 2.1 %collective-permute-start.4 = (bf16[1,128,384]{2,1,0:T(8,128)(2,1)S(1)}, bf16[1,128,384]{2,1,0:T(8,128)(2,1)S(1)}, u32[]{:S(2)}, u32[]{:S(2)}) collective-permute-start(bf16[1,128,384]{2,1,0:T(8,128)(2,1)S(1)} %get-tuple-element.39), channel_id=1, source_target_pairs={{0,1},{1,0},{2,3},{3,2},{4,5},{5,4},{6,7},{7,6},{8,9},{9,8},{10,11... | collective-permute-start | bytes 294920 | tf_op jit(solution)/shard_map/ppermute | solution.py:19
  11.8 2.6 %collective-permute-start.9 = (bf16[1,128,384]{2,1,0:T(8,128)(2,1)S(1)}, bf16[1,128,384]{2,1,0:T(8,128)(2,1)S(1)}, u32[]{:S(2)}, u32[]{:S(2)}) collective-permute-start(bf16[1,128,384]{2,1,0:T(8,128)(2,1)S(1)} %get-tuple-element.51), channel_id=1, source_target_pairs={{0,2},{1,3},{2,0},{3,1},{4,6},{5,7},{6,4},{7,5},{8,10},{9,11},{10,... | collective-permute-start | bytes 294920 | tf_op jit(solution)/shard_map/ppermute | solution.py:19
  14.8 1.2 %collective-permute-start.1 = (bf16[1,128,384]{2,1,0:T(8,128)(2,1)S(1)}, bf16[1,128,384]{2,1,0:T(8,128)(2,1)S(1)}, u32[]{:S(2)}, u32[]{:S(2)}) collective-permute-start(bf16[1,128,384]{2,1,0:T(8,128)(2,1)S(1)} %get-tuple-element.23), channel_id=1, source_target_pairs={{0,2},{1,3},{2,0},{3,1},{4,6},{5,7},{6,4},{7,5},{8,10},{9,11},{10,... | collective-permute-start | bytes 294920 | tf_op jit(solution)/shard_map/ppermute | solution.py:19
  16.3 1.8 %collective-permute-start.5 = (bf16[1,128,384]{2,1,0:T(8,128)(2,1)S(1)}, bf16[1,128,384]{2,1,0:T(8,128)(2,1)S(1)}, u32[]{:S(2)}, u32[]{:S(2)}) collective-permute-start(bf16[1,128,384]{2,1,0:T(8,128)(2,1)S(1)} %get-tuple-element.37), channel_id=1, source_target_pairs={{0,2},{1,3},{2,0},{3,1},{4,6},{5,7},{6,4},{7,5},{8,10},{9,11},{10,... | collective-permute-start | bytes 294920 | tf_op jit(solution)/shard_map/ppermute | solution.py:19
  18.1 5.8 %collective-permute-done.9 = bf16[1,128,384]{2,1,0:T(8,128)(2,1)S(1)} collective-permute-done((bf16[1,128,384]{2,1,0:T(8,128)(2,1)S(1)}, bf16[1,128,384]{2,1,0:T(8,128)(2,1)S(1)}, u32[]{:S(2)}, u32[]{:S(2)}) %collective-permute-start.9) | collective-permute-done | bytes 98336 | tf_op jit(solution)/shard_map/ppermute | solution.py:19
  24.2 5.3 %all_gather.33 = bf16[2,1,128,384]{3,2,1,0:T(8,128)(2,1)S(1)} all-gather(bf16[1,1,128,384]{3,2,1,0:T(8,128)(2,1)S(1)} %get-tuple-element.49), channel_id=1, replica_groups={{0,16},{4,20},{8,24},{12,28},{1,17},{5,21},{9,25},{13,29},{2,18},{6,22}..., dimensions={0}, use_global_device_ids=true | all-gather | bytes 294912 | tf_op jit(solution)/shard_map/all_gather | solution.py:25
  29.6 5.3 %all-gather.4 = bf16[4,1,64,384]{3,2,1,0:T(8,128)(2,1)S(1)} all-gather(bf16[2,1,64,384]{3,2,1,0:T(8,128)(2,1)S(1)} %get-tuple-element.47), channel_id=6, replica_groups={{0,8},{4,12},{16,24},{20,28},{1,9},{5,13},{17,25},{21,29},{2,10},{6,14}..., dimensions={0}, use_global_device_ids=true | all-gather | bytes 294912 | tf_op jit(solution)/shard_map/all_gather | solution.py:25
  35.0 1.9 %all-gather.5 = bf16[8,1,32,384]{3,2,1,0:T(8,128)(2,1)S(1)} all-gather(bf16[4,1,32,384]{3,2,1,0:T(8,128)(2,1)S(1)} %get-tuple-element.45), channel_id=7, replica_groups={{0,4},{8,12},{16,20},{24,28},{1,5},{9,13},{17,21},{25,29},{2,6},{10,14}..., dimensions={0}, use_global_device_ids=true | all-gather | bytes 294912 | tf_op jit(solution)/shard_map/all_gather | solution.py:25
  37.9 5.5 %all_gather.30 = bf16[2,1,128,384]{3,2,1,0:T(8,128)(2,1)S(1)} all-gather(bf16[1,1,128,384]{3,2,1,0:T(8,128)(2,1)S(1)} %get-tuple-element.35), channel_id=1, replica_groups={{0,16},{4,20},{8,24},{12,28},{1,17},{5,21},{9,25},{13,29},{2,18},{6,22}..., dimensions={0}, use_global_device_ids=true | all-gather | bytes 294912 | tf_op jit(solution)/shard_map/all_gather | solution.py:25
  43.5 5.3 %all-gather.2 = bf16[4,1,64,384]{3,2,1,0:T(8,128)(2,1)S(1)} all-gather(bf16[2,1,64,384]{3,2,1,0:T(8,128)(2,1)S(1)} %get-tuple-element.33), channel_id=4, replica_groups={{0,8},{4,12},{16,24},{20,28},{1,9},{5,13},{17,25},{21,29},{2,10},{6,14}..., dimensions={0}, use_global_device_ids=true | all-gather | bytes 294912 | tf_op jit(solution)/shard_map/all_gather | solution.py:25
  48.9 1.9 %all-gather.3 = bf16[8,1,32,384]{3,2,1,0:T(8,128)(2,1)S(1)} all-gather(bf16[4,1,32,384]{3,2,1,0:T(8,128)(2,1)S(1)} %get-tuple-element.31), channel_id=5, replica_groups={{0,4},{8,12},{16,20},{24,28},{1,5},{9,13},{17,21},{25,29},{2,6},{10,14}..., dimensions={0}, use_global_device_ids=true | all-gather | bytes 294912 | tf_op jit(solution)/shard_map/all_gather | solution.py:25
  51.2 2.7 %collective-permute-start.6 = (bf16[1,128,384]{2,1,0:T(8,128)(2,1)S(1)}, bf16[1,128,384]{2,1,0:T(8,128)(2,1)S(1)}, u32[]{:S(2)}, u32[]{:S(2)}) collective-permute-start(bf16[1,128,384]{2,1,0:T(8,128)(2,1)S(1)} %get-tuple-element.29), channel_id=1, source_target_pairs={{0,2},{1,3},{2,0},{3,1},{4,6},{5,7},{6,4},{7,5},{8,10},{9,11},{10,... | collective-permute-start | bytes 294920 | tf_op jit(solution)/shard_map/ppermute | solution.py:19
  53.9 5.3 %all_gather.27 = bf16[2,1,128,384]{3,2,1,0:T(8,128)(2,1)S(1)} all-gather(bf16[1,1,128,384]{3,2,1,0:T(8,128)(2,1)S(1)} %get-tuple-element.21), channel_id=1, replica_groups={{0,16},{4,20},{8,24},{12,28},{1,17},{5,21},{9,25},{13,29},{2,18},{6,22}..., dimensions={0}, use_global_device_ids=true | all-gather | bytes 294912 | tf_op jit(solution)/shard_map/all_gather | solution.py:25
  59.2 5.3 %all-gather = bf16[4,1,64,384]{3,2,1,0:T(8,128)(2,1)S(1)} all-gather(bf16[2,1,64,384]{3,2,1,0:T(8,128)(2,1)S(1)} %get-tuple-element.19), channel_id=2, replica_groups={{0,8},{4,12},{16,24},{20,28},{1,9},{5,13},{17,25},{21,29},{2,10},{6,14}..., dimensions={0}, use_global_device_ids=true | all-gather | bytes 294912 | tf_op jit(solution)/shard_map/all_gather | solution.py:25
  64.6 1.9 %all-gather.1 = bf16[8,1,32,384]{3,2,1,0:T(8,128)(2,1)S(1)} all-gather(bf16[4,1,32,384]{3,2,1,0:T(8,128)(2,1)S(1)} %get-tuple-element.17), channel_id=3, replica_groups={{0,4},{8,12},{16,20},{24,28},{1,5},{9,13},{17,21},{25,29},{2,6},{10,14}..., dimensions={0}, use_global_device_ids=true | all-gather | bytes 294912 | tf_op jit(solution)/shard_map/all_gather | solution.py:25
  67.5 2.8 %collective-permute-start.11 = (bf16[1,128,384]{2,1,0:T(8,128)(2,1)S(1)}, bf16[1,128,384]{2,1,0:T(8,128)(2,1)S(1)}, u32[]{:S(2)}, u32[]{:S(2)}) collective-permute-start(bf16[1,128,384]{2,1,0:T(8,128)(2,1)S(1)} %get-tuple-element.41), channel_id=1, source_target_pairs={{0,1},{1,0},{2,3},{3,2},{4,5},{5,4},{6,7},{7,6},{8,9},{9,8},{10,11... | collective-permute-start | bytes 294920 | tf_op jit(solution)/shard_map/ppermute | solution.py:19
  70.7 4.0 %collective-permute-done.2 = bf16[1,128,384]{2,1,0:T(8,128)(2,1)S(1)} collective-permute-done((bf16[1,128,384]{2,1,0:T(8,128)(2,1)S(1)}, bf16[1,128,384]{2,1,0:T(8,128)(2,1)S(1)}, u32[]{:S(2)}, u32[]{:S(2)}) %collective-permute-start.2) | collective-permute-done | bytes 98336 | tf_op jit(solution)/shard_map/ppermute | solution.py:19
  75.1 2.2 %collective-permute-done.7 = bf16[1,128,384]{2,1,0:T(8,128)(2,1)S(1)} collective-permute-done((bf16[1,128,384]{2,1,0:T(8,128)(2,1)S(1)}, bf16[1,128,384]{2,1,0:T(8,128)(2,1)S(1)}, u32[]{:S(2)}, u32[]{:S(2)}) %collective-permute-start.7) | collective-permute-done | bytes 98336 | tf_op jit(solution)/shard_map/ppermute | solution.py:19
  77.4 2.4 %collective-permute-done.3 = bf16[1,128,384]{2,1,0:T(8,128)(2,1)S(1)} collective-permute-done((bf16[1,128,384]{2,1,0:T(8,128)(2,1)S(1)}, bf16[1,128,384]{2,1,0:T(8,128)(2,1)S(1)}, u32[]{:S(2)}, u32[]{:S(2)}) %collective-permute-start.3) | collective-permute-done | bytes 98336 | tf_op jit(solution)/shard_map/ppermute | solution.py:19
  81.0 1.4 %fusion.2 = bf16[768,384]{0,1:T(8,128)(2,1)} fusion(bf16[768,256]{1,0:T(8,128)(2,1)S(1)} %copy-done, bf16[256,256]{1,0:T(8,128)(2,1)S(1)} %fusion.6, bf16[256,384]{1,0:T(8,128)(2,1)S(1)} %bitcast.176), kind=kOutput, calls=%fused_computation.9 | convolution fusion | flops 201719808 | bytes 1310720 | tf_op jit(solution)/shard_map/dot_general | solution.py:47
  83.6 2.2 %copy.12 = bf16[768,1152]{1,0:T(8,128)(2,1)} copy(bf16[768,1152]{0,1:T(8,128)(2,1)S(1)} %pad_maximum_fusion) | data formatting | bytes 3538944 | tf_op jit(solution)/shard_map/concatenate | solution.py:89
  (115 shorter events, 11.1 us)
Async XLA Ops:
  0.0 79.8 %copy-start = (bf16[768,256]{1,0:T(8,128)(2,1)S(1)}, bf16[768,256]{1,0:T(8,128)(2,1)}, u32[]{:S(2)}) copy-start(bf16[768,256]{1,0:T(8,128)(2,1)} %param.12) | copy-start | bytes 1179652
  0.0 5.9 %copy-start.5 = (bf16[768,1152]{1,0:T(8,128)(2,1)S(1)}, bf16[768,1152]{1,0:T(8,128)(2,1)}, u32[]{:S(2)}) copy-start(bf16[768,1152]{1,0:T(8,128)(2,1)} %param.7) | copy-start | bytes 5308420
  3.8 5.2 %copy-start.4 = (bf16[1,256,256]{2,1,0:T(8,128)(2,1)S(1)}, bf16[1,256,256]{2,1,0:T(8,128)(2,1)}, u32[]{:S(2)}) copy-start(bf16[1,256,256]{2,1,0:T(8,128)(2,1)} %param.10) | copy-start | bytes 393220
  3.8 5.3 %copy-start.3 = (bf16[1,2,256,256]{3,2,1,0:T(8,128)(2,1)S(1)}, bf16[1,2,256,256]{3,2,1,0:T(8,128)(2,1)}, u32[]{:S(2)}) copy-start(bf16[1,2,256,256]{3,2,1,0:T(8,128)(2,1)} %param.9) | copy-start | bytes 786436
  3.9 7.7 %collective-permute-start.8 = (bf16[1,128,384]{2,1,0:T(8,128)(2,1)S(1)}, bf16[1,128,384]{2,1,0:T(8,128)(2,1)S(1)}, u32[]{:S(2)}, u32[]{:S(2)}) collective-permute-start(bf16[1,128,384]{2,1,0:T(8,128)(2,1)S(1)} %get-tuple-element.53), channel_id=1, source_target_pairs={{0,1},{1,0},{2,3},{3,2},{4,5},{5,4},{6,7},{7,6},{8,9},{9,8},{10,11... | collective-permute-start | bytes 294920 | tf_op jit(solution)/shard_map/ppermute | solution.py:19
  6.3 2.8 %copy-start.2 = (bf16[1,2,256,256]{3,2,1,0:T(8,128)(2,1)S(1)}, bf16[1,2,256,256]{3,2,1,0:T(8,128)(2,1)}, u32[]{:S(2)}) copy-start(bf16[1,2,256,256]{3,2,1,0:T(8,128)(2,1)} %param.11) | copy-start | bytes 786436
  6.4 8.1 %collective-permute-start = (bf16[1,128,384]{2,1,0:T(8,128)(2,1)S(1)}, bf16[1,128,384]{2,1,0:T(8,128)(2,1)S(1)}, u32[]{:S(2)}, u32[]{:S(2)}) collective-permute-start(bf16[1,128,384]{2,1,0:T(8,128)(2,1)S(1)} %get-tuple-element.25), channel_id=1, source_target_pairs={{0,1},{1,0},{2,3},{3,2},{4,5},{5,4},{6,7},{7,6},{8,9},{9,8},{10,11... | collective-permute-start | bytes 294920 | tf_op jit(solution)/shard_map/ppermute | solution.py:19
  6.9 9.1 %collective-permute-start.4 = (bf16[1,128,384]{2,1,0:T(8,128)(2,1)S(1)}, bf16[1,128,384]{2,1,0:T(8,128)(2,1)S(1)}, u32[]{:S(2)}, u32[]{:S(2)}) collective-permute-start(bf16[1,128,384]{2,1,0:T(8,128)(2,1)S(1)} %get-tuple-element.39), channel_id=1, source_target_pairs={{0,1},{1,0},{2,3},{3,2},{4,5},{5,4},{6,7},{7,6},{8,9},{9,8},{10,11... | collective-permute-start | bytes 294920 | tf_op jit(solution)/shard_map/ppermute | solution.py:19
  9.4 0.8 copy-start.1
  11.8 12.1 %collective-permute-start.9 = (bf16[1,128,384]{2,1,0:T(8,128)(2,1)S(1)}, bf16[1,128,384]{2,1,0:T(8,128)(2,1)S(1)}, u32[]{:S(2)}, u32[]{:S(2)}) collective-permute-start(bf16[1,128,384]{2,1,0:T(8,128)(2,1)S(1)} %get-tuple-element.51), channel_id=1, source_target_pairs={{0,2},{1,3},{2,0},{3,1},{4,6},{5,7},{6,4},{7,5},{8,10},{9,11},{10,... | collective-permute-start | bytes 294920 | tf_op jit(solution)/shard_map/ppermute | solution.py:19
  14.8 22.6 %collective-permute-start.1 = (bf16[1,128,384]{2,1,0:T(8,128)(2,1)S(1)}, bf16[1,128,384]{2,1,0:T(8,128)(2,1)S(1)}, u32[]{:S(2)}, u32[]{:S(2)}) collective-permute-start(bf16[1,128,384]{2,1,0:T(8,128)(2,1)S(1)} %get-tuple-element.23), channel_id=1, source_target_pairs={{0,2},{1,3},{2,0},{3,1},{4,6},{5,7},{6,4},{7,5},{8,10},{9,11},{10,... | collective-permute-start | bytes 294920 | tf_op jit(solution)/shard_map/ppermute | solution.py:19
  16.3 21.3 %collective-permute-start.5 = (bf16[1,128,384]{2,1,0:T(8,128)(2,1)S(1)}, bf16[1,128,384]{2,1,0:T(8,128)(2,1)S(1)}, u32[]{:S(2)}, u32[]{:S(2)}) collective-permute-start(bf16[1,128,384]{2,1,0:T(8,128)(2,1)S(1)} %get-tuple-element.37), channel_id=1, source_target_pairs={{0,2},{1,3},{2,0},{3,1},{4,6},{5,7},{6,4},{7,5},{8,10},{9,11},{10,... | collective-permute-start | bytes 294920 | tf_op jit(solution)/shard_map/ppermute | solution.py:19
  37.2 30.0 %collective-permute-start.10 = (bf16[1,128,384]{2,1,0:T(8,128)(2,1)S(1)}, bf16[1,128,384]{2,1,0:T(8,128)(2,1)S(1)}, u32[]{:S(2)}, u32[]{:S(2)}) collective-permute-start(bf16[1,128,384]{2,1,0:T(8,128)(2,1)S(1)} %get-tuple-element.43), channel_id=1, source_target_pairs={{0,2},{1,3},{2,0},{3,1},{4,6},{5,7},{6,4},{7,5},{8,10},{9,11},{10,... | collective-permute-start | bytes 294920 | tf_op jit(solution)/shard_map/ppermute | solution.py:19
  51.2 19.2 %collective-permute-start.6 = (bf16[1,128,384]{2,1,0:T(8,128)(2,1)S(1)}, bf16[1,128,384]{2,1,0:T(8,128)(2,1)S(1)}, u32[]{:S(2)}, u32[]{:S(2)}) collective-permute-start(bf16[1,128,384]{2,1,0:T(8,128)(2,1)S(1)} %get-tuple-element.29), channel_id=1, source_target_pairs={{0,2},{1,3},{2,0},{3,1},{4,6},{5,7},{6,4},{7,5},{8,10},{9,11},{10,... | collective-permute-start | bytes 294920 | tf_op jit(solution)/shard_map/ppermute | solution.py:19
  66.9 7.8 %collective-permute-start.2 = (bf16[1,128,384]{2,1,0:T(8,128)(2,1)S(1)}, bf16[1,128,384]{2,1,0:T(8,128)(2,1)S(1)}, u32[]{:S(2)}, u32[]{:S(2)}) collective-permute-start(bf16[1,128,384]{2,1,0:T(8,128)(2,1)S(1)} %get-tuple-element.15), channel_id=1, source_target_pairs={{0,2},{1,3},{2,0},{3,1},{4,6},{5,7},{6,4},{7,5},{8,10},{9,11},{10,... | collective-permute-start | bytes 294920 | tf_op jit(solution)/shard_map/ppermute | solution.py:19
  67.5 13.4 %collective-permute-start.11 = (bf16[1,128,384]{2,1,0:T(8,128)(2,1)S(1)}, bf16[1,128,384]{2,1,0:T(8,128)(2,1)S(1)}, u32[]{:S(2)}, u32[]{:S(2)}) collective-permute-start(bf16[1,128,384]{2,1,0:T(8,128)(2,1)S(1)} %get-tuple-element.41), channel_id=1, source_target_pairs={{0,1},{1,0},{2,3},{3,2},{4,5},{5,4},{6,7},{7,6},{8,9},{9,8},{10,11... | collective-permute-start | bytes 294920 | tf_op jit(solution)/shard_map/ppermute | solution.py:19
  70.6 6.7 %collective-permute-start.7 = (bf16[1,128,384]{2,1,0:T(8,128)(2,1)S(1)}, bf16[1,128,384]{2,1,0:T(8,128)(2,1)S(1)}, u32[]{:S(2)}, u32[]{:S(2)}) collective-permute-start(bf16[1,128,384]{2,1,0:T(8,128)(2,1)S(1)} %get-tuple-element.27), channel_id=1, source_target_pairs={{0,1},{1,0},{2,3},{3,2},{4,5},{5,4},{6,7},{7,6},{8,9},{9,8},{10,11... | collective-permute-start | bytes 294920 | tf_op jit(solution)/shard_map/ppermute | solution.py:19
  75.0 4.7 %collective-permute-start.3 = (bf16[1,128,384]{2,1,0:T(8,128)(2,1)S(1)}, bf16[1,128,384]{2,1,0:T(8,128)(2,1)S(1)}, u32[]{:S(2)}, u32[]{:S(2)}) collective-permute-start(bf16[1,128,384]{2,1,0:T(8,128)(2,1)S(1)} %get-tuple-element.13), channel_id=1, source_target_pairs={{0,1},{1,0},{2,3},{3,2},{4,5},{5,4},{6,7},{7,6},{8,9},{9,8},{10,11... | collective-permute-start | bytes 294920 | tf_op jit(solution)/shard_map/ppermute | solution.py:19

commit v3 on v1

--- a/solution.py
+++ b/solution.py
@@ -49,17 +49,15 @@
 
 def local(signal, col_basis, right_coupling, middle_coupling, left_coupling, row_basis, node_order):
     place = lax.axis_index("sub")
-    group = lax.axis_index("mid")
     groups = lax.axis_size("mid")
     width = col_basis.shape[1]
     bit0 = place & 1
     bit1 = place >> 1 & 1
-    order = jnp.arange(groups, dtype=jnp.int32) ^ group
 
     first = halves(col_basis, 1, bit0)
     right0 = halves(halves(right_coupling[0, 0], 1, bit0), 0, bit1)
-    right1 = relative_rows(halves(right_coupling[0, 1], 1, bit1), node_order[order])
-    middle = halves(relative_columns(middle_coupling[0], order), 0, bit1)
+    right1 = relative_rows(halves(right_coupling[0, 1], 1, bit1), node_order)
+    middle = halves(middle_coupling[0], 0, bit1)
     left0 = halves(halves(left_coupling[0, 0], 1, bit1), 0, bit0)
     left1 = halves(left_coupling[0, 1], 1, bit0)
 
@@ -70,7 +68,8 @@
         ).astype(jnp.bfloat16)
         coeffs = product(right0, exchange(coeffs, "sub", 1, width // 2))
         coeffs = product(right1, exchange(coeffs, "sub", 2, width // 2))
-        distance = groups // 2
+        coeffs = lax.all_to_all(coeffs.reshape(groups, -1, high - low), "mid", 0, 0, tiled=True).reshape(coeffs.shape)
+        distance = 0
         while distance:
             coeffs = exchange(coeffs, "mid", distance, width // groups * distance)
             distance //= 2

time: 67.9 us -> 72.3 us (1.065)
  matrix products: 7.49 us -> 9.44 us
  starting transfers between devices: 22.8 us -> 24.5 us
  waiting for transfers between devices: 27.6 us -> 29.3 us
  local copies, waits for them, and re-layouts: 5.92 us -> 5 us
    all_to_all x0 -> x3, waiting for transfers between devices: none -> 16 us  [local(): lax.all_to_all(coeffs.reshape(groups, -1, high - low), 'mid', 0, 0, tiled...]
    ppermute x21 -> x12, waiting for transfers between devices: 27.6 us -> 13.3 us  [swap(): return lax.ppermute(block, axis, [(i, i ^ distance) for i in range(count)])]
    all_to_all x0 -> x3, starting transfers between devices: none -> 10.8 us  [local(): lax.all_to_all(coeffs.reshape(groups, -1, high - low), 'mid', 0, 0, tiled...]
    ppermute x21 -> x12, starting transfers between devices: 22.8 us -> 13.7 us  [swap(): return lax.ppermute(block, axis, [(i, i ^ distance) for i in range(count)])]
    dot_general x15, matrix products: 5.25 us -> 7.2 us  [product(): jnp.dot(left, right, preferred_element_type=jnp.float32)]
    gather x2 -> x0, local copies, waits for them, and re-layouts: 1.2 us -> none  [the longest x1 0.64 us: local(): node_order[order]]
  transfers between devices with their start and end apart: 21 -> 15, of which waited for: 12 -> 7; matrix products, arithmetic and copies ran while one was open for 12% -> 11% of each run, Pallas kernels for 0% -> 0%
where the time goes in v3:
time: 72.3 us; the launch traced here: 71.7 us
  waiting for transfers between devices  29.3 us (41%)
  starting transfers between devices  24.5 us (34%)
  matrix products  9.44 us (13%)
  local copies, waits for them, and re-layouts  5 us (7%)
  other arithmetic  2.93 us (4%)
    all_to_all x3, waiting for transfers between devices, local(): lax.all_to_all(coeffs.reshape(groups, -1, high - low), 'mid', 0, 0, tiled...  16 us
    ppermute x12, starting transfers between devices, swap(): return lax.ppermute(block, axis, [(i, i ^ distance) for i in range(count)])  13.7 us
    ppermute x12, waiting for transfers between devices, swap(): return lax.ppermute(block, axis, [(i, i ^ distance) for i in range(count)])  13.3 us
    all_to_all x3, starting transfers between devices, local(): lax.all_to_all(coeffs.reshape(groups, -1, high - low), 'mid', 0, 0, tiled...  10.8 us
    dot_general x15, matrix products, product(): jnp.dot(left, right, preferred_element_type=jnp.float32)  7.2 us
    dot_general x3, matrix products, local(): lax.dot_general(first, signal[:, low:high], (((0,), (0,)), ((), ())), pre...  2.24 us
    concatenate x1, local copies, waits for them, and re-layouts, local(): return jnp.concatenate(outs, axis=1)  2.21 us
  transfers between devices with their start and end apart: 15, of which 7 were waited for; matrix products, arithmetic and copies ran while one was open for 11% of the time, Pallas kernels for 0%

profile of v3, /device:TPU:0, one launch (start us, length us, event | category | flops | bytes accessed | tf_op | source)
XLA Modules:
  0.0 71.7 jit_solution(169901010235014206)
XLA Ops:
  0.0 1.2 %fusion.10 = (bf16[768,128]{1,0:T(8,128)(2,1)S(1)}, bf16[768,128]{1,0:T(8,128)(2,1)S(1)}) fusion(bf16[768,256]{1,0:T(8,128)(2,1)} %param.8), kind=kLoop, calls=%fused_computation.82 | loop fusion | bytes 786432 | tf_op jit(solution)/shard_map/split | solution.py:34
  1.2 1.1 %maximum_select_fusion = bf16[768,256]{1,0:T(8,128)(2,1)S(1)} fusion(bf16[768,256]{1,0:T(8,128)(2,1)} %param.8, bf16[768,128]{1,0:T(8,128)(2,1)S(1)} %get-tuple-element.6, bf16[768,128]{1,0:T(8,128)(2,1)S(1)} %get-tuple-element.5, pred[]{:T(512)S(6)} %eq.4), kind=kLoop, calls=%fused_computation.29 | loop fusion | flops 983040 | bytes 1179649 | tf_op jit(solution)/shard_map/jit(_where)/select_n | solution.py:35
  2.3 1.5 %convolution_convert_fusion.18 = bf16[256,384]{1,0:T(8,128)(2,1)S(1)} fusion(bf16[768,256]{1,0:T(8,128)(2,1)S(1)} %maximum_select_fusion, bf16[768,1152]{1,0:T(8,128)(2,1)} %param.7), kind=kOutput, calls=%fused_computation.23 | convolution fusion | flops 151093248 | bytes 1179648 | tf_op jit(solution)/shard_map/dot_general | solution.py:66
  3.9 2.1 %collective-permute-start.8 = (bf16[1,128,384]{2,1,0:T(8,128)(2,1)S(1)}, bf16[1,128,384]{2,1,0:T(8,128)(2,1)S(1)}, u32[]{:S(2)}, u32[]{:S(2)}) collective-permute-start(bf16[1,128,384]{2,1,0:T(8,128)(2,1)S(1)} %get-tuple-element.35), channel_id=1, source_target_pairs={{0,1},{1,0},{2,3},{3,2},{4,5},{5,4},{6,7},{7,6},{8,9},{9,8},{10,11... | collective-permute-start | bytes 294920 | tf_op jit(solution)/shard_map/ppermute | solution.py:19
  6.9 2.1 %collective-permute-start.4 = (bf16[1,128,384]{2,1,0:T(8,128)(2,1)S(1)}, bf16[1,128,384]{2,1,0:T(8,128)(2,1)S(1)}, u32[]{:S(2)}, u32[]{:S(2)}) collective-permute-start(bf16[1,128,384]{2,1,0:T(8,128)(2,1)S(1)} %get-tuple-element.27), channel_id=1, source_target_pairs={{0,1},{1,0},{2,3},{3,2},{4,5},{5,4},{6,7},{7,6},{8,9},{9,8},{10,11... | collective-permute-start | bytes 294920 | tf_op jit(solution)/shard_map/ppermute | solution.py:19
  11.0 2.9 %collective-permute-start.9 = (bf16[1,128,384]{2,1,0:T(8,128)(2,1)S(1)}, bf16[1,128,384]{2,1,0:T(8,128)(2,1)S(1)}, u32[]{:S(2)}, u32[]{:S(2)}) collective-permute-start(bf16[1,128,384]{2,1,0:T(8,128)(2,1)S(1)} %get-tuple-element.33), channel_id=1, source_target_pairs={{0,2},{1,3},{2,0},{3,1},{4,6},{5,7},{6,4},{7,5},{8,10},{9,11},{10,... | collective-permute-start | bytes 294920 | tf_op jit(solution)/shard_map/ppermute | solution.py:19
  14.3 1.8 %collective-permute-start.1 = (bf16[1,128,384]{2,1,0:T(8,128)(2,1)S(1)}, bf16[1,128,384]{2,1,0:T(8,128)(2,1)S(1)}, u32[]{:S(2)}, u32[]{:S(2)}) collective-permute-start(bf16[1,128,384]{2,1,0:T(8,128)(2,1)S(1)} %get-tuple-element.17), channel_id=1, source_target_pairs={{0,2},{1,3},{2,0},{3,1},{4,6},{5,7},{6,4},{7,5},{8,10},{9,11},{10,... | collective-permute-start | bytes 294920 | tf_op jit(solution)/shard_map/ppermute | solution.py:19
  16.4 1.7 %collective-permute-start.5 = (bf16[1,128,384]{2,1,0:T(8,128)(2,1)S(1)}, bf16[1,128,384]{2,1,0:T(8,128)(2,1)S(1)}, u32[]{:S(2)}, u32[]{:S(2)}) collective-permute-start(bf16[1,128,384]{2,1,0:T(8,128)(2,1)S(1)} %get-tuple-element.25), channel_id=1, source_target_pairs={{0,2},{1,3},{2,0},{3,1},{4,6},{5,7},{6,4},{7,5},{8,10},{9,11},{10,... | collective-permute-start | bytes 294920 | tf_op jit(solution)/shard_map/ppermute | solution.py:19
  18.1 5.3 %collective-permute-done.9 = bf16[1,128,384]{2,1,0:T(8,128)(2,1)S(1)} collective-permute-done((bf16[1,128,384]{2,1,0:T(8,128)(2,1)S(1)}, bf16[1,128,384]{2,1,0:T(8,128)(2,1)S(1)}, u32[]{:S(2)}, u32[]{:S(2)}) %collective-permute-start.9) | collective-permute-done | bytes 98336 | tf_op jit(solution)/shard_map/ppermute | solution.py:19
  24.3 4.0 %all-to-all-start.2 = ((bf16[8,32,384]{2,1,0:T(8,128)(2,1)}), bf16[8,32,384]{2,1,0:T(8,128)(2,1)S(1)}, u32[]{:S(2)}, u32[]{:S(2)}) async-start(bf16[8,32,384]{2,1,0:T(8,128)(2,1)} %bitcast.68), calls=%async_computation.2 | async-start | bytes 393216 | tf_op jit(solution)/shard_map/all_to_all | solution.py:71
  28.3 0.9 %convolution_convert_fusion.16 = bf16[256,384]{1,0:T(8,128)(2,1)} fusion(bf16[256,256]{1,0:T(8,128)(2,1)S(1)} %bitcast.153, bf16[256,384]{1,0:T(8,128)(2,1)S(1)} %bitcast.177), kind=kOutput, calls=%fused_computation.21 | convolution fusion | flops 50429952 | bytes 524288 | tf_op jit(solution)/shard_map/dot_general | solution.py:39
  29.3 0.9 %convolution_convert_fusion.11 = bf16[256,384]{1,0:T(8,128)(2,1)} fusion(bf16[256,256]{1,0:T(8,128)(2,1)S(1)} %bitcast.154, bf16[256,384]{1,0:T(8,128)(2,1)S(1)} %bitcast.168), kind=kOutput, calls=%fused_computation.16 | convolution fusion | flops 50429952 | bytes 524288 | tf_op jit(solution)/shard_map/dot_general | solution.py:39
  30.2 4.3 %all-to-all-done.2 = bf16[8,32,384]{2,1,0:T(8,128)(2,1)S(1)} async-done(((bf16[8,32,384]{2,1,0:T(8,128)(2,1)}), bf16[8,32,384]{2,1,0:T(8,128)(2,1)S(1)}, u32[]{:S(2)}, u32[]{:S(2)}) %all-to-all-start.2) | async-done | bytes 196640 | tf_op jit(solution)/shard_map/all_to_all | solution.py:71
  34.5 3.4 %all-to-all-start = ((bf16[8,32,384]{2,1,0:T(8,128)(2,1)}), bf16[8,32,384]{2,1,0:T(8,128)(2,1)S(1)}, u32[]{:S(2)}, u32[]{:S(2)}) async-start(bf16[8,32,384]{2,1,0:T(8,128)(2,1)} %bitcast.30), calls=%async_computation | async-start | bytes 393216 | tf_op jit(solution)/shard_map/all_to_all | solution.py:71
  38.3 5.8 %all-to-all-done = bf16[8,32,384]{2,1,0:T(8,128)(2,1)S(1)} async-done(((bf16[8,32,384]{2,1,0:T(8,128)(2,1)}), bf16[8,32,384]{2,1,0:T(8,128)(2,1)S(1)}, u32[]{:S(2)}, u32[]{:S(2)}) %all-to-all-start) | async-done | bytes 196640 | tf_op jit(solution)/shard_map/all_to_all | solution.py:71
  44.1 3.4 %all-to-all-start.1 = ((bf16[8,32,384]{2,1,0:T(8,128)(2,1)}), bf16[8,32,384]{2,1,0:T(8,128)(2,1)S(1)}, u32[]{:S(2)}, u32[]{:S(2)}) async-start(bf16[8,32,384]{2,1,0:T(8,128)(2,1)} %bitcast.49), calls=%async_computation.1 | async-start | bytes 393216 | tf_op jit(solution)/shard_map/all_to_all | solution.py:71
  47.8 5.8 %all-to-all-done.1 = bf16[8,32,384]{2,1,0:T(8,128)(2,1)S(1)} async-done(((bf16[8,32,384]{2,1,0:T(8,128)(2,1)}), bf16[8,32,384]{2,1,0:T(8,128)(2,1)S(1)}, u32[]{:S(2)}, u32[]{:S(2)}) %all-to-all-start.1) | async-done | bytes 196640 | tf_op jit(solution)/shard_map/all_to_all | solution.py:71
  54.3 2.6 %collective-permute-start.11 = (bf16[1,128,384]{2,1,0:T(8,128)(2,1)S(1)}, bf16[1,128,384]{2,1,0:T(8,128)(2,1)S(1)}, u32[]{:S(2)}, u32[]{:S(2)}) collective-permute-start(bf16[1,128,384]{2,1,0:T(8,128)(2,1)S(1)} %get-tuple-element.29), channel_id=1, source_target_pairs={{0,1},{1,0},{2,3},{3,2},{4,5},{5,4},{6,7},{7,6},{8,9},{9,8},{10,11... | collective-permute-start | bytes 294920 | tf_op jit(solution)/shard_map/ppermute | solution.py:19
  57.3 3.4 %collective-permute-done.6 = bf16[1,128,384]{2,1,0:T(8,128)(2,1)S(1)} collective-permute-done((bf16[1,128,384]{2,1,0:T(8,128)(2,1)S(1)}, bf16[1,128,384]{2,1,0:T(8,128)(2,1)S(1)}, u32[]{:S(2)}, u32[]{:S(2)}) %collective-permute-start.6) | collective-permute-done | bytes 98336 | tf_op jit(solution)/shard_map/ppermute | solution.py:19
  61.1 2.6 %collective-permute-done.3 = bf16[1,128,384]{2,1,0:T(8,128)(2,1)S(1)} collective-permute-done((bf16[1,128,384]{2,1,0:T(8,128)(2,1)S(1)}, bf16[1,128,384]{2,1,0:T(8,128)(2,1)S(1)}, u32[]{:S(2)}, u32[]{:S(2)}) %collective-permute-start.3) | collective-permute-done | bytes 98336 | tf_op jit(solution)/shard_map/ppermute | solution.py:19
  63.7 2.1 %collective-permute-done.7 = bf16[1,128,384]{2,1,0:T(8,128)(2,1)S(1)} collective-permute-done((bf16[1,128,384]{2,1,0:T(8,128)(2,1)S(1)}, bf16[1,128,384]{2,1,0:T(8,128)(2,1)S(1)}, u32[]{:S(2)}, u32[]{:S(2)}) %collective-permute-start.7) | collective-permute-done | bytes 98336 | tf_op jit(solution)/shard_map/ppermute | solution.py:19
  67.0 1.4 %fusion.2 = bf16[768,384]{0,1:T(8,128)(2,1)} fusion(bf16[768,256]{1,0:T(8,128)(2,1)S(1)} %copy-done, bf16[256,256]{1,0:T(8,128)(2,1)S(1)} %fusion.6, bf16[256,384]{1,0:T(8,128)(2,1)S(1)} %bitcast.156), kind=kOutput, calls=%fused_computation.7 | convolution fusion | flops 201719808 | bytes 1310720 | tf_op jit(solution)/shard_map/dot_general | solution.py:39
  68.3 1.2 %pad_maximum_fusion = bf16[768,1152]{0,1:T(8,128)(2,1)S(1)} fusion(bf16[768,384]{0,1:T(8,128)(2,1)} %fusion.2, bf16[768,384]{0,1:T(8,128)(2,1)S(1)} %fusion.1, bf16[768,384]{0,1:T(8,128)(2,1)S(1)} %fusion), kind=kLoop, calls=%fused_computation.1 | loop fusion | flops 5308416 | bytes 3538944 | tf_op jit(solution)/shard_map/concatenate | solution.py:80
  69.5 2.2 %copy.8 = bf16[768,1152]{1,0:T(8,128)(2,1)} copy(bf16[768,1152]{0,1:T(8,128)(2,1)S(1)} %pad_maximum_fusion) | data formatting | bytes 3538944 | tf_op jit(solution)/shard_map/concatenate | solution.py:80
  (82 shorter events, 7.5 us)
Async XLA Ops:
  0.0 65.8 %copy-start = (bf16[768,256]{1,0:T(8,128)(2,1)S(1)}, bf16[768,256]{1,0:T(8,128)(2,1)}, u32[]{:S(2)}) copy-start(bf16[768,256]{1,0:T(8,128)(2,1)} %param.12) | copy-start | bytes 1179652
  0.0 5.9 %copy-start.5 = (bf16[768,1152]{1,0:T(8,128)(2,1)S(1)}, bf16[768,1152]{1,0:T(8,128)(2,1)}, u32[]{:S(2)}) copy-start(bf16[768,1152]{1,0:T(8,128)(2,1)} %param.7) | copy-start | bytes 5308420
  3.8 5.2 %copy-start.2 = (bf16[1,2,256,256]{3,2,1,0:T(8,128)(2,1)S(1)}, bf16[1,2,256,256]{3,2,1,0:T(8,128)(2,1)}, u32[]{:S(2)}) copy-start(bf16[1,2,256,256]{3,2,1,0:T(8,128)(2,1)} %param.9) | copy-start | bytes 786436
  3.8 5.2 %copy-start.1 = (bf16[1,2,256,256]{3,2,1,0:T(8,128)(2,1)S(1)}, bf16[1,2,256,256]{3,2,1,0:T(8,128)(2,1)}, u32[]{:S(2)}) copy-start(bf16[1,2,256,256]{3,2,1,0:T(8,128)(2,1)} %param.11) | copy-start | bytes 786436
  3.9 6.9 %collective-permute-start.8 = (bf16[1,128,384]{2,1,0:T(8,128)(2,1)S(1)}, bf16[1,128,384]{2,1,0:T(8,128)(2,1)S(1)}, u32[]{:S(2)}, u32[]{:S(2)}) collective-permute-start(bf16[1,128,384]{2,1,0:T(8,128)(2,1)S(1)} %get-tuple-element.35), channel_id=1, source_target_pairs={{0,1},{1,0},{2,3},{3,2},{4,5},{5,4},{6,7},{7,6},{8,9},{9,8},{10,11... | collective-permute-start | bytes 294920 | tf_op jit(solution)/shard_map/ppermute | solution.py:19
  6.4 7.6 %collective-permute-start = (bf16[1,128,384]{2,1,0:T(8,128)(2,1)S(1)}, bf16[1,128,384]{2,1,0:T(8,128)(2,1)S(1)}, u32[]{:S(2)}, u32[]{:S(2)}) collective-permute-start(bf16[1,128,384]{2,1,0:T(8,128)(2,1)S(1)} %get-tuple-element.19), channel_id=1, source_target_pairs={{0,1},{1,0},{2,3},{3,2},{4,5},{5,4},{6,7},{7,6},{8,9},{9,8},{10,11... | collective-permute-start | bytes 294920 | tf_op jit(solution)/shard_map/ppermute | solution.py:19
  6.9 9.2 %collective-permute-start.4 = (bf16[1,128,384]{2,1,0:T(8,128)(2,1)S(1)}, bf16[1,128,384]{2,1,0:T(8,128)(2,1)S(1)}, u32[]{:S(2)}, u32[]{:S(2)}) collective-permute-start(bf16[1,128,384]{2,1,0:T(8,128)(2,1)S(1)} %get-tuple-element.27), channel_id=1, source_target_pairs={{0,1},{1,0},{2,3},{3,2},{4,5},{5,4},{6,7},{7,6},{8,9},{9,8},{10,11... | collective-permute-start | bytes 294920 | tf_op jit(solution)/shard_map/ppermute | solution.py:19
  9.1 0.9 %copy-start.3 = (bf16[1,256,256]{2,1,0:T(8,128)(2,1)S(1)}, bf16[1,256,256]{2,1,0:T(8,128)(2,1)}, u32[]{:S(2)}) copy-start(bf16[1,256,256]{2,1,0:T(8,128)(2,1)} %param.10) | copy-start | bytes 393220
  9.2 0.9 %copy-start.4 = (s32[8]{0:T(128)S(1)}, s32[8]{0:T(128)}, u32[]{:S(2)}) copy-start(s32[8]{0:T(128)} %param.13) | copy-start | bytes 100
  11.0 12.3 %collective-permute-start.9 = (bf16[1,128,384]{2,1,0:T(8,128)(2,1)S(1)}, bf16[1,128,384]{2,1,0:T(8,128)(2,1)S(1)}, u32[]{:S(2)}, u32[]{:S(2)}) collective-permute-start(bf16[1,128,384]{2,1,0:T(8,128)(2,1)S(1)} %get-tuple-element.33), channel_id=1, source_target_pairs={{0,2},{1,3},{2,0},{3,1},{4,6},{5,7},{6,4},{7,5},{8,10},{9,11},{10,... | collective-permute-start | bytes 294920 | tf_op jit(solution)/shard_map/ppermute | solution.py:19
  14.3 14.0 %collective-permute-start.1 = (bf16[1,128,384]{2,1,0:T(8,128)(2,1)S(1)}, bf16[1,128,384]{2,1,0:T(8,128)(2,1)S(1)}, u32[]{:S(2)}, u32[]{:S(2)}) collective-permute-start(bf16[1,128,384]{2,1,0:T(8,128)(2,1)S(1)} %get-tuple-element.17), channel_id=1, source_target_pairs={{0,2},{1,3},{2,0},{3,1},{4,6},{5,7},{6,4},{7,5},{8,10},{9,11},{10,... | collective-permute-start | bytes 294920 | tf_op jit(solution)/shard_map/ppermute | solution.py:19
  16.4 12.9 %collective-permute-start.5 = (bf16[1,128,384]{2,1,0:T(8,128)(2,1)S(1)}, bf16[1,128,384]{2,1,0:T(8,128)(2,1)S(1)}, u32[]{:S(2)}, u32[]{:S(2)}) collective-permute-start(bf16[1,128,384]{2,1,0:T(8,128)(2,1)S(1)} %get-tuple-element.25), channel_id=1, source_target_pairs={{0,2},{1,3},{2,0},{3,1},{4,6},{5,7},{6,4},{7,5},{8,10},{9,11},{10,... | collective-permute-start | bytes 294920 | tf_op jit(solution)/shard_map/ppermute | solution.py:19
  24.3 10.2 %all-to-all-start.2 = ((bf16[8,32,384]{2,1,0:T(8,128)(2,1)}), bf16[8,32,384]{2,1,0:T(8,128)(2,1)S(1)}, u32[]{:S(2)}, u32[]{:S(2)}) async-start(bf16[8,32,384]{2,1,0:T(8,128)(2,1)} %bitcast.68), calls=%async_computation.2 | async-start | bytes 393216 | tf_op jit(solution)/shard_map/all_to_all | solution.py:71
  34.5 9.6 %all-to-all-start = ((bf16[8,32,384]{2,1,0:T(8,128)(2,1)}), bf16[8,32,384]{2,1,0:T(8,128)(2,1)S(1)}, u32[]{:S(2)}, u32[]{:S(2)}) async-start(bf16[8,32,384]{2,1,0:T(8,128)(2,1)} %bitcast.30), calls=%async_computation | async-start | bytes 393216 | tf_op jit(solution)/shard_map/all_to_all | solution.py:71
  38.2 15.8 %collective-permute-start.10 = (bf16[1,128,384]{2,1,0:T(8,128)(2,1)S(1)}, bf16[1,128,384]{2,1,0:T(8,128)(2,1)S(1)}, u32[]{:S(2)}, u32[]{:S(2)}) collective-permute-start(bf16[1,128,384]{2,1,0:T(8,128)(2,1)S(1)} %get-tuple-element.31), channel_id=1, source_target_pairs={{0,2},{1,3},{2,0},{3,1},{4,6},{5,7},{6,4},{7,5},{8,10},{9,11},{10,... | collective-permute-start | bytes 294920 | tf_op jit(solution)/shard_map/ppermute | solution.py:19
  44.1 9.6 %all-to-all-start.1 = ((bf16[8,32,384]{2,1,0:T(8,128)(2,1)}), bf16[8,32,384]{2,1,0:T(8,128)(2,1)S(1)}, u32[]{:S(2)}, u32[]{:S(2)}) async-start(bf16[8,32,384]{2,1,0:T(8,128)(2,1)} %bitcast.49), calls=%async_computation.1 | async-start | bytes 393216 | tf_op jit(solution)/shard_map/all_to_all | solution.py:71
  47.8 9.2 %collective-permute-start.2 = (bf16[1,128,384]{2,1,0:T(8,128)(2,1)S(1)}, bf16[1,128,384]{2,1,0:T(8,128)(2,1)S(1)}, u32[]{:S(2)}, u32[]{:S(2)}) collective-permute-start(bf16[1,128,384]{2,1,0:T(8,128)(2,1)S(1)} %get-tuple-element.15), channel_id=1, source_target_pairs={{0,2},{1,3},{2,0},{3,1},{4,6},{5,7},{6,4},{7,5},{8,10},{9,11},{10,... | collective-permute-start | bytes 294920 | tf_op jit(solution)/shard_map/ppermute | solution.py:19
  53.9 6.8 %collective-permute-start.6 = (bf16[1,128,384]{2,1,0:T(8,128)(2,1)S(1)}, bf16[1,128,384]{2,1,0:T(8,128)(2,1)S(1)}, u32[]{:S(2)}, u32[]{:S(2)}) collective-permute-start(bf16[1,128,384]{2,1,0:T(8,128)(2,1)S(1)} %get-tuple-element.23), channel_id=1, source_target_pairs={{0,2},{1,3},{2,0},{3,1},{4,6},{5,7},{6,4},{7,5},{8,10},{9,11},{10,... | collective-permute-start | bytes 294920 | tf_op jit(solution)/shard_map/ppermute | solution.py:19
  54.3 12.6 %collective-permute-start.11 = (bf16[1,128,384]{2,1,0:T(8,128)(2,1)S(1)}, bf16[1,128,384]{2,1,0:T(8,128)(2,1)S(1)}, u32[]{:S(2)}, u32[]{:S(2)}) collective-permute-start(bf16[1,128,384]{2,1,0:T(8,128)(2,1)S(1)} %get-tuple-element.29), channel_id=1, source_target_pairs={{0,1},{1,0},{2,3},{3,2},{4,5},{5,4},{6,7},{7,6},{8,9},{9,8},{10,11... | collective-permute-start | bytes 294920 | tf_op jit(solution)/shard_map/ppermute | solution.py:19
  57.2 6.4 %collective-permute-start.3 = (bf16[1,128,384]{2,1,0:T(8,128)(2,1)S(1)}, bf16[1,128,384]{2,1,0:T(8,128)(2,1)S(1)}, u32[]{:S(2)}, u32[]{:S(2)}) collective-permute-start(bf16[1,128,384]{2,1,0:T(8,128)(2,1)S(1)} %get-tuple-element.13), channel_id=1, source_target_pairs={{0,1},{1,0},{2,3},{3,2},{4,5},{5,4},{6,7},{7,6},{8,9},{9,8},{10,11... | collective-permute-start | bytes 294920 | tf_op jit(solution)/shard_map/ppermute | solution.py:19
  61.0 4.7 %collective-permute-start.7 = (bf16[1,128,384]{2,1,0:T(8,128)(2,1)S(1)}, bf16[1,128,384]{2,1,0:T(8,128)(2,1)S(1)}, u32[]{:S(2)}, u32[]{:S(2)}) collective-permute-start(bf16[1,128,384]{2,1,0:T(8,128)(2,1)S(1)} %get-tuple-element.21), channel_id=1, source_target_pairs={{0,1},{1,0},{2,3},{3,2},{4,5},{5,4},{6,7},{7,6},{8,9},{9,8},{10,11... | collective-permute-start | bytes 294920 | tf_op jit(solution)/shard_map/ppermute | solution.py:19

commit v4 on v1

v4 whole, which is shorter than its diff:
```python
import jax
import jax.numpy as jnp
from jax import lax
from jax.experimental import pallas as pl
from jax.experimental.pallas import tpu as pltpu
from jax.sharding import PartitionSpec as P

LANES = 128
CHUNKS = 3
ROWS = 16
F32 = jnp.float32
BF16 = jnp.bfloat16
WHOLE = pl.BlockSpec(memory_space=pltpu.VMEM)
SCALARS = pl.BlockSpec(memory_space=pltpu.SMEM)
PLACE = pl.BlockSpec(memory_space=pl.ANY)
HBM = pl.BlockSpec(memory_space=pltpu.HBM)


def cuts(columns):
    tiles = max(columns // LANES, 1)
    count = min(CHUNKS, tiles)
    edges = [tiles * i // count * LANES for i in range(count)] + [columns]
    return list(zip(edges[:-1], edges[1:]))


def swap(block, axis, distance):
    count = lax.axis_size(axis)
    return lax.ppermute(block, axis, [(i, i ^ distance) for i in range(count)])


def swapped(matrix, axis, flag):
    half = matrix.shape[axis] // 2
    low = lax.slice_in_dim(matrix, 0, half, axis=axis)
    high = lax.slice_in_dim(matrix, half, 2 * half, axis=axis)
    return jnp.where(flag == 1, jnp.concatenate([high, low], axis=axis), matrix)


def matmul(left, right):
    return lax.dot_general(left, right, (((1,), (0,)), ((), ())), preferred_element_type=F32)


def cost(flops, moved):
    return pl.CostEstimate(flops=flops, bytes_accessed=moved, transcendentals=0)


def call(kernel, outs, specs, operands, after, **more):
    extra = [] if after is None else [after]

    def body(*refs):
        kernel(*refs[: len(operands)], *refs[len(operands) + len(extra) :])

    return pl.pallas_call(
        body,
        in_specs=specs + [PLACE] * len(extra),
        out_shape=outs,
        **more,
    )(*operands, *extra)


def prepare(bits, rows, columns, right, middle, left, after):
    width = middle.shape[-1]

    def kernel(bits, rows, columns, right, middle, left, right0, right1, middle0, left0, left1):
        bit0, bit1 = bits[0], bits[1]
        right0[...] = swapped(swapped(right[0, 0], 1, bit0), 0, bit1)
        place = lax.broadcasted_iota(jnp.int32, (width, width), 1)
        pick = jnp.where(place == rows[...], 1.0, 0.0).astype(BF16)
        right1[...] = matmul(pick, swapped(right[0, 1], 1, bit1)).astype(BF16)
        place = lax.broadcasted_iota(jnp.int32, (width, width), 0)
        pick = jnp.where(place == columns[...], 1.0, 0.0).astype(BF16)
        middle0[...] = swapped(matmul(middle[0], pick).astype(BF16), 0, bit1)
        left0[...] = swapped(swapped(left[0, 0], 1, bit1), 0, bit0)
        left1[...] = swapped(left[0, 1], 1, bit0)

    return call(
        kernel,
        [jax.ShapeDtypeStruct((width, width), BF16)] * 5,
        [SCALARS] + [WHOLE] * 5,
        [bits, rows, columns, right, middle, left],
        after,
        out_specs=[WHOLE] * 5,
        cost_estimate=cost(4 * width**3, 20 * width**2),
    )


def first(bits, basis, signal, low, high, after):
    rows, width = basis.shape
    half, columns = width // 2, high - low
    pieces = 3 if rows % (3 * ROWS) == 0 else 1
    depth = rows // pieces

    def kernel(bits, basis, signal, kept, send, basis_here, signal_here, arrived):
        copies = []
        for i in range(pieces):
            part = pl.ds(i * depth, depth)
            copies.append(
                [
                    pltpu.make_async_copy(basis.at[part], basis_here.at[part], arrived.at[i, 0]),
                    pltpu.make_async_copy(
                        signal.at[part, pl.ds(low, columns)], signal_here.at[part], arrived.at[i, 1]
                    ),
                ]
            )
            for copy in copies[-1]:
                copy.start()
        total = jnp.zeros((width, columns), F32)
        for i in range(pieces):
            part = pl.ds(i * depth, depth)
            for copy in copies[i]:
                copy.wait()
            total += lax.dot_general(
                basis_here[part, :],
                signal_here[part, :],
                (((0,), (0,)), ((), ())),
                preferred_element_type=F32,
            )
        top, bottom = total[:half].astype(BF16), total[half:].astype(BF16)
        kept[...] = jnp.where(bits[0] == 1, bottom, top)
        send[...] = jnp.where(bits[0] == 1, top, bottom)

    return call(
        kernel,
        [jax.ShapeDtypeStruct((half, columns), BF16)] * 2,
        [SCALARS, HBM, HBM],
        [bits, basis, signal],
        after,
        out_specs=[WHOLE] * 2,
        scratch_shapes=[
            pltpu.VMEM((rows, width), BF16),
            pltpu.VMEM((rows, columns), BF16),
            pltpu.SemaphoreType.DMA((pieces, 2)),
        ],
        cost_estimate=cost(2 * rows * width * columns, 2 * rows * (columns + width)),
    )


def level(weight, keep, got, after):
    half, columns = keep.shape

    def kernel(weight, keep, got, kept, send):
        total = matmul(weight[:, :half], keep[...]) + matmul(weight[:, half:], got[...])
        kept[...] = total[:half].astype(BF16)
        send[...] = total[half:].astype(BF16)

    return call(
        kernel,
        [jax.ShapeDtypeStruct((half, columns), BF16)] * 2,
        [WHOLE] * 3,
        [weight, keep, got],
        after,
        out_specs=[WHOLE] * 2,
        cost_estimate=cost(8 * half * half * columns, 8 * half * columns),
    )


def regroup(keep, got, block, after):
    half, columns = keep.shape

    def parts(value, which):
        return [value[i * block : (i + 1) * block] for i in range(which, half // block, 2)]

    def both(keep, got, which):
        return jnp.concatenate(parts(keep, which) + parts(got, which), axis=0)

    if block % ROWS:
        return both(keep, got, 0), both(keep, got, 1)

    def kernel(keep, got, kept, send):
        kept[...] = both(keep[...], got[...], 0)
        send[...] = both(keep[...], got[...], 1)

    return call(
        kernel,
        [jax.ShapeDtypeStruct((half, columns), BF16)] * 2,
        [WHOLE] * 2,
        [keep, got],
        after,
        out_specs=[WHOLE] * 2,
        cost_estimate=cost(0, 8 * half * columns),
    )


def last(weight, basis, keep, got, before, low, columns, after):
    rows, width = basis.shape
    half, wide = keep.shape
    pieces = 3 if rows % (3 * ROWS) == 0 else 1
    depth = rows // pieces
    given = [] if before is None else [before]

    def kernel(weight, basis, keep, got, *refs):
        out, here, left = refs[len(given) :]
        coeffs = matmul(weight[:, :half], keep[...]) + matmul(weight[:, half:], got[...])
        coeffs = coeffs.astype(BF16)
        copies = []
        for i in range(pieces):
            part = pl.ds(i * depth, depth)
            here[part, :] = matmul(basis[part, :], coeffs).astype(BF16)
            copy = pltpu.make_async_copy(here.at[part], out.at[part, pl.ds(low, wide)], left.at[i])
            copy.start()
            copies.append(copy)
        for copy in copies:
            copy.wait()

    return call(
        kernel,
        jax.ShapeDtypeStruct((rows, columns), BF16),
        [WHOLE] * 4 + [HBM] * len(given),
        [weight, basis, keep, got] + given,
        after,
        out_specs=HBM,
        scratch_shapes=[pltpu.VMEM((rows, wide), BF16), pltpu.SemaphoreType.DMA((pieces,))],
        input_output_aliases={4: 0} if given else {},
        cost_estimate=cost(2 * rows * width * wide, 2 * rows * wide),
    )


def slot_bits(groups):
    bits = []
    while 1 << len(bits) < groups:
        bits.insert(0, len(bits))
    return bits


def final_slots(groups):
    order = list(range(groups))
    half = groups // 2
    keep, got = order[:half], order[half:]
    block = half // 2
    while block:
        one = [[x[i : i + block] for i in range(0, half, block)] for x in (keep, got)]
        keep = sum(one[0][0::2] + one[1][0::2], [])
        got = sum(one[0][1::2] + one[1][1::2], [])
        block //= 2
    return keep + got


def stage_order(count, steps):
    times = [(0.0, 0.1), (4.0, 2.0), (9.5, 4.0)]
    times += [(9.5 + 2.6 * i, 4.0) for i in range(1, steps)]
    times += [(9.5 + 2.6 * steps, 4.0), (15.5 + 2.6 * steps, 4.0), (18.5 + 2.6 * steps, 4.0)]
    entries = [(t + i * gap, i, s) for s, (t, gap) in enumerate(times) for i in range(count)]
    return [(i, s) for _, i, s in sorted(entries)]


def local(signal, col_basis, right_coupling, middle_coupling, left_coupling, row_basis, node_order):
    place = lax.axis_index("sub")
    group = lax.axis_index("mid")
    groups = lax.axis_size("mid")
    width = col_basis.shape[1]
    block = width // groups
    steps = len(slot_bits(groups))
    columns = signal.shape[1]
    chunks = cuts(columns)
    bits = jnp.stack([place & 1, place >> 1 & 1])
    inside = jnp.arange(block, dtype=jnp.int32)
    slots = jnp.arange(groups, dtype=jnp.int32) ^ group
    rows = (node_order[slots][:, None] * block + inside).reshape(width, 1)
    slots = jnp.array(final_slots(groups), dtype=jnp.int32) ^ group
    picked = (slots[:, None] * block + inside).reshape(1, width)

    keep, got = [None] * len(chunks), [None] * len(chunks)
    weights, out, after = None, None, None
    for i, stage in stage_order(len(chunks), steps):
        low, high = chunks[i]
        if stage == 0:
            keep[i], send = first(bits, col_basis, signal, low, high, after)
            got[i] = swap(send, "sub", 1)
            after = keep[i]
            continue
        if weights is None:
            weights = prepare(
                bits, rows, picked, right_coupling, middle_coupling, left_coupling, after
            )
            right0, right1, middle, left0, left1 = weights
            after = right0
        if stage == 1:
            keep[i], send = level(right0, keep[i], got[i], after)
            got[i] = swap(send, "sub", 2)
        elif stage == 2:
            keep[i], send = level(right1, keep[i], got[i], after)
            got[i] = swap(send, "mid", groups // 2)
        elif stage < 2 + steps:
            slot = groups >> stage - 1
            keep[i], send = regroup(keep[i], got[i], slot * block, after)
            got[i] = swap(send, "mid", slot)
        elif stage == 2 + steps:
            keep[i], send = level(middle, keep[i], got[i], after)
            got[i] = swap(send, "sub", 2)
        elif stage == 3 + steps:
            keep[i], send = level(left0, keep[i], got[i], after)
            got[i] = swap(send, "sub", 1)
        else:
            out = last(left1, row_basis, keep[i], got[i], out, low, columns, after)
        after = keep[i]
    return out


def solution(mesh):
    return jax.shard_map(
        local,
        mesh=mesh,
        in_specs=(
            P(("mid", "sub"), None),
            P(("mid", "sub"), None),
            P(("mid", "sub"), None, None, None),
            P(("mid", "sub"), None, None),
            P(("mid", "sub"), None, None, None),
            P(("mid", "sub"), None),
            P(),
        ),
        out_specs=P(("mid", "sub"), None),
        check_vma=False,
    )
```

time: 67.9 us -> 100 us (1.47)
  Pallas kernels: 0 us -> 51.8 us
  waiting for transfers between devices: 27.6 us -> 9.25 us
  local copies, waits for them, and re-layouts: 5.92 us -> 15.5 us
  matrix products: 7.49 us -> 0 us
  other arithmetic: 3.18 us -> 0.78 us
    pallas_call x0 -> x25, Pallas kernels: none -> 51.8 us  [call(): pl.pallas_call(body, in_specs=specs + [PLACE] * len(extra), out_shape=out...]
    ppermute x21, waiting for transfers between devices: 27.6 us -> 9.25 us  [swap(): return lax.ppermute(block, axis, [(i, i ^ distance) for i in range(count)])]
    unnamed x16 -> x46, local copies, waits for them, and re-layouts: 0.2 us -> 13.4 us
    dot_general x18 -> x0, matrix products: 7.49 us -> none  [the longest x15 5.25 us: product(): jnp.dot(left, right, preferred_element_type=jnp.float32)]
    concatenate x6 -> x0, local copies, waits for them, and re-layouts: 2.32 us -> none  [the longest x1 2.21 us: local(): return jnp.concatenate(outs, axis=1)]
    select_n x9 -> x1, other arithmetic: 1.44 us -> 0.01 us  [local(): rows = (node_order[slots][:, None] * block + inside).reshape(width, 1)]
    add x0 -> x2, local copies, waits for them, and re-layouts: none -> 1.42 us  [the longest x1 0.79 us: local(): rows = (node_order[slots][:, None] * block + inside).reshape(width, 1)]
    split x3 -> x0, local copies, waits for them, and re-layouts: 1.23 us -> none  [halves(): low, high = jnp.split(matrix, 2, axis=axis)]
  transfers between devices with their start and end apart: 21 -> 21, of which waited for: 12 -> 6; matrix products, arithmetic and copies ran while one was open for 12% -> 2% of each run, Pallas kernels for 0% -> 45%
where the time goes in v4:
time: 100 us; the launch traced here: 99.4 us
  Pallas kernels  51.8 us (52%)
  starting transfers between devices  22 us (22%)
  local copies, waits for them, and re-layouts  15.5 us (16%)
  waiting for transfers between devices  9.25 us (9%)
    pallas_call x25, Pallas kernels, call(): pl.pallas_call(body, in_specs=specs + [PLACE] * len(extra), out_shape=out...  51.8 us
    ppermute x21, starting transfers between devices, swap(): return lax.ppermute(block, axis, [(i, i ^ distance) for i in range(count)])  22 us
    unnamed x46, local copies, waits for them, and re-layouts  13.4 us
    ppermute x21, waiting for transfers between devices, swap(): return lax.ppermute(block, axis, [(i, i ^ distance) for i in range(count)])  9.25 us
  transfers between devices with their start and end apart: 21, of which 6 were waited for; matrix products, arithmetic and copies ran while one was open for 2% of the time, Pallas kernels for 45%

profile of v4, /device:TPU:0, one launch (start us, length us, event | category | flops | bytes accessed | tf_op | source)
XLA Modules:
  0.0 99.4 jit_solution(10457092717242392812)
XLA Ops:
  0.6 3.1 %shard_map.82 = (bf16[128,384]{1,0:T(8,128)(2,1)}, bf16[128,384]{1,0:T(8,128)(2,1)}) custom-call(s32[2]{0:T(128)} %pad_add_fusion.refs_0_, bf16[768,256]{1,0:T(8,128)(2,1)} %refs_1_.8, bf16[768,1152]{1,0:T(8,128)(2,1)} %refs_2_.5), custom_call_target="tpu_custom_call" | custom-call | flops 150994944 | bytes 983040 | tf_op jit(solution)/shard_map/pallas_call | solution.py:52
  3.7 3.1 %collective-permute-start.2 = (bf16[128,384]{1,0:T(8,128)(2,1)}, bf16[128,384]{1,0:T(8,128)(2,1)S(1)}, u32[]{:S(2)}, u32[]{:S(2)}) collective-permute-start(bf16[128,384]{1,0:T(8,128)(2,1)} %get-tuple-element.62), channel_id=1, source_target_pairs={{0,1},{1,0},{2,3},{3,2},{4,5},{5,4},{6,7},{7,6},{8,9},{9,8},{10,11... | collective-permute-start | bytes 294920 | tf_op jit(solution)/shard_map/ppermute | solution.py:28
  6.8 3.3 %shard_map.83 = (bf16[128,384]{1,0:T(8,128)(2,1)}, bf16[128,384]{1,0:T(8,128)(2,1)}) custom-call(s32[2]{0:T(128)} %pad_add_fusion.refs_0_, bf16[768,256]{1,0:T(8,128)(2,1)} %refs_1_.8, bf16[768,1152]{1,0:T(8,128)(2,1)} %refs_2_.5, bf16[128,384]{1,0:T(8,128)(2,1)} %get-tuple-element.52.refs_3_.refs_1_), custom_call_target="tpu_custom_call" | custom-call | flops 150994944 | bytes 983040 | tf_op jit(solution)/shard_map/pallas_call | solution.py:52
  10.2 3.1 %shard_map.84 = (bf16[128,384]{1,0:T(8,128)(2,1)}, bf16[128,384]{1,0:T(8,128)(2,1)}) custom-call(s32[2]{0:T(128)} %pad_add_fusion.refs_0_, bf16[768,256]{1,0:T(8,128)(2,1)} %refs_1_.8, bf16[768,1152]{1,0:T(8,128)(2,1)} %refs_2_.5, bf16[128,384]{1,0:T(8,128)(2,1)} %get-tuple-element.53.refs_3_.refs_1_), custom_call_target="tpu_custom_call" | custom-call | flops 150994944 | bytes 983040 | tf_op jit(solution)/shard_map/pallas_call | solution.py:52
  13.3 2.1 %collective-permute-start = (bf16[128,384]{1,0:T(8,128)(2,1)}, bf16[128,384]{1,0:T(8,128)(2,1)S(1)}, u32[]{:S(2)}, u32[]{:S(2)}) collective-permute-start(bf16[128,384]{1,0:T(8,128)(2,1)} %get-tuple-element.60), channel_id=1, source_target_pairs={{0,1},{1,0},{2,3},{3,2},{4,5},{5,4},{6,7},{7,6},{8,9},{9,8},{10,11... | collective-permute-start | bytes 294920 | tf_op jit(solution)/shard_map/ppermute | solution.py:28
  17.6 2.3 %shard_map.85 = (bf16[256,256]{1,0:T(8,128)(2,1)}, bf16[256,256]{1,0:T(8,128)(2,1)}, bf16[256,256]{1,0:T(8,128)(2,1)}, bf16[256,256]{1,0:T(8,128)(2,1)}, bf16[256,256]{1,0:T(8,128)(2,1)}) custom-call(s32[2]{0:T(128)} %pad_add_fusion.refs_0_, s32[256,1]{1,0:T(8,128)} %add.65.refs_1_, s32[1,256]{1,0:T(1,128)} %add.64.refs_2_, ...), custom_call_target="tpu_custom_call" | custom-call | flops 67108864 | bytes 1310720 | tf_op jit(solution)/shard_map/pallas_call | solution.py:52
  20.5 1.9 %shard_map.86 = (bf16[128,384]{1,0:T(8,128)(2,1)}, bf16[128,384]{1,0:T(8,128)(2,1)}) custom-call(bf16[256,256]{1,0:T(8,128)(2,1)} %get-tuple-element.59.refs_0_.refs_3_, bf16[128,384]{1,0:T(8,128)(2,1)} %get-tuple-element.52.refs_3_.refs_1_, bf16[128,384]{1,0:T(8,128)(2,1)} %copy-done.2, bf16[256,256]{1,0:T(8,128)(2,1)} %get-tuple-element.59.refs_0_.refs_3_), custom_call_target="tpu_custom_call" | custom-call | flops 50331648 | bytes 393216 | tf_op jit(solution)/shard_map/pallas_call | solution.py:52
  22.5 2.6 %collective-permute-start.4 = (bf16[128,384]{1,0:T(8,128)(2,1)}, bf16[128,384]{1,0:T(8,128)(2,1)S(1)}, u32[]{:S(2)}, u32[]{:S(2)}) collective-permute-start(bf16[128,384]{1,0:T(8,128)(2,1)} %get-tuple-element.67), channel_id=1, source_target_pairs={{0,2},{1,3},{2,0},{3,1},{4,6},{5,7},{6,4},{7,5},{8,10},{9,11},{10,... | collective-permute-start | bytes 294920 | tf_op jit(solution)/shard_map/ppermute | solution.py:28
  25.7 1.9 %shard_map.87 = (bf16[128,384]{1,0:T(8,128)(2,1)}, bf16[128,384]{1,0:T(8,128)(2,1)}) custom-call(bf16[256,256]{1,0:T(8,128)(2,1)} %get-tuple-element.59.refs_0_.refs_3_, bf16[128,384]{1,0:T(8,128)(2,1)} %get-tuple-element.53.refs_3_.refs_1_, bf16[128,384]{1,0:T(8,128)(2,1)} %copy-done.10, bf16[128,384]{1,0:T(8,128)(2,1)} %get-tuple-element.63.refs_3_.refs_1_), custom_call_target="tpu_custom_call" | custom-call | flops 50331648 | bytes 393216 | tf_op jit(solution)/shard_map/pallas_call | solution.py:52
  28.3 1.9 %shard_map.88 = (bf16[128,384]{1,0:T(8,128)(2,1)}, bf16[128,384]{1,0:T(8,128)(2,1)}) custom-call(bf16[256,256]{1,0:T(8,128)(2,1)} %get-tuple-element.59.refs_0_.refs_3_, bf16[128,384]{1,0:T(8,128)(2,1)} %get-tuple-element.54.refs_6_.refs_1_, bf16[128,384]{1,0:T(8,128)(2,1)} %copy-done.9, bf16[128,384]{1,0:T(8,128)(2,1)} %get-tuple-element.64.refs_3_.refs_1_), custom_call_target="tpu_custom_call" | custom-call | flops 50331648 | bytes 393216 | tf_op jit(solution)/shard_map/pallas_call | solution.py:52
  30.8 1.9 %shard_map.89 = (bf16[128,384]{1,0:T(8,128)(2,1)}, bf16[128,384]{1,0:T(8,128)(2,1)}) custom-call(bf16[256,256]{1,0:T(8,128)(2,1)} %get-tuple-element.58.refs_0_, bf16[128,384]{1,0:T(8,128)(2,1)} %get-tuple-element.63.refs_3_.refs_1_, bf16[128,384]{1,0:T(8,128)(2,1)} %copy-done.14, bf16[128,384]{1,0:T(8,128)(2,1)} %get-tuple-element.65.refs_3_.refs_1_), custom_call_target="tpu_custom_call" | custom-call | flops 50331648 | bytes 393216 | tf_op jit(solution)/shard_map/pallas_call | solution.py:52
  35.0 2.6 %collective-permute-done.5.refs_1_ = bf16[128,384]{1,0:T(8,128)(2,1)S(1)} collective-permute-done((bf16[128,384]{1,0:T(8,128)(2,1)}, bf16[128,384]{1,0:T(8,128)(2,1)S(1)}, u32[]{:S(2)}, u32[]{:S(2)}) %collective-permute-start.5) | collective-permute-done | bytes 98336 | tf_op jit(solution)/shard_map/ppermute | solution.py:28
  42.0 1.9 %shard_map.91 = (bf16[128,384]{1,0:T(8,128)(2,1)}, bf16[128,384]{1,0:T(8,128)(2,1)}) custom-call(bf16[256,256]{1,0:T(8,128)(2,1)} %get-tuple-element.58.refs_0_, bf16[128,384]{1,0:T(8,128)(2,1)} %get-tuple-element.64.refs_3_.refs_1_, bf16[128,384]{1,0:T(8,128)(2,1)} %copy-done.19, bf16[128,384]{1,0:T(8,128)(2,1)} %get-tuple-element.70.refs_3_.refs_0_), custom_call_target="tpu_custom_call" | custom-call | flops 50331648 | bytes 393216 | tf_op jit(solution)/shard_map/pallas_call | solution.py:52
  52.7 1.9 %shard_map.94 = (bf16[128,384]{1,0:T(8,128)(2,1)}, bf16[128,384]{1,0:T(8,128)(2,1)}) custom-call(bf16[256,256]{1,0:T(8,128)(2,1)} %get-tuple-element.57.refs_0_, bf16[128,384]{1,0:T(8,128)(2,1)} %get-tuple-element.74.refs_2_.refs_1_, bf16[128,384]{1,0:T(8,128)(2,1)} %copy-done.15, bf16[128,384]{1,0:T(8,128)(2,1)} %get-tuple-element.77.refs_3_.refs_0_), custom_call_target="tpu_custom_call" | custom-call | flops 50331648 | bytes 393216 | tf_op jit(solution)/shard_map/pallas_call | solution.py:52
  61.6 1.9 %collective-permute-done.10.refs_1_ = bf16[128,384]{1,0:T(8,128)(2,1)S(1)} collective-permute-done((bf16[128,384]{1,0:T(8,128)(2,1)}, bf16[128,384]{1,0:T(8,128)(2,1)S(1)}, u32[]{:S(2)}, u32[]{:S(2)}) %collective-permute-start.10) | collective-permute-done | bytes 98336 | tf_op jit(solution)/shard_map/ppermute | solution.py:28
  67.8 1.9 %shard_map.98 = (bf16[128,384]{1,0:T(8,128)(2,1)}, bf16[128,384]{1,0:T(8,128)(2,1)}) custom-call(bf16[256,256]{1,0:T(8,128)(2,1)} %get-tuple-element.57.refs_0_, bf16[128,384]{1,0:T(8,128)(2,1)} %get-tuple-element.82.refs_2_.refs_1_, bf16[128,384]{1,0:T(8,128)(2,1)} %copy-done.16, bf16[128,384]{1,0:T(8,128)(2,1)} %get-tuple-element.83.refs_3_.refs_0_), custom_call_target="tpu_custom_call" | custom-call | flops 50331648 | bytes 393216 | tf_op jit(solution)/shard_map/pallas_call | solution.py:52
  75.0 1.9 %shard_map.100 = (bf16[128,384]{1,0:T(8,128)(2,1)}, bf16[128,384]{1,0:T(8,128)(2,1)}) custom-call(bf16[256,256]{1,0:T(8,128)(2,1)} %get-tuple-element.56.refs_0_, bf16[128,384]{1,0:T(8,128)(2,1)} %get-tuple-element.78.refs_3_.refs_1_, bf16[128,384]{1,0:T(8,128)(2,1)} %copy-done.11, bf16[128,384]{1,0:T(8,128)(2,1)} %get-tuple-element.87.refs_3_.refs_1_), custom_call_target="tpu_custom_call" | custom-call | flops 50331648 | bytes 393216 | tf_op jit(solution)/shard_map/pallas_call | solution.py:52
  77.5 1.9 %shard_map.101 = (bf16[128,384]{1,0:T(8,128)(2,1)}, bf16[128,384]{1,0:T(8,128)(2,1)}) custom-call(bf16[256,256]{1,0:T(8,128)(2,1)} %get-tuple-element.57.refs_0_, bf16[128,384]{1,0:T(8,128)(2,1)} %get-tuple-element.87.refs_3_.refs_1_, bf16[128,384]{1,0:T(8,128)(2,1)} %copy-done.18, bf16[128,384]{1,0:T(8,128)(2,1)} %get-tuple-element.90.refs_3_.refs_2_), custom_call_target="tpu_custom_call" | custom-call | flops 50331648 | bytes 393216 | tf_op jit(solution)/shard_map/pallas_call | solution.py:52
  82.4 1.9 %shard_map.102 = (bf16[128,384]{1,0:T(8,128)(2,1)}, bf16[128,384]{1,0:T(8,128)(2,1)}) custom-call(bf16[256,256]{1,0:T(8,128)(2,1)} %get-tuple-element.56.refs_0_, bf16[128,384]{1,0:T(8,128)(2,1)} %get-tuple-element.86.refs_2_.refs_1_, bf16[128,384]{1,0:T(8,128)(2,1)} %copy-done.12, bf16[128,384]{1,0:T(8,128)(2,1)} %get-tuple-element.90.refs_3_.refs_2_), custom_call_target="tpu_custom_call" | custom-call | flops 50331648 | bytes 393216 | tf_op jit(solution)/shard_map/pallas_call | solution.py:52
  85.5 2.1 %collective-permute-done.16.refs_2_ = bf16[128,384]{1,0:T(8,128)(2,1)S(1)} collective-permute-done((bf16[128,384]{1,0:T(8,128)(2,1)}, bf16[128,384]{1,0:T(8,128)(2,1)S(1)}, u32[]{:S(2)}, u32[]{:S(2)}) %collective-permute-start.16) | collective-permute-done | bytes 98336 | tf_op jit(solution)/shard_map/ppermute | solution.py:28
  88.3 1.9 %shard_map.103 = (bf16[128,384]{1,0:T(8,128)(2,1)}, bf16[128,384]{1,0:T(8,128)(2,1)}) custom-call(bf16[256,256]{1,0:T(8,128)(2,1)} %get-tuple-element.56.refs_0_, bf16[128,384]{1,0:T(8,128)(2,1)} %get-tuple-element.91.refs_1_.refs_4_, bf16[128,384]{1,0:T(8,128)(2,1)} %copy-done.17, bf16[128,384]{1,0:T(8,128)(2,1)} %get-tuple-element.94.refs_3_.refs_2_.refs_5_), custom_call_target="tpu_custom_call" | custom-call | flops 50331648 | bytes 393216 | tf_op jit(solution)/shard_map/pallas_call | solution.py:52
  90.9 2.4 %shard_map.104.refs_4_ = bf16[768,1152]{1,0:T(8,128)(2,1)} custom-call(bf16[256,256]{1,0:T(8,128)(2,1)} %get-tuple-element.55.refs_0_, bf16[768,256]{1,0:T(8,128)(2,1)} %refs_1_.11, bf16[128,384]{1,0:T(8,128)(2,1)} %get-tuple-element.90.refs_3_.refs_2_, bf16[128,384]{1,0:T(8,128)(2,1)} %copy-done.1, bf16[128,384]{1,0:T(8,128)(2,1)} %get-tuple-element.91.refs_1_.refs_4_), custom_call_target="tpu_custom_call" | custom-call | flops 150994944 | bytes 589824 | tf_op jit(solution)/shard_map/pallas_call | solution.py:52
  93.9 2.4 %shard_map.105.refs_4_ = bf16[768,1152]{1,0:T(8,128)(2,1)} custom-call(bf16[256,256]{1,0:T(8,128)(2,1)} %get-tuple-element.55.refs_0_, bf16[768,256]{1,0:T(8,128)(2,1)} %refs_1_.11, bf16[128,384]{1,0:T(8,128)(2,1)} %get-tuple-element.94.refs_3_.refs_2_.refs_5_, bf16[128,384]{1,0:T(8,128)(2,1)} %copy-done.20, ...), custom_call_target="tpu_custom_call", output_to_operand_aliasing={{}: (4, {})} | custom-call | flops 150994944 | bytes 589824 | tf_op jit(solution)/shard_map/pallas_call | solution.py:52
  97.0 2.4 %shard_map.106 = bf16[768,1152]{1,0:T(8,128)(2,1)} custom-call(bf16[256,256]{1,0:T(8,128)(2,1)} %get-tuple-element.55.refs_0_, bf16[768,256]{1,0:T(8,128)(2,1)} %refs_1_.11, bf16[128,384]{1,0:T(8,128)(2,1)} %get-tuple-element.95.refs_2_.refs_5_, bf16[128,384]{1,0:T(8,128)(2,1)} %copy-done.21, ...), custom_call_target="tpu_custom_call", output_to_operand_aliasing={{}: (4, {})} | custom-call | flops 150994944 | bytes 589824 | tf_op jit(solution)/shard_map/pallas_call | solution.py:52
  (99 shorter events, 44.8 us)
Async XLA Ops:
  0.0 15.4 %copy-start = (s32[8]{0:T(128)S(1)}, s32[8]{0:T(128)}, u32[]{:S(2)}) copy-start(s32[8]{0:T(128)} %param.14) | copy-start | bytes 100
  3.7 16.2 %collective-permute-start.2 = (bf16[128,384]{1,0:T(8,128)(2,1)}, bf16[128,384]{1,0:T(8,128)(2,1)S(1)}, u32[]{:S(2)}, u32[]{:S(2)}) collective-permute-start(bf16[128,384]{1,0:T(8,128)(2,1)} %get-tuple-element.62), channel_id=1, source_target_pairs={{0,1},{1,0},{2,3},{3,2},{4,5},{5,4},{6,7},{7,6},{8,9},{9,8},{10,11... | collective-permute-start | bytes 294920 | tf_op jit(solution)/shard_map/ppermute | solution.py:28
  6.8 8.6 %copy-start.22 = (s32[8]{0:T(128)S(1)}, s32[8]{0:T(128)}, u32[]{:S(2)}) copy-start(s32[8]{0:T(128)} %constant.19.clone) | copy-start | bytes 100
  10.1 15.0 %collective-permute-start.1 = (bf16[128,384]{1,0:T(8,128)(2,1)}, bf16[128,384]{1,0:T(8,128)(2,1)S(1)}, u32[]{:S(2)}, u32[]{:S(2)}) collective-permute-start(bf16[128,384]{1,0:T(8,128)(2,1)} %get-tuple-element.61), channel_id=1, source_target_pairs={{0,1},{1,0},{2,3},{3,2},{4,5},{5,4},{6,7},{7,6},{8,9},{9,8},{10,11... | collective-permute-start | bytes 294920 | tf_op jit(solution)/shard_map/ppermute | solution.py:28
  13.3 14.3 %collective-permute-start = (bf16[128,384]{1,0:T(8,128)(2,1)}, bf16[128,384]{1,0:T(8,128)(2,1)S(1)}, u32[]{:S(2)}, u32[]{:S(2)}) collective-permute-start(bf16[128,384]{1,0:T(8,128)(2,1)} %get-tuple-element.60), channel_id=1, source_target_pairs={{0,1},{1,0},{2,3},{3,2},{4,5},{5,4},{6,7},{7,6},{8,9},{9,8},{10,11... | collective-permute-start | bytes 294920 | tf_op jit(solution)/shard_map/ppermute | solution.py:28
  19.9 0.6 copy-start.2
  22.5 7.7 %collective-permute-start.4 = (bf16[128,384]{1,0:T(8,128)(2,1)}, bf16[128,384]{1,0:T(8,128)(2,1)S(1)}, u32[]{:S(2)}, u32[]{:S(2)}) collective-permute-start(bf16[128,384]{1,0:T(8,128)(2,1)} %get-tuple-element.67), channel_id=1, source_target_pairs={{0,2},{1,3},{2,0},{3,1},{4,6},{5,7},{6,4},{7,5},{8,10},{9,11},{10,... | collective-permute-start | bytes 294920 | tf_op jit(solution)/shard_map/ppermute | solution.py:28
  32.7 4.8 %collective-permute-start.5 = (bf16[128,384]{1,0:T(8,128)(2,1)}, bf16[128,384]{1,0:T(8,128)(2,1)S(1)}, u32[]{:S(2)}, u32[]{:S(2)}) collective-permute-start(bf16[128,384]{1,0:T(8,128)(2,1)} %get-tuple-element.69), channel_id=1, source_target_pairs={{0,16},{4,20},{8,24},{12,28},{16,0},{20,4},{24,8},{28,12},{1,17},{... | collective-permute-start | bytes 294920 | tf_op jit(solution)/shard_map/ppermute | solution.py:28
  34.3 7.1 %collective-permute-start.7 = (bf16[128,384]{1,0:T(8,128)(2,1)}, bf16[128,384]{1,0:T(8,128)(2,1)S(1)}, u32[]{:S(2)}, u32[]{:S(2)}) collective-permute-start(bf16[128,384]{1,0:T(8,128)(2,1)} %get-tuple-element.72), channel_id=1, source_target_pairs={{0,2},{1,3},{2,0},{3,1},{4,6},{5,7},{6,4},{7,5},{8,10},{9,11},{10,... | collective-permute-start | bytes 294920 | tf_op jit(solution)/shard_map/ppermute | solution.py:28
  39.8 5.6 %collective-permute-start.6 = (bf16[128,384]{1,0:T(8,128)(2,1)}, bf16[128,384]{1,0:T(8,128)(2,1)S(1)}, u32[]{:S(2)}, u32[]{:S(2)}) collective-permute-start(bf16[128,384]{1,0:T(8,128)(2,1)} %get-tuple-element.71), channel_id=1, source_target_pairs={{0,8},{4,12},{8,0},{12,4},{16,24},{20,28},{24,16},{28,20},{1,9},{5... | collective-permute-start | bytes 294920 | tf_op jit(solution)/shard_map/ppermute | solution.py:28
  43.9 4.8 %collective-permute-start.9 = (bf16[128,384]{1,0:T(8,128)(2,1)}, bf16[128,384]{1,0:T(8,128)(2,1)S(1)}, u32[]{:S(2)}, u32[]{:S(2)}) collective-permute-start(bf16[128,384]{1,0:T(8,128)(2,1)} %get-tuple-element.76), channel_id=1, source_target_pairs={{0,16},{4,20},{8,24},{12,28},{16,0},{20,4},{24,8},{28,12},{1,17},{... | collective-permute-start | bytes 294920 | tf_op jit(solution)/shard_map/ppermute | solution.py:28
  47.7 4.4 %collective-permute-start.8 = (bf16[128,384]{1,0:T(8,128)(2,1)}, bf16[128,384]{1,0:T(8,128)(2,1)S(1)}, u32[]{:S(2)}, u32[]{:S(2)}) collective-permute-start(bf16[128,384]{1,0:T(8,128)(2,1)} %get-tuple-element.75), channel_id=1, source_target_pairs={{0,4},{4,0},{8,12},{12,8},{16,20},{20,16},{24,28},{28,24},{1,5},{5... | collective-permute-start | bytes 294920 | tf_op jit(solution)/shard_map/ppermute | solution.py:28
  47.7 8.3 %collective-permute-start.3 = (bf16[128,384]{1,0:T(8,128)(2,1)}, bf16[128,384]{1,0:T(8,128)(2,1)S(1)}, u32[]{:S(2)}, u32[]{:S(2)}) collective-permute-start(bf16[128,384]{1,0:T(8,128)(2,1)} %get-tuple-element.66), channel_id=1, source_target_pairs={{0,2},{1,3},{2,0},{3,1},{4,6},{5,7},{6,4},{7,5},{8,10},{9,11},{10,... | collective-permute-start | bytes 294920 | tf_op jit(solution)/shard_map/ppermute | solution.py:28
  51.0 8.3 %collective-permute-start.11 = (bf16[128,384]{1,0:T(8,128)(2,1)}, bf16[128,384]{1,0:T(8,128)(2,1)S(1)}, u32[]{:S(2)}, u32[]{:S(2)}) collective-permute-start(bf16[128,384]{1,0:T(8,128)(2,1)} %get-tuple-element.81), channel_id=1, source_target_pairs={{0,8},{4,12},{8,0},{12,4},{16,24},{20,28},{24,16},{28,20},{1,9},{5... | collective-permute-start | bytes 294920 | tf_op jit(solution)/shard_map/ppermute | solution.py:28
  58.5 5.0 %collective-permute-start.10 = (bf16[128,384]{1,0:T(8,128)(2,1)}, bf16[128,384]{1,0:T(8,128)(2,1)S(1)}, u32[]{:S(2)}, u32[]{:S(2)}) collective-permute-start(bf16[128,384]{1,0:T(8,128)(2,1)} %get-tuple-element.80), channel_id=1, source_target_pairs={{0,16},{4,20},{8,24},{12,28},{16,0},{20,4},{24,8},{28,12},{1,17},{... | collective-permute-start | bytes 294920 | tf_op jit(solution)/shard_map/ppermute | solution.py:28
  61.6 5.6 %collective-permute-start.13 = (bf16[128,384]{1,0:T(8,128)(2,1)}, bf16[128,384]{1,0:T(8,128)(2,1)S(1)}, u32[]{:S(2)}, u32[]{:S(2)}) collective-permute-start(bf16[128,384]{1,0:T(8,128)(2,1)} %get-tuple-element.85), channel_id=1, source_target_pairs={{0,4},{4,0},{8,12},{12,8},{16,20},{20,16},{24,28},{28,24},{1,5},{5... | collective-permute-start | bytes 294920 | tf_op jit(solution)/shard_map/ppermute | solution.py:28
  65.8 4.8 %collective-permute-start.12 = (bf16[128,384]{1,0:T(8,128)(2,1)}, bf16[128,384]{1,0:T(8,128)(2,1)S(1)}, u32[]{:S(2)}, u32[]{:S(2)}) collective-permute-start(bf16[128,384]{1,0:T(8,128)(2,1)} %get-tuple-element.84), channel_id=1, source_target_pairs={{0,8},{4,12},{8,0},{12,4},{16,24},{20,28},{24,16},{28,20},{1,9},{5... | collective-permute-start | bytes 294920 | tf_op jit(solution)/shard_map/ppermute | solution.py:28
  66.6 7.8 %collective-permute-start.15 = (bf16[128,384]{1,0:T(8,128)(2,1)}, bf16[128,384]{1,0:T(8,128)(2,1)S(1)}, u32[]{:S(2)}, u32[]{:S(2)}) collective-permute-start(bf16[128,384]{1,0:T(8,128)(2,1)} %get-tuple-element.89), channel_id=1, source_target_pairs={{0,2},{1,3},{2,0},{3,1},{4,6},{5,7},{6,4},{7,5},{8,10},{9,11},{10,... | collective-permute-start | bytes 294920 | tf_op jit(solution)/shard_map/ppermute | solution.py:28
  72.9 4.0 %collective-permute-start.14 = (bf16[128,384]{1,0:T(8,128)(2,1)}, bf16[128,384]{1,0:T(8,128)(2,1)S(1)}, u32[]{:S(2)}, u32[]{:S(2)}) collective-permute-start(bf16[128,384]{1,0:T(8,128)(2,1)} %get-tuple-element.88), channel_id=1, source_target_pairs={{0,4},{4,0},{8,12},{12,8},{16,20},{20,16},{24,28},{28,24},{1,5},{5... | collective-permute-start | bytes 294920 | tf_op jit(solution)/shard_map/ppermute | solution.py:28
  72.9 8.8 %collective-permute-start.17 = (bf16[128,384]{1,0:T(8,128)(2,1)}, bf16[128,384]{1,0:T(8,128)(2,1)S(1)}, u32[]{:S(2)}, u32[]{:S(2)}) collective-permute-start(bf16[128,384]{1,0:T(8,128)(2,1)} %get-tuple-element.93), channel_id=1, source_target_pairs={{0,2},{1,3},{2,0},{3,1},{4,6},{5,7},{6,4},{7,5},{8,10},{9,11},{10,... | collective-permute-start | bytes 294920 | tf_op jit(solution)/shard_map/ppermute | solution.py:28
  79.4 8.2 %collective-permute-start.16 = (bf16[128,384]{1,0:T(8,128)(2,1)}, bf16[128,384]{1,0:T(8,128)(2,1)S(1)}, u32[]{:S(2)}, u32[]{:S(2)}) collective-permute-start(bf16[128,384]{1,0:T(8,128)(2,1)} %get-tuple-element.92), channel_id=1, source_target_pairs={{0,2},{1,3},{2,0},{3,1},{4,6},{5,7},{6,4},{7,5},{8,10},{9,11},{10,... | collective-permute-start | bytes 294920 | tf_op jit(solution)/shard_map/ppermute | solution.py:28
  80.9 9.3 %collective-permute-start.20 = (bf16[128,384]{1,0:T(8,128)(2,1)}, bf16[128,384]{1,0:T(8,128)(2,1)S(1)}, u32[]{:S(2)}, u32[]{:S(2)}) collective-permute-start(bf16[128,384]{1,0:T(8,128)(2,1)} %get-tuple-element.98), channel_id=1, source_target_pairs={{0,1},{1,0},{2,3},{3,2},{4,5},{5,4},{6,7},{7,6},{8,9},{9,8},{10,11... | collective-permute-start | bytes 294920 | tf_op jit(solution)/shard_map/ppermute | solution.py:28
  84.3 9.0 %collective-permute-start.19 = (bf16[128,384]{1,0:T(8,128)(2,1)}, bf16[128,384]{1,0:T(8,128)(2,1)S(1)}, u32[]{:S(2)}, u32[]{:S(2)}) collective-permute-start(bf16[128,384]{1,0:T(8,128)(2,1)} %get-tuple-element.97), channel_id=1, source_target_pairs={{0,1},{1,0},{2,3},{3,2},{4,5},{5,4},{6,7},{7,6},{8,9},{9,8},{10,11... | collective-permute-start | bytes 294920 | tf_op jit(solution)/shard_map/ppermute | solution.py:28
  90.2 6.1 %collective-permute-start.18 = (bf16[128,384]{1,0:T(8,128)(2,1)}, bf16[128,384]{1,0:T(8,128)(2,1)S(1)}, u32[]{:S(2)}, u32[]{:S(2)}) collective-permute-start(bf16[128,384]{1,0:T(8,128)(2,1)} %get-tuple-element.96), channel_id=1, source_target_pairs={{0,1},{1,0},{2,3},{3,2},{4,5},{5,4},{6,7},{7,6},{8,9},{9,8},{10,11... | collective-permute-start | bytes 294920 | tf_op jit(solution)/shard_map/ppermute | solution.py:28
  (20 other events, 12.8 us)

commit v5 on v4

--- a/solution.py
+++ b/solution.py
@@ -8,6 +8,7 @@
 LANES = 128
 CHUNKS = 3
 ROWS = 16
+SCOPED = 8 * 2**20
 F32 = jnp.float32
 BF16 = jnp.bfloat16
 WHOLE = pl.BlockSpec(memory_space=pltpu.VMEM)
@@ -53,6 +54,7 @@
         body,
         in_specs=specs + [PLACE] * len(extra),
         out_shape=outs,
+        compiler_params=pltpu.CompilerParams(vmem_limit_bytes=SCOPED),
         **more,
     )(*operands, *extra)
 

time: 100 us -> 68.7 us (0.69)
  Pallas kernels: 51.8 us -> 13.2 us
  waiting for transfers between devices: 9.25 us -> 28.7 us
  local copies, waits for them, and re-layouts: 15.5 us -> 3.36 us
    pallas_call x25, Pallas kernels: 51.8 us -> 13.2 us  [call(): pl.pallas_call(body, in_specs=specs + [PLACE] * len(extra), out_shape=out...]
    ppermute x21, waiting for transfers between devices: 9.25 us -> 28.7 us  [swap(): return lax.ppermute(block, axis, [(i, i ^ distance) for i in range(count)])]
    unnamed x46 -> x16, local copies, waits for them, and re-layouts: 13.4 us -> 2.5 us
  transfers between devices with their start and end apart: 21 -> 21, of which waited for: 6 -> 13; matrix products, arithmetic and copies ran while one was open for 2% -> 1% of each run, Pallas kernels for 45% -> 14%
where the time goes in v5:
time: 68.7 us; the launch traced here: 68.5 us
  waiting for transfers between devices  28.7 us (42%)
  starting transfers between devices  22.8 us (33%)
  Pallas kernels  13.2 us (19%)
  local copies, waits for them, and re-layouts  3.36 us (5%)
    ppermute x21, waiting for transfers between devices, swap(): return lax.ppermute(block, axis, [(i, i ^ distance) for i in range(count)])  28.7 us
    ppermute x21, starting transfers between devices, swap(): return lax.ppermute(block, axis, [(i, i ^ distance) for i in range(count)])  22.8 us
    pallas_call x25, Pallas kernels, call(): pl.pallas_call(body, in_specs=specs + [PLACE] * len(extra), out_shape=out...  13.2 us
    unnamed x16, local copies, waits for them, and re-layouts  2.5 us
  transfers between devices with their start and end apart: 21, of which 13 were waited for; matrix products, arithmetic and copies ran while one was open for 1% of the time, Pallas kernels for 14%

profile of v5, /device:TPU:0, one launch (start us, length us, event | category | flops | bytes accessed | tf_op | source)
XLA Modules:
  0.0 68.5 jit_solution(17149403884251650500)
XLA Ops:
  0.1 1.5 %copy-done.1 = bf16[768,1152]{1,0:T(8,128)(2,1)S(1)} copy-done((bf16[768,1152]{1,0:T(8,128)(2,1)S(1)}, bf16[768,1152]{1,0:T(8,128)(2,1)}, u32[]{:S(2)}) %copy-start.1) | copy-done | bytes 1769496
  2.6 1.8 %shard_map.82 = (bf16[128,384]{1,0:T(8,128)(2,1)S(1)}, bf16[128,384]{1,0:T(8,128)(2,1)S(1)}) custom-call(s32[2]{0:T(128)S(1)} %pad_add_fusion.refs_0_, bf16[768,256]{1,0:T(8,128)(2,1)S(1)} %copy-done.2, bf16[768,1152]{1,0:T(8,128)(2,1)S(1)} %copy-done.1), custom_call_target="tpu_custom_call" | custom-call | flops 150994944 | bytes 983040 | tf_op jit(solution)/shard_map/pallas_call | solution.py:53
  4.3 3.1 %collective-permute-start.2 = (bf16[128,384]{1,0:T(8,128)(2,1)S(1)}, bf16[128,384]{1,0:T(8,128)(2,1)S(1)}, u32[]{:S(2)}, u32[]{:S(2)}) collective-permute-start(bf16[128,384]{1,0:T(8,128)(2,1)S(1)} %get-tuple-element.62), channel_id=1, source_target_pairs={{0,1},{1,0},{2,3},{3,2},{4,5},{5,4},{6,7},{7,6},{8,9},{9,8},{10,11... | collective-permute-start | bytes 294920 | tf_op jit(solution)/shard_map/ppermute | solution.py:29
  7.4 1.8 %shard_map.83 = (bf16[128,384]{1,0:T(8,128)(2,1)S(1)}, bf16[128,384]{1,0:T(8,128)(2,1)S(1)}) custom-call(s32[2]{0:T(128)S(1)} %pad_add_fusion.refs_0_, bf16[768,256]{1,0:T(8,128)(2,1)S(1)} %copy-done.2, bf16[768,1152]{1,0:T(8,128)(2,1)S(1)} %copy-done.1, bf16[128,384]{1,0:T(8,128)(2,1)S(1)} %get-tuple-element.52.refs_3_.refs_1_), custom_call_target="tpu_custom_call" | custom-call | flops 150994944 | bytes 983040 | tf_op jit(solution)/shard_map/pallas_call | solution.py:53
  9.3 1.8 %shard_map.84 = (bf16[128,384]{1,0:T(8,128)(2,1)S(1)}, bf16[128,384]{1,0:T(8,128)(2,1)S(1)}) custom-call(s32[2]{0:T(128)S(1)} %pad_add_fusion.refs_0_, bf16[768,256]{1,0:T(8,128)(2,1)S(1)} %copy-done.2, bf16[768,1152]{1,0:T(8,128)(2,1)S(1)} %copy-done.1, bf16[128,384]{1,0:T(8,128)(2,1)S(1)} %get-tuple-element.53.refs_3_.refs_1_), custom_call_target="tpu_custom_call" | custom-call | flops 150994944 | bytes 983040 | tf_op jit(solution)/shard_map/pallas_call | solution.py:53
  11.1 2.1 %collective-permute-start = (bf16[128,384]{1,0:T(8,128)(2,1)S(1)}, bf16[128,384]{1,0:T(8,128)(2,1)S(1)}, u32[]{:S(2)}, u32[]{:S(2)}) collective-permute-start(bf16[128,384]{1,0:T(8,128)(2,1)S(1)} %get-tuple-element.60), channel_id=1, source_target_pairs={{0,1},{1,0},{2,3},{3,2},{4,5},{5,4},{6,7},{7,6},{8,9},{9,8},{10,11... | collective-permute-start | bytes 294920 | tf_op jit(solution)/shard_map/ppermute | solution.py:29
  15.4 2.6 %collective-permute-start.4 = (bf16[128,384]{1,0:T(8,128)(2,1)S(1)}, bf16[128,384]{1,0:T(8,128)(2,1)S(1)}, u32[]{:S(2)}, u32[]{:S(2)}) collective-permute-start(bf16[128,384]{1,0:T(8,128)(2,1)S(1)} %get-tuple-element.67), channel_id=1, source_target_pairs={{0,2},{1,3},{2,0},{3,1},{4,6},{5,7},{6,4},{7,5},{8,10},{9,11},{10,... | collective-permute-start | bytes 294920 | tf_op jit(solution)/shard_map/ppermute | solution.py:29
  18.5 3.5 %collective-permute-done.4.refs_2_ = bf16[128,384]{1,0:T(8,128)(2,1)S(1)} collective-permute-done((bf16[128,384]{1,0:T(8,128)(2,1)S(1)}, bf16[128,384]{1,0:T(8,128)(2,1)S(1)}, u32[]{:S(2)}, u32[]{:S(2)}) %collective-permute-start.4) | collective-permute-done | bytes 98336 | tf_op jit(solution)/shard_map/ppermute | solution.py:29
  22.3 1.6 %collective-permute-start.5 = (bf16[128,384]{1,0:T(8,128)(2,1)S(1)}, bf16[128,384]{1,0:T(8,128)(2,1)S(1)}, u32[]{:S(2)}, u32[]{:S(2)}) collective-permute-start(bf16[128,384]{1,0:T(8,128)(2,1)S(1)} %get-tuple-element.69), channel_id=1, source_target_pairs={{0,16},{4,20},{8,24},{12,28},{16,0},{20,4},{24,8},{28,12},{1,17},{... | collective-permute-start | bytes 294920 | tf_op jit(solution)/shard_map/ppermute | solution.py:29
  23.9 1.6 %collective-permute-start.7 = (bf16[128,384]{1,0:T(8,128)(2,1)S(1)}, bf16[128,384]{1,0:T(8,128)(2,1)S(1)}, u32[]{:S(2)}, u32[]{:S(2)}) collective-permute-start(bf16[128,384]{1,0:T(8,128)(2,1)S(1)} %get-tuple-element.72), channel_id=1, source_target_pairs={{0,2},{1,3},{2,0},{3,1},{4,6},{5,7},{6,4},{7,5},{8,10},{9,11},{10,... | collective-permute-start | bytes 294920 | tf_op jit(solution)/shard_map/ppermute | solution.py:29
  27.0 1.6 %collective-permute-start.6 = (bf16[128,384]{1,0:T(8,128)(2,1)S(1)}, bf16[128,384]{1,0:T(8,128)(2,1)S(1)}, u32[]{:S(2)}, u32[]{:S(2)}) collective-permute-start(bf16[128,384]{1,0:T(8,128)(2,1)S(1)} %get-tuple-element.71), channel_id=1, source_target_pairs={{0,8},{4,12},{8,0},{12,4},{16,24},{20,28},{24,16},{28,20},{1,9},{5... | collective-permute-start | bytes 294920 | tf_op jit(solution)/shard_map/ppermute | solution.py:29
  28.5 1.5 %collective-permute-done.7.refs_2_ = bf16[128,384]{1,0:T(8,128)(2,1)S(1)} collective-permute-done((bf16[128,384]{1,0:T(8,128)(2,1)S(1)}, bf16[128,384]{1,0:T(8,128)(2,1)S(1)}, u32[]{:S(2)}, u32[]{:S(2)}) %collective-permute-start.7) | collective-permute-done | bytes 98336 | tf_op jit(solution)/shard_map/ppermute | solution.py:29
  31.7 1.7 %collective-permute-start.3 = (bf16[128,384]{1,0:T(8,128)(2,1)S(1)}, bf16[128,384]{1,0:T(8,128)(2,1)S(1)}, u32[]{:S(2)}, u32[]{:S(2)}) collective-permute-start(bf16[128,384]{1,0:T(8,128)(2,1)S(1)} %get-tuple-element.66), channel_id=1, source_target_pairs={{0,2},{1,3},{2,0},{3,1},{4,6},{5,7},{6,4},{7,5},{8,10},{9,11},{10,... | collective-permute-start | bytes 294920 | tf_op jit(solution)/shard_map/ppermute | solution.py:29
  33.4 1.6 %collective-permute-done.9.refs_1_ = bf16[128,384]{1,0:T(8,128)(2,1)S(1)} collective-permute-done((bf16[128,384]{1,0:T(8,128)(2,1)S(1)}, bf16[128,384]{1,0:T(8,128)(2,1)S(1)}, u32[]{:S(2)}, u32[]{:S(2)}) %collective-permute-start.9) | collective-permute-done | bytes 98336 | tf_op jit(solution)/shard_map/ppermute | solution.py:29
  35.0 1.6 %collective-permute-start.11 = (bf16[128,384]{1,0:T(8,128)(2,1)S(1)}, bf16[128,384]{1,0:T(8,128)(2,1)S(1)}, u32[]{:S(2)}, u32[]{:S(2)}) collective-permute-start(bf16[128,384]{1,0:T(8,128)(2,1)S(1)} %get-tuple-element.81), channel_id=1, source_target_pairs={{0,8},{4,12},{8,0},{12,4},{16,24},{20,28},{24,16},{28,20},{1,9},{5... | collective-permute-start | bytes 294920 | tf_op jit(solution)/shard_map/ppermute | solution.py:29
  36.9 3.0 %collective-permute-done.3.refs_2_ = bf16[128,384]{1,0:T(8,128)(2,1)S(1)} collective-permute-done((bf16[128,384]{1,0:T(8,128)(2,1)S(1)}, bf16[128,384]{1,0:T(8,128)(2,1)S(1)}, u32[]{:S(2)}, u32[]{:S(2)}) %collective-permute-start.3) | collective-permute-done | bytes 98336 | tf_op jit(solution)/shard_map/ppermute | solution.py:29
  40.2 1.7 %collective-permute-start.10 = (bf16[128,384]{1,0:T(8,128)(2,1)S(1)}, bf16[128,384]{1,0:T(8,128)(2,1)S(1)}, u32[]{:S(2)}, u32[]{:S(2)}) collective-permute-start(bf16[128,384]{1,0:T(8,128)(2,1)S(1)} %get-tuple-element.80), channel_id=1, source_target_pairs={{0,16},{4,20},{8,24},{12,28},{16,0},{20,4},{24,8},{28,12},{1,17},{... | collective-permute-start | bytes 294920 | tf_op jit(solution)/shard_map/ppermute | solution.py:29
  41.9 3.0 %collective-permute-done.10.refs_1_ = bf16[128,384]{1,0:T(8,128)(2,1)S(1)} collective-permute-done((bf16[128,384]{1,0:T(8,128)(2,1)S(1)}, bf16[128,384]{1,0:T(8,128)(2,1)S(1)}, u32[]{:S(2)}, u32[]{:S(2)}) %collective-permute-start.10) | collective-permute-done | bytes 98336 | tf_op jit(solution)/shard_map/ppermute | solution.py:29
  45.0 1.6 %collective-permute-start.12 = (bf16[128,384]{1,0:T(8,128)(2,1)S(1)}, bf16[128,384]{1,0:T(8,128)(2,1)S(1)}, u32[]{:S(2)}, u32[]{:S(2)}) collective-permute-start(bf16[128,384]{1,0:T(8,128)(2,1)S(1)} %get-tuple-element.84), channel_id=1, source_target_pairs={{0,8},{4,12},{8,0},{12,4},{16,24},{20,28},{24,16},{28,20},{1,9},{5... | collective-permute-start | bytes 294920 | tf_op jit(solution)/shard_map/ppermute | solution.py:29
  46.8 2.8 %collective-permute-done.12.refs_1_ = bf16[128,384]{1,0:T(8,128)(2,1)S(1)} collective-permute-done((bf16[128,384]{1,0:T(8,128)(2,1)S(1)}, bf16[128,384]{1,0:T(8,128)(2,1)S(1)}, u32[]{:S(2)}, u32[]{:S(2)}) %collective-permute-start.12) | collective-permute-done | bytes 98336 | tf_op jit(solution)/shard_map/ppermute | solution.py:29
  49.9 3.2 %collective-permute-done.15.refs_2_ = bf16[128,384]{1,0:T(8,128)(2,1)S(1)} collective-permute-done((bf16[128,384]{1,0:T(8,128)(2,1)S(1)}, bf16[128,384]{1,0:T(8,128)(2,1)S(1)}, u32[]{:S(2)}, u32[]{:S(2)}) %collective-permute-start.15) | collective-permute-done | bytes 98336 | tf_op jit(solution)/shard_map/ppermute | solution.py:29
  53.8 2.1 %collective-permute-start.20 = (bf16[128,384]{1,0:T(8,128)(2,1)S(1)}, bf16[128,384]{1,0:T(8,128)(2,1)S(1)}, u32[]{:S(2)}, u32[]{:S(2)}) collective-permute-start(bf16[128,384]{1,0:T(8,128)(2,1)S(1)} %get-tuple-element.98), channel_id=1, source_target_pairs={{0,1},{1,0},{2,3},{3,2},{4,5},{5,4},{6,7},{7,6},{8,9},{9,8},{10,11... | collective-permute-start | bytes 294920 | tf_op jit(solution)/shard_map/ppermute | solution.py:29
  55.9 4.2 %collective-permute-done.17.refs_2_ = bf16[128,384]{1,0:T(8,128)(2,1)S(1)} collective-permute-done((bf16[128,384]{1,0:T(8,128)(2,1)S(1)}, bf16[128,384]{1,0:T(8,128)(2,1)S(1)}, u32[]{:S(2)}, u32[]{:S(2)}) %collective-permute-start.17) | collective-permute-done | bytes 98336 | tf_op jit(solution)/shard_map/ppermute | solution.py:29
  60.4 1.7 %collective-permute-done.16.refs_2_ = bf16[128,384]{1,0:T(8,128)(2,1)S(1)} collective-permute-done((bf16[128,384]{1,0:T(8,128)(2,1)S(1)}, bf16[128,384]{1,0:T(8,128)(2,1)S(1)}, u32[]{:S(2)}, u32[]{:S(2)}) %collective-permute-start.16) | collective-permute-done | bytes 98336 | tf_op jit(solution)/shard_map/ppermute | solution.py:29
  (69 shorter events, 15.6 us)
Async XLA Ops:
  0.0 13.2 %copy-start = (s32[8]{0:T(128)S(1)}, s32[8]{0:T(128)}, u32[]{:S(2)}) copy-start(s32[8]{0:T(128)} %param.14) | copy-start | bytes 100
  4.3 10.8 %collective-permute-start.2 = (bf16[128,384]{1,0:T(8,128)(2,1)S(1)}, bf16[128,384]{1,0:T(8,128)(2,1)S(1)}, u32[]{:S(2)}, u32[]{:S(2)}) collective-permute-start(bf16[128,384]{1,0:T(8,128)(2,1)S(1)} %get-tuple-element.62), channel_id=1, source_target_pairs={{0,1},{1,0},{2,3},{3,2},{4,5},{5,4},{6,7},{7,6},{8,9},{9,8},{10,11... | collective-permute-start | bytes 294920 | tf_op jit(solution)/shard_map/ppermute | solution.py:29
  7.4 5.8 %copy-start.7 = (s32[8]{0:T(128)S(1)}, s32[8]{0:T(128)}, u32[]{:S(2)}) copy-start(s32[8]{0:T(128)} %constant.19.clone) | copy-start | bytes 100
  9.2 8.8 %collective-permute-start.1 = (bf16[128,384]{1,0:T(8,128)(2,1)S(1)}, bf16[128,384]{1,0:T(8,128)(2,1)S(1)}, u32[]{:S(2)}, u32[]{:S(2)}) collective-permute-start(bf16[128,384]{1,0:T(8,128)(2,1)S(1)} %get-tuple-element.61), channel_id=1, source_target_pairs={{0,1},{1,0},{2,3},{3,2},{4,5},{5,4},{6,7},{7,6},{8,9},{9,8},{10,11... | collective-permute-start | bytes 294920 | tf_op jit(solution)/shard_map/ppermute | solution.py:29
  11.1 7.1 %collective-permute-start = (bf16[128,384]{1,0:T(8,128)(2,1)S(1)}, bf16[128,384]{1,0:T(8,128)(2,1)S(1)}, u32[]{:S(2)}, u32[]{:S(2)}) collective-permute-start(bf16[128,384]{1,0:T(8,128)(2,1)S(1)} %get-tuple-element.60), channel_id=1, source_target_pairs={{0,1},{1,0},{2,3},{3,2},{4,5},{5,4},{6,7},{7,6},{8,9},{9,8},{10,11... | collective-permute-start | bytes 294920 | tf_op jit(solution)/shard_map/ppermute | solution.py:29
  15.4 6.6 %collective-permute-start.4 = (bf16[128,384]{1,0:T(8,128)(2,1)S(1)}, bf16[128,384]{1,0:T(8,128)(2,1)S(1)}, u32[]{:S(2)}, u32[]{:S(2)}) collective-permute-start(bf16[128,384]{1,0:T(8,128)(2,1)S(1)} %get-tuple-element.67), channel_id=1, source_target_pairs={{0,2},{1,3},{2,0},{3,1},{4,6},{5,7},{6,4},{7,5},{8,10},{9,11},{10,... | collective-permute-start | bytes 294920 | tf_op jit(solution)/shard_map/ppermute | solution.py:29
  22.3 4.7 %collective-permute-start.5 = (bf16[128,384]{1,0:T(8,128)(2,1)S(1)}, bf16[128,384]{1,0:T(8,128)(2,1)S(1)}, u32[]{:S(2)}, u32[]{:S(2)}) collective-permute-start(bf16[128,384]{1,0:T(8,128)(2,1)S(1)} %get-tuple-element.69), channel_id=1, source_target_pairs={{0,16},{4,20},{8,24},{12,28},{16,0},{20,4},{24,8},{28,12},{1,17},{... | collective-permute-start | bytes 294920 | tf_op jit(solution)/shard_map/ppermute | solution.py:29
  23.9 6.2 %collective-permute-start.7 = (bf16[128,384]{1,0:T(8,128)(2,1)S(1)}, bf16[128,384]{1,0:T(8,128)(2,1)S(1)}, u32[]{:S(2)}, u32[]{:S(2)}) collective-permute-start(bf16[128,384]{1,0:T(8,128)(2,1)S(1)} %get-tuple-element.72), channel_id=1, source_target_pairs={{0,2},{1,3},{2,0},{3,1},{4,6},{5,7},{6,4},{7,5},{8,10},{9,11},{10,... | collective-permute-start | bytes 294920 | tf_op jit(solution)/shard_map/ppermute | solution.py:29
  27.0 4.7 %collective-permute-start.6 = (bf16[128,384]{1,0:T(8,128)(2,1)S(1)}, bf16[128,384]{1,0:T(8,128)(2,1)S(1)}, u32[]{:S(2)}, u32[]{:S(2)}) collective-permute-start(bf16[128,384]{1,0:T(8,128)(2,1)S(1)} %get-tuple-element.71), channel_id=1, source_target_pairs={{0,8},{4,12},{8,0},{12,4},{16,24},{20,28},{24,16},{28,20},{1,9},{5... | collective-permute-start | bytes 294920 | tf_op jit(solution)/shard_map/ppermute | solution.py:29
  30.3 4.7 %collective-permute-start.9 = (bf16[128,384]{1,0:T(8,128)(2,1)S(1)}, bf16[128,384]{1,0:T(8,128)(2,1)S(1)}, u32[]{:S(2)}, u32[]{:S(2)}) collective-permute-start(bf16[128,384]{1,0:T(8,128)(2,1)S(1)} %get-tuple-element.76), channel_id=1, source_target_pairs={{0,16},{4,20},{8,24},{12,28},{16,0},{20,4},{24,8},{28,12},{1,17},{... | collective-permute-start | bytes 294920 | tf_op jit(solution)/shard_map/ppermute | solution.py:29
  31.7 4.9 %collective-permute-start.8 = (bf16[128,384]{1,0:T(8,128)(2,1)S(1)}, bf16[128,384]{1,0:T(8,128)(2,1)S(1)}, u32[]{:S(2)}, u32[]{:S(2)}) collective-permute-start(bf16[128,384]{1,0:T(8,128)(2,1)S(1)} %get-tuple-element.75), channel_id=1, source_target_pairs={{0,4},{4,0},{8,12},{12,8},{16,20},{20,16},{24,28},{28,24},{1,5},{5... | collective-permute-start | bytes 294920 | tf_op jit(solution)/shard_map/ppermute | solution.py:29
  31.7 8.1 %collective-permute-start.3 = (bf16[128,384]{1,0:T(8,128)(2,1)S(1)}, bf16[128,384]{1,0:T(8,128)(2,1)S(1)}, u32[]{:S(2)}, u32[]{:S(2)}) collective-permute-start(bf16[128,384]{1,0:T(8,128)(2,1)S(1)} %get-tuple-element.66), channel_id=1, source_target_pairs={{0,2},{1,3},{2,0},{3,1},{4,6},{5,7},{6,4},{7,5},{8,10},{9,11},{10,... | collective-permute-start | bytes 294920 | tf_op jit(solution)/shard_map/ppermute | solution.py:29
  35.0 6.8 %collective-permute-start.11 = (bf16[128,384]{1,0:T(8,128)(2,1)S(1)}, bf16[128,384]{1,0:T(8,128)(2,1)S(1)}, u32[]{:S(2)}, u32[]{:S(2)}) collective-permute-start(bf16[128,384]{1,0:T(8,128)(2,1)S(1)} %get-tuple-element.81), channel_id=1, source_target_pairs={{0,8},{4,12},{8,0},{12,4},{16,24},{20,28},{24,16},{28,20},{1,9},{5... | collective-permute-start | bytes 294920 | tf_op jit(solution)/shard_map/ppermute | solution.py:29
  36.9 25.9 %copy-start.3 = (bf16[768,256]{1,0:T(8,128)(2,1)S(1)}, bf16[768,256]{1,0:T(8,128)(2,1)}, u32[]{:S(2)}) copy-start(bf16[768,256]{1,0:T(8,128)(2,1)} %refs_1_.11) | copy-start | bytes 1179652
  40.2 4.8 %collective-permute-start.10 = (bf16[128,384]{1,0:T(8,128)(2,1)S(1)}, bf16[128,384]{1,0:T(8,128)(2,1)S(1)}, u32[]{:S(2)}, u32[]{:S(2)}) collective-permute-start(bf16[128,384]{1,0:T(8,128)(2,1)S(1)} %get-tuple-element.80), channel_id=1, source_target_pairs={{0,16},{4,20},{8,24},{12,28},{16,0},{20,4},{24,8},{28,12},{1,17},{... | collective-permute-start | bytes 294920 | tf_op jit(solution)/shard_map/ppermute | solution.py:29
  41.9 4.7 %collective-permute-start.13 = (bf16[128,384]{1,0:T(8,128)(2,1)S(1)}, bf16[128,384]{1,0:T(8,128)(2,1)S(1)}, u32[]{:S(2)}, u32[]{:S(2)}) collective-permute-start(bf16[128,384]{1,0:T(8,128)(2,1)S(1)} %get-tuple-element.85), channel_id=1, source_target_pairs={{0,4},{4,0},{8,12},{12,8},{16,20},{20,16},{24,28},{28,24},{1,5},{5... | collective-permute-start | bytes 294920 | tf_op jit(solution)/shard_map/ppermute | solution.py:29
  45.0 4.7 %collective-permute-start.12 = (bf16[128,384]{1,0:T(8,128)(2,1)S(1)}, bf16[128,384]{1,0:T(8,128)(2,1)S(1)}, u32[]{:S(2)}, u32[]{:S(2)}) collective-permute-start(bf16[128,384]{1,0:T(8,128)(2,1)S(1)} %get-tuple-element.84), channel_id=1, source_target_pairs={{0,8},{4,12},{8,0},{12,4},{16,24},{20,28},{24,16},{28,20},{1,9},{5... | collective-permute-start | bytes 294920 | tf_op jit(solution)/shard_map/ppermute | solution.py:29
  46.6 6.6 %collective-permute-start.15 = (bf16[128,384]{1,0:T(8,128)(2,1)S(1)}, bf16[128,384]{1,0:T(8,128)(2,1)S(1)}, u32[]{:S(2)}, u32[]{:S(2)}) collective-permute-start(bf16[128,384]{1,0:T(8,128)(2,1)S(1)} %get-tuple-element.89), channel_id=1, source_target_pairs={{0,2},{1,3},{2,0},{3,1},{4,6},{5,7},{6,4},{7,5},{8,10},{9,11},{10,... | collective-permute-start | bytes 294920 | tf_op jit(solution)/shard_map/ppermute | solution.py:29
  49.7 3.7 %collective-permute-start.14 = (bf16[128,384]{1,0:T(8,128)(2,1)S(1)}, bf16[128,384]{1,0:T(8,128)(2,1)S(1)}, u32[]{:S(2)}, u32[]{:S(2)}) collective-permute-start(bf16[128,384]{1,0:T(8,128)(2,1)S(1)} %get-tuple-element.88), channel_id=1, source_target_pairs={{0,4},{4,0},{8,12},{12,8},{16,20},{20,16},{24,28},{28,24},{1,5},{5... | collective-permute-start | bytes 294920 | tf_op jit(solution)/shard_map/ppermute | solution.py:29
  49.8 10.3 %collective-permute-start.17 = (bf16[128,384]{1,0:T(8,128)(2,1)S(1)}, bf16[128,384]{1,0:T(8,128)(2,1)S(1)}, u32[]{:S(2)}, u32[]{:S(2)}) collective-permute-start(bf16[128,384]{1,0:T(8,128)(2,1)S(1)} %get-tuple-element.93), channel_id=1, source_target_pairs={{0,2},{1,3},{2,0},{3,1},{4,6},{5,7},{6,4},{7,5},{8,10},{9,11},{10,... | collective-permute-start | bytes 294920 | tf_op jit(solution)/shard_map/ppermute | solution.py:29
  53.7 8.4 %collective-permute-start.16 = (bf16[128,384]{1,0:T(8,128)(2,1)S(1)}, bf16[128,384]{1,0:T(8,128)(2,1)S(1)}, u32[]{:S(2)}, u32[]{:S(2)}) collective-permute-start(bf16[128,384]{1,0:T(8,128)(2,1)S(1)} %get-tuple-element.92), channel_id=1, source_target_pairs={{0,2},{1,3},{2,0},{3,1},{4,6},{5,7},{6,4},{7,5},{8,10},{9,11},{10,... | collective-permute-start | bytes 294920 | tf_op jit(solution)/shard_map/ppermute | solution.py:29
  53.8 9.0 %collective-permute-start.20 = (bf16[128,384]{1,0:T(8,128)(2,1)S(1)}, bf16[128,384]{1,0:T(8,128)(2,1)S(1)}, u32[]{:S(2)}, u32[]{:S(2)}) collective-permute-start(bf16[128,384]{1,0:T(8,128)(2,1)S(1)} %get-tuple-element.98), channel_id=1, source_target_pairs={{0,1},{1,0},{2,3},{3,2},{4,5},{5,4},{6,7},{7,6},{8,9},{9,8},{10,11... | collective-permute-start | bytes 294920 | tf_op jit(solution)/shard_map/ppermute | solution.py:29
  60.3 4.8 %collective-permute-start.19 = (bf16[128,384]{1,0:T(8,128)(2,1)S(1)}, bf16[128,384]{1,0:T(8,128)(2,1)S(1)}, u32[]{:S(2)}, u32[]{:S(2)}) collective-permute-start(bf16[128,384]{1,0:T(8,128)(2,1)S(1)} %get-tuple-element.97), channel_id=1, source_target_pairs={{0,1},{1,0},{2,3},{3,2},{4,5},{5,4},{6,7},{7,6},{8,9},{9,8},{10,11... | collective-permute-start | bytes 294920 | tf_op jit(solution)/shard_map/ppermute | solution.py:29
  62.4 4.8 %collective-permute-start.18 = (bf16[128,384]{1,0:T(8,128)(2,1)S(1)}, bf16[128,384]{1,0:T(8,128)(2,1)S(1)}, u32[]{:S(2)}, u32[]{:S(2)}) collective-permute-start(bf16[128,384]{1,0:T(8,128)(2,1)S(1)} %get-tuple-element.96), channel_id=1, source_target_pairs={{0,1},{1,0},{2,3},{3,2},{4,5},{5,4},{6,7},{7,6},{8,9},{9,8},{10,11... | collective-permute-start | bytes 294920 | tf_op jit(solution)/shard_map/ppermute | solution.py:29
  (5 other events, 17.6 us)

commit v6 on v5

v6 whole, which is shorter than its diff:
```python
import jax
import jax.numpy as jnp
from jax import lax
from jax.experimental import pallas as pl
from jax.experimental.pallas import tpu as pltpu
from jax.sharding import PartitionSpec as P

LANES = 128
CHUNKS = 3
ENTRY = (0, 0, 1)
ROWS = 16
SCOPED = 8 * 2**20
MOST = 59 * 2**20
F32 = jnp.float32
BF16 = jnp.bfloat16
WHOLE = pl.BlockSpec(memory_space=pltpu.VMEM)
SCALARS = pl.BlockSpec(memory_space=pltpu.SMEM)
PLACE = pl.BlockSpec(memory_space=pl.ANY)
HBM = pl.BlockSpec(memory_space=pltpu.HBM)


def cuts(columns):
    tiles = max(columns // LANES, 1)
    count = min(CHUNKS, tiles)
    edges = [tiles * i // count * LANES for i in range(count)] + [columns]
    return list(zip(edges[:-1], edges[1:]))


def swap(block, axis, distance):
    count = lax.axis_size(axis)
    return lax.ppermute(block, axis, [(i, i ^ distance) for i in range(count)])


def swapped(matrix, axis, flag):
    half = matrix.shape[axis] // 2
    low = lax.slice_in_dim(matrix, 0, half, axis=axis)
    high = lax.slice_in_dim(matrix, half, 2 * half, axis=axis)
    return jnp.where(flag == 1, jnp.concatenate([high, low], axis=axis), matrix)


def matmul(left, right):
    return lax.dot_general(left, right, (((1,), (0,)), ((), ())), preferred_element_type=F32)


def cost(flops, moved):
    return pl.CostEstimate(flops=flops, bytes_accessed=moved, transcendentals=0)


def call(kernel, name, outs, specs, operands, after, limit=SCOPED, **more):
    extra = [] if after is None else [after]

    def body(*refs):
        kernel(*refs[: len(operands)], *refs[len(operands) + len(extra) :])

    return pl.pallas_call(
        body,
        name=name,
        in_specs=specs + [PLACE] * len(extra),
        out_shape=outs,
        compiler_params=pltpu.CompilerParams(vmem_limit_bytes=limit),
        **more,
    )(*operands, *extra)


def prepare(name, info, node_order, right, middle, left, after):
    width = middle.shape[-1]
    groups = node_order.shape[0]
    block = width // groups
    last_slots = final_slots(groups)

    def kernel(info, node_order, right, middle, left, right0, right1, middle0, left0, left1):
        bit0, bit1, group = info[0], info[1], info[2]
        right0[...] = swapped(swapped(right[0, 0], 1, bit0), 0, bit1)
        place = lax.broadcasted_iota(jnp.int32, (width, 1), 0)
        source = place % block
        for slot in range(groups):
            piece = node_order[slot ^ group] * block
            source += jnp.where(place // block == slot, piece, 0)
        across = lax.broadcasted_iota(jnp.int32, (width, width), 1)
        pick = jnp.where(across == source, 1.0, 0.0).astype(BF16)
        right1[...] = matmul(pick, swapped(right[0, 1], 1, bit1)).astype(BF16)
        place = lax.broadcasted_iota(jnp.int32, (1, width), 1)
        source = place % block
        for i, slot in enumerate(last_slots):
            source += jnp.where(place // block == i, (slot ^ group) * block, 0)
        down = lax.broadcasted_iota(jnp.int32, (width, width), 0)
        pick = jnp.where(down == source, 1.0, 0.0).astype(BF16)
        middle0[...] = swapped(matmul(middle[0], pick).astype(BF16), 0, bit1)
        left0[...] = swapped(swapped(left[0, 0], 1, bit1), 0, bit0)
        left1[...] = swapped(left[0, 1], 1, bit0)

    return call(
        kernel,
        name,
        [jax.ShapeDtypeStruct((width, width), BF16)] * 5,
        [SCALARS] * 2 + [WHOLE] * 3,
        [info, node_order, right, middle, left],
        after,
        out_specs=[WHOLE] * 5,
        cost_estimate=cost(4 * width**3, 20 * width**2),
    )


def selected(total, flag, kept, send):
    half = total.shape[0] // 2
    top, bottom = total[:half].astype(BF16), total[half:].astype(BF16)
    kept[...] = jnp.where(flag == 1, bottom, top)
    send[...] = jnp.where(flag == 1, top, bottom)


def transposed_matmul(left, right):
    return lax.dot_general(left, right, (((0,), (0,)), ((), ())), preferred_element_type=F32)


def first(name, info, basis, signal, low, high, after):
    rows, width = basis.shape
    half, columns = width // 2, high - low

    def kernel(info, basis, signal, kept, send):
        total = transposed_matmul(basis[...], signal[:, low:high])
        selected(total, info[0], kept, send)

    return call(
        kernel,
        name,
        [jax.ShapeDtypeStruct((half, columns), BF16)] * 2,
        [SCALARS, WHOLE, WHOLE],
        [info, basis, signal],
        after,
        out_specs=[WHOLE] * 2,
        cost_estimate=cost(2 * rows * width * columns, 2 * rows * (columns + width)),
    )


def opening(name, info, basis, signal, low, high):
    rows, width = basis.shape
    half, columns = width // 2, high - low
    pieces = 3 if rows % (3 * ROWS) == 0 else 1
    depth = rows // pieces

    def kernel(info, basis, signal, kept, send, basis_here, signal_here, arrived):
        copies = []
        for i in range(pieces):
            part = pl.ds(i * depth, depth)
            columns_part = pl.ds(low, columns)
            copies += [
                pltpu.make_async_copy(basis.at[part], basis_here.at[part], arrived.at[i, 0]),
                pltpu.make_async_copy(
                    signal.at[part, columns_part], signal_here.at[part], arrived.at[i, 1]
                ),
            ]
        for copy in copies:
            copy.start()
        total = jnp.zeros((width, columns), F32)
        for i in range(pieces):
            part = pl.ds(i * depth, depth)
            copies[2 * i].wait()
            copies[2 * i + 1].wait()
            total += transposed_matmul(basis_here[part, :], signal_here[part, :])
        selected(total, info[0], kept, send)

    return call(
        kernel,
        name,
        [jax.ShapeDtypeStruct((half, columns), BF16)] * 2,
        [SCALARS, HBM, HBM],
        [info, basis, signal],
        None,
        limit=MOST,
        out_specs=[WHOLE] * 2,
        scratch_shapes=[
            pltpu.VMEM((rows, width), BF16),
            pltpu.VMEM((rows, columns), BF16),
            pltpu.SemaphoreType.DMA((pieces, 2)),
        ],
        cost_estimate=cost(2 * rows * width * columns, 2 * rows * (columns + width)),
    )


def level(name, weight, keep, got, after):
    half, columns = keep.shape

    def kernel(weight, keep, got, kept, send):
        total = matmul(weight[:, :half], keep[...]) + matmul(weight[:, half:], got[...])
        kept[...] = total[:half].astype(BF16)
        send[...] = total[half:].astype(BF16)

    return call(
        kernel,
        name,
        [jax.ShapeDtypeStruct((half, columns), BF16)] * 2,
        [WHOLE] * 3,
        [weight, keep, got],
        after,
        out_specs=[WHOLE] * 2,
        cost_estimate=cost(8 * half * half * columns, 8 * half * columns),
    )


def regroup(name, keep, got, block, after):
    half, columns = keep.shape

    def parts(value, which):
        return [value[i * block : (i + 1) * block] for i in range(which, half // block, 2)]

    def both(keep, got, which):
        return jnp.concatenate(parts(keep, which) + parts(got, which), axis=0)

    if block % ROWS:
        return both(keep, got, 0), both(keep, got, 1)

    def kernel(keep, got, kept, send):
        kept[...] = both(keep[...], got[...], 0)
        send[...] = both(keep[...], got[...], 1)

    return call(
        kernel,
        name,
        [jax.ShapeDtypeStruct((half, columns), BF16)] * 2,
        [WHOLE] * 2,
        [keep, got],
        after,
        out_specs=[WHOLE] * 2,
        cost_estimate=cost(0, 8 * half * columns),
    )


def last(name, weight, basis, keep, got, before, low, columns, after):
    rows, width = basis.shape
    half, wide = keep.shape
    pieces = 3 if rows % (3 * ROWS) == 0 else 1
    depth = rows // pieces
    given = [] if before is None else [before]

    def kernel(weight, basis, keep, got, *refs):
        out, here, left = refs[len(given) :]
        coeffs = matmul(weight[:, :half], keep[...]) + matmul(weight[:, half:], got[...])
        coeffs = coeffs.astype(BF16)
        copies = []
        for i in range(pieces):
            part = pl.ds(i * depth, depth)
            here[part, :] = matmul(basis[part, :], coeffs).astype(BF16)
            copy = pltpu.make_async_copy(here.at[part], out.at[part, pl.ds(low, wide)], left.at[i])
            copy.start()
            copies.append(copy)
        for copy in copies:
            copy.wait()

    return call(
        kernel,
        name,
        jax.ShapeDtypeStruct((rows, columns), BF16),
        [WHOLE] * 4 + [HBM] * len(given),
        [weight, basis, keep, got] + given,
        after,
        out_specs=HBM,
        scratch_shapes=[pltpu.VMEM((rows, wide), BF16), pltpu.SemaphoreType.DMA((pieces,))],
        input_output_aliases={4: 0} if given else {},
        cost_estimate=cost(2 * rows * width * wide, 2 * rows * wide),
    )


def final_slots(groups):
    order = list(range(groups))
    half = groups // 2
    keep, got = order[:half], order[half:]
    block = half // 2
    while block:
        one = [[x[i : i + block] for i in range(0, half, block)] for x in (keep, got)]
        keep = sum(one[0][0::2] + one[1][0::2], [])
        got = sum(one[0][1::2] + one[1][1::2], [])
        block //= 2
    return keep + got


def local(signal, col_basis, right_coupling, middle_coupling, left_coupling, row_basis, node_order):
    place = lax.axis_index("sub")
    group = lax.axis_index("mid")
    groups = lax.axis_size("mid")
    width = col_basis.shape[1]
    block = width // groups
    steps = groups.bit_length() - 1
    columns = signal.shape[1]
    chunks = cuts(columns)
    info = jnp.stack([place & 1, place >> 1 & 1, group])

    keep, got = [None] * len(chunks), [None] * len(chunks)
    weights, out, after = None, None, None
    waiting, pops, entered = [], 0, 0
    while waiting or entered < len(chunks):
        if entered < len(chunks) and pops >= ENTRY[entered]:
            i, entered = entered, entered + 1
            low, high = chunks[i]
            if i:
                keep[i], send = first(f"first{i}", info, col_basis, signal, low, high, after)
            else:
                keep[i], send = opening("opening", info, col_basis, signal, low, high)
            got[i] = swap(send, "sub", 1)
            waiting.append((i, 1))
            after = keep[i]
            continue
        i, stage = waiting.pop(0)
        pops += 1
        if weights is None:
            weights = prepare(
                "prepare", info, node_order, right_coupling, middle_coupling, left_coupling, after
            )
            right0, right1, middle, left0, left1 = weights
            after = right0
        if stage == 1:
            keep[i], send = level(f"right0_{i}", right0, keep[i], got[i], after)
            got[i] = swap(send, "sub", 2)
        elif stage == 2:
            keep[i], send = level(f"right1_{i}", right1, keep[i], got[i], after)
            got[i] = swap(send, "mid", groups // 2)
        elif stage < 2 + steps:
            slot = groups >> stage - 1
            keep[i], send = regroup(f"regroup{stage}_{i}", keep[i], got[i], slot * block, after)
            got[i] = swap(send, "mid", slot)
        elif stage == 2 + steps:
            keep[i], send = level(f"middle_{i}", middle, keep[i], got[i], after)
            got[i] = swap(send, "sub", 2)
        elif stage == 3 + steps:
            keep[i], send = level(f"left0_{i}", left0, keep[i], got[i], after)
            got[i] = swap(send, "sub", 1)
        else:
            low = chunks[i][0]
            out = last(f"last{i}", left1, row_basis, keep[i], got[i], out, low, columns, after)
            continue
        waiting.append((i, stage + 1))
        after = keep[i]
    return out


def solution(mesh):
    return jax.shard_map(
        local,
        mesh=mesh,
        in_specs=(
            P(("mid", "sub"), None),
            P(("mid", "sub"), None),
            P(("mid", "sub"), None, None, None),
            P(("mid", "sub"), None, None),
            P(("mid", "sub"), None, None, None),
            P(("mid", "sub"), None),
            P(),
        ),
        out_specs=P(("mid", "sub"), None),
        check_vma=False,
    )
```

time: 68.7 us -> 58.8 us (0.86)
  waiting for transfers between devices: 28.7 us -> 22.3 us
  local copies, waits for them, and re-layouts: 3.36 us -> 0.92 us
  starting transfers between devices: 22.8 us -> 21.6 us
    ppermute x21, waiting for transfers between devices: 28.7 us -> 22.3 us  [swap(): return lax.ppermute(block, axis, [(i, i ^ distance) for i in range(count)])]
    unnamed x16 -> x20, local copies, waits for them, and re-layouts: 2.5 us -> 0.92 us
    ppermute x21, starting transfers between devices: 22.8 us -> 21.6 us  [swap(): return lax.ppermute(block, axis, [(i, i ^ distance) for i in range(count)])]
  transfers between devices with their start and end apart: 21 -> 21, of which waited for: 13 -> 11; matrix products, arithmetic and copies ran while one was open for 1% -> 0% of each run, Pallas kernels for 14% -> 14%
where the time goes in v6:
time: 58.8 us; the launch traced here: 58.6 us
  waiting for transfers between devices  22.3 us (38%)
  starting transfers between devices  21.6 us (37%)
  Pallas kernels  13 us (22%)
  local copies, waits for them, and re-layouts  0.92 us (2%)
  other arithmetic  0.61 us (1%)
    ppermute x21, waiting for transfers between devices, swap(): return lax.ppermute(block, axis, [(i, i ^ distance) for i in range(count)])  22.3 us
    ppermute x21, starting transfers between devices, swap(): return lax.ppermute(block, axis, [(i, i ^ distance) for i in range(count)])  21.6 us
    pallas_call x25, Pallas kernels, call(): pl.pallas_call(body, name=name, in_specs=specs + [PLACE] * len(extra), ou...  13 us
  transfers between devices with their start and end apart: 21, of which 11 were waited for; matrix products, arithmetic and copies ran while one was open for 0% of the time, Pallas kernels for 14%

profile of v6, /device:TPU:0, one launch (start us, length us, event | category | flops | bytes accessed | tf_op | source)
XLA Modules:
  0.0 58.6 jit_solution(1002863541011772470)
XLA Ops:
  0.6 3.2 %opening.1 = (bf16[128,384]{1,0:T(8,128)(2,1)}, bf16[128,384]{1,0:T(8,128)(2,1)}) custom-call(s32[3]{0:T(128)} %pad_add_fusion.refs_0_, bf16[768,256]{1,0:T(8,128)(2,1)} %refs_1_.10, bf16[768,1152]{1,0:T(8,128)(2,1)} %refs_2_.7), custom_call_target="tpu_custom_call" | custom-call | flops 150994944 | bytes 983040 | tf_op jit(solution)/shard_map/opening/pallas_call | solution.py:55
  3.9 3.1 %collective-permute-start = (bf16[128,384]{1,0:T(8,128)(2,1)}, bf16[128,384]{1,0:T(8,128)(2,1)S(1)}, u32[]{:S(2)}, u32[]{:S(2)}) collective-permute-start(bf16[128,384]{1,0:T(8,128)(2,1)} %get-tuple-element.59), channel_id=1, source_target_pairs={{0,1},{1,0},{2,3},{3,2},{4,5},{5,4},{6,7},{7,6},{8,9},{9,8},{10,11... | collective-permute-start | bytes 294920 | tf_op jit(solution)/shard_map/ppermute | solution.py:31
  7.0 0.9 %copy-done.3 = bf16[128,384]{1,0:T(8,128)(2,1)S(1)} copy-done((bf16[128,384]{1,0:T(8,128)(2,1)S(1)}, bf16[128,384]{1,0:T(8,128)(2,1)}, u32[]{:S(2)}) %copy-start.3) | copy-done | bytes 98328
  7.9 0.9 %first1.1 = (bf16[128,384]{1,0:T(8,128)(2,1)S(1)}, bf16[128,384]{1,0:T(8,128)(2,1)S(1)}) custom-call(s32[3]{0:T(128)S(1)} %copy-done.8, bf16[768,256]{1,0:T(8,128)(2,1)S(1)} %copy-done.1, bf16[768,1152]{1,0:T(8,128)(2,1)S(1)} %copy-done, bf16[128,384]{1,0:T(8,128)(2,1)S(1)} %copy-done.3), custom_call_target="tpu_custom_call" | custom-call | flops 150994944 | bytes 983040 | tf_op jit(solution)/shard_map/first1/pallas_call | solution.py:55
  10.2 2.9 %collective-permute-start.2 = (bf16[128,384]{1,0:T(8,128)(2,1)S(1)}, bf16[128,384]{1,0:T(8,128)(2,1)S(1)}, u32[]{:S(2)}, u32[]{:S(2)}) collective-permute-start(bf16[128,384]{1,0:T(8,128)(2,1)S(1)} %get-tuple-element.63), channel_id=1, source_target_pairs={{0,2},{1,3},{2,0},{3,1},{4,6},{5,7},{6,4},{7,5},{8,10},{9,11},{10,... | collective-permute-start | bytes 294920 | tf_op jit(solution)/shard_map/ppermute | solution.py:31
  13.1 0.9 %first2.1 = (bf16[128,384]{1,0:T(8,128)(2,1)S(1)}, bf16[128,384]{1,0:T(8,128)(2,1)S(1)}) custom-call(s32[3]{0:T(128)S(1)} %copy-done.8, bf16[768,256]{1,0:T(8,128)(2,1)S(1)} %copy-done.1, bf16[768,1152]{1,0:T(8,128)(2,1)S(1)} %copy-done, bf16[128,384]{1,0:T(8,128)(2,1)S(1)} %get-tuple-element.60.refs_3_.refs_1_), custom_call_target="tpu_custom_call" | custom-call | flops 150994944 | bytes 983040 | tf_op jit(solution)/shard_map/first2/pallas_call | solution.py:55
  14.1 2.0 %collective-permute-start.1 = (bf16[128,384]{1,0:T(8,128)(2,1)S(1)}, bf16[128,384]{1,0:T(8,128)(2,1)S(1)}, u32[]{:S(2)}, u32[]{:S(2)}) collective-permute-start(bf16[128,384]{1,0:T(8,128)(2,1)S(1)} %get-tuple-element.62), channel_id=1, source_target_pairs={{0,1},{1,0},{2,3},{3,2},{4,5},{5,4},{6,7},{7,6},{8,9},{9,8},{10,11... | collective-permute-start | bytes 294920 | tf_op jit(solution)/shard_map/ppermute | solution.py:31
  16.3 1.2 %collective-permute-start.6 = (bf16[128,384]{1,0:T(8,128)(2,1)S(1)}, bf16[128,384]{1,0:T(8,128)(2,1)S(1)}, u32[]{:S(2)}, u32[]{:S(2)}) collective-permute-start(bf16[128,384]{1,0:T(8,128)(2,1)S(1)} %get-tuple-element.70), channel_id=1, source_target_pairs={{0,2},{1,3},{2,0},{3,1},{4,6},{5,7},{6,4},{7,5},{8,10},{9,11},{10,... | collective-permute-start | bytes 294920 | tf_op jit(solution)/shard_map/ppermute | solution.py:31
  17.7 1.6 %collective-permute-start.5 = (bf16[128,384]{1,0:T(8,128)(2,1)S(1)}, bf16[128,384]{1,0:T(8,128)(2,1)S(1)}, u32[]{:S(2)}, u32[]{:S(2)}) collective-permute-start(bf16[128,384]{1,0:T(8,128)(2,1)S(1)} %get-tuple-element.69), channel_id=1, source_target_pairs={{0,16},{4,20},{8,24},{12,28},{16,0},{20,4},{24,8},{28,12},{1,17},{... | collective-permute-start | bytes 294920 | tf_op jit(solution)/shard_map/ppermute | solution.py:31
  19.6 1.9 %collective-permute-start.4 = (bf16[128,384]{1,0:T(8,128)(2,1)S(1)}, bf16[128,384]{1,0:T(8,128)(2,1)S(1)}, u32[]{:S(2)}, u32[]{:S(2)}) collective-permute-start(bf16[128,384]{1,0:T(8,128)(2,1)S(1)} %get-tuple-element.68), channel_id=1, source_target_pairs={{0,2},{1,3},{2,0},{3,1},{4,6},{5,7},{6,4},{7,5},{8,10},{9,11},{10,... | collective-permute-start | bytes 294920 | tf_op jit(solution)/shard_map/ppermute | solution.py:31
  21.5 3.3 %collective-permute-done.6.refs_2_ = bf16[128,384]{1,0:T(8,128)(2,1)S(1)} collective-permute-done((bf16[128,384]{1,0:T(8,128)(2,1)S(1)}, bf16[128,384]{1,0:T(8,128)(2,1)S(1)}, u32[]{:S(2)}, u32[]{:S(2)}) %collective-permute-start.6) | collective-permute-done | bytes 98336 | tf_op jit(solution)/shard_map/ppermute | solution.py:31
  25.1 1.6 %collective-permute-start.9 = (bf16[128,384]{1,0:T(8,128)(2,1)S(1)}, bf16[128,384]{1,0:T(8,128)(2,1)S(1)}, u32[]{:S(2)}, u32[]{:S(2)}) collective-permute-start(bf16[128,384]{1,0:T(8,128)(2,1)S(1)} %get-tuple-element.76), channel_id=1, source_target_pairs={{0,16},{4,20},{8,24},{12,28},{16,0},{20,4},{24,8},{28,12},{1,17},{... | collective-permute-start | bytes 294920 | tf_op jit(solution)/shard_map/ppermute | solution.py:31
  26.7 1.6 %collective-permute-start.8 = (bf16[128,384]{1,0:T(8,128)(2,1)S(1)}, bf16[128,384]{1,0:T(8,128)(2,1)S(1)}, u32[]{:S(2)}, u32[]{:S(2)}) collective-permute-start(bf16[128,384]{1,0:T(8,128)(2,1)S(1)} %get-tuple-element.75), channel_id=1, source_target_pairs={{0,8},{4,12},{8,0},{12,4},{16,24},{20,28},{24,16},{28,20},{1,9},{5... | collective-permute-start | bytes 294920 | tf_op jit(solution)/shard_map/ppermute | solution.py:31
  29.1 0.9 %collective-permute-done.9.refs_1_ = bf16[128,384]{1,0:T(8,128)(2,1)S(1)} collective-permute-done((bf16[128,384]{1,0:T(8,128)(2,1)S(1)}, bf16[128,384]{1,0:T(8,128)(2,1)S(1)}, u32[]{:S(2)}, u32[]{:S(2)}) %collective-permute-start.9) | collective-permute-done | bytes 98336 | tf_op jit(solution)/shard_map/ppermute | solution.py:31
  30.0 1.6 %collective-permute-start.12 = (bf16[128,384]{1,0:T(8,128)(2,1)S(1)}, bf16[128,384]{1,0:T(8,128)(2,1)S(1)}, u32[]{:S(2)}, u32[]{:S(2)}) collective-permute-start(bf16[128,384]{1,0:T(8,128)(2,1)S(1)} %get-tuple-element.82), channel_id=1, source_target_pairs={{0,8},{4,12},{8,0},{12,4},{16,24},{20,28},{24,16},{28,20},{1,9},{5... | collective-permute-start | bytes 294920 | tf_op jit(solution)/shard_map/ppermute | solution.py:31
  31.7 1.5 %collective-permute-done.7.refs_1_ = bf16[128,384]{1,0:T(8,128)(2,1)S(1)} collective-permute-done((bf16[128,384]{1,0:T(8,128)(2,1)S(1)}, bf16[128,384]{1,0:T(8,128)(2,1)S(1)}, u32[]{:S(2)}, u32[]{:S(2)}) %collective-permute-start.7) | collective-permute-done | bytes 98336 | tf_op jit(solution)/shard_map/ppermute | solution.py:31
  33.8 0.8 %collective-permute-done.12.refs_1_ = bf16[128,384]{1,0:T(8,128)(2,1)S(1)} collective-permute-done((bf16[128,384]{1,0:T(8,128)(2,1)S(1)}, bf16[128,384]{1,0:T(8,128)(2,1)S(1)}, u32[]{:S(2)}, u32[]{:S(2)}) %collective-permute-start.12) | collective-permute-done | bytes 98336 | tf_op jit(solution)/shard_map/ppermute | solution.py:31
  35.1 2.8 %collective-permute-done.10.refs_1_ = bf16[128,384]{1,0:T(8,128)(2,1)S(1)} collective-permute-done((bf16[128,384]{1,0:T(8,128)(2,1)S(1)}, bf16[128,384]{1,0:T(8,128)(2,1)S(1)}, u32[]{:S(2)}, u32[]{:S(2)}) %collective-permute-start.10) | collective-permute-done | bytes 98336 | tf_op jit(solution)/shard_map/ppermute | solution.py:31
  38.7 7.2 %collective-permute-done.14.refs_2_ = bf16[128,384]{1,0:T(8,128)(2,1)S(1)} collective-permute-done((bf16[128,384]{1,0:T(8,128)(2,1)S(1)}, bf16[128,384]{1,0:T(8,128)(2,1)S(1)}, u32[]{:S(2)}, u32[]{:S(2)}) %collective-permute-start.14) | collective-permute-done | bytes 98336 | tf_op jit(solution)/shard_map/ppermute | solution.py:31
  46.4 2.0 %collective-permute-start.20 = (bf16[128,384]{1,0:T(8,128)(2,1)S(1)}, bf16[128,384]{1,0:T(8,128)(2,1)S(1)}, u32[]{:S(2)}, u32[]{:S(2)}) collective-permute-start(bf16[128,384]{1,0:T(8,128)(2,1)S(1)} %get-tuple-element.98), channel_id=1, source_target_pairs={{0,1},{1,0},{2,3},{3,2},{4,5},{5,4},{6,7},{7,6},{8,9},{9,8},{10,11... | collective-permute-start | bytes 294920 | tf_op jit(solution)/shard_map/ppermute | solution.py:31
  48.8 3.5 %collective-permute-done.16.refs_2_ = bf16[128,384]{1,0:T(8,128)(2,1)S(1)} collective-permute-done((bf16[128,384]{1,0:T(8,128)(2,1)S(1)}, bf16[128,384]{1,0:T(8,128)(2,1)S(1)}, u32[]{:S(2)}, u32[]{:S(2)}) %collective-permute-start.16) | collective-permute-done | bytes 98336 | tf_op jit(solution)/shard_map/ppermute | solution.py:31
  53.1 1.3 %last0.1.refs_4_ = bf16[768,1152]{1,0:T(8,128)(2,1)} custom-call(bf16[256,256]{1,0:T(8,128)(2,1)S(1)} %get-tuple-element.54.refs_0_, bf16[768,256]{1,0:T(8,128)(2,1)S(1)} %copy-done.2, bf16[128,384]{1,0:T(8,128)(2,1)S(1)} %get-tuple-element.90.refs_3_.refs_2_, bf16[128,384]{1,0:T(8,128)(2,1)S(1)} %collective-permute-done.20.refs_3_, ...), custom_call_target="tpu_custom_call" | custom-call | flops 150994944 | bytes 589824 | tf_op jit(solution)/shard_map/last0/pallas_call | solution.py:55
  55.2 1.3 %last1.1.refs_4_ = bf16[768,1152]{1,0:T(8,128)(2,1)} custom-call(bf16[256,256]{1,0:T(8,128)(2,1)S(1)} %get-tuple-element.54.refs_0_, bf16[768,256]{1,0:T(8,128)(2,1)S(1)} %copy-done.2, bf16[128,384]{1,0:T(8,128)(2,1)S(1)} %get-tuple-element.94.refs_3_.refs_4_.refs_2_, ...), custom_call_target="tpu_custom_call", output_to_operand_aliasing={{}: (4, {})} | custom-call | flops 150994944 | bytes 589824 | tf_op jit(solution)/shard_map/last1/pallas_call | solution.py:55
  57.3 1.3 %last2.1 = bf16[768,1152]{1,0:T(8,128)(2,1)} custom-call(bf16[256,256]{1,0:T(8,128)(2,1)S(1)} %get-tuple-element.54.refs_0_, bf16[768,256]{1,0:T(8,128)(2,1)S(1)} %copy-done.2, bf16[128,384]{1,0:T(8,128)(2,1)S(1)} %get-tuple-element.95.refs_5_.refs_2_, bf16[128,384]{1,0:T(8,128)(2,1)S(1)} %collective-permute-done.18.refs_3_, ...), custom_call_target="tpu_custom_call", output_to_operand_aliasing={{}: (4, {})} | custom-call | flops 150994944 | bytes 589824 | tf_op jit(solution)/shard_map/last2/pallas_call | solution.py:55
  (64 shorter events, 9.1 us)
Async XLA Ops:
  0.0 7.0 %copy-start = (bf16[768,1152]{1,0:T(8,128)(2,1)S(1)}, bf16[768,1152]{1,0:T(8,128)(2,1)}, u32[]{:S(2)}) copy-start(bf16[768,1152]{1,0:T(8,128)(2,1)} %refs_2_.7) | copy-start | bytes 5308420
  0.6 8.3 %copy-start.9 = (s32[8]{0:T(128)S(1)}, s32[8]{0:T(128)}, u32[]{:S(2)}) copy-start(s32[8]{0:T(128)} %refs_1_.9) | copy-start | bytes 100
  3.9 6.1 %collective-permute-start = (bf16[128,384]{1,0:T(8,128)(2,1)}, bf16[128,384]{1,0:T(8,128)(2,1)S(1)}, u32[]{:S(2)}, u32[]{:S(2)}) collective-permute-start(bf16[128,384]{1,0:T(8,128)(2,1)} %get-tuple-element.59), channel_id=1, source_target_pairs={{0,1},{1,0},{2,3},{3,2},{4,5},{5,4},{6,7},{7,6},{8,9},{9,8},{10,11... | collective-permute-start | bytes 294920 | tf_op jit(solution)/shard_map/ppermute | solution.py:31
  8.8 7.2 %collective-permute-start.3 = (bf16[128,384]{1,0:T(8,128)(2,1)S(1)}, bf16[128,384]{1,0:T(8,128)(2,1)S(1)}, u32[]{:S(2)}, u32[]{:S(2)}) collective-permute-start(bf16[128,384]{1,0:T(8,128)(2,1)S(1)} %get-tuple-element.64), channel_id=1, source_target_pairs={{0,1},{1,0},{2,3},{3,2},{4,5},{5,4},{6,7},{7,6},{8,9},{9,8},{10,11... | collective-permute-start | bytes 294920 | tf_op jit(solution)/shard_map/ppermute | solution.py:31
  10.2 7.2 %collective-permute-start.2 = (bf16[128,384]{1,0:T(8,128)(2,1)S(1)}, bf16[128,384]{1,0:T(8,128)(2,1)S(1)}, u32[]{:S(2)}, u32[]{:S(2)}) collective-permute-start(bf16[128,384]{1,0:T(8,128)(2,1)S(1)} %get-tuple-element.63), channel_id=1, source_target_pairs={{0,2},{1,3},{2,0},{3,1},{4,6},{5,7},{6,4},{7,5},{8,10},{9,11},{10,... | collective-permute-start | bytes 294920 | tf_op jit(solution)/shard_map/ppermute | solution.py:31
  14.1 5.2 %collective-permute-start.1 = (bf16[128,384]{1,0:T(8,128)(2,1)S(1)}, bf16[128,384]{1,0:T(8,128)(2,1)S(1)}, u32[]{:S(2)}, u32[]{:S(2)}) collective-permute-start(bf16[128,384]{1,0:T(8,128)(2,1)S(1)} %get-tuple-element.62), channel_id=1, source_target_pairs={{0,1},{1,0},{2,3},{3,2},{4,5},{5,4},{6,7},{7,6},{8,9},{9,8},{10,11... | collective-permute-start | bytes 294920 | tf_op jit(solution)/shard_map/ppermute | solution.py:31
  16.3 8.5 %collective-permute-start.6 = (bf16[128,384]{1,0:T(8,128)(2,1)S(1)}, bf16[128,384]{1,0:T(8,128)(2,1)S(1)}, u32[]{:S(2)}, u32[]{:S(2)}) collective-permute-start(bf16[128,384]{1,0:T(8,128)(2,1)S(1)} %get-tuple-element.70), channel_id=1, source_target_pairs={{0,2},{1,3},{2,0},{3,1},{4,6},{5,7},{6,4},{7,5},{8,10},{9,11},{10,... | collective-permute-start | bytes 294920 | tf_op jit(solution)/shard_map/ppermute | solution.py:31
  17.7 8.9 %collective-permute-start.5 = (bf16[128,384]{1,0:T(8,128)(2,1)S(1)}, bf16[128,384]{1,0:T(8,128)(2,1)S(1)}, u32[]{:S(2)}, u32[]{:S(2)}) collective-permute-start(bf16[128,384]{1,0:T(8,128)(2,1)S(1)} %get-tuple-element.69), channel_id=1, source_target_pairs={{0,16},{4,20},{8,24},{12,28},{16,0},{20,4},{24,8},{28,12},{1,17},{... | collective-permute-start | bytes 294920 | tf_op jit(solution)/shard_map/ppermute | solution.py:31
  19.6 8.7 %collective-permute-start.4 = (bf16[128,384]{1,0:T(8,128)(2,1)S(1)}, bf16[128,384]{1,0:T(8,128)(2,1)S(1)}, u32[]{:S(2)}, u32[]{:S(2)}) collective-permute-start(bf16[128,384]{1,0:T(8,128)(2,1)S(1)} %get-tuple-element.68), channel_id=1, source_target_pairs={{0,2},{1,3},{2,0},{3,1},{4,6},{5,7},{6,4},{7,5},{8,10},{9,11},{10,... | collective-permute-start | bytes 294920 | tf_op jit(solution)/shard_map/ppermute | solution.py:31
  25.1 4.9 %collective-permute-start.9 = (bf16[128,384]{1,0:T(8,128)(2,1)S(1)}, bf16[128,384]{1,0:T(8,128)(2,1)S(1)}, u32[]{:S(2)}, u32[]{:S(2)}) collective-permute-start(bf16[128,384]{1,0:T(8,128)(2,1)S(1)} %get-tuple-element.76), channel_id=1, source_target_pairs={{0,16},{4,20},{8,24},{12,28},{16,0},{20,4},{24,8},{28,12},{1,17},{... | collective-permute-start | bytes 294920 | tf_op jit(solution)/shard_map/ppermute | solution.py:31
  26.7 4.9 %collective-permute-start.8 = (bf16[128,384]{1,0:T(8,128)(2,1)S(1)}, bf16[128,384]{1,0:T(8,128)(2,1)S(1)}, u32[]{:S(2)}, u32[]{:S(2)}) collective-permute-start(bf16[128,384]{1,0:T(8,128)(2,1)S(1)} %get-tuple-element.75), channel_id=1, source_target_pairs={{0,8},{4,12},{8,0},{12,4},{16,24},{20,28},{24,16},{28,20},{1,9},{5... | collective-permute-start | bytes 294920 | tf_op jit(solution)/shard_map/ppermute | solution.py:31
  28.5 4.7 %collective-permute-start.7 = (bf16[128,384]{1,0:T(8,128)(2,1)S(1)}, bf16[128,384]{1,0:T(8,128)(2,1)S(1)}, u32[]{:S(2)}, u32[]{:S(2)}) collective-permute-start(bf16[128,384]{1,0:T(8,128)(2,1)S(1)} %get-tuple-element.74), channel_id=1, source_target_pairs={{0,16},{4,20},{8,24},{12,28},{16,0},{20,4},{24,8},{28,12},{1,17},{... | collective-permute-start | bytes 294920 | tf_op jit(solution)/shard_map/ppermute | solution.py:31
  30.0 4.7 %collective-permute-start.12 = (bf16[128,384]{1,0:T(8,128)(2,1)S(1)}, bf16[128,384]{1,0:T(8,128)(2,1)S(1)}, u32[]{:S(2)}, u32[]{:S(2)}) collective-permute-start(bf16[128,384]{1,0:T(8,128)(2,1)S(1)} %get-tuple-element.82), channel_id=1, source_target_pairs={{0,8},{4,12},{8,0},{12,4},{16,24},{20,28},{24,16},{28,20},{1,9},{5... | collective-permute-start | bytes 294920 | tf_op jit(solution)/shard_map/ppermute | solution.py:31
  31.6 21.5 %copy-start.2 = (bf16[768,256]{1,0:T(8,128)(2,1)S(1)}, bf16[768,256]{1,0:T(8,128)(2,1)}, u32[]{:S(2)}) copy-start(bf16[768,256]{1,0:T(8,128)(2,1)} %refs_1_.13) | copy-start | bytes 1179652
  31.6 3.2 %collective-permute-start.11 = (bf16[128,384]{1,0:T(8,128)(2,1)S(1)}, bf16[128,384]{1,0:T(8,128)(2,1)S(1)}, u32[]{:S(2)}, u32[]{:S(2)}) collective-permute-start(bf16[128,384]{1,0:T(8,128)(2,1)S(1)} %get-tuple-element.81), channel_id=1, source_target_pairs={{0,4},{4,0},{8,12},{12,8},{16,20},{20,16},{24,28},{28,24},{1,5},{5... | collective-permute-start | bytes 294920 | tf_op jit(solution)/shard_map/ppermute | solution.py:31
  33.2 4.7 %collective-permute-start.10 = (bf16[128,384]{1,0:T(8,128)(2,1)S(1)}, bf16[128,384]{1,0:T(8,128)(2,1)S(1)}, u32[]{:S(2)}, u32[]{:S(2)}) collective-permute-start(bf16[128,384]{1,0:T(8,128)(2,1)S(1)} %get-tuple-element.80), channel_id=1, source_target_pairs={{0,8},{4,12},{8,0},{12,4},{16,24},{20,28},{24,16},{28,20},{1,9},{5... | collective-permute-start | bytes 294920 | tf_op jit(solution)/shard_map/ppermute | solution.py:31
  34.7 3.3 %collective-permute-start.15 = (bf16[128,384]{1,0:T(8,128)(2,1)S(1)}, bf16[128,384]{1,0:T(8,128)(2,1)S(1)}, u32[]{:S(2)}, u32[]{:S(2)}) collective-permute-start(bf16[128,384]{1,0:T(8,128)(2,1)S(1)} %get-tuple-element.88), channel_id=1, source_target_pairs={{0,4},{4,0},{8,12},{12,8},{16,20},{20,16},{24,28},{28,24},{1,5},{5... | collective-permute-start | bytes 294920 | tf_op jit(solution)/shard_map/ppermute | solution.py:31
  35.0 10.8 %collective-permute-start.14 = (bf16[128,384]{1,0:T(8,128)(2,1)S(1)}, bf16[128,384]{1,0:T(8,128)(2,1)S(1)}, u32[]{:S(2)}, u32[]{:S(2)}) collective-permute-start(bf16[128,384]{1,0:T(8,128)(2,1)S(1)} %get-tuple-element.87), channel_id=1, source_target_pairs={{0,2},{1,3},{2,0},{3,1},{4,6},{5,7},{6,4},{7,5},{8,10},{9,11},{10,... | collective-permute-start | bytes 294920 | tf_op jit(solution)/shard_map/ppermute | solution.py:31
  37.9 8.1 %collective-permute-start.13 = (bf16[128,384]{1,0:T(8,128)(2,1)S(1)}, bf16[128,384]{1,0:T(8,128)(2,1)S(1)}, u32[]{:S(2)}, u32[]{:S(2)}) collective-permute-start(bf16[128,384]{1,0:T(8,128)(2,1)S(1)} %get-tuple-element.86), channel_id=1, source_target_pairs={{0,4},{4,0},{8,12},{12,8},{16,20},{20,16},{24,28},{28,24},{1,5},{5... | collective-permute-start | bytes 294920 | tf_op jit(solution)/shard_map/ppermute | solution.py:31
  38.3 10.1 %collective-permute-start.17 = (bf16[128,384]{1,0:T(8,128)(2,1)S(1)}, bf16[128,384]{1,0:T(8,128)(2,1)S(1)}, u32[]{:S(2)}, u32[]{:S(2)}) collective-permute-start(bf16[128,384]{1,0:T(8,128)(2,1)S(1)} %get-tuple-element.93), channel_id=1, source_target_pairs={{0,2},{1,3},{2,0},{3,1},{4,6},{5,7},{6,4},{7,5},{8,10},{9,11},{10,... | collective-permute-start | bytes 294920 | tf_op jit(solution)/shard_map/ppermute | solution.py:31
  46.3 6.0 %collective-permute-start.16 = (bf16[128,384]{1,0:T(8,128)(2,1)S(1)}, bf16[128,384]{1,0:T(8,128)(2,1)S(1)}, u32[]{:S(2)}, u32[]{:S(2)}) collective-permute-start(bf16[128,384]{1,0:T(8,128)(2,1)S(1)} %get-tuple-element.92), channel_id=1, source_target_pairs={{0,2},{1,3},{2,0},{3,1},{4,6},{5,7},{6,4},{7,5},{8,10},{9,11},{10,... | collective-permute-start | bytes 294920 | tf_op jit(solution)/shard_map/ppermute | solution.py:31
  46.4 6.7 %collective-permute-start.20 = (bf16[128,384]{1,0:T(8,128)(2,1)S(1)}, bf16[128,384]{1,0:T(8,128)(2,1)S(1)}, u32[]{:S(2)}, u32[]{:S(2)}) collective-permute-start(bf16[128,384]{1,0:T(8,128)(2,1)S(1)} %get-tuple-element.98), channel_id=1, source_target_pairs={{0,1},{1,0},{2,3},{3,2},{4,5},{5,4},{6,7},{7,6},{8,9},{9,8},{10,11... | collective-permute-start | bytes 294920 | tf_op jit(solution)/shard_map/ppermute | solution.py:31
  48.6 6.6 %collective-permute-start.19 = (bf16[128,384]{1,0:T(8,128)(2,1)S(1)}, bf16[128,384]{1,0:T(8,128)(2,1)S(1)}, u32[]{:S(2)}, u32[]{:S(2)}) collective-permute-start(bf16[128,384]{1,0:T(8,128)(2,1)S(1)} %get-tuple-element.97), channel_id=1, source_target_pairs={{0,1},{1,0},{2,3},{3,2},{4,5},{5,4},{6,7},{7,6},{8,9},{9,8},{10,11... | collective-permute-start | bytes 294920 | tf_op jit(solution)/shard_map/ppermute | solution.py:31
  52.6 4.7 %collective-permute-start.18 = (bf16[128,384]{1,0:T(8,128)(2,1)S(1)}, bf16[128,384]{1,0:T(8,128)(2,1)S(1)}, u32[]{:S(2)}, u32[]{:S(2)}) collective-permute-start(bf16[128,384]{1,0:T(8,128)(2,1)S(1)} %get-tuple-element.96), channel_id=1, source_target_pairs={{0,1},{1,0},{2,3},{3,2},{4,5},{5,4},{6,7},{7,6},{8,9},{9,8},{10,11... | collective-permute-start | bytes 294920 | tf_op jit(solution)/shard_map/ppermute | solution.py:31
  (7 other events, 19.5 us)

commit v7 on v6

v7 whole, which is shorter than its diff:
```python
import jax
import jax.numpy as jnp
from jax import lax
from jax.experimental import pallas as pl
from jax.experimental.pallas import tpu as pltpu
from jax.sharding import PartitionSpec as P

LANES = 128
ENTRY_SHARES = (3, 3, 3)
ENTRY = (0, 0, 1)
MERGED = ((0,), (1,), (2,))
SPLIT = {}
ROWS = 16
SCOPED = 8 * 2**20
MOST = 107 * 2**19
F32 = jnp.float32
BF16 = jnp.bfloat16
WHOLE = pl.BlockSpec(memory_space=pltpu.VMEM)
SCALARS = pl.BlockSpec(memory_space=pltpu.SMEM)
PLACE = pl.BlockSpec(memory_space=pl.ANY)
HBM = pl.BlockSpec(memory_space=pltpu.HBM)


def shares(columns, weights):
    tiles = columns // LANES
    if tiles < len(weights):
        return [columns]
    edges = [round(tiles * sum(weights[:i]) / sum(weights)) * LANES for i in range(len(weights))]
    edges.append(columns)
    return [high - low for low, high in zip(edges[:-1], edges[1:])]


def swap(block, axis, distance):
    count = lax.axis_size(axis)
    return lax.ppermute(block, axis, [(i, i ^ distance) for i in range(count)])


def swapped(matrix, axis, flag):
    half = matrix.shape[axis] // 2
    low = lax.slice_in_dim(matrix, 0, half, axis=axis)
    high = lax.slice_in_dim(matrix, half, 2 * half, axis=axis)
    return jnp.where(flag == 1, jnp.concatenate([high, low], axis=axis), matrix)


def matmul(left, right):
    return lax.dot_general(left, right, (((1,), (0,)), ((), ())), preferred_element_type=F32)


def cost(flops, moved):
    return pl.CostEstimate(flops=flops, bytes_accessed=moved, transcendentals=0)


def call(kernel, name, outs, specs, operands, after, limit=SCOPED, **more):
    extra = [] if after is None else [after]

    def body(*refs):
        kernel(*refs[: len(operands)], *refs[len(operands) + len(extra) :])

    return pl.pallas_call(
        body,
        name=name,
        in_specs=specs + [PLACE] * len(extra),
        out_shape=outs,
        compiler_params=pltpu.CompilerParams(vmem_limit_bytes=limit),
        **more,
    )(*operands, *extra)


def prepare(name, node_order, right, middle, left, after):
    width = middle.shape[-1]
    groups = node_order.shape[0]
    block = width // groups
    last_slots = final_slots(groups)

    def kernel(node_order, right, middle, left, right0, right1, middle0, left0, left1):
        place, group = lax.axis_index("sub"), lax.axis_index("mid")
        bit0, bit1 = place & 1, place >> 1 & 1
        right0[...] = swapped(swapped(right[0, 0], 1, bit0), 0, bit1)
        place = lax.broadcasted_iota(jnp.int32, (width, 1), 0)
        source = place % block
        for slot in range(groups):
            piece = node_order[slot ^ group] * block
            source += jnp.where(place // block == slot, piece, 0)
        across = lax.broadcasted_iota(jnp.int32, (width, width), 1)
        pick = jnp.where(across == source, 1.0, 0.0).astype(BF16)
        right1[...] = matmul(pick, swapped(right[0, 1], 1, bit1)).astype(BF16)
        place = lax.broadcasted_iota(jnp.int32, (1, width), 1)
        source = place % block
        for i, slot in enumerate(last_slots):
            source += jnp.where(place // block == i, (slot ^ group) * block, 0)
        down = lax.broadcasted_iota(jnp.int32, (width, width), 0)
        pick = jnp.where(down == source, 1.0, 0.0).astype(BF16)
        middle0[...] = swapped(matmul(middle[0], pick).astype(BF16), 0, bit1)
        left0[...] = swapped(swapped(left[0, 0], 1, bit1), 0, bit0)
        left1[...] = swapped(left[0, 1], 1, bit0)

    return call(
        kernel,
        name,
        [jax.ShapeDtypeStruct((width, width), BF16)] * 5,
        [SCALARS] + [WHOLE] * 3,
        [node_order, right, middle, left],
        after,
        out_specs=[WHOLE] * 5,
        cost_estimate=cost(4 * width**3, 20 * width**2),
    )


def fetched(basis, signal, here, low, arrived, pieces):
    depth = signal.shape[0] // pieces
    columns = pl.ds(low, here[-1].shape[1])
    copies = []
    for i in range(pieces):
        part = pl.ds(i * depth, depth)
        both = [pltpu.make_async_copy(signal.at[part, columns], here[-1].at[part], arrived.at[i, 0])]
        if basis is not None:
            both.append(pltpu.make_async_copy(basis.at[part], here[0].at[part], arrived.at[i, 1]))
        for copy in both:
            copy.start()
        copies.append((part, both))
    return copies


def row_pieces(rows, pieces):
    return pieces if rows % (pieces * ROWS) == 0 else 1


def opening(name, basis, signal, low, high):
    rows, width = basis.shape
    half, columns = width // 2, high - low
    pieces = row_pieces(rows, 3)

    def kernel(basis, signal, kept, send, flipped, basis_here, signal_here, arrived):
        copies = fetched(basis, signal, (basis_here, signal_here), low, arrived, pieces)
        flag = lax.axis_index("sub") & 1
        total = jnp.zeros((width, columns), F32)
        for part, both in copies:
            for copy in both:
                copy.wait()
            flipped[:, part] = swapped(basis_here[part, :].T, 0, flag)
            total += matmul(flipped[:, part], signal_here[part, :])
        kept[...] = total[:half].astype(BF16)
        send[...] = total[half:].astype(BF16)

    return call(
        kernel,
        name,
        [jax.ShapeDtypeStruct((half, columns), BF16)] * 2
        + [jax.ShapeDtypeStruct((width, rows), BF16)],
        [HBM, HBM],
        [basis, signal],
        None,
        limit=MOST,
        out_specs=[WHOLE] * 3,
        scratch_shapes=[
            pltpu.VMEM((rows, width), BF16),
            pltpu.VMEM((rows, columns), BF16),
            pltpu.SemaphoreType.DMA((pieces, 2)),
        ],
        cost_estimate=cost(2 * rows * width * columns, 2 * rows * (columns + width)),
    )


def first(name, flipped, signal, low, high, after):
    width, rows = flipped.shape
    half, columns = width // 2, high - low
    pieces = row_pieces(rows, 3)

    def kernel(flipped, signal, kept, send, signal_here, arrived):
        copies = fetched(None, signal, (signal_here,), low, arrived, pieces)
        total = jnp.zeros((width, columns), F32)
        for part, both in copies:
            both[0].wait()
            total += matmul(flipped[:, part], signal_here[part, :])
        kept[...] = total[:half].astype(BF16)
        send[...] = total[half:].astype(BF16)

    return call(
        kernel,
        name,
        [jax.ShapeDtypeStruct((half, columns), BF16)] * 2,
        [WHOLE, HBM],
        [flipped, signal],
        after,
        limit=MOST,
        out_specs=[WHOLE] * 2,
        scratch_shapes=[pltpu.VMEM((rows, columns), BF16), pltpu.SemaphoreType.DMA((pieces, 1))],
        cost_estimate=cost(2 * rows * width * columns, 2 * rows * (columns + width)),
    )


def level(name, weight, pairs, widths, after):
    half = weight.shape[0] // 2
    columns = sum(widths)

    def kernel(weight, *refs):
        ins, outs = refs[: 2 * len(pairs)], refs[2 * len(pairs) :]
        keep = jnp.concatenate([ref[...] for ref in ins[0::2]], axis=1)
        got = jnp.concatenate([ref[...] for ref in ins[1::2]], axis=1)
        total = matmul(weight[:, :half], keep) + matmul(weight[:, half:], got)
        low = 0
        for i, wide in enumerate(widths):
            outs[2 * i][...] = total[:half, low : low + wide].astype(BF16)
            outs[2 * i + 1][...] = total[half:, low : low + wide].astype(BF16)
            low += wide

    flat = [block for pair in pairs for block in pair]
    outs = call(
        kernel,
        name,
        [jax.ShapeDtypeStruct((half, wide), BF16) for wide in widths for _ in range(2)],
        [WHOLE] * (1 + len(flat)),
        [weight] + flat,
        after,
        out_specs=[WHOLE] * (2 * len(widths)),
        cost_estimate=cost(8 * half * half * columns, 8 * half * columns),
    )
    return list(zip(outs[0::2], outs[1::2]))


def regroup(name, keep, got, block, after):
    half, columns = keep.shape

    def parts(value, which):
        return [value[i * block : (i + 1) * block] for i in range(which, half // block, 2)]

    def both(keep, got, which):
        return jnp.concatenate(parts(keep, which) + parts(got, which), axis=0)

    if block % ROWS:
        return [(both(keep, got, 0), both(keep, got, 1))]

    def kernel(keep, got, kept, send):
        kept[...] = both(keep[...], got[...], 0)
        send[...] = both(keep[...], got[...], 1)

    outs = call(
        kernel,
        name,
        [jax.ShapeDtypeStruct((half, columns), BF16)] * 2,
        [WHOLE] * 2,
        [keep, got],
        after,
        out_specs=[WHOLE] * 2,
        cost_estimate=cost(0, 8 * half * columns),
    )
    return [tuple(outs)]


def last(name, weight, basis, keep, got, before, low, columns, after):
    rows, width = basis.shape
    half, wide = keep.shape
    pieces = row_pieces(rows, 6)
    depth = rows // pieces
    given = [] if before is None else [before]

    def kernel(weight, basis, keep, got, *refs):
        out, here, left = refs[len(given) :]
        coeffs = matmul(weight[:, :half], keep[...]) + matmul(weight[:, half:], got[...])
        coeffs = coeffs.astype(BF16)
        copies = []
        for i in range(pieces):
            part = pl.ds(i * depth, depth)
            here[part, :] = matmul(basis[part, :], coeffs).astype(BF16)
            copy = pltpu.make_async_copy(here.at[part], out.at[part, pl.ds(low, wide)], left.at[i])
            copy.start()
            copies.append(copy)
        for copy in copies:
            copy.wait()

    return call(
        kernel,
        name,
        jax.ShapeDtypeStruct((rows, columns), BF16),
        [WHOLE] * 4 + [HBM] * len(given),
        [weight, basis, keep, got] + given,
        after,
        out_specs=HBM,
        scratch_shapes=[pltpu.VMEM((rows, wide), BF16), pltpu.SemaphoreType.DMA((pieces,))],
        input_output_aliases={4: 0} if given else {},
        cost_estimate=cost(2 * rows * width * wide, 2 * rows * wide),
    )


def final_slots(groups):
    order = list(range(groups))
    half = groups // 2
    keep, got = order[:half], order[half:]
    block = half // 2
    while block:
        one = [[x[i : i + block] for i in range(0, half, block)] for x in (keep, got)]
        keep = sum(one[0][0::2] + one[1][0::2], [])
        got = sum(one[0][1::2] + one[1][1::2], [])
        block //= 2
    return keep + got


def local(signal, col_basis, right_coupling, middle_coupling, left_coupling, row_basis, node_order):
    groups = lax.axis_size("mid")
    width = col_basis.shape[1]
    block = width // groups
    steps = groups.bit_length() - 1
    columns = signal.shape[1]
    chunks = shares(columns, ENTRY_SHARES)
    starts = [sum(chunks[:i]) for i in range(len(chunks))]
    merged = {i: group for group in MERGED for i in group}
    if len(chunks) < len(ENTRY_SHARES):
        merged = {i: (i,) for i in range(len(chunks))}

    couplings, out, after, flipped = None, None, None, None
    waiting, pops, entered = [], 0, 0
    parked = {}
    while waiting or entered < len(chunks):
        if entered < len(chunks) and (pops >= ENTRY[entered] or not waiting):
            i, entered = entered, entered + 1
            low, high = starts[i], starts[i] + chunks[i]
            if i:
                keep, send = first(f"first{i}", flipped, signal, low, high, after)
            else:
                keep, send, flipped = opening("opening", col_basis, signal, low, high)
            waiting.append((1, (i,), low, keep, swap(send, "sub", 1)))
            after = keep
            continue
        stage, ids, low, keep, got = waiting.pop(0)
        pops += 1
        wide = keep.shape[1]
        name = "".join(str(i) for i in ids)
        if couplings is None:
            couplings = prepare(
                "prepare", node_order, right_coupling, middle_coupling, left_coupling, after
            )
            right0, right1, middle, left0, left1 = couplings
            after = right0
        if stage == 1:
            pairs = level(f"right0_{name}", right0, [(keep, got)], [wide], after)
            route = ("sub", 2)
        elif stage == 2:
            parked[ids[0]] = (keep, got)
            ids = merged[ids[0]]
            if any(i not in parked for i in ids):
                continue
            wide = sum(chunks[i] for i in ids)
            low = starts[ids[0]]
            pairs = level(f"right1_{name}", right1, [parked[i] for i in ids], [wide], after)
            route = ("mid", groups // 2)
        elif stage < 2 + steps:
            slot = groups >> stage - 1
            pairs = regroup(f"regroup{stage}_{name}", keep, got, slot * block, after)
            route = ("mid", slot)
        elif stage == 2 + steps:
            widths = shares(wide, SPLIT.get(ids, (1,)))
            pairs = level(f"middle_{name}", middle, [(keep, got)], widths, after)
            route = ("sub", 2)
        elif stage == 3 + steps:
            pairs = level(f"left0_{name}", left0, [(keep, got)], [wide], after)
            route = ("sub", 1)
        else:
            out = last(f"last{low}", left1, row_basis, keep, got, out, low, columns, after)
            continue
        for keep, send in pairs:
            waiting.append((stage + 1, ids, low, keep, swap(send, *route)))
            low += keep.shape[1]
        after = pairs[0][0]
    return out


def solution(mesh):
    return jax.shard_map(
        local,
        mesh=mesh,
        in_specs=(
            P(("mid", "sub"), None),
            P(("mid", "sub"), None),
            P(("mid", "sub"), None, None, None),
            P(("mid", "sub"), None, None),
            P(("mid", "sub"), None, None, None),
            P(("mid", "sub"), None),
            P(),
        ),
        out_specs=P(("mid", "sub"), None),
        check_vma=False,
    )
```

time: 58.8 us -> 58.1 us (0.988)
  waiting for transfers between devices: 22.3 us -> 19.6 us
  Pallas kernels: 13 us -> 15.5 us
  local copies, waits for them, and re-layouts: 0.92 us -> 0.02 us
  starting transfers between devices: 21.6 us -> 22.3 us
  other arithmetic: 0.61 us -> 0 us
    ppermute x21, waiting for transfers between devices: 22.3 us -> 19.6 us  [swap(): return lax.ppermute(block, axis, [(i, i ^ distance) for i in range(count)])]
    pallas_call x25, Pallas kernels: 13 us -> 15.5 us  [call(): pl.pallas_call(body, name=name, in_specs=specs + [PLACE] * len(extra), ou...]
    unnamed x20 -> x10, local copies, waits for them, and re-layouts: 0.92 us -> 0.02 us
    ppermute x21, starting transfers between devices: 21.6 us -> 22.3 us  [swap(): return lax.ppermute(block, axis, [(i, i ^ distance) for i in range(count)])]
    another operation x1 -> x0, other arithmetic: 0.61 us -> none  [local(): info = jnp.stack([place & 1, place >> 1 & 1, group])]
  transfers between devices with their start and end apart: 21 -> 21, of which waited for: 11 -> 11; matrix products, arithmetic and copies ran while one was open for 0% -> 0% of each run, Pallas kernels for 14% -> 20%
where the time goes in v7:
time: 58.1 us; the launch traced here: 57.8 us
  starting transfers between devices  22.3 us (38%)
  waiting for transfers between devices  19.6 us (34%)
  Pallas kernels  15.5 us (27%)
    ppermute x21, starting transfers between devices, swap(): return lax.ppermute(block, axis, [(i, i ^ distance) for i in range(count)])  22.3 us
    ppermute x21, waiting for transfers between devices, swap(): return lax.ppermute(block, axis, [(i, i ^ distance) for i in range(count)])  19.6 us
    pallas_call x25, Pallas kernels, call(): pl.pallas_call(body, name=name, in_specs=specs + [PLACE] * len(extra), ou...  15.5 us
  transfers between devices with their start and end apart: 21, of which 11 were waited for; matrix products, arithmetic and copies ran while one was open for 0% of the time, Pallas kernels for 20%

profile of v7, /device:TPU:0, one launch (start us, length us, event | category | flops | bytes accessed | tf_op | source)
XLA Modules:
  0.0 57.8 jit_solution(11284833434644517694)
XLA Ops:
  0.0 2.5 %opening.1 = (bf16[128,384]{1,0:T(8,128)(2,1)S(1)}, bf16[128,384]{1,0:T(8,128)(2,1)S(1)}, bf16[256,768]{1,0:T(8,128)(2,1)}) custom-call(bf16[768,256]{1,0:T(8,128)(2,1)} %refs_0_.2, bf16[768,1152]{1,0:T(8,128)(2,1)} %refs_1_.10), custom_call_target="tpu_custom_call" | custom-call | flops 150994944 | bytes 983040 | tf_op jit(solution)/shard_map/opening/pallas_call | solution.py:59
  2.5 3.1 %collective-permute-start = (bf16[128,384]{1,0:T(8,128)(2,1)S(1)}, bf16[128,384]{1,0:T(8,128)(2,1)S(1)}, u32[]{:S(2)}, u32[]{:S(2)}) collective-permute-start(bf16[128,384]{1,0:T(8,128)(2,1)S(1)} %get-tuple-element.61), channel_id=1, source_target_pairs={{0,1},{1,0},{2,3},{3,2},{4,5},{5,4},{6,7},{7,6},{8,9},{9,8},{10,11... | collective-permute-start | bytes 294920 | tf_op jit(solution)/shard_map/ppermute | solution.py:35
  5.6 2.5 %first1.1 = (bf16[128,384]{1,0:T(8,128)(2,1)S(1)}, bf16[128,384]{1,0:T(8,128)(2,1)S(1)}) custom-call(bf16[256,768]{1,0:T(8,128)(2,1)} %get-tuple-element.53.refs_0_, bf16[768,1152]{1,0:T(8,128)(2,1)} %refs_1_.10, bf16[128,384]{1,0:T(8,128)(2,1)S(1)} %get-tuple-element.54.refs_2_.refs_1_), custom_call_target="tpu_custom_call" | custom-call | flops 150994944 | bytes 983040 | tf_op jit(solution)/shard_map/first1/pallas_call | solution.py:59
  8.3 0.8 %prepare.1 = (bf16[256,256]{1,0:T(8,128)(2,1)S(1)}, bf16[256,256]{1,0:T(8,128)(2,1)S(1)}, bf16[256,256]{1,0:T(8,128)(2,1)S(1)}, bf16[256,256]{1,0:T(8,128)(2,1)S(1)}, bf16[256,256]{1,0:T(8,128)(2,1)S(1)}) custom-call(s32[8]{0:T(128)S(1)} %copy-done.4, bf16[1,2,256,256]{3,2,1,0:T(8,128)(2,1)S(1)} %copy-done.1, bf16[1,256,256]{2,1,0:T(8,128)(2,1)S(1)} %copy-done.3, ...), custom_call_target="tpu_custom_call" | custom-call | flops 67108864 | bytes 1310720 | tf_op jit(solution)/shard_map/prepare/pallas_call | solution.py:59
  9.4 3.1 %collective-permute-start.2 = (bf16[128,384]{1,0:T(8,128)(2,1)S(1)}, bf16[128,384]{1,0:T(8,128)(2,1)S(1)}, u32[]{:S(2)}, u32[]{:S(2)}) collective-permute-start(bf16[128,384]{1,0:T(8,128)(2,1)S(1)} %get-tuple-element.65), channel_id=1, source_target_pairs={{0,2},{1,3},{2,0},{3,1},{4,6},{5,7},{6,4},{7,5},{8,10},{9,11},{10,... | collective-permute-start | bytes 294920 | tf_op jit(solution)/shard_map/ppermute | solution.py:35
  12.4 2.5 %first2.1 = (bf16[128,384]{1,0:T(8,128)(2,1)S(1)}, bf16[128,384]{1,0:T(8,128)(2,1)S(1)}) custom-call(bf16[256,768]{1,0:T(8,128)(2,1)} %get-tuple-element.53.refs_0_, bf16[768,1152]{1,0:T(8,128)(2,1)} %refs_1_.10, bf16[128,384]{1,0:T(8,128)(2,1)S(1)} %get-tuple-element.62.refs_2_.refs_1_), custom_call_target="tpu_custom_call" | custom-call | flops 150994944 | bytes 983040 | tf_op jit(solution)/shard_map/first2/pallas_call | solution.py:59
  15.0 1.6 %collective-permute-start.1 = (bf16[128,384]{1,0:T(8,128)(2,1)S(1)}, bf16[128,384]{1,0:T(8,128)(2,1)S(1)}, u32[]{:S(2)}, u32[]{:S(2)}) collective-permute-start(bf16[128,384]{1,0:T(8,128)(2,1)S(1)} %get-tuple-element.64), channel_id=1, source_target_pairs={{0,1},{1,0},{2,3},{3,2},{4,5},{5,4},{6,7},{7,6},{8,9},{9,8},{10,11... | collective-permute-start | bytes 294920 | tf_op jit(solution)/shard_map/ppermute | solution.py:35
  17.5 1.6 %collective-permute-start.5 = (bf16[128,384]{1,0:T(8,128)(2,1)S(1)}, bf16[128,384]{1,0:T(8,128)(2,1)S(1)}, u32[]{:S(2)}, u32[]{:S(2)}) collective-permute-start(bf16[128,384]{1,0:T(8,128)(2,1)S(1)} %get-tuple-element.71), channel_id=1, source_target_pairs={{0,16},{4,20},{8,24},{12,28},{16,0},{20,4},{24,8},{28,12},{1,17},{... | collective-permute-start | bytes 294920 | tf_op jit(solution)/shard_map/ppermute | solution.py:35
  19.1 0.7 %collective-permute-done.1.refs_2_ = bf16[128,384]{1,0:T(8,128)(2,1)S(1)} collective-permute-done((bf16[128,384]{1,0:T(8,128)(2,1)S(1)}, bf16[128,384]{1,0:T(8,128)(2,1)S(1)}, u32[]{:S(2)}, u32[]{:S(2)}) %collective-permute-start.1) | collective-permute-done | bytes 98336 | tf_op jit(solution)/shard_map/ppermute | solution.py:35
  20.0 2.0 %collective-permute-start.4 = (bf16[128,384]{1,0:T(8,128)(2,1)S(1)}, bf16[128,384]{1,0:T(8,128)(2,1)S(1)}, u32[]{:S(2)}, u32[]{:S(2)}) collective-permute-start(bf16[128,384]{1,0:T(8,128)(2,1)S(1)} %get-tuple-element.70), channel_id=1, source_target_pairs={{0,2},{1,3},{2,0},{3,1},{4,6},{5,7},{6,4},{7,5},{8,10},{9,11},{10,... | collective-permute-start | bytes 294920 | tf_op jit(solution)/shard_map/ppermute | solution.py:35
  22.0 3.5 %collective-permute-done.6.refs_2_ = bf16[128,384]{1,0:T(8,128)(2,1)S(1)} collective-permute-done((bf16[128,384]{1,0:T(8,128)(2,1)S(1)}, bf16[128,384]{1,0:T(8,128)(2,1)S(1)}, u32[]{:S(2)}, u32[]{:S(2)}) %collective-permute-start.6) | collective-permute-done | bytes 98336 | tf_op jit(solution)/shard_map/ppermute | solution.py:35
  25.8 1.6 %collective-permute-start.9 = (bf16[128,384]{1,0:T(8,128)(2,1)S(1)}, bf16[128,384]{1,0:T(8,128)(2,1)S(1)}, u32[]{:S(2)}, u32[]{:S(2)}) collective-permute-start(bf16[128,384]{1,0:T(8,128)(2,1)S(1)} %get-tuple-element.78), channel_id=1, source_target_pairs={{0,16},{4,20},{8,24},{12,28},{16,0},{20,4},{24,8},{28,12},{1,17},{... | collective-permute-start | bytes 294920 | tf_op jit(solution)/shard_map/ppermute | solution.py:35
  27.4 1.6 %collective-permute-start.8 = (bf16[128,384]{1,0:T(8,128)(2,1)S(1)}, bf16[128,384]{1,0:T(8,128)(2,1)S(1)}, u32[]{:S(2)}, u32[]{:S(2)}) collective-permute-start(bf16[128,384]{1,0:T(8,128)(2,1)S(1)} %get-tuple-element.77), channel_id=1, source_target_pairs={{0,8},{4,12},{8,0},{12,4},{16,24},{20,28},{24,16},{28,20},{1,9},{5... | collective-permute-start | bytes 294920 | tf_op jit(solution)/shard_map/ppermute | solution.py:35
  29.8 0.9 %collective-permute-done.9.refs_1_ = bf16[128,384]{1,0:T(8,128)(2,1)S(1)} collective-permute-done((bf16[128,384]{1,0:T(8,128)(2,1)S(1)}, bf16[128,384]{1,0:T(8,128)(2,1)S(1)}, u32[]{:S(2)}, u32[]{:S(2)}) %collective-permute-start.9) | collective-permute-done | bytes 98336 | tf_op jit(solution)/shard_map/ppermute | solution.py:35
  30.7 1.6 %collective-permute-start.12 = (bf16[128,384]{1,0:T(8,128)(2,1)S(1)}, bf16[128,384]{1,0:T(8,128)(2,1)S(1)}, u32[]{:S(2)}, u32[]{:S(2)}) collective-permute-start(bf16[128,384]{1,0:T(8,128)(2,1)S(1)} %get-tuple-element.84), channel_id=1, source_target_pairs={{0,8},{4,12},{8,0},{12,4},{16,24},{20,28},{24,16},{28,20},{1,9},{5... | collective-permute-start | bytes 294920 | tf_op jit(solution)/shard_map/ppermute | solution.py:35
  32.3 1.5 %collective-permute-done.7.refs_1_ = bf16[128,384]{1,0:T(8,128)(2,1)S(1)} collective-permute-done((bf16[128,384]{1,0:T(8,128)(2,1)S(1)}, bf16[128,384]{1,0:T(8,128)(2,1)S(1)}, u32[]{:S(2)}, u32[]{:S(2)}) %collective-permute-start.7) | collective-permute-done | bytes 98336 | tf_op jit(solution)/shard_map/ppermute | solution.py:35
  34.5 0.9 %collective-permute-done.12.refs_1_ = bf16[128,384]{1,0:T(8,128)(2,1)S(1)} collective-permute-done((bf16[128,384]{1,0:T(8,128)(2,1)S(1)}, bf16[128,384]{1,0:T(8,128)(2,1)S(1)}, u32[]{:S(2)}, u32[]{:S(2)}) %collective-permute-start.12) | collective-permute-done | bytes 98336 | tf_op jit(solution)/shard_map/ppermute | solution.py:35
  35.8 2.8 %collective-permute-done.10.refs_1_ = bf16[128,384]{1,0:T(8,128)(2,1)S(1)} collective-permute-done((bf16[128,384]{1,0:T(8,128)(2,1)S(1)}, bf16[128,384]{1,0:T(8,128)(2,1)S(1)}, u32[]{:S(2)}, u32[]{:S(2)}) %collective-permute-start.10) | collective-permute-done | bytes 98336 | tf_op jit(solution)/shard_map/ppermute | solution.py:35
  39.3 5.1 %collective-permute-done.14.refs_2_ = bf16[128,384]{1,0:T(8,128)(2,1)S(1)} collective-permute-done((bf16[128,384]{1,0:T(8,128)(2,1)S(1)}, bf16[128,384]{1,0:T(8,128)(2,1)S(1)}, u32[]{:S(2)}, u32[]{:S(2)}) %collective-permute-start.14) | collective-permute-done | bytes 98336 | tf_op jit(solution)/shard_map/ppermute | solution.py:35
  45.1 3.3 %collective-permute-start.20 = (bf16[128,384]{1,0:T(8,128)(2,1)S(1)}, bf16[128,384]{1,0:T(8,128)(2,1)S(1)}, u32[]{:S(2)}, u32[]{:S(2)}) collective-permute-start(bf16[128,384]{1,0:T(8,128)(2,1)S(1)} %get-tuple-element.100), channel_id=1, source_target_pairs={{0,1},{1,0},{2,3},{3,2},{4,5},{5,4},{6,7},{7,6},{8,9},{9,8},{10,11... | collective-permute-start | bytes 294920 | tf_op jit(solution)/shard_map/ppermute | solution.py:35
  48.7 2.9 %collective-permute-done.16.refs_2_ = bf16[128,384]{1,0:T(8,128)(2,1)S(1)} collective-permute-done((bf16[128,384]{1,0:T(8,128)(2,1)S(1)}, bf16[128,384]{1,0:T(8,128)(2,1)S(1)}, u32[]{:S(2)}, u32[]{:S(2)}) %collective-permute-start.16) | collective-permute-done | bytes 98336 | tf_op jit(solution)/shard_map/ppermute | solution.py:35
  52.9 1.4 %last0.1.refs_4_ = bf16[768,1152]{1,0:T(8,128)(2,1)} custom-call(bf16[256,256]{1,0:T(8,128)(2,1)S(1)} %get-tuple-element.56.refs_0_, bf16[768,256]{1,0:T(8,128)(2,1)S(1)} %copy-done, bf16[128,384]{1,0:T(8,128)(2,1)S(1)} %get-tuple-element.92.refs_3_.refs_2_, bf16[128,384]{1,0:T(8,128)(2,1)S(1)} %collective-permute-done.20.refs_3_, ...), custom_call_target="tpu_custom_call" | custom-call | flops 150994944 | bytes 589824 | tf_op jit(solution)/shard_map/last0/pallas_call | solution.py:59
  54.7 1.4 %last384.1.refs_4_ = bf16[768,1152]{1,0:T(8,128)(2,1)} custom-call(bf16[256,256]{1,0:T(8,128)(2,1)S(1)} %get-tuple-element.56.refs_0_, bf16[768,256]{1,0:T(8,128)(2,1)S(1)} %copy-done, bf16[128,384]{1,0:T(8,128)(2,1)S(1)} %get-tuple-element.96.refs_3_.refs_4_.refs_2_, ...), custom_call_target="tpu_custom_call", output_to_operand_aliasing={{}: (4, {})} | custom-call | flops 150994944 | bytes 589824 | tf_op jit(solution)/shard_map/last384/pallas_call | solution.py:59
  56.5 1.4 %last768.1 = bf16[768,1152]{1,0:T(8,128)(2,1)} custom-call(bf16[256,256]{1,0:T(8,128)(2,1)S(1)} %get-tuple-element.56.refs_0_, bf16[768,256]{1,0:T(8,128)(2,1)S(1)} %copy-done, bf16[128,384]{1,0:T(8,128)(2,1)S(1)} %get-tuple-element.97.refs_5_.refs_2_, bf16[128,384]{1,0:T(8,128)(2,1)S(1)} %collective-permute-done.18.refs_3_, ...), custom_call_target="tpu_custom_call", output_to_operand_aliasing={{}: (4, {})} | custom-call | flops 150994944 | bytes 589824 | tf_op jit(solution)/shard_map/last768/pallas_call | solution.py:59
  (53 shorter events, 7.5 us)
Async XLA Ops:
  0.0 8.2 %copy-start.3 = (bf16[1,256,256]{2,1,0:T(8,128)(2,1)S(1)}, bf16[1,256,256]{2,1,0:T(8,128)(2,1)}, u32[]{:S(2)}) copy-start(bf16[1,256,256]{2,1,0:T(8,128)(2,1)} %refs_2_.1) | copy-start | bytes 393220
  0.0 8.2 %copy-start.1 = (bf16[1,2,256,256]{3,2,1,0:T(8,128)(2,1)S(1)}, bf16[1,2,256,256]{3,2,1,0:T(8,128)(2,1)}, u32[]{:S(2)}) copy-start(bf16[1,2,256,256]{3,2,1,0:T(8,128)(2,1)} %refs_1_.9) | copy-start | bytes 786436
  2.5 6.6 %collective-permute-start = (bf16[128,384]{1,0:T(8,128)(2,1)S(1)}, bf16[128,384]{1,0:T(8,128)(2,1)S(1)}, u32[]{:S(2)}, u32[]{:S(2)}) collective-permute-start(bf16[128,384]{1,0:T(8,128)(2,1)S(1)} %get-tuple-element.61), channel_id=1, source_target_pairs={{0,1},{1,0},{2,3},{3,2},{4,5},{5,4},{6,7},{7,6},{8,9},{9,8},{10,11... | collective-permute-start | bytes 294920 | tf_op jit(solution)/shard_map/ppermute | solution.py:35
  8.1 8.5 %collective-permute-start.3 = (bf16[128,384]{1,0:T(8,128)(2,1)S(1)}, bf16[128,384]{1,0:T(8,128)(2,1)S(1)}, u32[]{:S(2)}, u32[]{:S(2)}) collective-permute-start(bf16[128,384]{1,0:T(8,128)(2,1)S(1)} %get-tuple-element.66), channel_id=1, source_target_pairs={{0,1},{1,0},{2,3},{3,2},{4,5},{5,4},{6,7},{7,6},{8,9},{9,8},{10,11... | collective-permute-start | bytes 294920 | tf_op jit(solution)/shard_map/ppermute | solution.py:35
  9.4 7.9 %collective-permute-start.2 = (bf16[128,384]{1,0:T(8,128)(2,1)S(1)}, bf16[128,384]{1,0:T(8,128)(2,1)S(1)}, u32[]{:S(2)}, u32[]{:S(2)}) collective-permute-start(bf16[128,384]{1,0:T(8,128)(2,1)S(1)} %get-tuple-element.65), channel_id=1, source_target_pairs={{0,2},{1,3},{2,0},{3,1},{4,6},{5,7},{6,4},{7,5},{8,10},{9,11},{10,... | collective-permute-start | bytes 294920 | tf_op jit(solution)/shard_map/ppermute | solution.py:35
  15.0 4.8 %collective-permute-start.1 = (bf16[128,384]{1,0:T(8,128)(2,1)S(1)}, bf16[128,384]{1,0:T(8,128)(2,1)S(1)}, u32[]{:S(2)}, u32[]{:S(2)}) collective-permute-start(bf16[128,384]{1,0:T(8,128)(2,1)S(1)} %get-tuple-element.64), channel_id=1, source_target_pairs={{0,1},{1,0},{2,3},{3,2},{4,5},{5,4},{6,7},{7,6},{8,9},{9,8},{10,11... | collective-permute-start | bytes 294920 | tf_op jit(solution)/shard_map/ppermute | solution.py:35
  16.9 8.6 %collective-permute-start.6 = (bf16[128,384]{1,0:T(8,128)(2,1)S(1)}, bf16[128,384]{1,0:T(8,128)(2,1)S(1)}, u32[]{:S(2)}, u32[]{:S(2)}) collective-permute-start(bf16[128,384]{1,0:T(8,128)(2,1)S(1)} %get-tuple-element.72), channel_id=1, source_target_pairs={{0,2},{1,3},{2,0},{3,1},{4,6},{5,7},{6,4},{7,5},{8,10},{9,11},{10,... | collective-permute-start | bytes 294920 | tf_op jit(solution)/shard_map/ppermute | solution.py:35
  17.5 9.8 %collective-permute-start.5 = (bf16[128,384]{1,0:T(8,128)(2,1)S(1)}, bf16[128,384]{1,0:T(8,128)(2,1)S(1)}, u32[]{:S(2)}, u32[]{:S(2)}) collective-permute-start(bf16[128,384]{1,0:T(8,128)(2,1)S(1)} %get-tuple-element.71), channel_id=1, source_target_pairs={{0,16},{4,20},{8,24},{12,28},{16,0},{20,4},{24,8},{28,12},{1,17},{... | collective-permute-start | bytes 294920 | tf_op jit(solution)/shard_map/ppermute | solution.py:35
  20.0 8.9 %collective-permute-start.4 = (bf16[128,384]{1,0:T(8,128)(2,1)S(1)}, bf16[128,384]{1,0:T(8,128)(2,1)S(1)}, u32[]{:S(2)}, u32[]{:S(2)}) collective-permute-start(bf16[128,384]{1,0:T(8,128)(2,1)S(1)} %get-tuple-element.70), channel_id=1, source_target_pairs={{0,2},{1,3},{2,0},{3,1},{4,6},{5,7},{6,4},{7,5},{8,10},{9,11},{10,... | collective-permute-start | bytes 294920 | tf_op jit(solution)/shard_map/ppermute | solution.py:35
  25.8 4.9 %collective-permute-start.9 = (bf16[128,384]{1,0:T(8,128)(2,1)S(1)}, bf16[128,384]{1,0:T(8,128)(2,1)S(1)}, u32[]{:S(2)}, u32[]{:S(2)}) collective-permute-start(bf16[128,384]{1,0:T(8,128)(2,1)S(1)} %get-tuple-element.78), channel_id=1, source_target_pairs={{0,16},{4,20},{8,24},{12,28},{16,0},{20,4},{24,8},{28,12},{1,17},{... | collective-permute-start | bytes 294920 | tf_op jit(solution)/shard_map/ppermute | solution.py:35
  27.4 4.9 %collective-permute-start.8 = (bf16[128,384]{1,0:T(8,128)(2,1)S(1)}, bf16[128,384]{1,0:T(8,128)(2,1)S(1)}, u32[]{:S(2)}, u32[]{:S(2)}) collective-permute-start(bf16[128,384]{1,0:T(8,128)(2,1)S(1)} %get-tuple-element.77), channel_id=1, source_target_pairs={{0,8},{4,12},{8,0},{12,4},{16,24},{20,28},{24,16},{28,20},{1,9},{5... | collective-permute-start | bytes 294920 | tf_op jit(solution)/shard_map/ppermute | solution.py:35
  29.2 4.7 %collective-permute-start.7 = (bf16[128,384]{1,0:T(8,128)(2,1)S(1)}, bf16[128,384]{1,0:T(8,128)(2,1)S(1)}, u32[]{:S(2)}, u32[]{:S(2)}) collective-permute-start(bf16[128,384]{1,0:T(8,128)(2,1)S(1)} %get-tuple-element.76), channel_id=1, source_target_pairs={{0,16},{4,20},{8,24},{12,28},{16,0},{20,4},{24,8},{28,12},{1,17},{... | collective-permute-start | bytes 294920 | tf_op jit(solution)/shard_map/ppermute | solution.py:35
  30.7 4.7 %collective-permute-start.12 = (bf16[128,384]{1,0:T(8,128)(2,1)S(1)}, bf16[128,384]{1,0:T(8,128)(2,1)S(1)}, u32[]{:S(2)}, u32[]{:S(2)}) collective-permute-start(bf16[128,384]{1,0:T(8,128)(2,1)S(1)} %get-tuple-element.84), channel_id=1, source_target_pairs={{0,8},{4,12},{8,0},{12,4},{16,24},{20,28},{24,16},{28,20},{1,9},{5... | collective-permute-start | bytes 294920 | tf_op jit(solution)/shard_map/ppermute | solution.py:35
  32.2 20.7 %copy-start = (bf16[768,256]{1,0:T(8,128)(2,1)S(1)}, bf16[768,256]{1,0:T(8,128)(2,1)}, u32[]{:S(2)}) copy-start(bf16[768,256]{1,0:T(8,128)(2,1)} %refs_1_.13) | copy-start | bytes 1179652
  32.3 3.2 %collective-permute-start.11 = (bf16[128,384]{1,0:T(8,128)(2,1)S(1)}, bf16[128,384]{1,0:T(8,128)(2,1)S(1)}, u32[]{:S(2)}, u32[]{:S(2)}) collective-permute-start(bf16[128,384]{1,0:T(8,128)(2,1)S(1)} %get-tuple-element.83), channel_id=1, source_target_pairs={{0,4},{4,0},{8,12},{12,8},{16,20},{20,16},{24,28},{28,24},{1,5},{5... | collective-permute-start | bytes 294920 | tf_op jit(solution)/shard_map/ppermute | solution.py:35
  33.9 4.7 %collective-permute-start.10 = (bf16[128,384]{1,0:T(8,128)(2,1)S(1)}, bf16[128,384]{1,0:T(8,128)(2,1)S(1)}, u32[]{:S(2)}, u32[]{:S(2)}) collective-permute-start(bf16[128,384]{1,0:T(8,128)(2,1)S(1)} %get-tuple-element.82), channel_id=1, source_target_pairs={{0,8},{4,12},{8,0},{12,4},{16,24},{20,28},{24,16},{28,20},{1,9},{5... | collective-permute-start | bytes 294920 | tf_op jit(solution)/shard_map/ppermute | solution.py:35
  35.4 3.3 %collective-permute-start.15 = (bf16[128,384]{1,0:T(8,128)(2,1)S(1)}, bf16[128,384]{1,0:T(8,128)(2,1)S(1)}, u32[]{:S(2)}, u32[]{:S(2)}) collective-permute-start(bf16[128,384]{1,0:T(8,128)(2,1)S(1)} %get-tuple-element.90), channel_id=1, source_target_pairs={{0,4},{4,0},{8,12},{12,8},{16,20},{20,16},{24,28},{28,24},{1,5},{5... | collective-permute-start | bytes 294920 | tf_op jit(solution)/shard_map/ppermute | solution.py:35
  35.7 8.7 %collective-permute-start.14 = (bf16[128,384]{1,0:T(8,128)(2,1)S(1)}, bf16[128,384]{1,0:T(8,128)(2,1)S(1)}, u32[]{:S(2)}, u32[]{:S(2)}) collective-permute-start(bf16[128,384]{1,0:T(8,128)(2,1)S(1)} %get-tuple-element.89), channel_id=1, source_target_pairs={{0,2},{1,3},{2,0},{3,1},{4,6},{5,7},{6,4},{7,5},{8,10},{9,11},{10,... | collective-permute-start | bytes 294920 | tf_op jit(solution)/shard_map/ppermute | solution.py:35
  38.6 6.1 %collective-permute-start.13 = (bf16[128,384]{1,0:T(8,128)(2,1)S(1)}, bf16[128,384]{1,0:T(8,128)(2,1)S(1)}, u32[]{:S(2)}, u32[]{:S(2)}) collective-permute-start(bf16[128,384]{1,0:T(8,128)(2,1)S(1)} %get-tuple-element.88), channel_id=1, source_target_pairs={{0,4},{4,0},{8,12},{12,8},{16,20},{20,16},{24,28},{28,24},{1,5},{5... | collective-permute-start | bytes 294920 | tf_op jit(solution)/shard_map/ppermute | solution.py:35
  38.9 9.4 %collective-permute-start.17 = (bf16[128,384]{1,0:T(8,128)(2,1)S(1)}, bf16[128,384]{1,0:T(8,128)(2,1)S(1)}, u32[]{:S(2)}, u32[]{:S(2)}) collective-permute-start(bf16[128,384]{1,0:T(8,128)(2,1)S(1)} %get-tuple-element.95), channel_id=1, source_target_pairs={{0,2},{1,3},{2,0},{3,1},{4,6},{5,7},{6,4},{7,5},{8,10},{9,11},{10,... | collective-permute-start | bytes 294920 | tf_op jit(solution)/shard_map/ppermute | solution.py:35
  45.0 6.5 %collective-permute-start.16 = (bf16[128,384]{1,0:T(8,128)(2,1)S(1)}, bf16[128,384]{1,0:T(8,128)(2,1)S(1)}, u32[]{:S(2)}, u32[]{:S(2)}) collective-permute-start(bf16[128,384]{1,0:T(8,128)(2,1)S(1)} %get-tuple-element.94), channel_id=1, source_target_pairs={{0,2},{1,3},{2,0},{3,1},{4,6},{5,7},{6,4},{7,5},{8,10},{9,11},{10,... | collective-permute-start | bytes 294920 | tf_op jit(solution)/shard_map/ppermute | solution.py:35
  45.1 7.8 %collective-permute-start.20 = (bf16[128,384]{1,0:T(8,128)(2,1)S(1)}, bf16[128,384]{1,0:T(8,128)(2,1)S(1)}, u32[]{:S(2)}, u32[]{:S(2)}) collective-permute-start(bf16[128,384]{1,0:T(8,128)(2,1)S(1)} %get-tuple-element.100), channel_id=1, source_target_pairs={{0,1},{1,0},{2,3},{3,2},{4,5},{5,4},{6,7},{7,6},{8,9},{9,8},{10,11... | collective-permute-start | bytes 294920 | tf_op jit(solution)/shard_map/ppermute | solution.py:35
  48.6 6.1 %collective-permute-start.19 = (bf16[128,384]{1,0:T(8,128)(2,1)S(1)}, bf16[128,384]{1,0:T(8,128)(2,1)S(1)}, u32[]{:S(2)}, u32[]{:S(2)}) collective-permute-start(bf16[128,384]{1,0:T(8,128)(2,1)S(1)} %get-tuple-element.99), channel_id=1, source_target_pairs={{0,1},{1,0},{2,3},{3,2},{4,5},{5,4},{6,7},{7,6},{8,9},{9,8},{10,11... | collective-permute-start | bytes 294920 | tf_op jit(solution)/shard_map/ppermute | solution.py:35
  51.8 4.7 %collective-permute-start.18 = (bf16[128,384]{1,0:T(8,128)(2,1)S(1)}, bf16[128,384]{1,0:T(8,128)(2,1)S(1)}, u32[]{:S(2)}, u32[]{:S(2)}) collective-permute-start(bf16[128,384]{1,0:T(8,128)(2,1)S(1)} %get-tuple-element.98), channel_id=1, source_target_pairs={{0,1},{1,0},{2,3},{3,2},{4,5},{5,4},{6,7},{7,6},{8,9},{9,8},{10,11... | collective-permute-start | bytes 294920 | tf_op jit(solution)/shard_map/ppermute | solution.py:35
  (2 other events, 16.4 us)

commit v8 on v7

v8 whole, which is shorter than its diff:
```python
import jax
import jax.numpy as jnp
from jax import lax
from jax.experimental import pallas as pl
from jax.experimental.pallas import tpu as pltpu
from jax.sharding import PartitionSpec as P

LANES = 128
ENTRY_SHARES = (3, 3, 3)
ENTRY = (0, 0, 1)
MERGED = ((0,), (1,), (2,))
SPLIT = {}
ROWS = 16
SCOPED = 8 * 2**20
MOST = 213 * 2**18
F32 = jnp.float32
BF16 = jnp.bfloat16
WHOLE = pl.BlockSpec(memory_space=pltpu.VMEM)
SCALARS = pl.BlockSpec(memory_space=pltpu.SMEM)
PLACE = pl.BlockSpec(memory_space=pl.ANY)
HBM = pl.BlockSpec(memory_space=pltpu.HBM)


def shares(columns, weights):
    tiles = columns // LANES
    if tiles < len(weights):
        return [columns]
    edges = [round(tiles * sum(weights[:i]) / sum(weights)) * LANES for i in range(len(weights))]
    edges.append(columns)
    return [high - low for low, high in zip(edges[:-1], edges[1:])]


def swap(block, axis, distance):
    count = lax.axis_size(axis)
    return lax.ppermute(block, axis, [(i, i ^ distance) for i in range(count)])


def swapped(matrix, axis, flag):
    half = matrix.shape[axis] // 2
    low = lax.slice_in_dim(matrix, 0, half, axis=axis)
    high = lax.slice_in_dim(matrix, half, 2 * half, axis=axis)
    return jnp.where(flag == 1, jnp.concatenate([high, low], axis=axis), matrix)


def matmul(left, right):
    return lax.dot_general(left, right, (((1,), (0,)), ((), ())), preferred_element_type=F32)


def cost(flops, moved):
    return pl.CostEstimate(flops=flops, bytes_accessed=moved, transcendentals=0)


def call(kernel, name, outs, specs, operands, after, limit=SCOPED, **more):
    extra = [] if after is None else [after]

    def body(*refs):
        kernel(*refs[: len(operands)], *refs[len(operands) + len(extra) :])

    return pl.pallas_call(
        body,
        name=name,
        in_specs=specs + [PLACE] * len(extra),
        out_shape=outs,
        compiler_params=pltpu.CompilerParams(vmem_limit_bytes=limit),
        **more,
    )(*operands, *extra)


def prepare(name, node_order, slots_out, slots_in, right, middle, left, after):
    width = middle.shape[-1]
    groups = node_order.shape[0]
    block = width // groups

    def kernel(node_order, right, middle, left, right0, right1, middle0, left0, left1):
        place, group = lax.axis_index("sub"), lax.axis_index("mid")
        bit0, bit1 = place & 1, place >> 1 & 1
        right0[...] = swapped(swapped(right[0, 0], 1, bit0), 0, bit1)
        place = lax.broadcasted_iota(jnp.int32, (width, 1), 0)
        source = place % block
        for i, slot in enumerate(slots_out):
            piece = node_order[slot ^ group] * block
            source += jnp.where(place // block == i, piece, 0)
        across = lax.broadcasted_iota(jnp.int32, (width, width), 1)
        pick = jnp.where(across == source, 1.0, 0.0).astype(BF16)
        right1[...] = matmul(pick, swapped(right[0, 1], 1, bit1)).astype(BF16)
        place = lax.broadcasted_iota(jnp.int32, (1, width), 1)
        source = place % block
        for i, slot in enumerate(slots_in):
            source += jnp.where(place // block == i, (slot ^ group) * block, 0)
        down = lax.broadcasted_iota(jnp.int32, (width, width), 0)
        pick = jnp.where(down == source, 1.0, 0.0).astype(BF16)
        middle0[...] = swapped(matmul(middle[0], pick).astype(BF16), 0, bit1)
        left0[...] = swapped(swapped(left[0, 0], 1, bit1), 0, bit0)
        left1[...] = swapped(left[0, 1], 1, bit0)

    return call(
        kernel,
        name,
        [jax.ShapeDtypeStruct((width, width), BF16)] * 5,
        [SCALARS] + [WHOLE] * 3,
        [node_order, right, middle, left],
        after,
        out_specs=[WHOLE] * 5,
        cost_estimate=cost(4 * width**3, 20 * width**2),
    )


def row_pieces(rows, pieces):
    return pieces if rows % (pieces * ROWS) == 0 else 1


def opening(name, basis, signal, widths):
    rows, width = basis.shape
    half = width // 2
    pieces = row_pieces(rows, 6)
    depth = rows // pieces
    lows = [sum(widths[:i]) for i in range(len(widths))]

    def kernel(basis, signal, *refs):
        outs, (basis_here, signal_here, arrived, basis_arrived) = refs[:-4], refs[-4:]
        fetch_basis = pltpu.make_async_copy(basis, basis_here, basis_arrived)
        fetch_basis.start()
        copies = []
        for i in range(pieces):
            part = pl.ds(i * depth, depth)
            copies.append(
                pltpu.make_async_copy(signal.at[part], signal_here.at[part], arrived.at[i])
            )
            copies[-1].start()
        fetch_basis.wait()
        flipped = swapped(basis_here[...].T, 0, lax.axis_index("sub") & 1)
        for copy in copies:
            copy.wait()
        for i, (low, wide) in enumerate(zip(lows, widths)):
            total = matmul(flipped, signal_here[:, low : low + wide])
            outs[2 * i][...] = total[:half].astype(BF16)
            outs[2 * i + 1][...] = total[half:].astype(BF16)

    outs = call(
        kernel,
        name,
        [jax.ShapeDtypeStruct((half, wide), BF16) for wide in widths for _ in range(2)],
        [HBM, HBM],
        [basis, signal],
        None,
        limit=MOST,
        out_specs=[WHOLE] * (2 * len(widths)),
        scratch_shapes=[
            pltpu.VMEM((rows, width), BF16),
            pltpu.VMEM(signal.shape, BF16),
            pltpu.SemaphoreType.DMA((pieces,)),
            pltpu.SemaphoreType.DMA,
        ],
        cost_estimate=cost(2 * rows * width * sum(widths), 2 * rows * (sum(widths) + width)),
    )
    return list(zip(outs[0::2], outs[1::2]))


def level(name, weight, chunks, widths, count, after):
    width = weight.shape[0]
    depth = width // count
    columns = sum(widths)
    blocks = len(chunks[0])

    def kernel(weight, *refs):
        ins, outs = refs[: blocks * len(chunks)], refs[blocks * len(chunks) :]
        stacked = [
            jnp.concatenate([ref[...] for ref in ins[i * blocks : (i + 1) * blocks]], axis=0)
            for i in range(len(chunks))
        ]
        total = matmul(weight[...], jnp.concatenate(stacked, axis=1))
        low = 0
        for i, wide in enumerate(widths):
            for j in range(count):
                part = total[j * depth : (j + 1) * depth, low : low + wide]
                outs[i * count + j][...] = part.astype(BF16)
            low += wide

    flat = [block for chunk in chunks for block in chunk]
    outs = call(
        kernel,
        name,
        [jax.ShapeDtypeStruct((depth, wide), BF16) for wide in widths for _ in range(count)],
        [WHOLE] * (1 + len(flat)),
        [weight] + flat,
        after,
        out_specs=[WHOLE] * (count * len(widths)),
        cost_estimate=cost(2 * width * width * columns, 4 * width * columns),
    )
    return [list(outs[i * count : (i + 1) * count]) for i in range(len(widths))]


def digits(groups):
    bits = groups.bit_length() - 1
    found = [(0, 2)]
    while found[-1][0] + (found[-1][1].bit_length() - 1) < bits:
        shift = found[-1][0] + found[-1][1].bit_length() - 1
        found.append((shift, 4 if shift + 2 <= bits else 2))
    return found


def by_digit(slots, digit):
    shift, radix = digit
    return [[r for r in slots if r >> shift & radix - 1 == value] for value in range(radix)]


def regroup(name, blocks, layout, digit, block, after):
    columns = blocks[0].shape[1]
    place = {r: (i, j) for i, held in enumerate(layout) for j, r in enumerate(held)}
    wanted = by_digit(sum(layout, []), digit)

    def sort(values):
        parts = [[values[place[r][0]][place[r][1] * block :][:block] for r in held] for held in wanted]
        return [jnp.concatenate(part, axis=0) for part in parts]

    if block % ROWS:
        return sort(blocks), wanted

    def kernel(*refs):
        for ref, value in zip(refs[len(blocks) :], sort([ref[...] for ref in refs[: len(blocks)]])):
            ref[...] = value

    outs = call(
        kernel,
        name,
        [jax.ShapeDtypeStruct((len(held) * block, columns), BF16) for held in wanted],
        [WHOLE] * len(blocks),
        blocks,
        after,
        out_specs=[WHOLE] * len(wanted),
        cost_estimate=cost(0, 4 * block * len(place) * columns),
    )
    return list(outs), wanted


def last(name, weight, basis, keep, got, before, low, columns, after):
    rows, width = basis.shape
    wide = keep.shape[1]
    pieces = row_pieces(rows, 6)
    depth = rows // pieces
    given = [] if before is None else [before]

    def kernel(weight, basis, keep, got, *refs):
        out, here, left = refs[len(given) :]
        stacked = jnp.concatenate([keep[...], got[...]], axis=0)
        coeffs = matmul(weight[...], stacked).astype(BF16)
        copies = []
        for i in range(pieces):
            part = pl.ds(i * depth, depth)
            here[part, :] = matmul(basis[part, :], coeffs).astype(BF16)
            copy = pltpu.make_async_copy(here.at[part], out.at[part, pl.ds(low, wide)], left.at[i])
            copy.start()
            copies.append(copy)
        for copy in copies:
            copy.wait()

    return call(
        kernel,
        name,
        jax.ShapeDtypeStruct((rows, columns), BF16),
        [WHOLE] * 4 + [HBM] * len(given),
        [weight, basis, keep, got] + given,
        after,
        out_specs=HBM,
        scratch_shapes=[pltpu.VMEM((rows, wide), BF16), pltpu.SemaphoreType.DMA((pieces,))],
        input_output_aliases={4: 0} if given else {},
        cost_estimate=cost(2 * rows * width * wide, 2 * rows * wide),
    )


def local(signal, col_basis, right_coupling, middle_coupling, left_coupling, row_basis, node_order):
    groups = lax.axis_size("mid")
    width = col_basis.shape[1]
    block = width // groups
    columns = signal.shape[1]
    chunks = shares(columns, ENTRY_SHARES)
    starts = [sum(chunks[:i]) for i in range(len(chunks))]
    merged = {i: group for group in MERGED for i in group}
    if len(chunks) < len(ENTRY_SHARES):
        merged = {i: (i,) for i in range(len(chunks))}
    steps = digits(groups)
    layouts = [by_digit(range(groups), steps[0])]
    for step in steps[1:]:
        layouts.append(by_digit(sum(layouts[-1], []), step))

    opened = opening("opening", col_basis, signal, chunks)
    couplings, out, after = None, None, None
    waiting, pops, entered = [], 0, 0
    parked = {}
    while waiting or entered < len(chunks):
        if entered < len(chunks) and (pops >= ENTRY[entered] or not waiting):
            i, entered = entered, entered + 1
            keep, send = opened[i]
            waiting.append((1, (i,), starts[i], [keep, swap(send, "sub", 1)]))
            continue
        stage, ids, low, blocks = waiting.pop(0)
        pops += 1
        wide = blocks[0].shape[1]
        name = "".join(str(i) for i in ids)
        if couplings is None:
            couplings = prepare(
                "prepare",
                node_order,
                sum(layouts[0], []),
                sum(layouts[-1], []),
                right_coupling,
                middle_coupling,
                left_coupling,
                after,
            )
            right0, right1, middle, left0, left1 = couplings
            after = right0
        if stage == 1:
            results = level(f"right0_{name}", right0, [blocks], [wide], 2, after)
            axis, shift = "sub", 1
        elif stage == 2:
            parked[ids[0]] = blocks
            ids = merged[ids[0]]
            if any(i not in parked for i in ids):
                continue
            wide = sum(chunks[i] for i in ids)
            low = starts[ids[0]]
            blocks = [parked[i] for i in ids]
            results = level(f"right1_{name}", right1, blocks, [wide], steps[0][1], after)
            axis, shift = "mid", steps[0][0]
        elif stage < 2 + len(steps):
            step = steps[stage - 2]
            held_as = layouts[stage - 3]
            results = [regroup(f"regroup{stage}_{name}", blocks, held_as, step, block, after)[0]]
            axis, shift = "mid", step[0]
        elif stage == 2 + len(steps):
            widths = shares(wide, SPLIT.get(ids, (1,)))
            results = level(f"middle_{name}", middle, [blocks], widths, 2, after)
            axis, shift = "sub", 1
        elif stage == 3 + len(steps):
            results = level(f"left0_{name}", left0, [blocks], [wide], 2, after)
            axis, shift = "sub", 0
        else:
            out = last(f"last{low}", left1, row_basis, *blocks, out, low, columns, after)
            continue
        after = results[0][0]
        for result in results:
            moved = [swap(send, axis, i + 1 << shift) for i, send in enumerate(result[1:])]
            waiting.append((stage + 1, ids, low, result[:1] + moved))
            low += result[0].shape[1]
    return out


def solution(mesh):
    return jax.shard_map(
        local,
        mesh=mesh,
        in_specs=(
            P(("mid", "sub"), None),
            P(("mid", "sub"), None),
            P(("mid", "sub"), None, None, None),
            P(("mid", "sub"), None, None),
            P(("mid", "sub"), None, None, None),
            P(("mid", "sub"), None),
            P(),
        ),
        out_specs=P(("mid", "sub"), None),
        check_vma=False,
    )
```

time: 58.1 us -> 53.5 us (0.921)
  starting transfers between devices: 22.3 us -> 29.7 us
  waiting for transfers between devices: 19.6 us -> 13.5 us
  Pallas kernels: 15.5 us -> 9.8 us
    ppermute x21 -> x24, starting transfers between devices: 22.3 us -> 29.7 us  [swap(): return lax.ppermute(block, axis, [(i, i ^ distance) for i in range(count)])]
    ppermute x21 -> x24, waiting for transfers between devices: 19.6 us -> 13.5 us  [swap(): return lax.ppermute(block, axis, [(i, i ^ distance) for i in range(count)])]
    pallas_call x25 -> x20, Pallas kernels: 15.5 us -> 9.8 us  [call(): pl.pallas_call(body, name=name, in_specs=specs + [PLACE] * len(extra), ou...]
  transfers between devices with their start and end apart: 21 -> 24, of which waited for: 11 -> 12; matrix products, arithmetic and copies ran while one was open for 0% -> 0% of each run, Pallas kernels for 20% -> 11%
where the time goes in v8:
time: 53.5 us; the launch traced here: 53.3 us
  starting transfers between devices  29.7 us (56%)
  waiting for transfers between devices  13.5 us (25%)
  Pallas kernels  9.8 us (18%)
    ppermute x24, starting transfers between devices, swap(): return lax.ppermute(block, axis, [(i, i ^ distance) for i in range(count)])  29.7 us
    ppermute x24, waiting for transfers between devices, swap(): return lax.ppermute(block, axis, [(i, i ^ distance) for i in range(count)])  13.5 us
    pallas_call x20, Pallas kernels, call(): pl.pallas_call(body, name=name, in_specs=specs + [PLACE] * len(extra), ou...  9.8 us
  transfers between devices with their start and end apart: 24, of which 12 were waited for; matrix products, arithmetic and copies ran while one was open for 0% of the time, Pallas kernels for 11%

profile of v8, /device:TPU:0, one launch (start us, length us, event | category | flops | bytes accessed | tf_op | source)
XLA Modules:
  0.0 53.3 jit_solution(6741706265518891141)
XLA Ops:
  0.0 2.5 %opening.1 = (bf16[128,384]{1,0:T(8,128)(2,1)S(1)}, bf16[128,384]{1,0:T(8,128)(2,1)S(1)}, bf16[128,384]{1,0:T(8,128)(2,1)S(1)}, bf16[128,384]{1,0:T(8,128)(2,1)S...) custom-call(bf16[768,256]{1,0:T(8,128)(2,1)} %refs_0_.3, bf16[768,1152]{1,0:T(8,128)(2,1)} %refs_1_.6), custom_call_target="tpu_custom_call" | custom-call | flops 452984832 | bytes 2162688 | tf_op jit(solution)/shard_map/opening/pallas_call | solution.py:59
  2.5 3.1 %collective-permute-start.1 = (bf16[128,384]{1,0:T(8,128)(2,1)S(1)}, bf16[128,384]{1,0:T(8,128)(2,1)S(1)}, u32[]{:S(2)}, u32[]{:S(2)}) collective-permute-start(bf16[128,384]{1,0:T(8,128)(2,1)S(1)} %get-tuple-element.60), channel_id=1, source_target_pairs={{0,1},{1,0},{2,3},{3,2},{4,5},{5,4},{6,7},{7,6},{8,9},{9,8},{10,11... | collective-permute-start | bytes 294920 | tf_op jit(solution)/shard_map/ppermute | solution.py:35
  6.6 2.6 %collective-permute-done.1.refs_2_ = bf16[128,384]{1,0:T(8,128)(2,1)S(1)} collective-permute-done((bf16[128,384]{1,0:T(8,128)(2,1)S(1)}, bf16[128,384]{1,0:T(8,128)(2,1)S(1)}, u32[]{:S(2)}, u32[]{:S(2)}) %collective-permute-start.1) | collective-permute-done | bytes 98336 | tf_op jit(solution)/shard_map/ppermute | solution.py:35
  9.3 3.1 %collective-permute-start.2 = (bf16[128,384]{1,0:T(8,128)(2,1)S(1)}, bf16[128,384]{1,0:T(8,128)(2,1)S(1)}, u32[]{:S(2)}, u32[]{:S(2)}) collective-permute-start(bf16[128,384]{1,0:T(8,128)(2,1)S(1)} %get-tuple-element.62), channel_id=1, source_target_pairs={{0,2},{1,3},{2,0},{3,1},{4,6},{5,7},{6,4},{7,5},{8,10},{9,11},{10,... | collective-permute-start | bytes 294920 | tf_op jit(solution)/shard_map/ppermute | solution.py:35
  12.4 1.7 %collective-permute-start = (bf16[128,384]{1,0:T(8,128)(2,1)S(1)}, bf16[128,384]{1,0:T(8,128)(2,1)S(1)}, u32[]{:S(2)}, u32[]{:S(2)}) collective-permute-start(bf16[128,384]{1,0:T(8,128)(2,1)S(1)} %get-tuple-element.58), channel_id=1, source_target_pairs={{0,1},{1,0},{2,3},{3,2},{4,5},{5,4},{6,7},{7,6},{8,9},{9,8},{10,11... | collective-permute-start | bytes 294920 | tf_op jit(solution)/shard_map/ppermute | solution.py:35
  14.7 2.4 %collective-permute-done.2.refs_2_ = bf16[128,384]{1,0:T(8,128)(2,1)S(1)} collective-permute-done((bf16[128,384]{1,0:T(8,128)(2,1)S(1)}, bf16[128,384]{1,0:T(8,128)(2,1)S(1)}, u32[]{:S(2)}, u32[]{:S(2)}) %collective-permute-start.2) | collective-permute-done | bytes 98336 | tf_op jit(solution)/shard_map/ppermute | solution.py:35
  17.7 1.5 %collective-permute-start.4 = (bf16[128,384]{1,0:T(8,128)(2,1)S(1)}, bf16[128,384]{1,0:T(8,128)(2,1)S(1)}, u32[]{:S(2)}, u32[]{:S(2)}) collective-permute-start(bf16[128,384]{1,0:T(8,128)(2,1)S(1)} %get-tuple-element.68), channel_id=1, source_target_pairs={{0,2},{1,3},{2,0},{3,1},{4,6},{5,7},{6,4},{7,5},{8,10},{9,11},{10,... | collective-permute-start | bytes 294920 | tf_op jit(solution)/shard_map/ppermute | solution.py:35
  19.2 1.6 %collective-permute-done.6.refs_2_ = bf16[128,384]{1,0:T(8,128)(2,1)S(1)} collective-permute-done((bf16[128,384]{1,0:T(8,128)(2,1)S(1)}, bf16[128,384]{1,0:T(8,128)(2,1)S(1)}, u32[]{:S(2)}, u32[]{:S(2)}) %collective-permute-start.6) | collective-permute-done | bytes 98336 | tf_op jit(solution)/shard_map/ppermute | solution.py:35
  21.1 1.6 %collective-permute-start.8 = (bf16[64,384]{1,0:T(8,128)(2,1)S(1)}, bf16[64,384]{1,0:T(8,128)(2,1)S(1)}, u32[]{:S(2)}, u32[]{:S(2)}) collective-permute-start(bf16[64,384]{1,0:T(8,128)(2,1)S(1)} %get-tuple-element.75), channel_id=1, source_target_pairs={{0,8},{4,12},{8,0},{12,4},{16,24},{20,28},{24,16},{28,20},{1,9},{5... | collective-permute-start | bytes 147464 | tf_op jit(solution)/shard_map/ppermute | solution.py:35
  22.7 1.5 %collective-permute-start.9 = (bf16[64,384]{1,0:T(8,128)(2,1)S(1)}, bf16[64,384]{1,0:T(8,128)(2,1)S(1)}, u32[]{:S(2)}, u32[]{:S(2)}) collective-permute-start(bf16[64,384]{1,0:T(8,128)(2,1)S(1)} %get-tuple-element.76), channel_id=1, source_target_pairs={{0,16},{4,20},{8,24},{12,28},{16,0},{20,4},{24,8},{28,12},{1,17},{... | collective-permute-start | bytes 147464 | tf_op jit(solution)/shard_map/ppermute | solution.py:35
  25.3 1.5 %collective-permute-done.9.refs_3_ = bf16[64,384]{1,0:T(8,128)(2,1)S(1)} collective-permute-done((bf16[64,384]{1,0:T(8,128)(2,1)S(1)}, bf16[64,384]{1,0:T(8,128)(2,1)S(1)}, u32[]{:S(2)}, u32[]{:S(2)}) %collective-permute-start.9) | collective-permute-done | bytes 49184 | tf_op jit(solution)/shard_map/ppermute | solution.py:35
  26.8 2.4 %collective-permute-done.10.refs_4_ = bf16[64,384]{1,0:T(8,128)(2,1)S(1)} collective-permute-done((bf16[64,384]{1,0:T(8,128)(2,1)S(1)}, bf16[64,384]{1,0:T(8,128)(2,1)S(1)}, u32[]{:S(2)}, u32[]{:S(2)}) %collective-permute-start.10) | collective-permute-done | bytes 49184 | tf_op jit(solution)/shard_map/ppermute | solution.py:35
  29.4 0.9 %collective-permute-start.15 = (bf16[128,384]{1,0:T(8,128)(2,1)S(1)}, bf16[128,384]{1,0:T(8,128)(2,1)S(1)}, u32[]{:S(2)}, u32[]{:S(2)}) collective-permute-start(bf16[128,384]{1,0:T(8,128)(2,1)S(1)} %get-tuple-element.85), channel_id=1, source_target_pairs={{0,2},{1,3},{2,0},{3,1},{4,6},{5,7},{6,4},{7,5},{8,10},{9,11},{10,... | collective-permute-start | bytes 294920 | tf_op jit(solution)/shard_map/ppermute | solution.py:35
  31.0 2.8 %collective-permute-start.18 = (bf16[64,384]{1,0:T(8,128)(2,1)S(1)}, bf16[64,384]{1,0:T(8,128)(2,1)S(1)}, u32[]{:S(2)}, u32[]{:S(2)}) collective-permute-start(bf16[64,384]{1,0:T(8,128)(2,1)S(1)} %get-tuple-element.88), channel_id=1, source_target_pairs={{0,24},{4,28},{8,16},{12,20},{16,8},{20,12},{24,0},{28,4},{1,25},{... | collective-permute-start | bytes 147464 | tf_op jit(solution)/shard_map/ppermute | solution.py:35
  36.2 1.2 %collective-permute-start.14 = (bf16[64,384]{1,0:T(8,128)(2,1)S(1)}, bf16[64,384]{1,0:T(8,128)(2,1)S(1)}, u32[]{:S(2)}, u32[]{:S(2)}) collective-permute-start(bf16[64,384]{1,0:T(8,128)(2,1)S(1)} %get-tuple-element.84), channel_id=1, source_target_pairs={{0,24},{4,28},{8,16},{12,20},{16,8},{20,12},{24,0},{28,4},{1,25},{... | collective-permute-start | bytes 147464 | tf_op jit(solution)/shard_map/ppermute | solution.py:35
  37.6 2.2 %collective-permute-start.20 = (bf16[128,384]{1,0:T(8,128)(2,1)S(1)}, bf16[128,384]{1,0:T(8,128)(2,1)S(1)}, u32[]{:S(2)}, u32[]{:S(2)}) collective-permute-start(bf16[128,384]{1,0:T(8,128)(2,1)S(1)} %get-tuple-element.93), channel_id=1, source_target_pairs={{0,2},{1,3},{2,0},{3,1},{4,6},{5,7},{6,4},{7,5},{8,10},{9,11},{10,... | collective-permute-start | bytes 294920 | tf_op jit(solution)/shard_map/ppermute | solution.py:35
  40.0 1.1 %collective-permute-done.14.refs_4_ = bf16[64,384]{1,0:T(8,128)(2,1)S(1)} collective-permute-done((bf16[64,384]{1,0:T(8,128)(2,1)S(1)}, bf16[64,384]{1,0:T(8,128)(2,1)S(1)}, u32[]{:S(2)}, u32[]{:S(2)}) %collective-permute-start.14) | collective-permute-done | bytes 49184 | tf_op jit(solution)/shard_map/ppermute | solution.py:35
  41.4 1.8 %collective-permute-start.19 = (bf16[128,384]{1,0:T(8,128)(2,1)S(1)}, bf16[128,384]{1,0:T(8,128)(2,1)S(1)}, u32[]{:S(2)}, u32[]{:S(2)}) collective-permute-start(bf16[128,384]{1,0:T(8,128)(2,1)S(1)} %get-tuple-element.92), channel_id=1, source_target_pairs={{0,2},{1,3},{2,0},{3,1},{4,6},{5,7},{6,4},{7,5},{8,10},{9,11},{10,... | collective-permute-start | bytes 294920 | tf_op jit(solution)/shard_map/ppermute | solution.py:35
  43.1 2.4 %collective-permute-start.23 = (bf16[128,384]{1,0:T(8,128)(2,1)S(1)}, bf16[128,384]{1,0:T(8,128)(2,1)S(1)}, u32[]{:S(2)}, u32[]{:S(2)}) collective-permute-start(bf16[128,384]{1,0:T(8,128)(2,1)S(1)} %get-tuple-element.98), channel_id=1, source_target_pairs={{0,1},{1,0},{2,3},{3,2},{4,5},{5,4},{6,7},{7,6},{8,9},{9,8},{10,11... | collective-permute-start | bytes 294920 | tf_op jit(solution)/shard_map/ppermute | solution.py:35
  46.0 1.2 %collective-permute-start.22 = (bf16[128,384]{1,0:T(8,128)(2,1)S(1)}, bf16[128,384]{1,0:T(8,128)(2,1)S(1)}, u32[]{:S(2)}, u32[]{:S(2)}) collective-permute-start(bf16[128,384]{1,0:T(8,128)(2,1)S(1)} %get-tuple-element.97), channel_id=1, source_target_pairs={{0,1},{1,0},{2,3},{3,2},{4,5},{5,4},{6,7},{7,6},{8,9},{9,8},{10,11... | collective-permute-start | bytes 294920 | tf_op jit(solution)/shard_map/ppermute | solution.py:35
  47.4 1.9 %collective-permute-start.21 = (bf16[128,384]{1,0:T(8,128)(2,1)S(1)}, bf16[128,384]{1,0:T(8,128)(2,1)S(1)}, u32[]{:S(2)}, u32[]{:S(2)}) collective-permute-start(bf16[128,384]{1,0:T(8,128)(2,1)S(1)} %get-tuple-element.96), channel_id=1, source_target_pairs={{0,1},{1,0},{2,3},{3,2},{4,5},{5,4},{6,7},{7,6},{8,9},{9,8},{10,11... | collective-permute-start | bytes 294920 | tf_op jit(solution)/shard_map/ppermute | solution.py:35
  49.3 1.3 %last0.1.refs_4_ = bf16[768,1152]{1,0:T(8,128)(2,1)} custom-call(bf16[256,256]{1,0:T(8,128)(2,1)S(1)} %get-tuple-element.52.refs_0_, bf16[768,256]{1,0:T(8,128)(2,1)S(1)} %copy-done, bf16[128,384]{1,0:T(8,128)(2,1)S(1)} %get-tuple-element.90.refs_5_.refs_2_, bf16[128,384]{1,0:T(8,128)(2,1)S(1)} %collective-permute-done.23.refs_3_, ...), custom_call_target="tpu_custom_call" | custom-call | flops 150994944 | bytes 589824 | tf_op jit(solution)/shard_map/last0/pallas_call | solution.py:59
  50.6 1.2 %last384.1.refs_4_ = bf16[768,1152]{1,0:T(8,128)(2,1)} custom-call(bf16[256,256]{1,0:T(8,128)(2,1)S(1)} %get-tuple-element.52.refs_0_, bf16[768,256]{1,0:T(8,128)(2,1)S(1)} %copy-done, bf16[128,384]{1,0:T(8,128)(2,1)S(1)} %get-tuple-element.94.refs_3_.refs_4_.refs_2_, ...), custom_call_target="tpu_custom_call", output_to_operand_aliasing={{}: (4, {})} | custom-call | flops 150994944 | bytes 589824 | tf_op jit(solution)/shard_map/last384/pallas_call | solution.py:59
  52.1 1.3 %last768.1 = bf16[768,1152]{1,0:T(8,128)(2,1)} custom-call(bf16[256,256]{1,0:T(8,128)(2,1)S(1)} %get-tuple-element.52.refs_0_, bf16[768,256]{1,0:T(8,128)(2,1)S(1)} %copy-done, bf16[128,384]{1,0:T(8,128)(2,1)S(1)} %get-tuple-element.95.refs_5_.refs_2_, bf16[128,384]{1,0:T(8,128)(2,1)S(1)} %collective-permute-done.21.refs_3_, ...), custom_call_target="tpu_custom_call", output_to_operand_aliasing={{}: (4, {})} | custom-call | flops 150994944 | bytes 589824 | tf_op jit(solution)/shard_map/last768/pallas_call | solution.py:59
  (54 shorter events, 8.6 us)
Async XLA Ops:
  2.5 6.6 %collective-permute-start.1 = (bf16[128,384]{1,0:T(8,128)(2,1)S(1)}, bf16[128,384]{1,0:T(8,128)(2,1)S(1)}, u32[]{:S(2)}, u32[]{:S(2)}) collective-permute-start(bf16[128,384]{1,0:T(8,128)(2,1)S(1)} %get-tuple-element.60), channel_id=1, source_target_pairs={{0,1},{1,0},{2,3},{3,2},{4,5},{5,4},{6,7},{7,6},{8,9},{9,8},{10,11... | collective-permute-start | bytes 294920 | tf_op jit(solution)/shard_map/ppermute | solution.py:35
  5.6 8.5 %collective-permute-start.3 = (bf16[128,384]{1,0:T(8,128)(2,1)S(1)}, bf16[128,384]{1,0:T(8,128)(2,1)S(1)}, u32[]{:S(2)}, u32[]{:S(2)}) collective-permute-start(bf16[128,384]{1,0:T(8,128)(2,1)S(1)} %get-tuple-element.64), channel_id=1, source_target_pairs={{0,1},{1,0},{2,3},{3,2},{4,5},{5,4},{6,7},{7,6},{8,9},{9,8},{10,11... | collective-permute-start | bytes 294920 | tf_op jit(solution)/shard_map/ppermute | solution.py:35
  9.3 7.8 %collective-permute-start.2 = (bf16[128,384]{1,0:T(8,128)(2,1)S(1)}, bf16[128,384]{1,0:T(8,128)(2,1)S(1)}, u32[]{:S(2)}, u32[]{:S(2)}) collective-permute-start(bf16[128,384]{1,0:T(8,128)(2,1)S(1)} %get-tuple-element.62), channel_id=1, source_target_pairs={{0,2},{1,3},{2,0},{3,1},{4,6},{5,7},{6,4},{7,5},{8,10},{9,11},{10,... | collective-permute-start | bytes 294920 | tf_op jit(solution)/shard_map/ppermute | solution.py:35
  12.4 5.0 %collective-permute-start = (bf16[128,384]{1,0:T(8,128)(2,1)S(1)}, bf16[128,384]{1,0:T(8,128)(2,1)S(1)}, u32[]{:S(2)}, u32[]{:S(2)}) collective-permute-start(bf16[128,384]{1,0:T(8,128)(2,1)S(1)} %get-tuple-element.58), channel_id=1, source_target_pairs={{0,1},{1,0},{2,3},{3,2},{4,5},{5,4},{6,7},{7,6},{8,9},{9,8},{10,11... | collective-permute-start | bytes 294920 | tf_op jit(solution)/shard_map/ppermute | solution.py:35
  14.3 6.4 %collective-permute-start.6 = (bf16[128,384]{1,0:T(8,128)(2,1)S(1)}, bf16[128,384]{1,0:T(8,128)(2,1)S(1)}, u32[]{:S(2)}, u32[]{:S(2)}) collective-permute-start(bf16[128,384]{1,0:T(8,128)(2,1)S(1)} %get-tuple-element.70), channel_id=1, source_target_pairs={{0,2},{1,3},{2,0},{3,1},{4,6},{5,7},{6,4},{7,5},{8,10},{9,11},{10,... | collective-permute-start | bytes 294920 | tf_op jit(solution)/shard_map/ppermute | solution.py:35
  17.4 3.7 %collective-permute-start.5 = (bf16[128,384]{1,0:T(8,128)(2,1)S(1)}, bf16[128,384]{1,0:T(8,128)(2,1)S(1)}, u32[]{:S(2)}, u32[]{:S(2)}) collective-permute-start(bf16[128,384]{1,0:T(8,128)(2,1)S(1)} %get-tuple-element.69), channel_id=1, source_target_pairs={{0,4},{4,0},{8,12},{12,8},{16,20},{20,16},{24,28},{28,24},{1,5},{5... | collective-permute-start | bytes 294920 | tf_op jit(solution)/shard_map/ppermute | solution.py:35
  17.7 7.0 %collective-permute-start.4 = (bf16[128,384]{1,0:T(8,128)(2,1)S(1)}, bf16[128,384]{1,0:T(8,128)(2,1)S(1)}, u32[]{:S(2)}, u32[]{:S(2)}) collective-permute-start(bf16[128,384]{1,0:T(8,128)(2,1)S(1)} %get-tuple-element.68), channel_id=1, source_target_pairs={{0,2},{1,3},{2,0},{3,1},{4,6},{5,7},{6,4},{7,5},{8,10},{9,11},{10,... | collective-permute-start | bytes 294920 | tf_op jit(solution)/shard_map/ppermute | solution.py:35
  21.0 4.0 %collective-permute-start.11 = (bf16[128,384]{1,0:T(8,128)(2,1)S(1)}, bf16[128,384]{1,0:T(8,128)(2,1)S(1)}, u32[]{:S(2)}, u32[]{:S(2)}) collective-permute-start(bf16[128,384]{1,0:T(8,128)(2,1)S(1)} %get-tuple-element.78), channel_id=1, source_target_pairs={{0,4},{4,0},{8,12},{12,8},{16,20},{20,16},{24,28},{28,24},{1,5},{5... | collective-permute-start | bytes 294920 | tf_op jit(solution)/shard_map/ppermute | solution.py:35
  21.1 4.2 %collective-permute-start.8 = (bf16[64,384]{1,0:T(8,128)(2,1)S(1)}, bf16[64,384]{1,0:T(8,128)(2,1)S(1)}, u32[]{:S(2)}, u32[]{:S(2)}) collective-permute-start(bf16[64,384]{1,0:T(8,128)(2,1)S(1)} %get-tuple-element.75), channel_id=1, source_target_pairs={{0,8},{4,12},{8,0},{12,4},{16,24},{20,28},{24,16},{28,20},{1,9},{5... | collective-permute-start | bytes 147464 | tf_op jit(solution)/shard_map/ppermute | solution.py:35
  22.7 4.1 %collective-permute-start.9 = (bf16[64,384]{1,0:T(8,128)(2,1)S(1)}, bf16[64,384]{1,0:T(8,128)(2,1)S(1)}, u32[]{:S(2)}, u32[]{:S(2)}) collective-permute-start(bf16[64,384]{1,0:T(8,128)(2,1)S(1)} %get-tuple-element.76), channel_id=1, source_target_pairs={{0,16},{4,20},{8,24},{12,28},{16,0},{20,4},{24,8},{28,12},{1,17},{... | collective-permute-start | bytes 147464 | tf_op jit(solution)/shard_map/ppermute | solution.py:35
  24.2 5.0 %collective-permute-start.10 = (bf16[64,384]{1,0:T(8,128)(2,1)S(1)}, bf16[64,384]{1,0:T(8,128)(2,1)S(1)}, u32[]{:S(2)}, u32[]{:S(2)}) collective-permute-start(bf16[64,384]{1,0:T(8,128)(2,1)S(1)} %get-tuple-element.77), channel_id=1, source_target_pairs={{0,24},{4,28},{8,16},{12,20},{16,8},{20,12},{24,0},{28,4},{1,25},{... | collective-permute-start | bytes 147464 | tf_op jit(solution)/shard_map/ppermute | solution.py:35
  24.9 8.9 %collective-permute-start.7 = (bf16[128,384]{1,0:T(8,128)(2,1)S(1)}, bf16[128,384]{1,0:T(8,128)(2,1)S(1)}, u32[]{:S(2)}, u32[]{:S(2)}) collective-permute-start(bf16[128,384]{1,0:T(8,128)(2,1)S(1)} %get-tuple-element.74), channel_id=1, source_target_pairs={{0,4},{4,0},{8,12},{12,8},{16,20},{20,16},{24,28},{28,24},{1,5},{5... | collective-permute-start | bytes 294920 | tf_op jit(solution)/shard_map/ppermute | solution.py:35
  29.4 10.4 %collective-permute-start.15 = (bf16[128,384]{1,0:T(8,128)(2,1)S(1)}, bf16[128,384]{1,0:T(8,128)(2,1)S(1)}, u32[]{:S(2)}, u32[]{:S(2)}) collective-permute-start(bf16[128,384]{1,0:T(8,128)(2,1)S(1)} %get-tuple-element.85), channel_id=1, source_target_pairs={{0,2},{1,3},{2,0},{3,1},{4,6},{5,7},{6,4},{7,5},{8,10},{9,11},{10,... | collective-permute-start | bytes 294920 | tf_op jit(solution)/shard_map/ppermute | solution.py:35
  30.3 4.5 %collective-permute-start.16 = (bf16[64,384]{1,0:T(8,128)(2,1)S(1)}, bf16[64,384]{1,0:T(8,128)(2,1)S(1)}, u32[]{:S(2)}, u32[]{:S(2)}) collective-permute-start(bf16[64,384]{1,0:T(8,128)(2,1)S(1)} %get-tuple-element.86), channel_id=1, source_target_pairs={{0,8},{4,12},{8,0},{12,4},{16,24},{20,28},{24,16},{28,20},{1,9},{5... | collective-permute-start | bytes 147464 | tf_op jit(solution)/shard_map/ppermute | solution.py:35
  30.8 5.4 %collective-permute-start.17 = (bf16[64,384]{1,0:T(8,128)(2,1)S(1)}, bf16[64,384]{1,0:T(8,128)(2,1)S(1)}, u32[]{:S(2)}, u32[]{:S(2)}) collective-permute-start(bf16[64,384]{1,0:T(8,128)(2,1)S(1)} %get-tuple-element.87), channel_id=1, source_target_pairs={{0,16},{4,20},{8,24},{12,28},{16,0},{20,4},{24,8},{28,12},{1,17},{... | collective-permute-start | bytes 147464 | tf_op jit(solution)/shard_map/ppermute | solution.py:35
  31.0 6.4 %collective-permute-start.18 = (bf16[64,384]{1,0:T(8,128)(2,1)S(1)}, bf16[64,384]{1,0:T(8,128)(2,1)S(1)}, u32[]{:S(2)}, u32[]{:S(2)}) collective-permute-start(bf16[64,384]{1,0:T(8,128)(2,1)S(1)} %get-tuple-element.88), channel_id=1, source_target_pairs={{0,24},{4,28},{8,16},{12,20},{16,8},{20,12},{24,0},{28,4},{1,25},{... | collective-permute-start | bytes 147464 | tf_op jit(solution)/shard_map/ppermute | solution.py:35
  33.8 6.2 %collective-permute-start.12 = (bf16[64,384]{1,0:T(8,128)(2,1)S(1)}, bf16[64,384]{1,0:T(8,128)(2,1)S(1)}, u32[]{:S(2)}, u32[]{:S(2)}) collective-permute-start(bf16[64,384]{1,0:T(8,128)(2,1)S(1)} %get-tuple-element.82), channel_id=1, source_target_pairs={{0,8},{4,12},{8,0},{12,4},{16,24},{20,28},{24,16},{28,20},{1,9},{5... | collective-permute-start | bytes 147464 | tf_op jit(solution)/shard_map/ppermute | solution.py:35
  34.8 5.2 %collective-permute-start.13 = (bf16[64,384]{1,0:T(8,128)(2,1)S(1)}, bf16[64,384]{1,0:T(8,128)(2,1)S(1)}, u32[]{:S(2)}, u32[]{:S(2)}) collective-permute-start(bf16[64,384]{1,0:T(8,128)(2,1)S(1)} %get-tuple-element.83), channel_id=1, source_target_pairs={{0,16},{4,20},{8,24},{12,28},{16,0},{20,4},{24,8},{28,12},{1,17},{... | collective-permute-start | bytes 147464 | tf_op jit(solution)/shard_map/ppermute | solution.py:35
  36.2 5.0 %collective-permute-start.14 = (bf16[64,384]{1,0:T(8,128)(2,1)S(1)}, bf16[64,384]{1,0:T(8,128)(2,1)S(1)}, u32[]{:S(2)}, u32[]{:S(2)}) collective-permute-start(bf16[64,384]{1,0:T(8,128)(2,1)S(1)} %get-tuple-element.84), channel_id=1, source_target_pairs={{0,24},{4,28},{8,16},{12,20},{16,8},{20,12},{24,0},{28,4},{1,25},{... | collective-permute-start | bytes 147464 | tf_op jit(solution)/shard_map/ppermute | solution.py:35
  37.6 8.2 %collective-permute-start.20 = (bf16[128,384]{1,0:T(8,128)(2,1)S(1)}, bf16[128,384]{1,0:T(8,128)(2,1)S(1)}, u32[]{:S(2)}, u32[]{:S(2)}) collective-permute-start(bf16[128,384]{1,0:T(8,128)(2,1)S(1)} %get-tuple-element.93), channel_id=1, source_target_pairs={{0,2},{1,3},{2,0},{3,1},{4,6},{5,7},{6,4},{7,5},{8,10},{9,11},{10,... | collective-permute-start | bytes 294920 | tf_op jit(solution)/shard_map/ppermute | solution.py:35
  41.4 5.8 %collective-permute-start.19 = (bf16[128,384]{1,0:T(8,128)(2,1)S(1)}, bf16[128,384]{1,0:T(8,128)(2,1)S(1)}, u32[]{:S(2)}, u32[]{:S(2)}) collective-permute-start(bf16[128,384]{1,0:T(8,128)(2,1)S(1)} %get-tuple-element.92), channel_id=1, source_target_pairs={{0,2},{1,3},{2,0},{3,1},{4,6},{5,7},{6,4},{7,5},{8,10},{9,11},{10,... | collective-permute-start | bytes 294920 | tf_op jit(solution)/shard_map/ppermute | solution.py:35
  43.1 6.2 %collective-permute-start.23 = (bf16[128,384]{1,0:T(8,128)(2,1)S(1)}, bf16[128,384]{1,0:T(8,128)(2,1)S(1)}, u32[]{:S(2)}, u32[]{:S(2)}) collective-permute-start(bf16[128,384]{1,0:T(8,128)(2,1)S(1)} %get-tuple-element.98), channel_id=1, source_target_pairs={{0,1},{1,0},{2,3},{3,2},{4,5},{5,4},{6,7},{7,6},{8,9},{9,8},{10,11... | collective-permute-start | bytes 294920 | tf_op jit(solution)/shard_map/ppermute | solution.py:35
  46.0 4.7 %collective-permute-start.22 = (bf16[128,384]{1,0:T(8,128)(2,1)S(1)}, bf16[128,384]{1,0:T(8,128)(2,1)S(1)}, u32[]{:S(2)}, u32[]{:S(2)}) collective-permute-start(bf16[128,384]{1,0:T(8,128)(2,1)S(1)} %get-tuple-element.97), channel_id=1, source_target_pairs={{0,1},{1,0},{2,3},{3,2},{4,5},{5,4},{6,7},{7,6},{8,9},{9,8},{10,11... | collective-permute-start | bytes 294920 | tf_op jit(solution)/shard_map/ppermute | solution.py:35
  47.4 4.7 %collective-permute-start.21 = (bf16[128,384]{1,0:T(8,128)(2,1)S(1)}, bf16[128,384]{1,0:T(8,128)(2,1)S(1)}, u32[]{:S(2)}, u32[]{:S(2)}) collective-permute-start(bf16[128,384]{1,0:T(8,128)(2,1)S(1)} %get-tuple-element.96), channel_id=1, source_target_pairs={{0,1},{1,0},{2,3},{3,2},{4,5},{5,4},{6,7},{7,6},{8,9},{9,8},{10,11... | collective-permute-start | bytes 294920 | tf_op jit(solution)/shard_map/ppermute | solution.py:35
  (5 other events, 51.0 us)

commit v9 on v8

--- a/solution.py
+++ b/solution.py
@@ -6,9 +6,9 @@
 from jax.sharding import PartitionSpec as P
 
 LANES = 128
-ENTRY_SHARES = (3, 3, 3)
-ENTRY = (0, 0, 1)
-MERGED = ((0,), (1,), (2,))
+ENTRY_SHARES = (1, 2, 3, 3)
+ENTRY = (0, 0, 0, 2)
+MERGED = ((0, 1), (2,), (3,))
 SPLIT = {}
 ROWS = 16
 SCOPED = 8 * 2**20

time: 53.5 us -> 59.1 us (1.10)
  waiting for transfers between devices: 13.5 us -> 20.2 us
  starting transfers between devices: 29.7 us -> 28.6 us
    ppermute x24 -> x26, waiting for transfers between devices: 13.5 us -> 20.2 us  [swap(): return lax.ppermute(block, axis, [(i, i ^ distance) for i in range(count)])]
    ppermute x24 -> x26, starting transfers between devices: 29.7 us -> 28.6 us  [swap(): return lax.ppermute(block, axis, [(i, i ^ distance) for i in range(count)])]
    pallas_call x20 -> x21, Pallas kernels: 9.8 us -> 9.92 us  [call(): pl.pallas_call(body, name=name, in_specs=specs + [PLACE] * len(extra), ou...]
  transfers between devices with their start and end apart: 24 -> 26, of which waited for: 12 -> 13; matrix products, arithmetic and copies ran while one was open for 0% -> 0% of each run, Pallas kernels for 11% -> 10%
where the time goes in v9:
time: 59.1 us; the launch traced here: 58.9 us
  starting transfers between devices  28.6 us (48%)
  waiting for transfers between devices  20.2 us (34%)
  Pallas kernels  9.92 us (17%)
    ppermute x26, starting transfers between devices, swap(): return lax.ppermute(block, axis, [(i, i ^ distance) for i in range(count)])  28.6 us
    ppermute x26, waiting for transfers between devices, swap(): return lax.ppermute(block, axis, [(i, i ^ distance) for i in range(count)])  20.2 us
    pallas_call x21, Pallas kernels, call(): pl.pallas_call(body, name=name, in_specs=specs + [PLACE] * len(extra), ou...  9.92 us
  transfers between devices with their start and end apart: 26, of which 13 were waited for; matrix products, arithmetic and copies ran while one was open for 0% of the time, Pallas kernels for 10%

profile of v9, /device:TPU:0, one launch (start us, length us, event | category | flops | bytes accessed | tf_op | source)
XLA Modules:
  0.0 58.9 jit_solution(15757146911698733253)
XLA Ops:
  0.0 2.5 %opening.1 = (bf16[128,128]{1,0:T(8,128)(2,1)S(1)}, bf16[128,128]{1,0:T(8,128)(2,1)S(1)}, bf16[128,256]{1,0:T(8,128)(2,1)S(1)}, bf16[128,256]{1,0:T(8,128)(2,1)S...) custom-call(bf16[768,256]{1,0:T(8,128)(2,1)} %refs_0_.3, ...), custom_call_target="tpu_custom_call" | custom-call | flops 452984832 | bytes 2162688 | tf_op jit(solution)/shard_map/opening/pallas_call | solution.py:59
  2.5 3.1 %collective-permute-start.5 = (bf16[128,384]{1,0:T(8,128)(2,1)S(1)}, bf16[128,384]{1,0:T(8,128)(2,1)S(1)}, u32[]{:S(2)}, u32[]{:S(2)}) collective-permute-start(bf16[128,384]{1,0:T(8,128)(2,1)S(1)} %get-tuple-element.72), channel_id=1, source_target_pairs={{0,1},{1,0},{2,3},{3,2},{4,5},{5,4},{6,7},{7,6},{8,9},{9,8},{10,11... | collective-permute-start | bytes 294920 | tf_op jit(solution)/shard_map/ppermute | solution.py:35
  5.7 1.9 %collective-permute-start.1 = (bf16[128,128]{1,0:T(8,128)(2,1)S(1)}, bf16[128,128]{1,0:T(8,128)(2,1)S(1)}, u32[]{:S(2)}, u32[]{:S(2)}) collective-permute-start(bf16[128,128]{1,0:T(8,128)(2,1)S(1)} %get-tuple-element.64), channel_id=1, source_target_pairs={{0,1},{1,0},{2,3},{3,2},{4,5},{5,4},{6,7},{7,6},{8,9},{9,8},{10,11... | collective-permute-start | bytes 98312 | tf_op jit(solution)/shard_map/ppermute | solution.py:35
  7.7 0.8 %prepare.1 = (bf16[256,256]{1,0:T(8,128)(2,1)S(1)}, bf16[256,256]{1,0:T(8,128)(2,1)S(1)}, bf16[256,256]{1,0:T(8,128)(2,1)S(1)}, bf16[256,256]{1,0:T(8,128)(2,1)S(1)}, bf16[256,256]{1,0:T(8,128)(2,1)S(1)}) custom-call(s32[8]{0:T(128)S(1)} %copy-done.4, bf16[1,2,256,256]{3,2,1,0:T(8,128)(2,1)S(1)} %copy-done.1, bf16[1,256,256]{2,1,0:T(8,128)(2,1)S(1)} %copy-done.3, ...), custom_call_target="tpu_custom_call" | custom-call | flops 67108864 | bytes 1310720 | tf_op jit(solution)/shard_map/prepare/pallas_call | solution.py:59
  8.6 2.8 %collective-permute-done.1.refs_2_ = bf16[128,128]{1,0:T(8,128)(2,1)S(1)} collective-permute-done((bf16[128,128]{1,0:T(8,128)(2,1)S(1)}, bf16[128,128]{1,0:T(8,128)(2,1)S(1)}, u32[]{:S(2)}, u32[]{:S(2)}) %collective-permute-start.1) | collective-permute-done | bytes 32800 | tf_op jit(solution)/shard_map/ppermute | solution.py:35
  11.7 3.0 %collective-permute-start.4 = (bf16[128,256]{1,0:T(8,128)(2,1)S(1)}, bf16[128,256]{1,0:T(8,128)(2,1)S(1)}, u32[]{:S(2)}, u32[]{:S(2)}) collective-permute-start(bf16[128,256]{1,0:T(8,128)(2,1)S(1)} %get-tuple-element.70), channel_id=1, source_target_pairs={{0,2},{1,3},{2,0},{3,1},{4,6},{5,7},{6,4},{7,5},{8,10},{9,11},{10,... | collective-permute-start | bytes 196616 | tf_op jit(solution)/shard_map/ppermute | solution.py:35
  15.0 2.9 %collective-permute-start.2 = (bf16[128,128]{1,0:T(8,128)(2,1)S(1)}, bf16[128,128]{1,0:T(8,128)(2,1)S(1)}, u32[]{:S(2)}, u32[]{:S(2)}) collective-permute-start(bf16[128,128]{1,0:T(8,128)(2,1)S(1)} %get-tuple-element.66), channel_id=1, source_target_pairs={{0,2},{1,3},{2,0},{3,1},{4,6},{5,7},{6,4},{7,5},{8,10},{9,11},{10,... | collective-permute-start | bytes 98312 | tf_op jit(solution)/shard_map/ppermute | solution.py:35
  17.9 5.4 %collective-permute-done.2.refs_2_ = bf16[128,128]{1,0:T(8,128)(2,1)S(1)} collective-permute-done((bf16[128,128]{1,0:T(8,128)(2,1)S(1)}, bf16[128,128]{1,0:T(8,128)(2,1)S(1)}, u32[]{:S(2)}, u32[]{:S(2)}) %collective-permute-start.2) | collective-permute-done | bytes 32800 | tf_op jit(solution)/shard_map/ppermute | solution.py:35
  24.9 1.8 %collective-permute-start.10 = (bf16[64,384]{1,0:T(8,128)(2,1)S(1)}, bf16[64,384]{1,0:T(8,128)(2,1)S(1)}, u32[]{:S(2)}, u32[]{:S(2)}) collective-permute-start(bf16[64,384]{1,0:T(8,128)(2,1)S(1)} %get-tuple-element.83), channel_id=1, source_target_pairs={{0,8},{4,12},{8,0},{12,4},{16,24},{20,28},{24,16},{28,20},{1,9},{5... | collective-permute-start | bytes 147464 | tf_op jit(solution)/shard_map/ppermute | solution.py:35
  26.7 1.5 %collective-permute-start.11 = (bf16[64,384]{1,0:T(8,128)(2,1)S(1)}, bf16[64,384]{1,0:T(8,128)(2,1)S(1)}, u32[]{:S(2)}, u32[]{:S(2)}) collective-permute-start(bf16[64,384]{1,0:T(8,128)(2,1)S(1)} %get-tuple-element.84), channel_id=1, source_target_pairs={{0,16},{4,20},{8,24},{12,28},{16,0},{20,4},{24,8},{28,12},{1,17},{... | collective-permute-start | bytes 147464 | tf_op jit(solution)/shard_map/ppermute | solution.py:35
  28.5 3.3 %collective-permute-done.6.refs_2_ = bf16[128,384]{1,0:T(8,128)(2,1)S(1)} collective-permute-done((bf16[128,384]{1,0:T(8,128)(2,1)S(1)}, bf16[128,384]{1,0:T(8,128)(2,1)S(1)}, u32[]{:S(2)}, u32[]{:S(2)}) %collective-permute-start.6) | collective-permute-done | bytes 98336 | tf_op jit(solution)/shard_map/ppermute | solution.py:35
  32.2 1.1 %collective-permute-done.12.refs_4_ = bf16[64,384]{1,0:T(8,128)(2,1)S(1)} collective-permute-done((bf16[64,384]{1,0:T(8,128)(2,1)S(1)}, bf16[64,384]{1,0:T(8,128)(2,1)S(1)}, u32[]{:S(2)}, u32[]{:S(2)}) %collective-permute-start.12) | collective-permute-done | bytes 49184 | tf_op jit(solution)/shard_map/ppermute | solution.py:35
  33.5 2.5 %collective-permute-start.17 = (bf16[128,384]{1,0:T(8,128)(2,1)S(1)}, bf16[128,384]{1,0:T(8,128)(2,1)S(1)}, u32[]{:S(2)}, u32[]{:S(2)}) collective-permute-start(bf16[128,384]{1,0:T(8,128)(2,1)S(1)} %get-tuple-element.93), channel_id=1, source_target_pairs={{0,2},{1,3},{2,0},{3,1},{4,6},{5,7},{6,4},{7,5},{8,10},{9,11},{10,... | collective-permute-start | bytes 294920 | tf_op jit(solution)/shard_map/ppermute | solution.py:35
  36.7 2.7 %collective-permute-start.20 = (bf16[64,384]{1,0:T(8,128)(2,1)S(1)}, bf16[64,384]{1,0:T(8,128)(2,1)S(1)}, u32[]{:S(2)}, u32[]{:S(2)}) collective-permute-start(bf16[64,384]{1,0:T(8,128)(2,1)S(1)} %get-tuple-element.96), channel_id=1, source_target_pairs={{0,24},{4,28},{8,16},{12,20},{16,8},{20,12},{24,0},{28,4},{1,25},{... | collective-permute-start | bytes 147464 | tf_op jit(solution)/shard_map/ppermute | solution.py:35
  40.9 2.1 %collective-permute-start.16 = (bf16[64,384]{1,0:T(8,128)(2,1)S(1)}, bf16[64,384]{1,0:T(8,128)(2,1)S(1)}, u32[]{:S(2)}, u32[]{:S(2)}) collective-permute-start(bf16[64,384]{1,0:T(8,128)(2,1)S(1)} %get-tuple-element.92), channel_id=1, source_target_pairs={{0,24},{4,28},{8,16},{12,20},{16,8},{20,12},{24,0},{28,4},{1,25},{... | collective-permute-start | bytes 147464 | tf_op jit(solution)/shard_map/ppermute | solution.py:35
  44.6 1.3 %collective-permute-done.16.refs_4_ = bf16[64,384]{1,0:T(8,128)(2,1)S(1)} collective-permute-done((bf16[64,384]{1,0:T(8,128)(2,1)S(1)}, bf16[64,384]{1,0:T(8,128)(2,1)S(1)}, u32[]{:S(2)}, u32[]{:S(2)}) %collective-permute-start.16) | collective-permute-done | bytes 49184 | tf_op jit(solution)/shard_map/ppermute | solution.py:35
  46.2 1.1 %collective-permute-start.21 = (bf16[128,384]{1,0:T(8,128)(2,1)S(1)}, bf16[128,384]{1,0:T(8,128)(2,1)S(1)}, u32[]{:S(2)}, u32[]{:S(2)}) collective-permute-start(bf16[128,384]{1,0:T(8,128)(2,1)S(1)} %get-tuple-element.100), channel_id=1, source_target_pairs={{0,2},{1,3},{2,0},{3,1},{4,6},{5,7},{6,4},{7,5},{8,10},{9,11},{10,... | collective-permute-start | bytes 294920 | tf_op jit(solution)/shard_map/ppermute | solution.py:35
  47.3 1.6 %collective-permute-start.25 = (bf16[128,384]{1,0:T(8,128)(2,1)S(1)}, bf16[128,384]{1,0:T(8,128)(2,1)S(1)}, u32[]{:S(2)}, u32[]{:S(2)}) collective-permute-start(bf16[128,384]{1,0:T(8,128)(2,1)S(1)} %get-tuple-element.106), channel_id=1, source_target_pairs={{0,1},{1,0},{2,3},{3,2},{4,5},{5,4},{6,7},{7,6},{8,9},{9,8},{10,11... | collective-permute-start | bytes 294920 | tf_op jit(solution)/shard_map/ppermute | solution.py:35
  48.9 1.7 %collective-permute-done.22.refs_2_ = bf16[128,384]{1,0:T(8,128)(2,1)S(1)} collective-permute-done((bf16[128,384]{1,0:T(8,128)(2,1)S(1)}, bf16[128,384]{1,0:T(8,128)(2,1)S(1)}, u32[]{:S(2)}, u32[]{:S(2)}) %collective-permute-start.22) | collective-permute-done | bytes 98336 | tf_op jit(solution)/shard_map/ppermute | solution.py:35
  50.8 2.0 %collective-permute-done.21.refs_2_ = bf16[128,384]{1,0:T(8,128)(2,1)S(1)} collective-permute-done((bf16[128,384]{1,0:T(8,128)(2,1)S(1)}, bf16[128,384]{1,0:T(8,128)(2,1)S(1)}, u32[]{:S(2)}, u32[]{:S(2)}) %collective-permute-start.21) | collective-permute-done | bytes 98336 | tf_op jit(solution)/shard_map/ppermute | solution.py:35
  53.7 1.3 %last0.1.refs_4_ = bf16[768,1152]{1,0:T(8,128)(2,1)} custom-call(bf16[256,256]{1,0:T(8,128)(2,1)S(1)} %get-tuple-element.56.refs_0_, bf16[768,256]{1,0:T(8,128)(2,1)S(1)} %copy-done, bf16[128,384]{1,0:T(8,128)(2,1)S(1)} %get-tuple-element.98.refs_5_.refs_2_, bf16[128,384]{1,0:T(8,128)(2,1)S(1)} %collective-permute-done.25.refs_3_, ...), custom_call_target="tpu_custom_call" | custom-call | flops 150994944 | bytes 589824 | tf_op jit(solution)/shard_map/last0/pallas_call | solution.py:59
  55.4 1.2 %last384.1.refs_4_ = bf16[768,1152]{1,0:T(8,128)(2,1)} custom-call(bf16[256,256]{1,0:T(8,128)(2,1)S(1)} %get-tuple-element.56.refs_0_, bf16[768,256]{1,0:T(8,128)(2,1)S(1)} %copy-done, bf16[128,384]{1,0:T(8,128)(2,1)S(1)} %get-tuple-element.102.refs_3_.refs_4_.refs_2_, ...), custom_call_target="tpu_custom_call", output_to_operand_aliasing={{}: (4, {})} | custom-call | flops 150994944 | bytes 589824 | tf_op jit(solution)/shard_map/last384/pallas_call | solution.py:59
  56.7 1.0 %collective-permute-done.23.refs_3_ = bf16[128,384]{1,0:T(8,128)(2,1)S(1)} collective-permute-done((bf16[128,384]{1,0:T(8,128)(2,1)S(1)}, bf16[128,384]{1,0:T(8,128)(2,1)S(1)}, u32[]{:S(2)}, u32[]{:S(2)}) %collective-permute-start.23) | collective-permute-done | bytes 98336 | tf_op jit(solution)/shard_map/ppermute | solution.py:35
  57.7 1.2 %last768.1 = bf16[768,1152]{1,0:T(8,128)(2,1)} custom-call(bf16[256,256]{1,0:T(8,128)(2,1)S(1)} %get-tuple-element.56.refs_0_, bf16[768,256]{1,0:T(8,128)(2,1)S(1)} %copy-done, bf16[128,384]{1,0:T(8,128)(2,1)S(1)} %get-tuple-element.103.refs_5_.refs_2_, bf16[128,384]{1,0:T(8,128)(2,1)S(1)} %collective-permute-done.23.refs_3_, ...), custom_call_target="tpu_custom_call", output_to_operand_aliasing={{}: (4, {})} | custom-call | flops 150994944 | bytes 589824 | tf_op jit(solution)/shard_map/last768/pallas_call | solution.py:59
  (59 shorter events, 8.8 us)
Async XLA Ops:
  2.5 12.2 %collective-permute-start.5 = (bf16[128,384]{1,0:T(8,128)(2,1)S(1)}, bf16[128,384]{1,0:T(8,128)(2,1)S(1)}, u32[]{:S(2)}, u32[]{:S(2)}) collective-permute-start(bf16[128,384]{1,0:T(8,128)(2,1)S(1)} %get-tuple-element.72), channel_id=1, source_target_pairs={{0,1},{1,0},{2,3},{3,2},{4,5},{5,4},{6,7},{7,6},{8,9},{9,8},{10,11... | collective-permute-start | bytes 294920 | tf_op jit(solution)/shard_map/ppermute | solution.py:35
  5.6 5.9 %collective-permute-start.3 = (bf16[128,256]{1,0:T(8,128)(2,1)S(1)}, bf16[128,256]{1,0:T(8,128)(2,1)S(1)}, u32[]{:S(2)}, u32[]{:S(2)}) collective-permute-start(bf16[128,256]{1,0:T(8,128)(2,1)S(1)} %get-tuple-element.68), channel_id=1, source_target_pairs={{0,1},{1,0},{2,3},{3,2},{4,5},{5,4},{6,7},{7,6},{8,9},{9,8},{10,11... | collective-permute-start | bytes 196616 | tf_op jit(solution)/shard_map/ppermute | solution.py:35
  5.7 5.6 %collective-permute-start.1 = (bf16[128,128]{1,0:T(8,128)(2,1)S(1)}, bf16[128,128]{1,0:T(8,128)(2,1)S(1)}, u32[]{:S(2)}, u32[]{:S(2)}) collective-permute-start(bf16[128,128]{1,0:T(8,128)(2,1)S(1)} %get-tuple-element.64), channel_id=1, source_target_pairs={{0,1},{1,0},{2,3},{3,2},{4,5},{5,4},{6,7},{7,6},{8,9},{9,8},{10,11... | collective-permute-start | bytes 98312 | tf_op jit(solution)/shard_map/ppermute | solution.py:35
  7.6 15.9 %collective-permute-start = (bf16[128,384]{1,0:T(8,128)(2,1)S(1)}, bf16[128,384]{1,0:T(8,128)(2,1)S(1)}, u32[]{:S(2)}, u32[]{:S(2)}) collective-permute-start(bf16[128,384]{1,0:T(8,128)(2,1)S(1)} %get-tuple-element.62), channel_id=1, source_target_pairs={{0,1},{1,0},{2,3},{3,2},{4,5},{5,4},{6,7},{7,6},{8,9},{9,8},{10,11... | collective-permute-start | bytes 294920 | tf_op jit(solution)/shard_map/ppermute | solution.py:35
  11.7 11.6 %collective-permute-start.4 = (bf16[128,256]{1,0:T(8,128)(2,1)S(1)}, bf16[128,256]{1,0:T(8,128)(2,1)S(1)}, u32[]{:S(2)}, u32[]{:S(2)}) collective-permute-start(bf16[128,256]{1,0:T(8,128)(2,1)S(1)} %get-tuple-element.70), channel_id=1, source_target_pairs={{0,2},{1,3},{2,0},{3,1},{4,6},{5,7},{6,4},{7,5},{8,10},{9,11},{10,... | collective-permute-start | bytes 196616 | tf_op jit(solution)/shard_map/ppermute | solution.py:35
  14.9 9.0 %collective-permute-start.8 = (bf16[128,384]{1,0:T(8,128)(2,1)S(1)}, bf16[128,384]{1,0:T(8,128)(2,1)S(1)}, u32[]{:S(2)}, u32[]{:S(2)}) collective-permute-start(bf16[128,384]{1,0:T(8,128)(2,1)S(1)} %get-tuple-element.78), channel_id=1, source_target_pairs={{0,2},{1,3},{2,0},{3,1},{4,6},{5,7},{6,4},{7,5},{8,10},{9,11},{10,... | collective-permute-start | bytes 294920 | tf_op jit(solution)/shard_map/ppermute | solution.py:35
  15.0 8.3 %collective-permute-start.2 = (bf16[128,128]{1,0:T(8,128)(2,1)S(1)}, bf16[128,128]{1,0:T(8,128)(2,1)S(1)}, u32[]{:S(2)}, u32[]{:S(2)}) collective-permute-start(bf16[128,128]{1,0:T(8,128)(2,1)S(1)} %get-tuple-element.66), channel_id=1, source_target_pairs={{0,2},{1,3},{2,0},{3,1},{4,6},{5,7},{6,4},{7,5},{8,10},{9,11},{10,... | collective-permute-start | bytes 98312 | tf_op jit(solution)/shard_map/ppermute | solution.py:35
  23.8 8.0 %collective-permute-start.6 = (bf16[128,384]{1,0:T(8,128)(2,1)S(1)}, bf16[128,384]{1,0:T(8,128)(2,1)S(1)}, u32[]{:S(2)}, u32[]{:S(2)}) collective-permute-start(bf16[128,384]{1,0:T(8,128)(2,1)S(1)} %get-tuple-element.76), channel_id=1, source_target_pairs={{0,2},{1,3},{2,0},{3,1},{4,6},{5,7},{6,4},{7,5},{8,10},{9,11},{10,... | collective-permute-start | bytes 294920 | tf_op jit(solution)/shard_map/ppermute | solution.py:35
  24.1 8.0 %collective-permute-start.13 = (bf16[128,384]{1,0:T(8,128)(2,1)S(1)}, bf16[128,384]{1,0:T(8,128)(2,1)S(1)}, u32[]{:S(2)}, u32[]{:S(2)}) collective-permute-start(bf16[128,384]{1,0:T(8,128)(2,1)S(1)} %get-tuple-element.86), channel_id=1, source_target_pairs={{0,4},{4,0},{8,12},{12,8},{16,20},{20,16},{24,28},{28,24},{1,5},{5... | collective-permute-start | bytes 294920 | tf_op jit(solution)/shard_map/ppermute | solution.py:35
  24.9 7.3 %collective-permute-start.10 = (bf16[64,384]{1,0:T(8,128)(2,1)S(1)}, bf16[64,384]{1,0:T(8,128)(2,1)S(1)}, u32[]{:S(2)}, u32[]{:S(2)}) collective-permute-start(bf16[64,384]{1,0:T(8,128)(2,1)S(1)} %get-tuple-element.83), channel_id=1, source_target_pairs={{0,8},{4,12},{8,0},{12,4},{16,24},{20,28},{24,16},{28,20},{1,9},{5... | collective-permute-start | bytes 147464 | tf_op jit(solution)/shard_map/ppermute | solution.py:35
  26.7 5.4 %collective-permute-start.11 = (bf16[64,384]{1,0:T(8,128)(2,1)S(1)}, bf16[64,384]{1,0:T(8,128)(2,1)S(1)}, u32[]{:S(2)}, u32[]{:S(2)}) collective-permute-start(bf16[64,384]{1,0:T(8,128)(2,1)S(1)} %get-tuple-element.84), channel_id=1, source_target_pairs={{0,16},{4,20},{8,24},{12,28},{16,0},{20,4},{24,8},{28,12},{1,17},{... | collective-permute-start | bytes 147464 | tf_op jit(solution)/shard_map/ppermute | solution.py:35
  28.3 5.0 %collective-permute-start.12 = (bf16[64,384]{1,0:T(8,128)(2,1)S(1)}, bf16[64,384]{1,0:T(8,128)(2,1)S(1)}, u32[]{:S(2)}, u32[]{:S(2)}) collective-permute-start(bf16[64,384]{1,0:T(8,128)(2,1)S(1)} %get-tuple-element.85), channel_id=1, source_target_pairs={{0,24},{4,28},{8,16},{12,20},{16,8},{20,12},{24,0},{28,4},{1,25},{... | collective-permute-start | bytes 147464 | tf_op jit(solution)/shard_map/ppermute | solution.py:35
  32.0 7.5 %collective-permute-start.9 = (bf16[128,384]{1,0:T(8,128)(2,1)S(1)}, bf16[128,384]{1,0:T(8,128)(2,1)S(1)}, u32[]{:S(2)}, u32[]{:S(2)}) collective-permute-start(bf16[128,384]{1,0:T(8,128)(2,1)S(1)} %get-tuple-element.82), channel_id=1, source_target_pairs={{0,4},{4,0},{8,12},{12,8},{16,20},{20,16},{24,28},{28,24},{1,5},{5... | collective-permute-start | bytes 294920 | tf_op jit(solution)/shard_map/ppermute | solution.py:35
  33.5 10.4 %collective-permute-start.17 = (bf16[128,384]{1,0:T(8,128)(2,1)S(1)}, bf16[128,384]{1,0:T(8,128)(2,1)S(1)}, u32[]{:S(2)}, u32[]{:S(2)}) collective-permute-start(bf16[128,384]{1,0:T(8,128)(2,1)S(1)} %get-tuple-element.93), channel_id=1, source_target_pairs={{0,2},{1,3},{2,0},{3,1},{4,6},{5,7},{6,4},{7,5},{8,10},{9,11},{10,... | collective-permute-start | bytes 294920 | tf_op jit(solution)/shard_map/ppermute | solution.py:35
  36.0 4.5 %collective-permute-start.18 = (bf16[64,384]{1,0:T(8,128)(2,1)S(1)}, bf16[64,384]{1,0:T(8,128)(2,1)S(1)}, u32[]{:S(2)}, u32[]{:S(2)}) collective-permute-start(bf16[64,384]{1,0:T(8,128)(2,1)S(1)} %get-tuple-element.94), channel_id=1, source_target_pairs={{0,8},{4,12},{8,0},{12,4},{16,24},{20,28},{24,16},{28,20},{1,9},{5... | collective-permute-start | bytes 147464 | tf_op jit(solution)/shard_map/ppermute | solution.py:35
  36.5 4.4 %collective-permute-start.19 = (bf16[64,384]{1,0:T(8,128)(2,1)S(1)}, bf16[64,384]{1,0:T(8,128)(2,1)S(1)}, u32[]{:S(2)}, u32[]{:S(2)}) collective-permute-start(bf16[64,384]{1,0:T(8,128)(2,1)S(1)} %get-tuple-element.95), channel_id=1, source_target_pairs={{0,16},{4,20},{8,24},{12,28},{16,0},{20,4},{24,8},{28,12},{1,17},{... | collective-permute-start | bytes 147464 | tf_op jit(solution)/shard_map/ppermute | solution.py:35
  36.7 6.3 %collective-permute-start.20 = (bf16[64,384]{1,0:T(8,128)(2,1)S(1)}, bf16[64,384]{1,0:T(8,128)(2,1)S(1)}, u32[]{:S(2)}, u32[]{:S(2)}) collective-permute-start(bf16[64,384]{1,0:T(8,128)(2,1)S(1)} %get-tuple-element.96), channel_id=1, source_target_pairs={{0,24},{4,28},{8,16},{12,20},{16,8},{20,12},{24,0},{28,4},{1,25},{... | collective-permute-start | bytes 147464 | tf_op jit(solution)/shard_map/ppermute | solution.py:35
  39.5 4.6 %collective-permute-start.14 = (bf16[64,384]{1,0:T(8,128)(2,1)S(1)}, bf16[64,384]{1,0:T(8,128)(2,1)S(1)}, u32[]{:S(2)}, u32[]{:S(2)}) collective-permute-start(bf16[64,384]{1,0:T(8,128)(2,1)S(1)} %get-tuple-element.90), channel_id=1, source_target_pairs={{0,8},{4,12},{8,0},{12,4},{16,24},{20,28},{24,16},{28,20},{1,9},{5... | collective-permute-start | bytes 147464 | tf_op jit(solution)/shard_map/ppermute | solution.py:35
  40.9 5.0 %collective-permute-start.16 = (bf16[64,384]{1,0:T(8,128)(2,1)S(1)}, bf16[64,384]{1,0:T(8,128)(2,1)S(1)}, u32[]{:S(2)}, u32[]{:S(2)}) collective-permute-start(bf16[64,384]{1,0:T(8,128)(2,1)S(1)} %get-tuple-element.92), channel_id=1, source_target_pairs={{0,24},{4,28},{8,16},{12,20},{16,8},{20,12},{24,0},{28,4},{1,25},{... | collective-permute-start | bytes 147464 | tf_op jit(solution)/shard_map/ppermute | solution.py:35
  43.3 7.2 %collective-permute-start.22 = (bf16[128,384]{1,0:T(8,128)(2,1)S(1)}, bf16[128,384]{1,0:T(8,128)(2,1)S(1)}, u32[]{:S(2)}, u32[]{:S(2)}) collective-permute-start(bf16[128,384]{1,0:T(8,128)(2,1)S(1)} %get-tuple-element.101), channel_id=1, source_target_pairs={{0,2},{1,3},{2,0},{3,1},{4,6},{5,7},{6,4},{7,5},{8,10},{9,11},{10,... | collective-permute-start | bytes 294920 | tf_op jit(solution)/shard_map/ppermute | solution.py:35
  46.2 6.6 %collective-permute-start.21 = (bf16[128,384]{1,0:T(8,128)(2,1)S(1)}, bf16[128,384]{1,0:T(8,128)(2,1)S(1)}, u32[]{:S(2)}, u32[]{:S(2)}) collective-permute-start(bf16[128,384]{1,0:T(8,128)(2,1)S(1)} %get-tuple-element.100), channel_id=1, source_target_pairs={{0,2},{1,3},{2,0},{3,1},{4,6},{5,7},{6,4},{7,5},{8,10},{9,11},{10,... | collective-permute-start | bytes 294920 | tf_op jit(solution)/shard_map/ppermute | solution.py:35
  47.3 6.5 %collective-permute-start.25 = (bf16[128,384]{1,0:T(8,128)(2,1)S(1)}, bf16[128,384]{1,0:T(8,128)(2,1)S(1)}, u32[]{:S(2)}, u32[]{:S(2)}) collective-permute-start(bf16[128,384]{1,0:T(8,128)(2,1)S(1)} %get-tuple-element.106), channel_id=1, source_target_pairs={{0,1},{1,0},{2,3},{3,2},{4,5},{5,4},{6,7},{7,6},{8,9},{9,8},{10,11... | collective-permute-start | bytes 294920 | tf_op jit(solution)/shard_map/ppermute | solution.py:35
  50.7 4.7 %collective-permute-start.24 = (bf16[128,384]{1,0:T(8,128)(2,1)S(1)}, bf16[128,384]{1,0:T(8,128)(2,1)S(1)}, u32[]{:S(2)}, u32[]{:S(2)}) collective-permute-start(bf16[128,384]{1,0:T(8,128)(2,1)S(1)} %get-tuple-element.105), channel_id=1, source_target_pairs={{0,1},{1,0},{2,3},{3,2},{4,5},{5,4},{6,7},{7,6},{8,9},{9,8},{10,11... | collective-permute-start | bytes 294920 | tf_op jit(solution)/shard_map/ppermute | solution.py:35
  53.0 4.7 %collective-permute-start.23 = (bf16[128,384]{1,0:T(8,128)(2,1)S(1)}, bf16[128,384]{1,0:T(8,128)(2,1)S(1)}, u32[]{:S(2)}, u32[]{:S(2)}) collective-permute-start(bf16[128,384]{1,0:T(8,128)(2,1)S(1)} %get-tuple-element.104), channel_id=1, source_target_pairs={{0,1},{1,0},{2,3},{3,2},{4,5},{5,4},{6,7},{7,6},{8,9},{9,8},{10,11... | collective-permute-start | bytes 294920 | tf_op jit(solution)/shard_map/ppermute | solution.py:35
  (7 other events, 65.2 us)

commit v10 on v8

--- a/solution.py
+++ b/solution.py
@@ -66,27 +66,31 @@
     )(*operands, *extra)
 
 
-def prepare(name, node_order, slots_out, slots_in, right, middle, left, after):
+def prepare(name, node_order, right, middle, left, held):
     width = middle.shape[-1]
     groups = node_order.shape[0]
     block = width // groups
 
-    def kernel(node_order, right, middle, left, right0, right1, middle0, left0, left1):
+    def kernel(node_order, right, middle, left, *refs):
+        right0, right1, middle0, left0, left1 = refs[len(held) : len(held) + 5]
+        for block_in, block_out in zip(refs[: len(held)], refs[len(held) + 5 :]):
+            block_out[...] = block_in[...]
         place, group = lax.axis_index("sub"), lax.axis_index("mid")
         bit0, bit1 = place & 1, place >> 1 & 1
         right0[...] = swapped(swapped(right[0, 0], 1, bit0), 0, bit1)
         place = lax.broadcasted_iota(jnp.int32, (width, 1), 0)
         source = place % block
-        for i, slot in enumerate(slots_out):
-            piece = node_order[slot ^ group] * block
+        for i in range(groups):
+            chip, other = i % (groups // 2), i // (groups // 2)
+            piece = node_order[2 * chip + (group & 1 ^ other)] * block
             source += jnp.where(place // block == i, piece, 0)
         across = lax.broadcasted_iota(jnp.int32, (width, width), 1)
         pick = jnp.where(across == source, 1.0, 0.0).astype(BF16)
         right1[...] = matmul(pick, swapped(right[0, 1], 1, bit1)).astype(BF16)
         place = lax.broadcasted_iota(jnp.int32, (1, width), 1)
         source = place % block
-        for i, slot in enumerate(slots_in):
-            source += jnp.where(place // block == i, (slot ^ group) * block, 0)
+        for i in range(groups):
+            source += jnp.where(place // block == i, (i ^ group & 1) * block, 0)
         down = lax.broadcasted_iota(jnp.int32, (width, width), 0)
         pick = jnp.where(down == source, 1.0, 0.0).astype(BF16)
         middle0[...] = swapped(matmul(middle[0], pick).astype(BF16), 0, bit1)
@@ -96,11 +100,12 @@
     return call(
         kernel,
         name,
-        [jax.ShapeDtypeStruct((width, width), BF16)] * 5,
-        [SCALARS] + [WHOLE] * 3,
-        [node_order, right, middle, left],
-        after,
-        out_specs=[WHOLE] * 5,
+        [jax.ShapeDtypeStruct((width, width), BF16)] * 5
+        + [jax.ShapeDtypeStruct(block.shape, BF16) for block in held],
+        [SCALARS] + [WHOLE] * (3 + len(held)),
+        [node_order, right, middle, left] + held,
+        None,
+        out_specs=[WHOLE] * (5 + len(held)),
         cost_estimate=cost(4 * width**3, 20 * width**2),
     )
 
@@ -190,47 +195,38 @@
     return [list(outs[i * count : (i + 1) * count]) for i in range(len(widths))]
 
 
-def digits(groups):
-    bits = groups.bit_length() - 1
-    found = [(0, 2)]
-    while found[-1][0] + (found[-1][1].bit_length() - 1) < bits:
-        shift = found[-1][0] + found[-1][1].bit_length() - 1
-        found.append((shift, 4 if shift + 2 <= bits else 2))
-    return found
-
-
-def by_digit(slots, digit):
-    shift, radix = digit
-    return [[r for r in slots if r >> shift & radix - 1 == value] for value in range(radix)]
-
-
-def regroup(name, blocks, layout, digit, block, after):
-    columns = blocks[0].shape[1]
-    place = {r: (i, j) for i, held in enumerate(layout) for j, r in enumerate(held)}
-    wanted = by_digit(sum(layout, []), digit)
-
-    def sort(values):
-        parts = [[values[place[r][0]][place[r][1] * block :][:block] for r in held] for held in wanted]
-        return [jnp.concatenate(part, axis=0) for part in parts]
+def interleave(name, keep, got, block, after):
+    half, columns = keep.shape
+
+    def turns(one, other):
+        parts = [x[i : i + block] for i in range(0, half, block) for x in (one, other)]
+        return jnp.concatenate(parts, axis=0)
 
     if block % ROWS:
-        return sort(blocks), wanted
-
-    def kernel(*refs):
-        for ref, value in zip(refs[len(blocks) :], sort([ref[...] for ref in refs[: len(blocks)]])):
-            ref[...] = value
-
-    outs = call(
-        kernel,
-        name,
-        [jax.ShapeDtypeStruct((len(held) * block, columns), BF16) for held in wanted],
-        [WHOLE] * len(blocks),
-        blocks,
+        return turns(keep, got)
+
+    def kernel(keep, got, out):
+        out[...] = turns(keep[...], got[...])
+
+    return call(
+        kernel,
+        name,
+        jax.ShapeDtypeStruct((2 * half, columns), BF16),
+        [WHOLE] * 2,
+        [keep, got],
         after,
-        out_specs=[WHOLE] * len(wanted),
-        cost_estimate=cost(0, 4 * block * len(place) * columns),
-    )
-    return list(outs), wanted
+        out_specs=WHOLE,
+        cost_estimate=cost(0, 8 * half * columns),
+    )
+
+
+def among_chips(block):
+    groups = lax.axis_size("mid")
+    chips = groups // 2
+    members = [[2 * chip + core for chip in range(chips)] for core in range(2)]
+    pieces = block.reshape(chips, -1, block.shape[1])
+    moved = lax.all_to_all(pieces, "mid", 0, 0, axis_index_groups=members, tiled=True)
+    return moved.reshape(block.shape)
 
 
 def last(name, weight, basis, keep, got, before, low, columns, after):
@@ -278,13 +274,18 @@
     merged = {i: group for group in MERGED for i in group}
     if len(chunks) < len(ENTRY_SHARES):
         merged = {i: (i,) for i in range(len(chunks))}
-    steps = digits(groups)
-    layouts = [by_digit(range(groups), steps[0])]
-    for step in steps[1:]:
-        layouts.append(by_digit(sum(layouts[-1], []), step))
 
     opened = opening("opening", col_basis, signal, chunks)
-    couplings, out, after = None, None, None
+    right0, right1, middle, left0, left1, *sends = prepare(
+        "prepare",
+        node_order,
+        right_coupling,
+        middle_coupling,
+        left_coupling,
+        [send for _, send in opened[1:]],
+    )
+    opened = opened[:1] + [(keep, send) for (keep, _), send in zip(opened[1:], sends)]
+    out, after = None, right0
     waiting, pops, entered = [], 0, 0
     parked = {}
     while waiting or entered < len(chunks):
@@ -297,19 +298,6 @@
         pops += 1
         wide = blocks[0].shape[1]
         name = "".join(str(i) for i in ids)
-        if couplings is None:
-            couplings = prepare(
-                "prepare",
-                node_order,
-                sum(layouts[0], []),
-                sum(layouts[-1], []),
-                right_coupling,
-                middle_coupling,
-                left_coupling,
-                after,
-            )
-            right0, right1, middle, left0, left1 = couplings
-            after = right0
         if stage == 1:
             results = level(f"right0_{name}", right0, [blocks], [wide], 2, after)
             axis, shift = "sub", 1
@@ -321,18 +309,18 @@
             wide = sum(chunks[i] for i in ids)
             low = starts[ids[0]]
             blocks = [parked[i] for i in ids]
-            results = level(f"right1_{name}", right1, blocks, [wide], steps[0][1], after)
-            axis, shift = "mid", steps[0][0]
-        elif stage < 2 + len(steps):
-            step = steps[stage - 2]
-            held_as = layouts[stage - 3]
-            results = [regroup(f"regroup{stage}_{name}", blocks, held_as, step, block, after)[0]]
-            axis, shift = "mid", step[0]
-        elif stage == 2 + len(steps):
+            results = level(f"right1_{name}", right1, blocks, [wide], 2, after)
+            axis, shift = "mid", 0
+        elif stage == 3:
+            mixed = interleave(f"interleave_{name}", *blocks, block, after)
+            waiting.append((stage + 1, ids, low, [among_chips(mixed)]))
+            after = mixed
+            continue
+        elif stage == 4:
             widths = shares(wide, SPLIT.get(ids, (1,)))
             results = level(f"middle_{name}", middle, [blocks], widths, 2, after)
             axis, shift = "sub", 1
-        elif stage == 3 + len(steps):
+        elif stage == 5:
             results = level(f"left0_{name}", left0, [blocks], [wide], 2, after)
             axis, shift = "sub", 0
         else:

time: 53.5 us -> 68.3 us (1.28)
  waiting for transfers between devices: 13.5 us -> 30.1 us
  starting transfers between devices: 29.7 us -> 25.8 us
  Pallas kernels: 9.8 us -> 11.8 us
    ppermute x24 -> x15, starting transfers between devices: 29.7 us -> 14.8 us  [swap(): return lax.ppermute(block, axis, [(i, i ^ distance) for i in range(count)])]
    ppermute x24 -> x15, waiting for transfers between devices: 13.5 us -> 26.9 us  [swap(): return lax.ppermute(block, axis, [(i, i ^ distance) for i in range(count)])]
    all_to_all x0 -> x3, starting transfers between devices: none -> 11 us  [among_chips(): lax.all_to_all(pieces, 'mid', 0, 0, axis_index_groups=members, tiled=True)]
    all_to_all x0 -> x3, waiting for transfers between devices: none -> 3.2 us  [among_chips(): lax.all_to_all(pieces, 'mid', 0, 0, axis_index_groups=members, tiled=True)]
    pallas_call x20, Pallas kernels: 9.8 us -> 11.8 us  [call(): pl.pallas_call(body, name=name, in_specs=specs + [PLACE] * len(extra), ou...]
  transfers between devices with their start and end apart: 24 -> 18, of which waited for: 12 -> 10; matrix products, arithmetic and copies ran while one was open for 0% -> 0% of each run, Pallas kernels for 11% -> 11%
where the time goes in v10:
time: 68.3 us; the launch traced here: 67.9 us
  waiting for transfers between devices  30.1 us (44%)
  starting transfers between devices  25.8 us (38%)
  Pallas kernels  11.8 us (17%)
    ppermute x15, waiting for transfers between devices, swap(): return lax.ppermute(block, axis, [(i, i ^ distance) for i in range(count)])  26.9 us
    ppermute x15, starting transfers between devices, swap(): return lax.ppermute(block, axis, [(i, i ^ distance) for i in range(count)])  14.8 us
    pallas_call x20, Pallas kernels, call(): pl.pallas_call(body, name=name, in_specs=specs + [PLACE] * len(extra), ou...  11.8 us
    all_to_all x3, starting transfers between devices, among_chips(): lax.all_to_all(pieces, 'mid', 0, 0, axis_index_groups=members, tiled=True)  11 us
    all_to_all x3, waiting for transfers between devices, among_chips(): lax.all_to_all(pieces, 'mid', 0, 0, axis_index_groups=members, tiled=True)  3.2 us
  transfers between devices with their start and end apart: 18, of which 10 were waited for; matrix products, arithmetic and copies ran while one was open for 0% of the time, Pallas kernels for 11%

profile of v10, /device:TPU:0, one launch (start us, length us, event | category | flops | bytes accessed | tf_op | source)
XLA Modules:
  0.0 67.9 jit_solution(3920260212338006003)
XLA Ops:
  0.0 2.5 %opening.1 = (bf16[128,384]{1,0:T(8,128)(2,1)S(1)}, bf16[128,384]{1,0:T(8,128)(2,1)S(1)}, bf16[128,384]{1,0:T(8,128)(2,1)S(1)}, bf16[128,384]{1,0:T(8,128)(2,1)S...) custom-call(bf16[768,256]{1,0:T(8,128)(2,1)} %refs_0_.2, bf16[768,1152]{1,0:T(8,128)(2,1)} %refs_1_.5), custom_call_target="tpu_custom_call" | custom-call | flops 452984832 | bytes 2162688 | tf_op jit(solution)/shard_map/opening/pallas_call | solution.py:59
  2.5 3.1 %collective-permute-start.1 = (bf16[128,384]{1,0:T(8,128)(2,1)S(1)}, bf16[128,384]{1,0:T(8,128)(2,1)S(1)}, u32[]{:S(2)}, u32[]{:S(2)}) collective-permute-start(bf16[128,384]{1,0:T(8,128)(2,1)S(1)} %get-tuple-element.52), channel_id=1, source_target_pairs={{0,1},{1,0},{2,3},{3,2},{4,5},{5,4},{6,7},{7,6},{8,9},{9,8},{10,11... | collective-permute-start | bytes 294920 | tf_op jit(solution)/shard_map/ppermute | solution.py:35
  5.6 0.9 %prepare.1 = (bf16[256,256]{1,0:T(8,128)(2,1)S(1)}, bf16[256,256]{1,0:T(8,128)(2,1)S(1)}, bf16[256,256]{1,0:T(8,128)(2,1)S(1)}, bf16[256,256]{1,0:T(8,128)(2,1)S...) custom-call(s32[8]{0:T(128)S(1)} %copy-done.4, ...), custom_call_target="tpu_custom_call" | custom-call | flops 67108864 | bytes 1310720 | tf_op jit(solution)/shard_map/prepare/pallas_call | solution.py:59
  6.6 2.1 %collective-permute-done.1.refs_2_ = bf16[128,384]{1,0:T(8,128)(2,1)S(1)} collective-permute-done((bf16[128,384]{1,0:T(8,128)(2,1)S(1)}, bf16[128,384]{1,0:T(8,128)(2,1)S(1)}, u32[]{:S(2)}, u32[]{:S(2)}) %collective-permute-start.1) | collective-permute-done | bytes 98336 | tf_op jit(solution)/shard_map/ppermute | solution.py:35
  9.0 2.7 %collective-permute-start.2 = (bf16[128,384]{1,0:T(8,128)(2,1)S(1)}, bf16[128,384]{1,0:T(8,128)(2,1)S(1)}, u32[]{:S(2)}, u32[]{:S(2)}) collective-permute-start(bf16[128,384]{1,0:T(8,128)(2,1)S(1)} %get-tuple-element.54), channel_id=1, source_target_pairs={{0,2},{1,3},{2,0},{3,1},{4,6},{5,7},{6,4},{7,5},{8,10},{9,11},{10,... | collective-permute-start | bytes 294920 | tf_op jit(solution)/shard_map/ppermute | solution.py:35
  11.7 2.5 %collective-permute-start = (bf16[128,384]{1,0:T(8,128)(2,1)S(1)}, bf16[128,384]{1,0:T(8,128)(2,1)S(1)}, u32[]{:S(2)}, u32[]{:S(2)}) collective-permute-start(bf16[128,384]{1,0:T(8,128)(2,1)S(1)} %get-tuple-element.50), channel_id=1, source_target_pairs={{0,1},{1,0},{2,3},{3,2},{4,5},{5,4},{6,7},{7,6},{8,9},{9,8},{10,11... | collective-permute-start | bytes 294920 | tf_op jit(solution)/shard_map/ppermute | solution.py:35
  14.4 0.7 %collective-permute-start.6 = (bf16[128,384]{1,0:T(8,128)(2,1)S(1)}, bf16[128,384]{1,0:T(8,128)(2,1)S(1)}, u32[]{:S(2)}, u32[]{:S(2)}) collective-permute-start(bf16[128,384]{1,0:T(8,128)(2,1)S(1)} %get-tuple-element.62), channel_id=1, source_target_pairs={{0,2},{1,3},{2,0},{3,1},{4,6},{5,7},{6,4},{7,5},{8,10},{9,11},{10,... | collective-permute-start | bytes 294920 | tf_op jit(solution)/shard_map/ppermute | solution.py:35
  15.4 1.3 %collective-permute-done.refs_2_ = bf16[128,384]{1,0:T(8,128)(2,1)S(1)} collective-permute-done((bf16[128,384]{1,0:T(8,128)(2,1)S(1)}, bf16[128,384]{1,0:T(8,128)(2,1)S(1)}, u32[]{:S(2)}, u32[]{:S(2)}) %collective-permute-start) | collective-permute-done | bytes 98336 | tf_op jit(solution)/shard_map/ppermute | solution.py:35
  17.0 3.6 %collective-permute-done.6.refs_2_ = bf16[128,384]{1,0:T(8,128)(2,1)S(1)} collective-permute-done((bf16[128,384]{1,0:T(8,128)(2,1)S(1)}, bf16[128,384]{1,0:T(8,128)(2,1)S(1)}, u32[]{:S(2)}, u32[]{:S(2)}) %collective-permute-start.6) | collective-permute-done | bytes 98336 | tf_op jit(solution)/shard_map/ppermute | solution.py:35
  20.9 0.7 %interleave_0.1.refs_3_ = bf16[256,384]{1,0:T(8,128)(2,1)} custom-call(bf16[128,384]{1,0:T(8,128)(2,1)S(1)} %get-tuple-element.58.refs_3_.refs_0_, bf16[128,384]{1,0:T(8,128)(2,1)S(1)} %collective-permute-done.5.refs_1_, bf16[128,384]{1,0:T(8,128)(2,1)S(1)} %get-tuple-element.63.refs_2_.refs_0_), custom_call_target="tpu_custom_call" | custom-call | bytes 393216 | tf_op jit(solution)/shard_map/interleave_0/pallas_call | solution.py:59
  21.5 3.7 %all-to-all-start = ((bf16[4,64,384]{2,1,0:T(8,128)(2,1)}), bf16[4,64,384]{2,1,0:T(8,128)(2,1)S(1)}, u32[]{:S(2)}, u32[]{:S(2)}) async-start(bf16[4,64,384]{2,1,0:T(8,128)(2,1)} %bitcast), calls=%async_computation | async-start | bytes 393216 | tf_op jit(solution)/shard_map/all_to_all | solution.py:228
  25.5 6.6 %collective-permute-done.4.refs_2_ = bf16[128,384]{1,0:T(8,128)(2,1)S(1)} collective-permute-done((bf16[128,384]{1,0:T(8,128)(2,1)S(1)}, bf16[128,384]{1,0:T(8,128)(2,1)S(1)}, u32[]{:S(2)}, u32[]{:S(2)}) %collective-permute-start.4) | collective-permute-done | bytes 98336 | tf_op jit(solution)/shard_map/ppermute | solution.py:35
  33.1 3.9 %all-to-all-start.2 = ((bf16[4,64,384]{2,1,0:T(8,128)(2,1)}), bf16[4,64,384]{2,1,0:T(8,128)(2,1)S(1)}, u32[]{:S(2)}, u32[]{:S(2)}) async-start(bf16[4,64,384]{2,1,0:T(8,128)(2,1)} %bitcast.4), calls=%async_computation.2 | async-start | bytes 393216 | tf_op jit(solution)/shard_map/all_to_all | solution.py:228
  37.2 1.1 %collective-permute-done.7.refs_1_ = bf16[128,384]{1,0:T(8,128)(2,1)S(1)} collective-permute-done((bf16[128,384]{1,0:T(8,128)(2,1)S(1)}, bf16[128,384]{1,0:T(8,128)(2,1)S(1)}, u32[]{:S(2)}, u32[]{:S(2)}) %collective-permute-start.7) | collective-permute-done | bytes 98336 | tf_op jit(solution)/shard_map/ppermute | solution.py:35
  39.0 3.2 %all-to-all-done.2 = bf16[4,64,384]{2,1,0:T(8,128)(2,1)S(1)} async-done(((bf16[4,64,384]{2,1,0:T(8,128)(2,1)}), bf16[4,64,384]{2,1,0:T(8,128)(2,1)S(1)}, u32[]{:S(2)}, u32[]{:S(2)}) %all-to-all-start.2) | async-done | bytes 196640 | tf_op jit(solution)/shard_map/all_to_all | solution.py:228
  42.2 3.4 %all-to-all-start.1 = ((bf16[4,64,384]{2,1,0:T(8,128)(2,1)}), bf16[4,64,384]{2,1,0:T(8,128)(2,1)S(1)}, u32[]{:S(2)}, u32[]{:S(2)}) async-start(bf16[4,64,384]{2,1,0:T(8,128)(2,1)} %bitcast.2), calls=%async_computation.1 | async-start | bytes 393216 | tf_op jit(solution)/shard_map/all_to_all | solution.py:228
  45.8 3.0 %collective-permute-start.11 = (bf16[128,384]{1,0:T(8,128)(2,1)S(1)}, bf16[128,384]{1,0:T(8,128)(2,1)S(1)}, u32[]{:S(2)}, u32[]{:S(2)}) collective-permute-start(bf16[128,384]{1,0:T(8,128)(2,1)S(1)} %get-tuple-element.73), channel_id=1, source_target_pairs={{0,2},{1,3},{2,0},{3,1},{4,6},{5,7},{6,4},{7,5},{8,10},{9,11},{10,... | collective-permute-start | bytes 294920 | tf_op jit(solution)/shard_map/ppermute | solution.py:35
  48.8 6.8 %collective-permute-done.9.refs_2_ = bf16[128,384]{1,0:T(8,128)(2,1)S(1)} collective-permute-done((bf16[128,384]{1,0:T(8,128)(2,1)S(1)}, bf16[128,384]{1,0:T(8,128)(2,1)S(1)}, u32[]{:S(2)}, u32[]{:S(2)}) %collective-permute-start.9) | collective-permute-done | bytes 98336 | tf_op jit(solution)/shard_map/ppermute | solution.py:35
  56.1 1.8 %collective-permute-start.14 = (bf16[128,384]{1,0:T(8,128)(2,1)S(1)}, bf16[128,384]{1,0:T(8,128)(2,1)S(1)}, u32[]{:S(2)}, u32[]{:S(2)}) collective-permute-start(bf16[128,384]{1,0:T(8,128)(2,1)S(1)} %get-tuple-element.78), channel_id=1, source_target_pairs={{0,1},{1,0},{2,3},{3,2},{4,5},{5,4},{6,7},{7,6},{8,9},{9,8},{10,11... | collective-permute-start | bytes 294920 | tf_op jit(solution)/shard_map/ppermute | solution.py:35
  58.5 3.2 %collective-permute-done.10.refs_2_ = bf16[128,384]{1,0:T(8,128)(2,1)S(1)} collective-permute-done((bf16[128,384]{1,0:T(8,128)(2,1)S(1)}, bf16[128,384]{1,0:T(8,128)(2,1)S(1)}, u32[]{:S(2)}, u32[]{:S(2)}) %collective-permute-start.10) | collective-permute-done | bytes 98336 | tf_op jit(solution)/shard_map/ppermute | solution.py:35
  62.4 1.2 %last0.1.refs_4_ = bf16[768,1152]{1,0:T(8,128)(2,1)} custom-call(bf16[256,256]{1,0:T(8,128)(2,1)S(1)} %get-tuple-element.44.refs_0_, bf16[768,256]{1,0:T(8,128)(2,1)S(1)} %copy-done, bf16[128,384]{1,0:T(8,128)(2,1)S(1)} %get-tuple-element.70.refs_2_, bf16[128,384]{1,0:T(8,128)(2,1)S(1)} %collective-permute-done.14.refs_3_, ...), custom_call_target="tpu_custom_call" | custom-call | flops 150994944 | bytes 589824 | tf_op jit(solution)/shard_map/last0/pallas_call | solution.py:59
  63.7 1.3 %last384.1.refs_4_ = bf16[768,1152]{1,0:T(8,128)(2,1)} custom-call(bf16[256,256]{1,0:T(8,128)(2,1)S(1)} %get-tuple-element.44.refs_0_, bf16[768,256]{1,0:T(8,128)(2,1)S(1)} %copy-done, bf16[128,384]{1,0:T(8,128)(2,1)S(1)} %get-tuple-element.74.refs_3_.refs_4_.refs_2_, ...), custom_call_target="tpu_custom_call", output_to_operand_aliasing={{}: (4, {})} | custom-call | flops 150994944 | bytes 589824 | tf_op jit(solution)/shard_map/last384/pallas_call | solution.py:59
  65.0 1.7 %collective-permute-done.12.refs_3_ = bf16[128,384]{1,0:T(8,128)(2,1)S(1)} collective-permute-done((bf16[128,384]{1,0:T(8,128)(2,1)S(1)}, bf16[128,384]{1,0:T(8,128)(2,1)S(1)}, u32[]{:S(2)}, u32[]{:S(2)}) %collective-permute-start.12) | collective-permute-done | bytes 98336 | tf_op jit(solution)/shard_map/ppermute | solution.py:35
  66.6 1.2 %last768.1 = bf16[768,1152]{1,0:T(8,128)(2,1)} custom-call(bf16[256,256]{1,0:T(8,128)(2,1)S(1)} %get-tuple-element.44.refs_0_, bf16[768,256]{1,0:T(8,128)(2,1)S(1)} %copy-done, bf16[128,384]{1,0:T(8,128)(2,1)S(1)} %get-tuple-element.75.refs_5_.refs_2_, bf16[128,384]{1,0:T(8,128)(2,1)S(1)} %collective-permute-done.12.refs_3_, ...), custom_call_target="tpu_custom_call", output_to_operand_aliasing={{}: (4, {})} | custom-call | flops 150994944 | bytes 589824 | tf_op jit(solution)/shard_map/last768/pallas_call | solution.py:59
  (42 shorter events, 5.4 us)
Async XLA Ops:
  0.0 5.6 %copy-start.4 = (s32[8]{0:T(128)S(1)}, s32[8]{0:T(128)}, u32[]{:S(2)}) copy-start(s32[8]{0:T(128)} %refs_0_.3) | copy-start | bytes 100
  0.0 5.6 %copy-start.2 = (bf16[1,2,256,256]{3,2,1,0:T(8,128)(2,1)S(1)}, bf16[1,2,256,256]{3,2,1,0:T(8,128)(2,1)}, u32[]{:S(2)}) copy-start(bf16[1,2,256,256]{3,2,1,0:T(8,128)(2,1)} %refs_3_.1) | copy-start | bytes 786436
  0.0 5.6 %copy-start.3 = (bf16[1,256,256]{2,1,0:T(8,128)(2,1)S(1)}, bf16[1,256,256]{2,1,0:T(8,128)(2,1)}, u32[]{:S(2)}) copy-start(bf16[1,256,256]{2,1,0:T(8,128)(2,1)} %refs_2_.1) | copy-start | bytes 393220
  0.0 5.6 %copy-start.1 = (bf16[1,2,256,256]{3,2,1,0:T(8,128)(2,1)S(1)}, bf16[1,2,256,256]{3,2,1,0:T(8,128)(2,1)}, u32[]{:S(2)}) copy-start(bf16[1,2,256,256]{3,2,1,0:T(8,128)(2,1)} %refs_1_.6) | copy-start | bytes 786436
  2.5 6.2 %collective-permute-start.1 = (bf16[128,384]{1,0:T(8,128)(2,1)S(1)}, bf16[128,384]{1,0:T(8,128)(2,1)S(1)}, u32[]{:S(2)}, u32[]{:S(2)}) collective-permute-start(bf16[128,384]{1,0:T(8,128)(2,1)S(1)} %get-tuple-element.52), channel_id=1, source_target_pairs={{0,1},{1,0},{2,3},{3,2},{4,5},{5,4},{6,7},{7,6},{8,9},{9,8},{10,11... | collective-permute-start | bytes 294920 | tf_op jit(solution)/shard_map/ppermute | solution.py:35
  6.5 7.7 %collective-permute-start.3 = (bf16[128,384]{1,0:T(8,128)(2,1)S(1)}, bf16[128,384]{1,0:T(8,128)(2,1)S(1)}, u32[]{:S(2)}, u32[]{:S(2)}) collective-permute-start(bf16[128,384]{1,0:T(8,128)(2,1)S(1)} %get-tuple-element.56), channel_id=1, source_target_pairs={{0,1},{1,0},{2,3},{3,2},{4,5},{5,4},{6,7},{7,6},{8,9},{9,8},{10,11... | collective-permute-start | bytes 294920 | tf_op jit(solution)/shard_map/ppermute | solution.py:35
  9.0 6.2 %collective-permute-start.2 = (bf16[128,384]{1,0:T(8,128)(2,1)S(1)}, bf16[128,384]{1,0:T(8,128)(2,1)S(1)}, u32[]{:S(2)}, u32[]{:S(2)}) collective-permute-start(bf16[128,384]{1,0:T(8,128)(2,1)S(1)} %get-tuple-element.54), channel_id=1, source_target_pairs={{0,2},{1,3},{2,0},{3,1},{4,6},{5,7},{6,4},{7,5},{8,10},{9,11},{10,... | collective-permute-start | bytes 294920 | tf_op jit(solution)/shard_map/ppermute | solution.py:35
  11.7 5.1 %collective-permute-start = (bf16[128,384]{1,0:T(8,128)(2,1)S(1)}, bf16[128,384]{1,0:T(8,128)(2,1)S(1)}, u32[]{:S(2)}, u32[]{:S(2)}) collective-permute-start(bf16[128,384]{1,0:T(8,128)(2,1)S(1)} %get-tuple-element.50), channel_id=1, source_target_pairs={{0,1},{1,0},{2,3},{3,2},{4,5},{5,4},{6,7},{7,6},{8,9},{9,8},{10,11... | collective-permute-start | bytes 294920 | tf_op jit(solution)/shard_map/ppermute | solution.py:35
  14.4 6.2 %collective-permute-start.6 = (bf16[128,384]{1,0:T(8,128)(2,1)S(1)}, bf16[128,384]{1,0:T(8,128)(2,1)S(1)}, u32[]{:S(2)}, u32[]{:S(2)}) collective-permute-start(bf16[128,384]{1,0:T(8,128)(2,1)S(1)} %get-tuple-element.62), channel_id=1, source_target_pairs={{0,2},{1,3},{2,0},{3,1},{4,6},{5,7},{6,4},{7,5},{8,10},{9,11},{10,... | collective-permute-start | bytes 294920 | tf_op jit(solution)/shard_map/ppermute | solution.py:35
  15.4 5.5 %collective-permute-start.5 = (bf16[128,384]{1,0:T(8,128)(2,1)S(1)}, bf16[128,384]{1,0:T(8,128)(2,1)S(1)}, u32[]{:S(2)}, u32[]{:S(2)}) collective-permute-start(bf16[128,384]{1,0:T(8,128)(2,1)S(1)} %get-tuple-element.61), channel_id=1, source_target_pairs={{0,4},{4,0},{8,12},{12,8},{16,20},{20,16},{24,28},{28,24},{1,5},{5... | collective-permute-start | bytes 294920 | tf_op jit(solution)/shard_map/ppermute | solution.py:35
  21.5 11.5 %all-to-all-start = ((bf16[4,64,384]{2,1,0:T(8,128)(2,1)}), bf16[4,64,384]{2,1,0:T(8,128)(2,1)S(1)}, u32[]{:S(2)}, u32[]{:S(2)}) async-start(bf16[4,64,384]{2,1,0:T(8,128)(2,1)} %bitcast), calls=%async_computation | async-start | bytes 393216 | tf_op jit(solution)/shard_map/all_to_all | solution.py:228
  25.3 6.9 %collective-permute-start.4 = (bf16[128,384]{1,0:T(8,128)(2,1)S(1)}, bf16[128,384]{1,0:T(8,128)(2,1)S(1)}, u32[]{:S(2)}, u32[]{:S(2)}) collective-permute-start(bf16[128,384]{1,0:T(8,128)(2,1)S(1)} %get-tuple-element.60), channel_id=1, source_target_pairs={{0,2},{1,3},{2,0},{3,1},{4,6},{5,7},{6,4},{7,5},{8,10},{9,11},{10,... | collective-permute-start | bytes 294920 | tf_op jit(solution)/shard_map/ppermute | solution.py:35
  25.5 6.9 %collective-permute-start.8 = (bf16[128,384]{1,0:T(8,128)(2,1)S(1)}, bf16[128,384]{1,0:T(8,128)(2,1)S(1)}, u32[]{:S(2)}, u32[]{:S(2)}) collective-permute-start(bf16[128,384]{1,0:T(8,128)(2,1)S(1)} %get-tuple-element.66), channel_id=1, source_target_pairs={{0,4},{4,0},{8,12},{12,8},{16,20},{20,16},{24,28},{28,24},{1,5},{5... | collective-permute-start | bytes 294920 | tf_op jit(solution)/shard_map/ppermute | solution.py:35
  33.1 9.1 %all-to-all-start.2 = ((bf16[4,64,384]{2,1,0:T(8,128)(2,1)}), bf16[4,64,384]{2,1,0:T(8,128)(2,1)S(1)}, u32[]{:S(2)}, u32[]{:S(2)}) async-start(bf16[4,64,384]{2,1,0:T(8,128)(2,1)} %bitcast.4), calls=%async_computation.2 | async-start | bytes 393216 | tf_op jit(solution)/shard_map/all_to_all | solution.py:228
  37.0 1.3 %collective-permute-start.7 = (bf16[128,384]{1,0:T(8,128)(2,1)S(1)}, bf16[128,384]{1,0:T(8,128)(2,1)S(1)}, u32[]{:S(2)}, u32[]{:S(2)}) collective-permute-start(bf16[128,384]{1,0:T(8,128)(2,1)S(1)} %get-tuple-element.65), channel_id=1, source_target_pairs={{0,4},{4,0},{8,12},{12,8},{16,20},{20,16},{24,28},{28,24},{1,5},{5... | collective-permute-start | bytes 294920 | tf_op jit(solution)/shard_map/ppermute | solution.py:35
  37.0 25.5 %copy-start = (bf16[768,256]{1,0:T(8,128)(2,1)S(1)}, bf16[768,256]{1,0:T(8,128)(2,1)}, u32[]{:S(2)}) copy-start(bf16[768,256]{1,0:T(8,128)(2,1)} %refs_1_.9) | copy-start | bytes 1179652
  42.2 13.6 %all-to-all-start.1 = ((bf16[4,64,384]{2,1,0:T(8,128)(2,1)}), bf16[4,64,384]{2,1,0:T(8,128)(2,1)S(1)}, u32[]{:S(2)}, u32[]{:S(2)}) async-start(bf16[4,64,384]{2,1,0:T(8,128)(2,1)} %bitcast.2), calls=%async_computation.1 | async-start | bytes 393216 | tf_op jit(solution)/shard_map/all_to_all | solution.py:228
  45.5 10.0 %collective-permute-start.9 = (bf16[128,384]{1,0:T(8,128)(2,1)S(1)}, bf16[128,384]{1,0:T(8,128)(2,1)S(1)}, u32[]{:S(2)}, u32[]{:S(2)}) collective-permute-start(bf16[128,384]{1,0:T(8,128)(2,1)S(1)} %get-tuple-element.68), channel_id=1, source_target_pairs={{0,2},{1,3},{2,0},{3,1},{4,6},{5,7},{6,4},{7,5},{8,10},{9,11},{10,... | collective-permute-start | bytes 294920 | tf_op jit(solution)/shard_map/ppermute | solution.py:35
  45.8 12.1 %collective-permute-start.11 = (bf16[128,384]{1,0:T(8,128)(2,1)S(1)}, bf16[128,384]{1,0:T(8,128)(2,1)S(1)}, u32[]{:S(2)}, u32[]{:S(2)}) collective-permute-start(bf16[128,384]{1,0:T(8,128)(2,1)S(1)} %get-tuple-element.73), channel_id=1, source_target_pairs={{0,2},{1,3},{2,0},{3,1},{4,6},{5,7},{6,4},{7,5},{8,10},{9,11},{10,... | collective-permute-start | bytes 294920 | tf_op jit(solution)/shard_map/ppermute | solution.py:35
  56.0 5.7 %collective-permute-start.10 = (bf16[128,384]{1,0:T(8,128)(2,1)S(1)}, bf16[128,384]{1,0:T(8,128)(2,1)S(1)}, u32[]{:S(2)}, u32[]{:S(2)}) collective-permute-start(bf16[128,384]{1,0:T(8,128)(2,1)S(1)} %get-tuple-element.72), channel_id=1, source_target_pairs={{0,2},{1,3},{2,0},{3,1},{4,6},{5,7},{6,4},{7,5},{8,10},{9,11},{10,... | collective-permute-start | bytes 294920 | tf_op jit(solution)/shard_map/ppermute | solution.py:35
  56.1 6.3 %collective-permute-start.14 = (bf16[128,384]{1,0:T(8,128)(2,1)S(1)}, bf16[128,384]{1,0:T(8,128)(2,1)S(1)}, u32[]{:S(2)}, u32[]{:S(2)}) collective-permute-start(bf16[128,384]{1,0:T(8,128)(2,1)S(1)} %get-tuple-element.78), channel_id=1, source_target_pairs={{0,1},{1,0},{2,3},{3,2},{4,5},{5,4},{6,7},{7,6},{8,9},{9,8},{10,11... | collective-permute-start | bytes 294920 | tf_op jit(solution)/shard_map/ppermute | solution.py:35
  58.2 5.5 %collective-permute-start.13 = (bf16[128,384]{1,0:T(8,128)(2,1)S(1)}, bf16[128,384]{1,0:T(8,128)(2,1)S(1)}, u32[]{:S(2)}, u32[]{:S(2)}) collective-permute-start(bf16[128,384]{1,0:T(8,128)(2,1)S(1)} %get-tuple-element.77), channel_id=1, source_target_pairs={{0,1},{1,0},{2,3},{3,2},{4,5},{5,4},{6,7},{7,6},{8,9},{9,8},{10,11... | collective-permute-start | bytes 294920 | tf_op jit(solution)/shard_map/ppermute | solution.py:35
  61.9 4.7 %collective-permute-start.12 = (bf16[128,384]{1,0:T(8,128)(2,1)S(1)}, bf16[128,384]{1,0:T(8,128)(2,1)S(1)}, u32[]{:S(2)}, u32[]{:S(2)}) collective-permute-start(bf16[128,384]{1,0:T(8,128)(2,1)S(1)} %get-tuple-element.76), channel_id=1, source_target_pairs={{0,1},{1,0},{2,3},{3,2},{4,5},{5,4},{6,7},{7,6},{8,9},{9,8},{10,11... | collective-permute-start | bytes 294920 | tf_op jit(solution)/shard_map/ppermute | solution.py:35

commit v11 on v8

--- a/solution.py
+++ b/solution.py
@@ -17,6 +17,7 @@
 BF16 = jnp.bfloat16
 WHOLE = pl.BlockSpec(memory_space=pltpu.VMEM)
 SCALARS = pl.BlockSpec(memory_space=pltpu.SMEM)
+SPAN = pl.CostEstimate(flops=2 * 10**9, bytes_accessed=0, transcendentals=0)
 PLACE = pl.BlockSpec(memory_space=pl.ANY)
 HBM = pl.BlockSpec(memory_space=pltpu.HBM)
 
@@ -44,10 +45,6 @@
 
 def matmul(left, right):
     return lax.dot_general(left, right, (((1,), (0,)), ((), ())), preferred_element_type=F32)
-
-
-def cost(flops, moved):
-    return pl.CostEstimate(flops=flops, bytes_accessed=moved, transcendentals=0)
 
 
 def call(kernel, name, outs, specs, operands, after, limit=SCOPED, **more):
@@ -66,12 +63,15 @@
     )(*operands, *extra)
 
 
-def prepare(name, node_order, slots_out, slots_in, right, middle, left, after):
+def prepare(name, node_order, slots_out, slots_in, right, middle, left, held):
     width = middle.shape[-1]
     groups = node_order.shape[0]
     block = width // groups
 
-    def kernel(node_order, right, middle, left, right0, right1, middle0, left0, left1):
+    def kernel(node_order, right, middle, left, *refs):
+        right0, right1, middle0, left0, left1 = refs[len(held) : len(held) + 5]
+        for block_in, block_out in zip(refs[: len(held)], refs[len(held) + 5 :]):
+            block_out[...] = block_in[...]
         place, group = lax.axis_index("sub"), lax.axis_index("mid")
         bit0, bit1 = place & 1, place >> 1 & 1
         right0[...] = swapped(swapped(right[0, 0], 1, bit0), 0, bit1)
@@ -96,12 +96,13 @@
     return call(
         kernel,
         name,
-        [jax.ShapeDtypeStruct((width, width), BF16)] * 5,
-        [SCALARS] + [WHOLE] * 3,
-        [node_order, right, middle, left],
-        after,
-        out_specs=[WHOLE] * 5,
-        cost_estimate=cost(4 * width**3, 20 * width**2),
+        [jax.ShapeDtypeStruct((width, width), BF16)] * 5
+        + [jax.ShapeDtypeStruct(block.shape, BF16) for block in held],
+        [SCALARS] + [WHOLE] * (3 + len(held)),
+        [node_order, right, middle, left] + held,
+        None,
+        out_specs=[WHOLE] * (5 + len(held)),
+        cost_estimate=SPAN,
     )
 
 
@@ -112,12 +113,12 @@
 def opening(name, basis, signal, widths):
     rows, width = basis.shape
     half = width // 2
-    pieces = row_pieces(rows, 6)
+    pieces = row_pieces(rows, 3)
     depth = rows // pieces
     lows = [sum(widths[:i]) for i in range(len(widths))]
 
     def kernel(basis, signal, *refs):
-        outs, (basis_here, signal_here, arrived, basis_arrived) = refs[:-4], refs[-4:]
+        outs, (basis_here, signal_here, sums, arrived, basis_arrived) = refs[:-5], refs[-5:]
         fetch_basis = pltpu.make_async_copy(basis, basis_here, basis_arrived)
         fetch_basis.start()
         copies = []
@@ -129,10 +130,17 @@
             copies[-1].start()
         fetch_basis.wait()
         flipped = swapped(basis_here[...].T, 0, lax.axis_index("sub") & 1)
-        for copy in copies:
+        for i, copy in enumerate(copies):
             copy.wait()
+            rows_here = slice(i * depth, (i + 1) * depth)
+            if i < pieces - 1:
+                part = matmul(flipped[:, rows_here], signal_here[rows_here, :])
+                sums[...] = part if i == 0 else sums[...] + part
         for i, (low, wide) in enumerate(zip(lows, widths)):
-            total = matmul(flipped, signal_here[:, low : low + wide])
+            here = slice(low, low + wide)
+            total = matmul(flipped[:, rows_here], signal_here[rows_here, here])
+            if pieces > 1:
+                total += sums[:, here]
             outs[2 * i][...] = total[:half].astype(BF16)
             outs[2 * i + 1][...] = total[half:].astype(BF16)
 
@@ -148,10 +156,11 @@
         scratch_shapes=[
             pltpu.VMEM((rows, width), BF16),
             pltpu.VMEM(signal.shape, BF16),
+            pltpu.VMEM((width, signal.shape[1]), F32),
             pltpu.SemaphoreType.DMA((pieces,)),
             pltpu.SemaphoreType.DMA,
         ],
-        cost_estimate=cost(2 * rows * width * sum(widths), 2 * rows * (sum(widths) + width)),
+        cost_estimate=SPAN,
     )
     return list(zip(outs[0::2], outs[1::2]))
 
@@ -185,7 +194,7 @@
         [weight] + flat,
         after,
         out_specs=[WHOLE] * (count * len(widths)),
-        cost_estimate=cost(2 * width * width * columns, 4 * width * columns),
+        cost_estimate=SPAN,
     )
     return [list(outs[i * count : (i + 1) * count]) for i in range(len(widths))]
 
@@ -228,7 +237,7 @@
         blocks,
         after,
         out_specs=[WHOLE] * len(wanted),
-        cost_estimate=cost(0, 4 * block * len(place) * columns),
+        cost_estimate=SPAN,
     )
     return list(outs), wanted
 
@@ -264,7 +273,7 @@
         out_specs=HBM,
         scratch_shapes=[pltpu.VMEM((rows, wide), BF16), pltpu.SemaphoreType.DMA((pieces,))],
         input_output_aliases={4: 0} if given else {},
-        cost_estimate=cost(2 * rows * width * wide, 2 * rows * wide),
+        cost_estimate=SPAN,
     )
 
 
@@ -284,7 +293,18 @@
         layouts.append(by_digit(sum(layouts[-1], []), step))
 
     opened = opening("opening", col_basis, signal, chunks)
-    couplings, out, after = None, None, None
+    right0, right1, middle, left0, left1, *sends = prepare(
+        "prepare",
+        node_order,
+        sum(layouts[0], []),
+        sum(layouts[-1], []),
+        right_coupling,
+        middle_coupling,
+        left_coupling,
+        [send for _, send in opened[1:]],
+    )
+    opened = opened[:1] + [(keep, send) for (keep, _), send in zip(opened[1:], sends)]
+    out, after = None, right0
     waiting, pops, entered = [], 0, 0
     parked = {}
     while waiting or entered < len(chunks):
@@ -297,19 +317,6 @@
         pops += 1
         wide = blocks[0].shape[1]
         name = "".join(str(i) for i in ids)
-        if couplings is None:
-            couplings = prepare(
-                "prepare",
-                node_order,
-                sum(layouts[0], []),
-                sum(layouts[-1], []),
-                right_coupling,
-                middle_coupling,
-                left_coupling,
-                after,
-            )
-            right0, right1, middle, left0, left1 = couplings
-            after = right0
         if stage == 1:
             results = level(f"right0_{name}", right0, [blocks], [wide], 2, after)
             axis, shift = "sub", 1

time: 53.5 us -> 54 us (level)
  starting transfers between devices: 29.7 us -> 33.1 us
  waiting for transfers between devices: 13.5 us -> 10.5 us
    ppermute x24, starting transfers between devices: 29.7 us -> 33.1 us  [swap(): return lax.ppermute(block, axis, [(i, i ^ distance) for i in range(count)])]
    ppermute x24, waiting for transfers between devices: 13.5 us -> 10.5 us  [swap(): return lax.ppermute(block, axis, [(i, i ^ distance) for i in range(count)])]
  transfers between devices with their start and end apart: 24 -> 24, of which waited for: 12 -> 7; matrix products, arithmetic and copies ran while one was open for 0% -> 0% of each run, Pallas kernels for 11% -> 11%
where the time goes in v11:
time: 54 us; the launch traced here: 53.9 us
  starting transfers between devices  33.1 us (61%)
  waiting for transfers between devices  10.5 us (19%)
  Pallas kernels  10 us (19%)
    ppermute x24, starting transfers between devices, swap(): return lax.ppermute(block, axis, [(i, i ^ distance) for i in range(count)])  33.1 us
    ppermute x24, waiting for transfers between devices, swap(): return lax.ppermute(block, axis, [(i, i ^ distance) for i in range(count)])  10.5 us
    pallas_call x20, Pallas kernels, call(): pl.pallas_call(body, name=name, in_specs=specs + [PLACE] * len(extra), ou...  10 us
  transfers between devices with their start and end apart: 24, of which 7 were waited for; matrix products, arithmetic and copies ran while one was open for 0% of the time, Pallas kernels for 11%

profile of v11, /device:TPU:0, one launch (start us, length us, event | category | flops | bytes accessed | tf_op | source)
XLA Modules:
  0.0 53.9 jit_solution(2271707021332610971)
XLA Ops:
  0.0 2.7 %opening.1 = (bf16[128,384]{1,0:T(8,128)(2,1)S(1)}, bf16[128,384]{1,0:T(8,128)(2,1)S(1)}, bf16[128,384]{1,0:T(8,128)(2,1)S(1)}, bf16[128,384]{1,0:T(8,128)(2,1)S...) custom-call(bf16[768,256]{1,0:T(8,128)(2,1)} %refs_0_.2, bf16[768,1152]{1,0:T(8,128)(2,1)} %refs_1_.5), custom_call_target="tpu_custom_call" | custom-call | flops 2000000000 | tf_op jit(solution)/shard_map/opening/pallas_call | solution.py:56
  2.7 3.1 %collective-permute-start.1 = (bf16[128,384]{1,0:T(8,128)(2,1)S(1)}, bf16[128,384]{1,0:T(8,128)(2,1)S(1)}, u32[]{:S(2)}, u32[]{:S(2)}) collective-permute-start(bf16[128,384]{1,0:T(8,128)(2,1)S(1)} %get-tuple-element.64), channel_id=1, source_target_pairs={{0,1},{1,0},{2,3},{3,2},{4,5},{5,4},{6,7},{7,6},{8,9},{9,8},{10,11... | collective-permute-start | bytes 294920 | tf_op jit(solution)/shard_map/ppermute | solution.py:36
  5.8 0.9 %prepare.1 = (bf16[256,256]{1,0:T(8,128)(2,1)S(1)}, bf16[256,256]{1,0:T(8,128)(2,1)S(1)}, bf16[256,256]{1,0:T(8,128)(2,1)S(1)}, bf16[256,256]{1,0:T(8,128)(2,1)S...) custom-call(s32[8]{0:T(128)S(1)} %copy-done.4, ...), custom_call_target="tpu_custom_call" | custom-call | flops 2000000000 | tf_op jit(solution)/shard_map/prepare/pallas_call | solution.py:56
  6.8 2.0 %collective-permute-start.3 = (bf16[128,384]{1,0:T(8,128)(2,1)S(1)}, bf16[128,384]{1,0:T(8,128)(2,1)S(1)}, u32[]{:S(2)}, u32[]{:S(2)}) collective-permute-start(bf16[128,384]{1,0:T(8,128)(2,1)S(1)} %get-tuple-element.68), channel_id=1, source_target_pairs={{0,1},{1,0},{2,3},{3,2},{4,5},{5,4},{6,7},{7,6},{8,9},{9,8},{10,11... | collective-permute-start | bytes 294920 | tf_op jit(solution)/shard_map/ppermute | solution.py:36
  9.2 2.6 %collective-permute-start.2 = (bf16[128,384]{1,0:T(8,128)(2,1)S(1)}, bf16[128,384]{1,0:T(8,128)(2,1)S(1)}, u32[]{:S(2)}, u32[]{:S(2)}) collective-permute-start(bf16[128,384]{1,0:T(8,128)(2,1)S(1)} %get-tuple-element.66), channel_id=1, source_target_pairs={{0,2},{1,3},{2,0},{3,1},{4,6},{5,7},{6,4},{7,5},{8,10},{9,11},{10,... | collective-permute-start | bytes 294920 | tf_op jit(solution)/shard_map/ppermute | solution.py:36
  11.9 2.7 %collective-permute-done.3.refs_2_ = bf16[128,384]{1,0:T(8,128)(2,1)S(1)} collective-permute-done((bf16[128,384]{1,0:T(8,128)(2,1)S(1)}, bf16[128,384]{1,0:T(8,128)(2,1)S(1)}, u32[]{:S(2)}, u32[]{:S(2)}) %collective-permute-start.3) | collective-permute-done | bytes 98336 | tf_op jit(solution)/shard_map/ppermute | solution.py:36
  14.8 2.3 %collective-permute-start.6 = (bf16[128,384]{1,0:T(8,128)(2,1)S(1)}, bf16[128,384]{1,0:T(8,128)(2,1)S(1)}, u32[]{:S(2)}, u32[]{:S(2)}) collective-permute-start(bf16[128,384]{1,0:T(8,128)(2,1)S(1)} %get-tuple-element.74), channel_id=1, source_target_pairs={{0,2},{1,3},{2,0},{3,1},{4,6},{5,7},{6,4},{7,5},{8,10},{9,11},{10,... | collective-permute-start | bytes 294920 | tf_op jit(solution)/shard_map/ppermute | solution.py:36
  17.5 0.8 %collective-permute-start.4 = (bf16[128,384]{1,0:T(8,128)(2,1)S(1)}, bf16[128,384]{1,0:T(8,128)(2,1)S(1)}, u32[]{:S(2)}, u32[]{:S(2)}) collective-permute-start(bf16[128,384]{1,0:T(8,128)(2,1)S(1)} %get-tuple-element.72), channel_id=1, source_target_pairs={{0,2},{1,3},{2,0},{3,1},{4,6},{5,7},{6,4},{7,5},{8,10},{9,11},{10,... | collective-permute-start | bytes 294920 | tf_op jit(solution)/shard_map/ppermute | solution.py:36
  18.3 5.9 %collective-permute-done.6.refs_2_ = bf16[128,384]{1,0:T(8,128)(2,1)S(1)} collective-permute-done((bf16[128,384]{1,0:T(8,128)(2,1)S(1)}, bf16[128,384]{1,0:T(8,128)(2,1)S(1)}, u32[]{:S(2)}, u32[]{:S(2)}) %collective-permute-start.6) | collective-permute-done | bytes 98336 | tf_op jit(solution)/shard_map/ppermute | solution.py:36
  24.6 1.5 %collective-permute-start.8 = (bf16[64,384]{1,0:T(8,128)(2,1)S(1)}, bf16[64,384]{1,0:T(8,128)(2,1)S(1)}, u32[]{:S(2)}, u32[]{:S(2)}) collective-permute-start(bf16[64,384]{1,0:T(8,128)(2,1)S(1)} %get-tuple-element.79), channel_id=1, source_target_pairs={{0,8},{4,12},{8,0},{12,4},{16,24},{20,28},{24,16},{28,20},{1,9},{5... | collective-permute-start | bytes 147464 | tf_op jit(solution)/shard_map/ppermute | solution.py:36
  26.2 1.5 %collective-permute-start.9 = (bf16[64,384]{1,0:T(8,128)(2,1)S(1)}, bf16[64,384]{1,0:T(8,128)(2,1)S(1)}, u32[]{:S(2)}, u32[]{:S(2)}) collective-permute-start(bf16[64,384]{1,0:T(8,128)(2,1)S(1)} %get-tuple-element.80), channel_id=1, source_target_pairs={{0,16},{4,20},{8,24},{12,28},{16,0},{20,4},{24,8},{28,12},{1,17},{... | collective-permute-start | bytes 147464 | tf_op jit(solution)/shard_map/ppermute | solution.py:36
  28.5 1.5 %collective-permute-start.16 = (bf16[64,384]{1,0:T(8,128)(2,1)S(1)}, bf16[64,384]{1,0:T(8,128)(2,1)S(1)}, u32[]{:S(2)}, u32[]{:S(2)}) collective-permute-start(bf16[64,384]{1,0:T(8,128)(2,1)S(1)} %get-tuple-element.90), channel_id=1, source_target_pairs={{0,8},{4,12},{8,0},{12,4},{16,24},{20,28},{24,16},{28,20},{1,9},{5... | collective-permute-start | bytes 147464 | tf_op jit(solution)/shard_map/ppermute | solution.py:36
  30.1 1.5 %collective-permute-start.17 = (bf16[64,384]{1,0:T(8,128)(2,1)S(1)}, bf16[64,384]{1,0:T(8,128)(2,1)S(1)}, u32[]{:S(2)}, u32[]{:S(2)}) collective-permute-start(bf16[64,384]{1,0:T(8,128)(2,1)S(1)} %get-tuple-element.91), channel_id=1, source_target_pairs={{0,16},{4,20},{8,24},{12,28},{16,0},{20,4},{24,8},{28,12},{1,17},{... | collective-permute-start | bytes 147464 | tf_op jit(solution)/shard_map/ppermute | solution.py:36
  31.6 0.7 %collective-permute-start.18 = (bf16[64,384]{1,0:T(8,128)(2,1)S(1)}, bf16[64,384]{1,0:T(8,128)(2,1)S(1)}, u32[]{:S(2)}, u32[]{:S(2)}) collective-permute-start(bf16[64,384]{1,0:T(8,128)(2,1)S(1)} %get-tuple-element.92), channel_id=1, source_target_pairs={{0,24},{4,28},{8,16},{12,20},{16,8},{20,12},{24,0},{28,4},{1,25},{... | collective-permute-start | bytes 147464 | tf_op jit(solution)/shard_map/ppermute | solution.py:36
  33.1 1.0 %collective-permute-start.12 = (bf16[64,384]{1,0:T(8,128)(2,1)S(1)}, bf16[64,384]{1,0:T(8,128)(2,1)S(1)}, u32[]{:S(2)}, u32[]{:S(2)}) collective-permute-start(bf16[64,384]{1,0:T(8,128)(2,1)S(1)} %get-tuple-element.86), channel_id=1, source_target_pairs={{0,8},{4,12},{8,0},{12,4},{16,24},{20,28},{24,16},{28,20},{1,9},{5... | collective-permute-start | bytes 147464 | tf_op jit(solution)/shard_map/ppermute | solution.py:36
  34.2 1.3 %collective-permute-start.13 = (bf16[64,384]{1,0:T(8,128)(2,1)S(1)}, bf16[64,384]{1,0:T(8,128)(2,1)S(1)}, u32[]{:S(2)}, u32[]{:S(2)}) collective-permute-start(bf16[64,384]{1,0:T(8,128)(2,1)S(1)} %get-tuple-element.87), channel_id=1, source_target_pairs={{0,16},{4,20},{8,24},{12,28},{16,0},{20,4},{24,8},{28,12},{1,17},{... | collective-permute-start | bytes 147464 | tf_op jit(solution)/shard_map/ppermute | solution.py:36
  35.5 1.2 %collective-permute-start.14 = (bf16[64,384]{1,0:T(8,128)(2,1)S(1)}, bf16[64,384]{1,0:T(8,128)(2,1)S(1)}, u32[]{:S(2)}, u32[]{:S(2)}) collective-permute-start(bf16[64,384]{1,0:T(8,128)(2,1)S(1)} %get-tuple-element.88), channel_id=1, source_target_pairs={{0,24},{4,28},{8,16},{12,20},{16,8},{20,12},{24,0},{28,4},{1,25},{... | collective-permute-start | bytes 147464 | tf_op jit(solution)/shard_map/ppermute | solution.py:36
  37.0 2.9 %collective-permute-start.20 = (bf16[128,384]{1,0:T(8,128)(2,1)S(1)}, bf16[128,384]{1,0:T(8,128)(2,1)S(1)}, u32[]{:S(2)}, u32[]{:S(2)}) collective-permute-start(bf16[128,384]{1,0:T(8,128)(2,1)S(1)} %get-tuple-element.97), channel_id=1, source_target_pairs={{0,2},{1,3},{2,0},{3,1},{4,6},{5,7},{6,4},{7,5},{8,10},{9,11},{10,... | collective-permute-start | bytes 294920 | tf_op jit(solution)/shard_map/ppermute | solution.py:36
  40.7 3.0 %collective-permute-start.19 = (bf16[128,384]{1,0:T(8,128)(2,1)S(1)}, bf16[128,384]{1,0:T(8,128)(2,1)S(1)}, u32[]{:S(2)}, u32[]{:S(2)}) collective-permute-start(bf16[128,384]{1,0:T(8,128)(2,1)S(1)} %get-tuple-element.96), channel_id=1, source_target_pairs={{0,2},{1,3},{2,0},{3,1},{4,6},{5,7},{6,4},{7,5},{8,10},{9,11},{10,... | collective-permute-start | bytes 294920 | tf_op jit(solution)/shard_map/ppermute | solution.py:36
  44.1 2.3 %collective-permute-start.22 = (bf16[128,384]{1,0:T(8,128)(2,1)S(1)}, bf16[128,384]{1,0:T(8,128)(2,1)S(1)}, u32[]{:S(2)}, u32[]{:S(2)}) collective-permute-start(bf16[128,384]{1,0:T(8,128)(2,1)S(1)} %get-tuple-element.101), channel_id=1, source_target_pairs={{0,1},{1,0},{2,3},{3,2},{4,5},{5,4},{6,7},{7,6},{8,9},{9,8},{10,11... | collective-permute-start | bytes 294920 | tf_op jit(solution)/shard_map/ppermute | solution.py:36
  47.3 2.7 %collective-permute-start.21 = (bf16[128,384]{1,0:T(8,128)(2,1)S(1)}, bf16[128,384]{1,0:T(8,128)(2,1)S(1)}, u32[]{:S(2)}, u32[]{:S(2)}) collective-permute-start(bf16[128,384]{1,0:T(8,128)(2,1)S(1)} %get-tuple-element.100), channel_id=1, source_target_pairs={{0,1},{1,0},{2,3},{3,2},{4,5},{5,4},{6,7},{7,6},{8,9},{9,8},{10,11... | collective-permute-start | bytes 294920 | tf_op jit(solution)/shard_map/ppermute | solution.py:36
  50.1 1.3 %last0.1.refs_4_ = bf16[768,1152]{1,0:T(8,128)(2,1)} custom-call(bf16[256,256]{1,0:T(8,128)(2,1)S(1)} %get-tuple-element.56.refs_0_, bf16[768,256]{1,0:T(8,128)(2,1)S(1)} %copy-done, bf16[128,384]{1,0:T(8,128)(2,1)S(1)} %get-tuple-element.94.refs_5_.refs_2_, bf16[128,384]{1,0:T(8,128)(2,1)S(1)} %collective-permute-done.23.refs_3_, ...), custom_call_target="tpu_custom_call" | custom-call | flops 2000000000 | tf_op jit(solution)/shard_map/last0/pallas_call | solution.py:56
  51.3 1.3 %last384.1.refs_4_ = bf16[768,1152]{1,0:T(8,128)(2,1)} custom-call(bf16[256,256]{1,0:T(8,128)(2,1)S(1)} %get-tuple-element.56.refs_0_, bf16[768,256]{1,0:T(8,128)(2,1)S(1)} %copy-done, bf16[128,384]{1,0:T(8,128)(2,1)S(1)} %get-tuple-element.98.refs_3_.refs_4_.refs_2_, ...), custom_call_target="tpu_custom_call", output_to_operand_aliasing={{}: (4, {})} | custom-call | flops 2000000000 | tf_op jit(solution)/shard_map/last384/pallas_call | solution.py:56
  52.6 1.3 %last768.1 = bf16[768,1152]{1,0:T(8,128)(2,1)} custom-call(bf16[256,256]{1,0:T(8,128)(2,1)S(1)} %get-tuple-element.56.refs_0_, bf16[768,256]{1,0:T(8,128)(2,1)S(1)} %copy-done, bf16[128,384]{1,0:T(8,128)(2,1)S(1)} %get-tuple-element.99.refs_5_.refs_2_, bf16[128,384]{1,0:T(8,128)(2,1)S(1)} %collective-permute-done.21.refs_3_, ...), custom_call_target="tpu_custom_call", output_to_operand_aliasing={{}: (4, {})} | custom-call | flops 2000000000 | tf_op jit(solution)/shard_map/last768/pallas_call | solution.py:56
  (54 shorter events, 5.6 us)
Async XLA Ops:
  2.7 6.3 %collective-permute-start.1 = (bf16[128,384]{1,0:T(8,128)(2,1)S(1)}, bf16[128,384]{1,0:T(8,128)(2,1)S(1)}, u32[]{:S(2)}, u32[]{:S(2)}) collective-permute-start(bf16[128,384]{1,0:T(8,128)(2,1)S(1)} %get-tuple-element.64), channel_id=1, source_target_pairs={{0,1},{1,0},{2,3},{3,2},{4,5},{5,4},{6,7},{7,6},{8,9},{9,8},{10,11... | collective-permute-start | bytes 294920 | tf_op jit(solution)/shard_map/ppermute | solution.py:36
  6.7 10.6 %collective-permute-start = (bf16[128,384]{1,0:T(8,128)(2,1)S(1)}, bf16[128,384]{1,0:T(8,128)(2,1)S(1)}, u32[]{:S(2)}, u32[]{:S(2)}) collective-permute-start(bf16[128,384]{1,0:T(8,128)(2,1)S(1)} %get-tuple-element.62), channel_id=1, source_target_pairs={{0,1},{1,0},{2,3},{3,2},{4,5},{5,4},{6,7},{7,6},{8,9},{9,8},{10,11... | collective-permute-start | bytes 294920 | tf_op jit(solution)/shard_map/ppermute | solution.py:36
  6.8 7.8 %collective-permute-start.3 = (bf16[128,384]{1,0:T(8,128)(2,1)S(1)}, bf16[128,384]{1,0:T(8,128)(2,1)S(1)}, u32[]{:S(2)}, u32[]{:S(2)}) collective-permute-start(bf16[128,384]{1,0:T(8,128)(2,1)S(1)} %get-tuple-element.68), channel_id=1, source_target_pairs={{0,1},{1,0},{2,3},{3,2},{4,5},{5,4},{6,7},{7,6},{8,9},{9,8},{10,11... | collective-permute-start | bytes 294920 | tf_op jit(solution)/shard_map/ppermute | solution.py:36
  9.2 7.8 %collective-permute-start.2 = (bf16[128,384]{1,0:T(8,128)(2,1)S(1)}, bf16[128,384]{1,0:T(8,128)(2,1)S(1)}, u32[]{:S(2)}, u32[]{:S(2)}) collective-permute-start(bf16[128,384]{1,0:T(8,128)(2,1)S(1)} %get-tuple-element.66), channel_id=1, source_target_pairs={{0,2},{1,3},{2,0},{3,1},{4,6},{5,7},{6,4},{7,5},{8,10},{9,11},{10,... | collective-permute-start | bytes 294920 | tf_op jit(solution)/shard_map/ppermute | solution.py:36
  14.8 9.4 %collective-permute-start.6 = (bf16[128,384]{1,0:T(8,128)(2,1)S(1)}, bf16[128,384]{1,0:T(8,128)(2,1)S(1)}, u32[]{:S(2)}, u32[]{:S(2)}) collective-permute-start(bf16[128,384]{1,0:T(8,128)(2,1)S(1)} %get-tuple-element.74), channel_id=1, source_target_pairs={{0,2},{1,3},{2,0},{3,1},{4,6},{5,7},{6,4},{7,5},{8,10},{9,11},{10,... | collective-permute-start | bytes 294920 | tf_op jit(solution)/shard_map/ppermute | solution.py:36
  17.5 10.6 %collective-permute-start.4 = (bf16[128,384]{1,0:T(8,128)(2,1)S(1)}, bf16[128,384]{1,0:T(8,128)(2,1)S(1)}, u32[]{:S(2)}, u32[]{:S(2)}) collective-permute-start(bf16[128,384]{1,0:T(8,128)(2,1)S(1)} %get-tuple-element.72), channel_id=1, source_target_pairs={{0,2},{1,3},{2,0},{3,1},{4,6},{5,7},{6,4},{7,5},{8,10},{9,11},{10,... | collective-permute-start | bytes 294920 | tf_op jit(solution)/shard_map/ppermute | solution.py:36
  18.3 6.2 %collective-permute-start.5 = (bf16[128,384]{1,0:T(8,128)(2,1)S(1)}, bf16[128,384]{1,0:T(8,128)(2,1)S(1)}, u32[]{:S(2)}, u32[]{:S(2)}) collective-permute-start(bf16[128,384]{1,0:T(8,128)(2,1)S(1)} %get-tuple-element.73), channel_id=1, source_target_pairs={{0,4},{4,0},{8,12},{12,8},{16,20},{20,16},{24,28},{28,24},{1,5},{5... | collective-permute-start | bytes 294920 | tf_op jit(solution)/shard_map/ppermute | solution.py:36
  24.5 4.0 %collective-permute-start.11 = (bf16[128,384]{1,0:T(8,128)(2,1)S(1)}, bf16[128,384]{1,0:T(8,128)(2,1)S(1)}, u32[]{:S(2)}, u32[]{:S(2)}) collective-permute-start(bf16[128,384]{1,0:T(8,128)(2,1)S(1)} %get-tuple-element.82), channel_id=1, source_target_pairs={{0,4},{4,0},{8,12},{12,8},{16,20},{20,16},{24,28},{28,24},{1,5},{5... | collective-permute-start | bytes 294920 | tf_op jit(solution)/shard_map/ppermute | solution.py:36
  24.6 5.5 %collective-permute-start.8 = (bf16[64,384]{1,0:T(8,128)(2,1)S(1)}, bf16[64,384]{1,0:T(8,128)(2,1)S(1)}, u32[]{:S(2)}, u32[]{:S(2)}) collective-permute-start(bf16[64,384]{1,0:T(8,128)(2,1)S(1)} %get-tuple-element.79), channel_id=1, source_target_pairs={{0,8},{4,12},{8,0},{12,4},{16,24},{20,28},{24,16},{28,20},{1,9},{5... | collective-permute-start | bytes 147464 | tf_op jit(solution)/shard_map/ppermute | solution.py:36
  26.2 5.4 %collective-permute-start.9 = (bf16[64,384]{1,0:T(8,128)(2,1)S(1)}, bf16[64,384]{1,0:T(8,128)(2,1)S(1)}, u32[]{:S(2)}, u32[]{:S(2)}) collective-permute-start(bf16[64,384]{1,0:T(8,128)(2,1)S(1)} %get-tuple-element.80), channel_id=1, source_target_pairs={{0,16},{4,20},{8,24},{12,28},{16,0},{20,4},{24,8},{28,12},{1,17},{... | collective-permute-start | bytes 147464 | tf_op jit(solution)/shard_map/ppermute | solution.py:36
  27.7 5.1 %collective-permute-start.10 = (bf16[64,384]{1,0:T(8,128)(2,1)S(1)}, bf16[64,384]{1,0:T(8,128)(2,1)S(1)}, u32[]{:S(2)}, u32[]{:S(2)}) collective-permute-start(bf16[64,384]{1,0:T(8,128)(2,1)S(1)} %get-tuple-element.81), channel_id=1, source_target_pairs={{0,24},{4,28},{8,16},{12,20},{16,8},{20,12},{24,0},{28,4},{1,25},{... | collective-permute-start | bytes 147464 | tf_op jit(solution)/shard_map/ppermute | solution.py:36
  28.4 4.7 %collective-permute-start.7 = (bf16[128,384]{1,0:T(8,128)(2,1)S(1)}, bf16[128,384]{1,0:T(8,128)(2,1)S(1)}, u32[]{:S(2)}, u32[]{:S(2)}) collective-permute-start(bf16[128,384]{1,0:T(8,128)(2,1)S(1)} %get-tuple-element.78), channel_id=1, source_target_pairs={{0,4},{4,0},{8,12},{12,8},{16,20},{20,16},{24,28},{28,24},{1,5},{5... | collective-permute-start | bytes 294920 | tf_op jit(solution)/shard_map/ppermute | solution.py:36
  28.5 5.7 %collective-permute-start.16 = (bf16[64,384]{1,0:T(8,128)(2,1)S(1)}, bf16[64,384]{1,0:T(8,128)(2,1)S(1)}, u32[]{:S(2)}, u32[]{:S(2)}) collective-permute-start(bf16[64,384]{1,0:T(8,128)(2,1)S(1)} %get-tuple-element.90), channel_id=1, source_target_pairs={{0,8},{4,12},{8,0},{12,4},{16,24},{20,28},{24,16},{28,20},{1,9},{5... | collective-permute-start | bytes 147464 | tf_op jit(solution)/shard_map/ppermute | solution.py:36
  30.1 5.4 %collective-permute-start.17 = (bf16[64,384]{1,0:T(8,128)(2,1)S(1)}, bf16[64,384]{1,0:T(8,128)(2,1)S(1)}, u32[]{:S(2)}, u32[]{:S(2)}) collective-permute-start(bf16[64,384]{1,0:T(8,128)(2,1)S(1)} %get-tuple-element.91), channel_id=1, source_target_pairs={{0,16},{4,20},{8,24},{12,28},{16,0},{20,4},{24,8},{28,12},{1,17},{... | collective-permute-start | bytes 147464 | tf_op jit(solution)/shard_map/ppermute | solution.py:36
  31.6 5.2 %collective-permute-start.18 = (bf16[64,384]{1,0:T(8,128)(2,1)S(1)}, bf16[64,384]{1,0:T(8,128)(2,1)S(1)}, u32[]{:S(2)}, u32[]{:S(2)}) collective-permute-start(bf16[64,384]{1,0:T(8,128)(2,1)S(1)} %get-tuple-element.92), channel_id=1, source_target_pairs={{0,24},{4,28},{8,16},{12,20},{16,8},{20,12},{24,0},{28,4},{1,25},{... | collective-permute-start | bytes 147464 | tf_op jit(solution)/shard_map/ppermute | solution.py:36
  33.0 6.9 %collective-permute-start.15 = (bf16[128,384]{1,0:T(8,128)(2,1)S(1)}, bf16[128,384]{1,0:T(8,128)(2,1)S(1)}, u32[]{:S(2)}, u32[]{:S(2)}) collective-permute-start(bf16[128,384]{1,0:T(8,128)(2,1)S(1)} %get-tuple-element.89), channel_id=1, source_target_pairs={{0,2},{1,3},{2,0},{3,1},{4,6},{5,7},{6,4},{7,5},{8,10},{9,11},{10,... | collective-permute-start | bytes 294920 | tf_op jit(solution)/shard_map/ppermute | solution.py:36
  33.1 7.0 %collective-permute-start.12 = (bf16[64,384]{1,0:T(8,128)(2,1)S(1)}, bf16[64,384]{1,0:T(8,128)(2,1)S(1)}, u32[]{:S(2)}, u32[]{:S(2)}) collective-permute-start(bf16[64,384]{1,0:T(8,128)(2,1)S(1)} %get-tuple-element.86), channel_id=1, source_target_pairs={{0,8},{4,12},{8,0},{12,4},{16,24},{20,28},{24,16},{28,20},{1,9},{5... | collective-permute-start | bytes 147464 | tf_op jit(solution)/shard_map/ppermute | solution.py:36
  34.2 6.0 %collective-permute-start.13 = (bf16[64,384]{1,0:T(8,128)(2,1)S(1)}, bf16[64,384]{1,0:T(8,128)(2,1)S(1)}, u32[]{:S(2)}, u32[]{:S(2)}) collective-permute-start(bf16[64,384]{1,0:T(8,128)(2,1)S(1)} %get-tuple-element.87), channel_id=1, source_target_pairs={{0,16},{4,20},{8,24},{12,28},{16,0},{20,4},{24,8},{28,12},{1,17},{... | collective-permute-start | bytes 147464 | tf_op jit(solution)/shard_map/ppermute | solution.py:36
  35.5 5.0 %collective-permute-start.14 = (bf16[64,384]{1,0:T(8,128)(2,1)S(1)}, bf16[64,384]{1,0:T(8,128)(2,1)S(1)}, u32[]{:S(2)}, u32[]{:S(2)}) collective-permute-start(bf16[64,384]{1,0:T(8,128)(2,1)S(1)} %get-tuple-element.88), channel_id=1, source_target_pairs={{0,24},{4,28},{8,16},{12,20},{16,8},{20,12},{24,0},{28,4},{1,25},{... | collective-permute-start | bytes 147464 | tf_op jit(solution)/shard_map/ppermute | solution.py:36
  37.0 6.9 %collective-permute-start.20 = (bf16[128,384]{1,0:T(8,128)(2,1)S(1)}, bf16[128,384]{1,0:T(8,128)(2,1)S(1)}, u32[]{:S(2)}, u32[]{:S(2)}) collective-permute-start(bf16[128,384]{1,0:T(8,128)(2,1)S(1)} %get-tuple-element.97), channel_id=1, source_target_pairs={{0,2},{1,3},{2,0},{3,1},{4,6},{5,7},{6,4},{7,5},{8,10},{9,11},{10,... | collective-permute-start | bytes 294920 | tf_op jit(solution)/shard_map/ppermute | solution.py:36
  40.7 6.4 %collective-permute-start.19 = (bf16[128,384]{1,0:T(8,128)(2,1)S(1)}, bf16[128,384]{1,0:T(8,128)(2,1)S(1)}, u32[]{:S(2)}, u32[]{:S(2)}) collective-permute-start(bf16[128,384]{1,0:T(8,128)(2,1)S(1)} %get-tuple-element.96), channel_id=1, source_target_pairs={{0,2},{1,3},{2,0},{3,1},{4,6},{5,7},{6,4},{7,5},{8,10},{9,11},{10,... | collective-permute-start | bytes 294920 | tf_op jit(solution)/shard_map/ppermute | solution.py:36
  43.7 6.4 %collective-permute-start.23 = (bf16[128,384]{1,0:T(8,128)(2,1)S(1)}, bf16[128,384]{1,0:T(8,128)(2,1)S(1)}, u32[]{:S(2)}, u32[]{:S(2)}) collective-permute-start(bf16[128,384]{1,0:T(8,128)(2,1)S(1)} %get-tuple-element.102), channel_id=1, source_target_pairs={{0,1},{1,0},{2,3},{3,2},{4,5},{5,4},{6,7},{7,6},{8,9},{9,8},{10,11... | collective-permute-start | bytes 294920 | tf_op jit(solution)/shard_map/ppermute | solution.py:36
  44.1 7.2 %collective-permute-start.22 = (bf16[128,384]{1,0:T(8,128)(2,1)S(1)}, bf16[128,384]{1,0:T(8,128)(2,1)S(1)}, u32[]{:S(2)}, u32[]{:S(2)}) collective-permute-start(bf16[128,384]{1,0:T(8,128)(2,1)S(1)} %get-tuple-element.101), channel_id=1, source_target_pairs={{0,1},{1,0},{2,3},{3,2},{4,5},{5,4},{6,7},{7,6},{8,9},{9,8},{10,11... | collective-permute-start | bytes 294920 | tf_op jit(solution)/shard_map/ppermute | solution.py:36
  47.3 5.3 %collective-permute-start.21 = (bf16[128,384]{1,0:T(8,128)(2,1)S(1)}, bf16[128,384]{1,0:T(8,128)(2,1)S(1)}, u32[]{:S(2)}, u32[]{:S(2)}) collective-permute-start(bf16[128,384]{1,0:T(8,128)(2,1)S(1)} %get-tuple-element.100), channel_id=1, source_target_pairs={{0,1},{1,0},{2,3},{3,2},{4,5},{5,4},{6,7},{7,6},{8,9},{9,8},{10,11... | collective-permute-start | bytes 294920 | tf_op jit(solution)/shard_map/ppermute | solution.py:36
  (5 other events, 26.2 us)

commit v12 on v11

--- a/solution.py
+++ b/solution.py
@@ -10,6 +10,9 @@
 ENTRY = (0, 0, 1)
 MERGED = ((0,), (1,), (2,))
 SPLIT = {}
+DIRECT = (True, True, True)
+TURNS = {}
+SPANS = {"right0": 2 * 10**9}
 ROWS = 16
 SCOPED = 8 * 2**20
 MOST = 213 * 2**18
@@ -17,7 +20,6 @@
 BF16 = jnp.bfloat16
 WHOLE = pl.BlockSpec(memory_space=pltpu.VMEM)
 SCALARS = pl.BlockSpec(memory_space=pltpu.SMEM)
-SPAN = pl.CostEstimate(flops=2 * 10**9, bytes_accessed=0, transcendentals=0)
 PLACE = pl.BlockSpec(memory_space=pl.ANY)
 HBM = pl.BlockSpec(memory_space=pltpu.HBM)
 
@@ -45,6 +47,11 @@
 
 def matmul(left, right):
     return lax.dot_general(left, right, (((1,), (0,)), ((), ())), preferred_element_type=F32)
+
+
+def span(name):
+    flops = SPANS.get(name.split("_")[0], 6 * 10**8)
+    return pl.CostEstimate(flops=flops, bytes_accessed=0, transcendentals=0)
 
 
 def call(kernel, name, outs, specs, operands, after, limit=SCOPED, **more):
@@ -69,8 +76,9 @@
     block = width // groups
 
     def kernel(node_order, right, middle, left, *refs):
-        right0, right1, middle0, left0, left1 = refs[len(held) : len(held) + 5]
-        for block_in, block_out in zip(refs[: len(held)], refs[len(held) + 5 :]):
+        right0, right1, left0, left1, *rest = refs[len(held) :]
+        middles, passed = rest[: len(slots_in)], rest[len(slots_in) :]
+        for block_in, block_out in zip(refs[: len(held)], passed):
             block_out[...] = block_in[...]
         place, group = lax.axis_index("sub"), lax.axis_index("mid")
         bit0, bit1 = place & 1, place >> 1 & 1
@@ -83,26 +91,27 @@
         across = lax.broadcasted_iota(jnp.int32, (width, width), 1)
         pick = jnp.where(across == source, 1.0, 0.0).astype(BF16)
         right1[...] = matmul(pick, swapped(right[0, 1], 1, bit1)).astype(BF16)
-        place = lax.broadcasted_iota(jnp.int32, (1, width), 1)
-        source = place % block
-        for i, slot in enumerate(slots_in):
-            source += jnp.where(place // block == i, (slot ^ group) * block, 0)
         down = lax.broadcasted_iota(jnp.int32, (width, width), 0)
-        pick = jnp.where(down == source, 1.0, 0.0).astype(BF16)
-        middle0[...] = swapped(matmul(middle[0], pick).astype(BF16), 0, bit1)
+        for slots, out in zip(slots_in, middles):
+            place = lax.broadcasted_iota(jnp.int32, (1, width), 1)
+            source = place % block
+            for i, slot in enumerate(slots):
+                source += jnp.where(place // block == i, (slot ^ group) * block, 0)
+            pick = jnp.where(down == source, 1.0, 0.0).astype(BF16)
+            out[...] = swapped(matmul(middle[0], pick).astype(BF16), 0, bit1)
         left0[...] = swapped(swapped(left[0, 0], 1, bit1), 0, bit0)
         left1[...] = swapped(left[0, 1], 1, bit0)
 
     return call(
         kernel,
         name,
-        [jax.ShapeDtypeStruct((width, width), BF16)] * 5
+        [jax.ShapeDtypeStruct((width, width), BF16)] * (4 + len(slots_in))
         + [jax.ShapeDtypeStruct(block.shape, BF16) for block in held],
         [SCALARS] + [WHOLE] * (3 + len(held)),
         [node_order, right, middle, left] + held,
         None,
-        out_specs=[WHOLE] * (5 + len(held)),
-        cost_estimate=SPAN,
+        out_specs=[WHOLE] * (4 + len(slots_in) + len(held)),
+        cost_estimate=span(name),
     )
 
 
@@ -113,12 +122,12 @@
 def opening(name, basis, signal, widths):
     rows, width = basis.shape
     half = width // 2
-    pieces = row_pieces(rows, 3)
+    pieces = row_pieces(rows, 6)
     depth = rows // pieces
     lows = [sum(widths[:i]) for i in range(len(widths))]
 
     def kernel(basis, signal, *refs):
-        outs, (basis_here, signal_here, sums, arrived, basis_arrived) = refs[:-5], refs[-5:]
+        outs, (basis_here, signal_here, arrived, basis_arrived) = refs[:-4], refs[-4:]
         fetch_basis = pltpu.make_async_copy(basis, basis_here, basis_arrived)
         fetch_basis.start()
         copies = []
@@ -130,17 +139,10 @@
             copies[-1].start()
         fetch_basis.wait()
         flipped = swapped(basis_here[...].T, 0, lax.axis_index("sub") & 1)
-        for i, copy in enumerate(copies):
+        for copy in copies:
             copy.wait()
-            rows_here = slice(i * depth, (i + 1) * depth)
-            if i < pieces - 1:
-                part = matmul(flipped[:, rows_here], signal_here[rows_here, :])
-                sums[...] = part if i == 0 else sums[...] + part
         for i, (low, wide) in enumerate(zip(lows, widths)):
-            here = slice(low, low + wide)
-            total = matmul(flipped[:, rows_here], signal_here[rows_here, here])
-            if pieces > 1:
-                total += sums[:, here]
+            total = matmul(flipped, signal_here[:, low : low + wide])
             outs[2 * i][...] = total[:half].astype(BF16)
             outs[2 * i + 1][...] = total[half:].astype(BF16)
 
@@ -156,11 +158,10 @@
         scratch_shapes=[
             pltpu.VMEM((rows, width), BF16),
             pltpu.VMEM(signal.shape, BF16),
-            pltpu.VMEM((width, signal.shape[1]), F32),
             pltpu.SemaphoreType.DMA((pieces,)),
             pltpu.SemaphoreType.DMA,
         ],
-        cost_estimate=SPAN,
+        cost_estimate=span(name),
     )
     return list(zip(outs[0::2], outs[1::2]))
 
@@ -194,23 +195,35 @@
         [weight] + flat,
         after,
         out_specs=[WHOLE] * (count * len(widths)),
-        cost_estimate=SPAN,
+        cost_estimate=span(name),
     )
     return [list(outs[i * count : (i + 1) * count]) for i in range(len(widths))]
 
 
-def digits(groups):
+def digits(groups, direct):
     bits = groups.bit_length() - 1
-    found = [(0, 2)]
-    while found[-1][0] + (found[-1][1].bit_length() - 1) < bits:
-        shift = found[-1][0] + found[-1][1].bit_length() - 1
-        found.append((shift, 4 if shift + 2 <= bits else 2))
+    found, shift = [(0, 2)], 1
+    while shift < bits:
+        count = 2 if direct and shift + 2 <= bits else 1
+        found.append((shift, 1 << count))
+        shift += count
     return found
+
+
+def layouts_of(groups, steps):
+    layouts = [by_digit(range(groups), steps[0])]
+    for step in steps[1:]:
+        layouts.append(by_digit(sum(layouts[-1], []), step))
+    return layouts
+
+
+def values_of(radix):
+    return [0] + sorted(range(1, radix), key=lambda value: -value.bit_count())
 
 
 def by_digit(slots, digit):
     shift, radix = digit
-    return [[r for r in slots if r >> shift & radix - 1 == value] for value in range(radix)]
+    return [[r for r in slots if r >> shift & radix - 1 == value] for value in values_of(radix)]
 
 
 def regroup(name, blocks, layout, digit, block, after):
@@ -237,7 +250,7 @@
         blocks,
         after,
         out_specs=[WHOLE] * len(wanted),
-        cost_estimate=SPAN,
+        cost_estimate=span(name),
     )
     return list(outs), wanted
 
@@ -273,7 +286,7 @@
         out_specs=HBM,
         scratch_shapes=[pltpu.VMEM((rows, wide), BF16), pltpu.SemaphoreType.DMA((pieces,))],
         input_output_aliases={4: 0} if given else {},
-        cost_estimate=SPAN,
+        cost_estimate=span(name),
     )
 
 
@@ -287,22 +300,22 @@
     merged = {i: group for group in MERGED for i in group}
     if len(chunks) < len(ENTRY_SHARES):
         merged = {i: (i,) for i in range(len(chunks))}
-    steps = digits(groups)
-    layouts = [by_digit(range(groups), steps[0])]
-    for step in steps[1:]:
-        layouts.append(by_digit(sum(layouts[-1], []), step))
+    plans = {flag: digits(groups, flag) for flag in sorted(set(DIRECT))}
+    layouts_by = {flag: layouts_of(groups, plan) for flag, plan in plans.items()}
 
     opened = opening("opening", col_basis, signal, chunks)
-    right0, right1, middle, left0, left1, *sends = prepare(
+    right0, right1, left0, left1, *rest = prepare(
         "prepare",
         node_order,
-        sum(layouts[0], []),
-        sum(layouts[-1], []),
+        sum(by_digit(range(groups), (0, 2)), []),
+        [sum(layouts[-1], []) for layouts in layouts_by.values()],
         right_coupling,
         middle_coupling,
         left_coupling,
         [send for _, send in opened[1:]],
     )
+    middles = dict(zip(layouts_by, rest))
+    sends = rest[len(middles) :]
     opened = opened[:1] + [(keep, send) for (keep, _), send in zip(opened[1:], sends)]
     out, after = None, right0
     waiting, pops, entered = [], 0, 0
@@ -313,13 +326,16 @@
             keep, send = opened[i]
             waiting.append((1, (i,), starts[i], [keep, swap(send, "sub", 1)]))
             continue
-        stage, ids, low, blocks = waiting.pop(0)
+        turn = TURNS.get(pops, 0)
+        stage, ids, low, blocks = waiting.pop(turn if turn < len(waiting) else 0)
         pops += 1
+        flag = DIRECT[ids[0]]
+        steps, layouts, middle = plans[flag], layouts_by[flag], middles[flag]
         wide = blocks[0].shape[1]
         name = "".join(str(i) for i in ids)
         if stage == 1:
             results = level(f"right0_{name}", right0, [blocks], [wide], 2, after)
-            axis, shift = "sub", 1
+            axis, shift, radix = "sub", 1, 2
         elif stage == 2:
             parked[ids[0]] = blocks
             ids = merged[ids[0]]
@@ -329,25 +345,26 @@
             low = starts[ids[0]]
             blocks = [parked[i] for i in ids]
             results = level(f"right1_{name}", right1, blocks, [wide], steps[0][1], after)
-            axis, shift = "mid", steps[0][0]
+            axis, shift, radix = "mid", *steps[0]
         elif stage < 2 + len(steps):
             step = steps[stage - 2]
             held_as = layouts[stage - 3]
             results = [regroup(f"regroup{stage}_{name}", blocks, held_as, step, block, after)[0]]
-            axis, shift = "mid", step[0]
+            axis, shift, radix = "mid", *step
         elif stage == 2 + len(steps):
             widths = shares(wide, SPLIT.get(ids, (1,)))
             results = level(f"middle_{name}", middle, [blocks], widths, 2, after)
-            axis, shift = "sub", 1
+            axis, shift, radix = "sub", 1, 2
         elif stage == 3 + len(steps):
             results = level(f"left0_{name}", left0, [blocks], [wide], 2, after)
-            axis, shift = "sub", 0
+            axis, shift, radix = "sub", 0, 2
         else:
             out = last(f"last{low}", left1, row_basis, *blocks, out, low, columns, after)
             continue
         after = results[0][0]
         for result in results:
-            moved = [swap(send, axis, i + 1 << shift) for i, send in enumerate(result[1:])]
+            routes = [value << shift for value in values_of(radix)[1:]]
+            moved = [swap(send, axis, route) for send, route in zip(result[1:], routes)]
             waiting.append((stage + 1, ids, low, result[:1] + moved))
             low += result[0].shape[1]
     return out

time: 54 us -> 54.1 us (level)
  starting transfers between devices: 33.1 us -> 36.8 us
  waiting for transfers between devices: 10.5 us -> 7.06 us
    ppermute x24, starting transfers between devices: 33.1 us -> 36.8 us  [swap(): return lax.ppermute(block, axis, [(i, i ^ distance) for i in range(count)])]
    ppermute x24, waiting for transfers between devices: 10.5 us -> 7.06 us  [swap(): return lax.ppermute(block, axis, [(i, i ^ distance) for i in range(count)])]
  transfers between devices with their start and end apart: 24 -> 24, of which waited for: 7 -> 6; matrix products, arithmetic and copies ran while one was open for 0% -> 0% of each run, Pallas kernels for 11% -> 11%
where the time goes in v12:
time: 54.1 us; the launch traced here: 54 us
  starting transfers between devices  36.8 us (68%)
  Pallas kernels  9.87 us (18%)
  waiting for transfers between devices  7.06 us (13%)
    ppermute x24, starting transfers between devices, swap(): return lax.ppermute(block, axis, [(i, i ^ distance) for i in range(count)])  36.8 us
    pallas_call x20, Pallas kernels, call(): pl.pallas_call(body, name=name, in_specs=specs + [PLACE] * len(extra), ou...  9.87 us
    ppermute x24, waiting for transfers between devices, swap(): return lax.ppermute(block, axis, [(i, i ^ distance) for i in range(count)])  7.06 us
  transfers between devices with their start and end apart: 24, of which 6 were waited for; matrix products, arithmetic and copies ran while one was open for 0% of the time, Pallas kernels for 11%

profile of v12, /device:TPU:0, one launch (start us, length us, event | category | flops | bytes accessed | tf_op | source)
XLA Modules:
  0.0 54.0 jit_solution(10432483153106318717)
XLA Ops:
  0.0 2.5 %opening.1 = (bf16[128,384]{1,0:T(8,128)(2,1)S(1)}, bf16[128,384]{1,0:T(8,128)(2,1)S(1)}, bf16[128,384]{1,0:T(8,128)(2,1)S(1)}, bf16[128,384]{1,0:T(8,128)(2,1)S...) custom-call(bf16[768,256]{1,0:T(8,128)(2,1)} %refs_0_.2, bf16[768,1152]{1,0:T(8,128)(2,1)} %refs_1_.5), custom_call_target="tpu_custom_call" | custom-call | flops 600000000 | tf_op jit(solution)/shard_map/opening/pallas_call | solution.py:63
  2.5 3.1 %collective-permute-start.1 = (bf16[128,384]{1,0:T(8,128)(2,1)S(1)}, bf16[128,384]{1,0:T(8,128)(2,1)S(1)}, u32[]{:S(2)}, u32[]{:S(2)}) collective-permute-start(bf16[128,384]{1,0:T(8,128)(2,1)S(1)} %get-tuple-element.64), channel_id=1, source_target_pairs={{0,1},{1,0},{2,3},{3,2},{4,5},{5,4},{6,7},{7,6},{8,9},{9,8},{10,11... | collective-permute-start | bytes 294920 | tf_op jit(solution)/shard_map/ppermute | solution.py:38
  5.6 0.9 %prepare.1 = (bf16[256,256]{1,0:T(8,128)(2,1)S(1)}, bf16[256,256]{1,0:T(8,128)(2,1)S(1)}, bf16[256,256]{1,0:T(8,128)(2,1)S(1)}, bf16[256,256]{1,0:T(8,128)(2,1)S...) custom-call(s32[8]{0:T(128)S(1)} %copy-done.4, ...), custom_call_target="tpu_custom_call" | custom-call | flops 600000000 | tf_op jit(solution)/shard_map/prepare/pallas_call | solution.py:63
  6.6 2.0 %collective-permute-start.3 = (bf16[128,384]{1,0:T(8,128)(2,1)S(1)}, bf16[128,384]{1,0:T(8,128)(2,1)S(1)}, u32[]{:S(2)}, u32[]{:S(2)}) collective-permute-start(bf16[128,384]{1,0:T(8,128)(2,1)S(1)} %get-tuple-element.68), channel_id=1, source_target_pairs={{0,1},{1,0},{2,3},{3,2},{4,5},{5,4},{6,7},{7,6},{8,9},{9,8},{10,11... | collective-permute-start | bytes 294920 | tf_op jit(solution)/shard_map/ppermute | solution.py:38
  9.1 2.6 %collective-permute-start.2 = (bf16[128,384]{1,0:T(8,128)(2,1)S(1)}, bf16[128,384]{1,0:T(8,128)(2,1)S(1)}, u32[]{:S(2)}, u32[]{:S(2)}) collective-permute-start(bf16[128,384]{1,0:T(8,128)(2,1)S(1)} %get-tuple-element.66), channel_id=1, source_target_pairs={{0,2},{1,3},{2,0},{3,1},{4,6},{5,7},{6,4},{7,5},{8,10},{9,11},{10,... | collective-permute-start | bytes 294920 | tf_op jit(solution)/shard_map/ppermute | solution.py:38
  11.7 2.7 %collective-permute-done.3.refs_2_ = bf16[128,384]{1,0:T(8,128)(2,1)S(1)} collective-permute-done((bf16[128,384]{1,0:T(8,128)(2,1)S(1)}, bf16[128,384]{1,0:T(8,128)(2,1)S(1)}, u32[]{:S(2)}, u32[]{:S(2)}) %collective-permute-start.3) | collective-permute-done | bytes 98336 | tf_op jit(solution)/shard_map/ppermute | solution.py:38
  14.6 2.2 %collective-permute-start.6 = (bf16[128,384]{1,0:T(8,128)(2,1)S(1)}, bf16[128,384]{1,0:T(8,128)(2,1)S(1)}, u32[]{:S(2)}, u32[]{:S(2)}) collective-permute-start(bf16[128,384]{1,0:T(8,128)(2,1)S(1)} %get-tuple-element.74), channel_id=1, source_target_pairs={{0,2},{1,3},{2,0},{3,1},{4,6},{5,7},{6,4},{7,5},{8,10},{9,11},{10,... | collective-permute-start | bytes 294920 | tf_op jit(solution)/shard_map/ppermute | solution.py:38
  17.4 0.8 %collective-permute-start.4 = (bf16[128,384]{1,0:T(8,128)(2,1)S(1)}, bf16[128,384]{1,0:T(8,128)(2,1)S(1)}, u32[]{:S(2)}, u32[]{:S(2)}) collective-permute-start(bf16[128,384]{1,0:T(8,128)(2,1)S(1)} %get-tuple-element.72), channel_id=1, source_target_pairs={{0,2},{1,3},{2,0},{3,1},{4,6},{5,7},{6,4},{7,5},{8,10},{9,11},{10,... | collective-permute-start | bytes 294920 | tf_op jit(solution)/shard_map/ppermute | solution.py:38
  18.2 3.0 %collective-permute-done.6.refs_2_ = bf16[128,384]{1,0:T(8,128)(2,1)S(1)} collective-permute-done((bf16[128,384]{1,0:T(8,128)(2,1)S(1)}, bf16[128,384]{1,0:T(8,128)(2,1)S(1)}, u32[]{:S(2)}, u32[]{:S(2)}) %collective-permute-start.6) | collective-permute-done | bytes 98336 | tf_op jit(solution)/shard_map/ppermute | solution.py:38
  21.6 2.5 %collective-permute-start.8 = (bf16[64,384]{1,0:T(8,128)(2,1)S(1)}, bf16[64,384]{1,0:T(8,128)(2,1)S(1)}, u32[]{:S(2)}, u32[]{:S(2)}) collective-permute-start(bf16[64,384]{1,0:T(8,128)(2,1)S(1)} %get-tuple-element.79), channel_id=1, source_target_pairs={{0,24},{4,28},{8,16},{12,20},{16,8},{20,12},{24,0},{28,4},{1,25},{... | collective-permute-start | bytes 147464 | tf_op jit(solution)/shard_map/ppermute | solution.py:38
  26.0 2.5 %collective-permute-start.16 = (bf16[64,384]{1,0:T(8,128)(2,1)S(1)}, bf16[64,384]{1,0:T(8,128)(2,1)S(1)}, u32[]{:S(2)}, u32[]{:S(2)}) collective-permute-start(bf16[64,384]{1,0:T(8,128)(2,1)S(1)} %get-tuple-element.90), channel_id=1, source_target_pairs={{0,24},{4,28},{8,16},{12,20},{16,8},{20,12},{24,0},{28,4},{1,25},{... | collective-permute-start | bytes 147464 | tf_op jit(solution)/shard_map/ppermute | solution.py:38
  29.1 1.0 %collective-permute-start.18 = (bf16[64,384]{1,0:T(8,128)(2,1)S(1)}, bf16[64,384]{1,0:T(8,128)(2,1)S(1)}, u32[]{:S(2)}, u32[]{:S(2)}) collective-permute-start(bf16[64,384]{1,0:T(8,128)(2,1)S(1)} %get-tuple-element.92), channel_id=1, source_target_pairs={{0,16},{4,20},{8,24},{12,28},{16,0},{20,4},{24,8},{28,12},{1,17},{... | collective-permute-start | bytes 147464 | tf_op jit(solution)/shard_map/ppermute | solution.py:38
  30.4 1.4 %collective-permute-start.15 = (bf16[128,384]{1,0:T(8,128)(2,1)S(1)}, bf16[128,384]{1,0:T(8,128)(2,1)S(1)}, u32[]{:S(2)}, u32[]{:S(2)}) collective-permute-start(bf16[128,384]{1,0:T(8,128)(2,1)S(1)} %get-tuple-element.89), channel_id=1, source_target_pairs={{0,2},{1,3},{2,0},{3,1},{4,6},{5,7},{6,4},{7,5},{8,10},{9,11},{10,... | collective-permute-start | bytes 294920 | tf_op jit(solution)/shard_map/ppermute | solution.py:38
  31.8 1.5 %collective-permute-start.12 = (bf16[64,384]{1,0:T(8,128)(2,1)S(1)}, bf16[64,384]{1,0:T(8,128)(2,1)S(1)}, u32[]{:S(2)}, u32[]{:S(2)}) collective-permute-start(bf16[64,384]{1,0:T(8,128)(2,1)S(1)} %get-tuple-element.86), channel_id=1, source_target_pairs={{0,24},{4,28},{8,16},{12,20},{16,8},{20,12},{24,0},{28,4},{1,25},{... | collective-permute-start | bytes 147464 | tf_op jit(solution)/shard_map/ppermute | solution.py:38
  33.3 0.6 %collective-permute-start.13 = (bf16[64,384]{1,0:T(8,128)(2,1)S(1)}, bf16[64,384]{1,0:T(8,128)(2,1)S(1)}, u32[]{:S(2)}, u32[]{:S(2)}) collective-permute-start(bf16[64,384]{1,0:T(8,128)(2,1)S(1)} %get-tuple-element.87), channel_id=1, source_target_pairs={{0,8},{4,12},{8,0},{12,4},{16,24},{20,28},{24,16},{28,20},{1,9},{5... | collective-permute-start | bytes 147464 | tf_op jit(solution)/shard_map/ppermute | solution.py:38
  33.9 1.5 %collective-permute-start.14 = (bf16[64,384]{1,0:T(8,128)(2,1)S(1)}, bf16[64,384]{1,0:T(8,128)(2,1)S(1)}, u32[]{:S(2)}, u32[]{:S(2)}) collective-permute-start(bf16[64,384]{1,0:T(8,128)(2,1)S(1)} %get-tuple-element.88), channel_id=1, source_target_pairs={{0,16},{4,20},{8,24},{12,28},{16,0},{20,4},{24,8},{28,12},{1,17},{... | collective-permute-start | bytes 147464 | tf_op jit(solution)/shard_map/ppermute | solution.py:38
  35.6 1.6 %collective-permute-start.20 = (bf16[128,384]{1,0:T(8,128)(2,1)S(1)}, bf16[128,384]{1,0:T(8,128)(2,1)S(1)}, u32[]{:S(2)}, u32[]{:S(2)}) collective-permute-start(bf16[128,384]{1,0:T(8,128)(2,1)S(1)} %get-tuple-element.97), channel_id=1, source_target_pairs={{0,2},{1,3},{2,0},{3,1},{4,6},{5,7},{6,4},{7,5},{8,10},{9,11},{10,... | collective-permute-start | bytes 294920 | tf_op jit(solution)/shard_map/ppermute | solution.py:38
  38.2 2.1 %collective-permute-start.19 = (bf16[128,384]{1,0:T(8,128)(2,1)S(1)}, bf16[128,384]{1,0:T(8,128)(2,1)S(1)}, u32[]{:S(2)}, u32[]{:S(2)}) collective-permute-start(bf16[128,384]{1,0:T(8,128)(2,1)S(1)} %get-tuple-element.96), channel_id=1, source_target_pairs={{0,2},{1,3},{2,0},{3,1},{4,6},{5,7},{6,4},{7,5},{8,10},{9,11},{10,... | collective-permute-start | bytes 294920 | tf_op jit(solution)/shard_map/ppermute | solution.py:38
  40.3 4.2 %collective-permute-start.23 = (bf16[128,384]{1,0:T(8,128)(2,1)S(1)}, bf16[128,384]{1,0:T(8,128)(2,1)S(1)}, u32[]{:S(2)}, u32[]{:S(2)}) collective-permute-start(bf16[128,384]{1,0:T(8,128)(2,1)S(1)} %get-tuple-element.102), channel_id=1, source_target_pairs={{0,1},{1,0},{2,3},{3,2},{4,5},{5,4},{6,7},{7,6},{8,9},{9,8},{10,11... | collective-permute-start | bytes 294920 | tf_op jit(solution)/shard_map/ppermute | solution.py:38
  44.7 3.1 %collective-permute-start.22 = (bf16[128,384]{1,0:T(8,128)(2,1)S(1)}, bf16[128,384]{1,0:T(8,128)(2,1)S(1)}, u32[]{:S(2)}, u32[]{:S(2)}) collective-permute-start(bf16[128,384]{1,0:T(8,128)(2,1)S(1)} %get-tuple-element.101), channel_id=1, source_target_pairs={{0,1},{1,0},{2,3},{3,2},{4,5},{5,4},{6,7},{7,6},{8,9},{9,8},{10,11... | collective-permute-start | bytes 294920 | tf_op jit(solution)/shard_map/ppermute | solution.py:38
  48.1 2.1 %collective-permute-start.21 = (bf16[128,384]{1,0:T(8,128)(2,1)S(1)}, bf16[128,384]{1,0:T(8,128)(2,1)S(1)}, u32[]{:S(2)}, u32[]{:S(2)}) collective-permute-start(bf16[128,384]{1,0:T(8,128)(2,1)S(1)} %get-tuple-element.100), channel_id=1, source_target_pairs={{0,1},{1,0},{2,3},{3,2},{4,5},{5,4},{6,7},{7,6},{8,9},{9,8},{10,11... | collective-permute-start | bytes 294920 | tf_op jit(solution)/shard_map/ppermute | solution.py:38
  50.1 1.3 %last0.1.refs_4_ = bf16[768,1152]{1,0:T(8,128)(2,1)} custom-call(bf16[256,256]{1,0:T(8,128)(2,1)S(1)} %get-tuple-element.56.refs_0_, bf16[768,256]{1,0:T(8,128)(2,1)S(1)} %copy-done, bf16[128,384]{1,0:T(8,128)(2,1)S(1)} %get-tuple-element.94.refs_5_.refs_2_, bf16[128,384]{1,0:T(8,128)(2,1)S(1)} %collective-permute-done.23.refs_3_, ...), custom_call_target="tpu_custom_call" | custom-call | flops 600000000 | tf_op jit(solution)/shard_map/last0/pallas_call | solution.py:63
  51.4 1.3 %last384.1.refs_4_ = bf16[768,1152]{1,0:T(8,128)(2,1)} custom-call(bf16[256,256]{1,0:T(8,128)(2,1)S(1)} %get-tuple-element.56.refs_0_, bf16[768,256]{1,0:T(8,128)(2,1)S(1)} %copy-done, bf16[128,384]{1,0:T(8,128)(2,1)S(1)} %get-tuple-element.98.refs_3_.refs_4_.refs_2_, ...), custom_call_target="tpu_custom_call", output_to_operand_aliasing={{}: (4, {})} | custom-call | flops 600000000 | tf_op jit(solution)/shard_map/last384/pallas_call | solution.py:63
  52.7 1.3 %last768.1 = bf16[768,1152]{1,0:T(8,128)(2,1)} custom-call(bf16[256,256]{1,0:T(8,128)(2,1)S(1)} %get-tuple-element.56.refs_0_, bf16[768,256]{1,0:T(8,128)(2,1)S(1)} %copy-done, bf16[128,384]{1,0:T(8,128)(2,1)S(1)} %get-tuple-element.99.refs_5_.refs_2_, bf16[128,384]{1,0:T(8,128)(2,1)S(1)} %collective-permute-done.21.refs_3_, ...), custom_call_target="tpu_custom_call", output_to_operand_aliasing={{}: (4, {})} | custom-call | flops 600000000 | tf_op jit(solution)/shard_map/last768/pallas_call | solution.py:63
  (54 shorter events, 6.0 us)
Async XLA Ops:
  2.5 6.3 %collective-permute-start.1 = (bf16[128,384]{1,0:T(8,128)(2,1)S(1)}, bf16[128,384]{1,0:T(8,128)(2,1)S(1)}, u32[]{:S(2)}, u32[]{:S(2)}) collective-permute-start(bf16[128,384]{1,0:T(8,128)(2,1)S(1)} %get-tuple-element.64), channel_id=1, source_target_pairs={{0,1},{1,0},{2,3},{3,2},{4,5},{5,4},{6,7},{7,6},{8,9},{9,8},{10,11... | collective-permute-start | bytes 294920 | tf_op jit(solution)/shard_map/ppermute | solution.py:38
  6.5 10.7 %collective-permute-start = (bf16[128,384]{1,0:T(8,128)(2,1)S(1)}, bf16[128,384]{1,0:T(8,128)(2,1)S(1)}, u32[]{:S(2)}, u32[]{:S(2)}) collective-permute-start(bf16[128,384]{1,0:T(8,128)(2,1)S(1)} %get-tuple-element.62), channel_id=1, source_target_pairs={{0,1},{1,0},{2,3},{3,2},{4,5},{5,4},{6,7},{7,6},{8,9},{9,8},{10,11... | collective-permute-start | bytes 294920 | tf_op jit(solution)/shard_map/ppermute | solution.py:38
  6.6 7.8 %collective-permute-start.3 = (bf16[128,384]{1,0:T(8,128)(2,1)S(1)}, bf16[128,384]{1,0:T(8,128)(2,1)S(1)}, u32[]{:S(2)}, u32[]{:S(2)}) collective-permute-start(bf16[128,384]{1,0:T(8,128)(2,1)S(1)} %get-tuple-element.68), channel_id=1, source_target_pairs={{0,1},{1,0},{2,3},{3,2},{4,5},{5,4},{6,7},{7,6},{8,9},{9,8},{10,11... | collective-permute-start | bytes 294920 | tf_op jit(solution)/shard_map/ppermute | solution.py:38
  9.1 7.8 %collective-permute-start.2 = (bf16[128,384]{1,0:T(8,128)(2,1)S(1)}, bf16[128,384]{1,0:T(8,128)(2,1)S(1)}, u32[]{:S(2)}, u32[]{:S(2)}) collective-permute-start(bf16[128,384]{1,0:T(8,128)(2,1)S(1)} %get-tuple-element.66), channel_id=1, source_target_pairs={{0,2},{1,3},{2,0},{3,1},{4,6},{5,7},{6,4},{7,5},{8,10},{9,11},{10,... | collective-permute-start | bytes 294920 | tf_op jit(solution)/shard_map/ppermute | solution.py:38
  14.6 6.6 %collective-permute-start.6 = (bf16[128,384]{1,0:T(8,128)(2,1)S(1)}, bf16[128,384]{1,0:T(8,128)(2,1)S(1)}, u32[]{:S(2)}, u32[]{:S(2)}) collective-permute-start(bf16[128,384]{1,0:T(8,128)(2,1)S(1)} %get-tuple-element.74), channel_id=1, source_target_pairs={{0,2},{1,3},{2,0},{3,1},{4,6},{5,7},{6,4},{7,5},{8,10},{9,11},{10,... | collective-permute-start | bytes 294920 | tf_op jit(solution)/shard_map/ppermute | solution.py:38
  17.1 4.5 %collective-permute-start.5 = (bf16[128,384]{1,0:T(8,128)(2,1)S(1)}, bf16[128,384]{1,0:T(8,128)(2,1)S(1)}, u32[]{:S(2)}, u32[]{:S(2)}) collective-permute-start(bf16[128,384]{1,0:T(8,128)(2,1)S(1)} %get-tuple-element.73), channel_id=1, source_target_pairs={{0,4},{4,0},{8,12},{12,8},{16,20},{20,16},{24,28},{28,24},{1,5},{5... | collective-permute-start | bytes 294920 | tf_op jit(solution)/shard_map/ppermute | solution.py:38
  17.4 8.3 %collective-permute-start.4 = (bf16[128,384]{1,0:T(8,128)(2,1)S(1)}, bf16[128,384]{1,0:T(8,128)(2,1)S(1)}, u32[]{:S(2)}, u32[]{:S(2)}) collective-permute-start(bf16[128,384]{1,0:T(8,128)(2,1)S(1)} %get-tuple-element.72), channel_id=1, source_target_pairs={{0,2},{1,3},{2,0},{3,1},{4,6},{5,7},{6,4},{7,5},{8,10},{9,11},{10,... | collective-permute-start | bytes 294920 | tf_op jit(solution)/shard_map/ppermute | solution.py:38
  21.5 4.5 %collective-permute-start.11 = (bf16[128,384]{1,0:T(8,128)(2,1)S(1)}, bf16[128,384]{1,0:T(8,128)(2,1)S(1)}, u32[]{:S(2)}, u32[]{:S(2)}) collective-permute-start(bf16[128,384]{1,0:T(8,128)(2,1)S(1)} %get-tuple-element.82), channel_id=1, source_target_pairs={{0,4},{4,0},{8,12},{12,8},{16,20},{20,16},{24,28},{28,24},{1,5},{5... | collective-permute-start | bytes 294920 | tf_op jit(solution)/shard_map/ppermute | solution.py:38
  21.6 6.9 %collective-permute-start.8 = (bf16[64,384]{1,0:T(8,128)(2,1)S(1)}, bf16[64,384]{1,0:T(8,128)(2,1)S(1)}, u32[]{:S(2)}, u32[]{:S(2)}) collective-permute-start(bf16[64,384]{1,0:T(8,128)(2,1)S(1)} %get-tuple-element.79), channel_id=1, source_target_pairs={{0,24},{4,28},{8,16},{12,20},{16,8},{20,12},{24,0},{28,4},{1,25},{... | collective-permute-start | bytes 147464 | tf_op jit(solution)/shard_map/ppermute | solution.py:38
  24.1 5.0 %collective-permute-start.9 = (bf16[64,384]{1,0:T(8,128)(2,1)S(1)}, bf16[64,384]{1,0:T(8,128)(2,1)S(1)}, u32[]{:S(2)}, u32[]{:S(2)}) collective-permute-start(bf16[64,384]{1,0:T(8,128)(2,1)S(1)} %get-tuple-element.80), channel_id=1, source_target_pairs={{0,8},{4,12},{8,0},{12,4},{16,24},{20,28},{24,16},{28,20},{1,9},{5... | collective-permute-start | bytes 147464 | tf_op jit(solution)/shard_map/ppermute | solution.py:38
  24.7 5.5 %collective-permute-start.10 = (bf16[64,384]{1,0:T(8,128)(2,1)S(1)}, bf16[64,384]{1,0:T(8,128)(2,1)S(1)}, u32[]{:S(2)}, u32[]{:S(2)}) collective-permute-start(bf16[64,384]{1,0:T(8,128)(2,1)S(1)} %get-tuple-element.81), channel_id=1, source_target_pairs={{0,16},{4,20},{8,24},{12,28},{16,0},{20,4},{24,8},{28,12},{1,17},{... | collective-permute-start | bytes 147464 | tf_op jit(solution)/shard_map/ppermute | solution.py:38
  25.9 5.9 %collective-permute-start.7 = (bf16[128,384]{1,0:T(8,128)(2,1)S(1)}, bf16[128,384]{1,0:T(8,128)(2,1)S(1)}, u32[]{:S(2)}, u32[]{:S(2)}) collective-permute-start(bf16[128,384]{1,0:T(8,128)(2,1)S(1)} %get-tuple-element.78), channel_id=1, source_target_pairs={{0,4},{4,0},{8,12},{12,8},{16,20},{20,16},{24,28},{28,24},{1,5},{5... | collective-permute-start | bytes 294920 | tf_op jit(solution)/shard_map/ppermute | solution.py:38
  26.0 7.3 %collective-permute-start.16 = (bf16[64,384]{1,0:T(8,128)(2,1)S(1)}, bf16[64,384]{1,0:T(8,128)(2,1)S(1)}, u32[]{:S(2)}, u32[]{:S(2)}) collective-permute-start(bf16[64,384]{1,0:T(8,128)(2,1)S(1)} %get-tuple-element.90), channel_id=1, source_target_pairs={{0,24},{4,28},{8,16},{12,20},{16,8},{20,12},{24,0},{28,4},{1,25},{... | collective-permute-start | bytes 147464 | tf_op jit(solution)/shard_map/ppermute | solution.py:38
  28.5 5.3 %collective-permute-start.17 = (bf16[64,384]{1,0:T(8,128)(2,1)S(1)}, bf16[64,384]{1,0:T(8,128)(2,1)S(1)}, u32[]{:S(2)}, u32[]{:S(2)}) collective-permute-start(bf16[64,384]{1,0:T(8,128)(2,1)S(1)} %get-tuple-element.91), channel_id=1, source_target_pairs={{0,8},{4,12},{8,0},{12,4},{16,24},{20,28},{24,16},{28,20},{1,9},{5... | collective-permute-start | bytes 147464 | tf_op jit(solution)/shard_map/ppermute | solution.py:38
  29.1 6.3 %collective-permute-start.18 = (bf16[64,384]{1,0:T(8,128)(2,1)S(1)}, bf16[64,384]{1,0:T(8,128)(2,1)S(1)}, u32[]{:S(2)}, u32[]{:S(2)}) collective-permute-start(bf16[64,384]{1,0:T(8,128)(2,1)S(1)} %get-tuple-element.92), channel_id=1, source_target_pairs={{0,16},{4,20},{8,24},{12,28},{16,0},{20,4},{24,8},{28,12},{1,17},{... | collective-permute-start | bytes 147464 | tf_op jit(solution)/shard_map/ppermute | solution.py:38
  30.4 6.9 %collective-permute-start.15 = (bf16[128,384]{1,0:T(8,128)(2,1)S(1)}, bf16[128,384]{1,0:T(8,128)(2,1)S(1)}, u32[]{:S(2)}, u32[]{:S(2)}) collective-permute-start(bf16[128,384]{1,0:T(8,128)(2,1)S(1)} %get-tuple-element.89), channel_id=1, source_target_pairs={{0,2},{1,3},{2,0},{3,1},{4,6},{5,7},{6,4},{7,5},{8,10},{9,11},{10,... | collective-permute-start | bytes 294920 | tf_op jit(solution)/shard_map/ppermute | solution.py:38
  31.8 5.6 %collective-permute-start.12 = (bf16[64,384]{1,0:T(8,128)(2,1)S(1)}, bf16[64,384]{1,0:T(8,128)(2,1)S(1)}, u32[]{:S(2)}, u32[]{:S(2)}) collective-permute-start(bf16[64,384]{1,0:T(8,128)(2,1)S(1)} %get-tuple-element.86), channel_id=1, source_target_pairs={{0,24},{4,28},{8,16},{12,20},{16,8},{20,12},{24,0},{28,4},{1,25},{... | collective-permute-start | bytes 147464 | tf_op jit(solution)/shard_map/ppermute | solution.py:38
  33.3 4.2 %collective-permute-start.13 = (bf16[64,384]{1,0:T(8,128)(2,1)S(1)}, bf16[64,384]{1,0:T(8,128)(2,1)S(1)}, u32[]{:S(2)}, u32[]{:S(2)}) collective-permute-start(bf16[64,384]{1,0:T(8,128)(2,1)S(1)} %get-tuple-element.87), channel_id=1, source_target_pairs={{0,8},{4,12},{8,0},{12,4},{16,24},{20,28},{24,16},{28,20},{1,9},{5... | collective-permute-start | bytes 147464 | tf_op jit(solution)/shard_map/ppermute | solution.py:38
  33.9 4.1 %collective-permute-start.14 = (bf16[64,384]{1,0:T(8,128)(2,1)S(1)}, bf16[64,384]{1,0:T(8,128)(2,1)S(1)}, u32[]{:S(2)}, u32[]{:S(2)}) collective-permute-start(bf16[64,384]{1,0:T(8,128)(2,1)S(1)} %get-tuple-element.88), channel_id=1, source_target_pairs={{0,16},{4,20},{8,24},{12,28},{16,0},{20,4},{24,8},{28,12},{1,17},{... | collective-permute-start | bytes 147464 | tf_op jit(solution)/shard_map/ppermute | solution.py:38
  35.6 8.9 %collective-permute-start.20 = (bf16[128,384]{1,0:T(8,128)(2,1)S(1)}, bf16[128,384]{1,0:T(8,128)(2,1)S(1)}, u32[]{:S(2)}, u32[]{:S(2)}) collective-permute-start(bf16[128,384]{1,0:T(8,128)(2,1)S(1)} %get-tuple-element.97), channel_id=1, source_target_pairs={{0,2},{1,3},{2,0},{3,1},{4,6},{5,7},{6,4},{7,5},{8,10},{9,11},{10,... | collective-permute-start | bytes 294920 | tf_op jit(solution)/shard_map/ppermute | solution.py:38
  38.2 9.6 %collective-permute-start.19 = (bf16[128,384]{1,0:T(8,128)(2,1)S(1)}, bf16[128,384]{1,0:T(8,128)(2,1)S(1)}, u32[]{:S(2)}, u32[]{:S(2)}) collective-permute-start(bf16[128,384]{1,0:T(8,128)(2,1)S(1)} %get-tuple-element.96), channel_id=1, source_target_pairs={{0,2},{1,3},{2,0},{3,1},{4,6},{5,7},{6,4},{7,5},{8,10},{9,11},{10,... | collective-permute-start | bytes 294920 | tf_op jit(solution)/shard_map/ppermute | solution.py:38
  40.3 9.9 %collective-permute-start.23 = (bf16[128,384]{1,0:T(8,128)(2,1)S(1)}, bf16[128,384]{1,0:T(8,128)(2,1)S(1)}, u32[]{:S(2)}, u32[]{:S(2)}) collective-permute-start(bf16[128,384]{1,0:T(8,128)(2,1)S(1)} %get-tuple-element.102), channel_id=1, source_target_pairs={{0,1},{1,0},{2,3},{3,2},{4,5},{5,4},{6,7},{7,6},{8,9},{9,8},{10,11... | collective-permute-start | bytes 294920 | tf_op jit(solution)/shard_map/ppermute | solution.py:38
  44.7 6.7 %collective-permute-start.22 = (bf16[128,384]{1,0:T(8,128)(2,1)S(1)}, bf16[128,384]{1,0:T(8,128)(2,1)S(1)}, u32[]{:S(2)}, u32[]{:S(2)}) collective-permute-start(bf16[128,384]{1,0:T(8,128)(2,1)S(1)} %get-tuple-element.101), channel_id=1, source_target_pairs={{0,1},{1,0},{2,3},{3,2},{4,5},{5,4},{6,7},{7,6},{8,9},{9,8},{10,11... | collective-permute-start | bytes 294920 | tf_op jit(solution)/shard_map/ppermute | solution.py:38
  48.1 4.7 %collective-permute-start.21 = (bf16[128,384]{1,0:T(8,128)(2,1)S(1)}, bf16[128,384]{1,0:T(8,128)(2,1)S(1)}, u32[]{:S(2)}, u32[]{:S(2)}) collective-permute-start(bf16[128,384]{1,0:T(8,128)(2,1)S(1)} %get-tuple-element.100), channel_id=1, source_target_pairs={{0,1},{1,0},{2,3},{3,2},{4,5},{5,4},{6,7},{7,6},{8,9},{9,8},{10,11... | collective-permute-start | bytes 294920 | tf_op jit(solution)/shard_map/ppermute | solution.py:38
  (5 other events, 28.1 us)

commit v13 on v12

v13 whole, which is shorter than its diff:
```python
import jax
import jax.numpy as jnp
from jax import lax
from jax.experimental import pallas as pl
from jax.experimental.pallas import tpu as pltpu
from jax.sharding import PartitionSpec as P

LANES = 128
SHARES = (3, 3, 3)
HEADS = ((0,), (1,), (2,))
TAILS = ((0,), (1,), (2,))
ENTRY = (0, 0, 1)
TURNS = {}
SPANS = {}
ROWS = 16
SCOPED = 8 * 2**20
MOST = 213 * 2**18
F32 = jnp.float32
BF16 = jnp.bfloat16
WHOLE = pl.BlockSpec(memory_space=pltpu.VMEM)
SCALARS = pl.BlockSpec(memory_space=pltpu.SMEM)
PLACE = pl.BlockSpec(memory_space=pl.ANY)
HBM = pl.BlockSpec(memory_space=pltpu.HBM)


def shares(columns, weights):
    tiles = columns // LANES
    if tiles < len(weights):
        return [columns]
    edges = [round(tiles * sum(weights[:i]) / sum(weights)) * LANES for i in range(len(weights))]
    edges.append(columns)
    return [high - low for low, high in zip(edges[:-1], edges[1:])]


def swap(block, axis, distances):
    count = lax.axis_size(axis)
    return lax.ppermute(block, axis, [(i, i ^ distances[i & 1]) for i in range(count)])


def swapped(matrix, axis, flag):
    half = matrix.shape[axis] // 2
    low = lax.slice_in_dim(matrix, 0, half, axis=axis)
    high = lax.slice_in_dim(matrix, half, 2 * half, axis=axis)
    return jnp.where(flag == 1, jnp.concatenate([high, low], axis=axis), matrix)


def matmul(left, right):
    return lax.dot_general(left, right, (((1,), (0,)), ((), ())), preferred_element_type=F32)


def span(name):
    flops = SPANS.get(name.split("_")[0], 0)
    return pl.CostEstimate(flops=flops, bytes_accessed=0, transcendentals=0)


def call(kernel, name, outs, specs, operands, after, limit=SCOPED, **more):
    extra = [] if after is None else [after]

    def body(*refs):
        kernel(*refs[: len(operands)], *refs[len(operands) + len(extra) :])

    return pl.pallas_call(
        body,
        name=name,
        in_specs=specs + [PLACE] * len(extra),
        out_shape=outs,
        compiler_params=pltpu.CompilerParams(vmem_limit_bytes=limit),
        **more,
    )(*operands, *extra)


def prepare(name, node_order, places_out, places_in, right, middle, left, held):
    width = middle.shape[-1]
    groups = node_order.shape[0]
    block = width // groups

    orders = bit_orders(groups)

    def slot(place, core):
        return jnp.where(core == 1, slot_number(place, orders[1]), slot_number(place, orders[0]))

    def kernel(node_order, right, middle, left, *refs):
        right0, right1, middle0, left0, left1, *passed = refs[len(held) :]
        for block_in, block_out in zip(refs[: len(held)], passed):
            block_out[...] = block_in[...]
        place, group = lax.axis_index("sub"), lax.axis_index("mid")
        bit0, bit1 = place & 1, place >> 1 & 1
        right0[...] = swapped(swapped(right[0, 0], 1, bit0), 0, bit1)
        place = lax.broadcasted_iota(jnp.int32, (width, 1), 0)
        source = place % block
        for i, p in enumerate(places_out):
            piece = node_order[slot(p, group & 1 ^ p & 1) ^ group] * block
            source += jnp.where(place // block == i, piece, 0)
        across = lax.broadcasted_iota(jnp.int32, (width, width), 1)
        pick = jnp.where(across == source, 1.0, 0.0).astype(BF16)
        right1[...] = matmul(pick, swapped(right[0, 1], 1, bit1)).astype(BF16)
        place = lax.broadcasted_iota(jnp.int32, (1, width), 1)
        source = place % block
        for i, p in enumerate(places_in):
            piece = (slot(p, group & 1) ^ group) * block
            source += jnp.where(place // block == i, piece, 0)
        down = lax.broadcasted_iota(jnp.int32, (width, width), 0)
        pick = jnp.where(down == source, 1.0, 0.0).astype(BF16)
        middle0[...] = swapped(matmul(middle[0], pick).astype(BF16), 0, bit1)
        left0[...] = swapped(swapped(left[0, 0], 1, bit1), 0, bit0)
        left1[...] = swapped(left[0, 1], 1, bit0)

    return call(
        kernel,
        name,
        [jax.ShapeDtypeStruct((width, width), BF16)] * 5
        + [jax.ShapeDtypeStruct(block.shape, BF16) for block in held],
        [SCALARS] + [WHOLE] * (3 + len(held)),
        [node_order, right, middle, left] + held,
        None,
        out_specs=[WHOLE] * (5 + len(held)),
        cost_estimate=span(name),
    )


def row_pieces(rows, pieces):
    return pieces if rows % (pieces * ROWS) == 0 else 1


def opening(name, basis, signal, widths, groups):
    rows, width = basis.shape
    half = width // 2
    pieces = row_pieces(rows, 6)
    depth = rows // pieces
    lows = [sum(widths[:i]) for i in range(len(widths))]
    all_widths = widths + [sum(widths[i] for i in group) for group in groups]

    def kernel(basis, signal, *refs):
        outs, (basis_here, signal_here, arrived, basis_arrived) = refs[:-4], refs[-4:]
        fetch_basis = pltpu.make_async_copy(basis, basis_here, basis_arrived)
        fetch_basis.start()
        copies = []
        for i in range(pieces):
            part = pl.ds(i * depth, depth)
            copies.append(
                pltpu.make_async_copy(signal.at[part], signal_here.at[part], arrived.at[i])
            )
            copies[-1].start()
        fetch_basis.wait()
        flipped = swapped(basis_here[...].T, 0, lax.axis_index("sub") & 1)
        for copy in copies:
            copy.wait()
        for group, send in zip(groups, outs[len(widths) :]):
            for i in group:
                low, wide = lows[i], widths[i]
                total = matmul(flipped, signal_here[:, low : low + wide])
                outs[i][...] = total[:half].astype(BF16)
                place = low - lows[group[0]]
                send[:, place : place + wide] = total[half:].astype(BF16)

    outs = call(
        kernel,
        name,
        [jax.ShapeDtypeStruct((half, wide), BF16) for wide in all_widths],
        [HBM, HBM],
        [basis, signal],
        None,
        limit=MOST,
        out_specs=[WHOLE] * len(all_widths),
        scratch_shapes=[
            pltpu.VMEM((rows, width), BF16),
            pltpu.VMEM(signal.shape, BF16),
            pltpu.SemaphoreType.DMA((pieces,)),
            pltpu.SemaphoreType.DMA,
        ],
        cost_estimate=span(name),
    )
    return outs[: len(widths)], outs[len(widths) :]


def level(name, weight, blocks, low, wide, count, before, after):
    width = weight.shape[0]
    depth = width // count
    ahead = sum(block.shape[1] for block in before)

    def kernel(weight, *refs):
        ins, outs = refs[: len(blocks)], refs[len(blocks) + len(before) :]
        here = [slice(low, low + wide) if ref.shape[1] > wide else slice(None) for ref in ins]
        stacked = jnp.concatenate([ref[:, part] for ref, part in zip(ins, here)], axis=0)
        total = matmul(weight[...], stacked)
        for i, out in enumerate(outs):
            value = total[i * depth : (i + 1) * depth].astype(BF16)
            if before and i == count - 1:
                out[:, :ahead] = refs[len(blocks)][...]
                out[:, ahead:] = value
            else:
                out[...] = value

    widths = [wide] * (count - 1) + [ahead + wide]
    return call(
        kernel,
        name,
        [jax.ShapeDtypeStruct((depth, columns), BF16) for columns in widths],
        [WHOLE] * (1 + len(blocks) + len(before)),
        [weight] + blocks + before,
        after,
        out_specs=[WHOLE] * count,
        cost_estimate=span(name),
    )


def bit_orders(groups):
    bits = list(range(1, groups.bit_length() - 1))
    return [bits[::-1], bits]


def slot_number(place, order):
    return place & 1 | sum((place >> 1 + t & 1) << bit for t, bit in enumerate(order))


def by_bit(places, bit):
    return [[p for p in places if p >> bit & 1 == value] for value in range(2)]


def layouts_of(groups):
    layouts = [by_bit(range(groups), 0)]
    for bit in range(1, groups.bit_length() - 1):
        layouts.append(by_bit(sum(layouts[-1], []), bit))
    return layouts


def regroup(name, blocks, layout, bit, block, after):
    columns = blocks[0].shape[1]
    place = {r: (i, j) for i, held in enumerate(layout) for j, r in enumerate(held)}
    wanted = by_bit(sum(layout, []), bit)

    def sort(values):
        parts = [[values[place[r][0]][place[r][1] * block :][:block] for r in held] for held in wanted]
        return [jnp.concatenate(part, axis=0) for part in parts]

    if block % ROWS:
        return sort(blocks), wanted

    def kernel(*refs):
        for ref, value in zip(refs[len(blocks) :], sort([ref[...] for ref in refs[: len(blocks)]])):
            ref[...] = value

    outs = call(
        kernel,
        name,
        [jax.ShapeDtypeStruct((len(held) * block, columns), BF16) for held in wanted],
        [WHOLE] * len(blocks),
        blocks,
        after,
        out_specs=[WHOLE] * len(wanted),
        cost_estimate=span(name),
    )
    return list(outs), wanted


def last(name, weight, basis, keeps, got, before, low, columns, after):
    rows, width = basis.shape
    wide = got.shape[1]
    pieces = row_pieces(rows, 6)
    depth = rows // pieces
    given = [] if before is None else [before]

    def kernel(weight, basis, got, *refs):
        out, here, left = refs[len(keeps) + len(given) :]
        keep = jnp.concatenate([ref[...] for ref in refs[: len(keeps)]], axis=1)
        stacked = jnp.concatenate([keep, got[...]], axis=0)
        coeffs = matmul(weight[...], stacked).astype(BF16)
        copies = []
        for i in range(pieces):
            part = pl.ds(i * depth, depth)
            here[part, :] = matmul(basis[part, :], coeffs).astype(BF16)
            copy = pltpu.make_async_copy(here.at[part], out.at[part, pl.ds(low, wide)], left.at[i])
            copy.start()
            copies.append(copy)
        for copy in copies:
            copy.wait()

    return call(
        kernel,
        name,
        jax.ShapeDtypeStruct((rows, columns), BF16),
        [WHOLE] * (3 + len(keeps)) + [HBM] * len(given),
        [weight, basis, got] + keeps + given,
        after,
        out_specs=HBM,
        scratch_shapes=[pltpu.VMEM((rows, wide), BF16), pltpu.SemaphoreType.DMA((pieces,))],
        input_output_aliases={3 + len(keeps): 0} if given else {},
        cost_estimate=span(name),
    )


def local(signal, col_basis, right_coupling, middle_coupling, left_coupling, row_basis, node_order):
    groups = lax.axis_size("mid")
    width = col_basis.shape[1]
    block = width // groups
    columns = signal.shape[1]
    chunks = shares(columns, SHARES)
    lows = [sum(chunks[:i]) for i in range(len(chunks))]
    whole = len(chunks) == len(SHARES)
    heads = HEADS if whole else ((0,),)
    tails = TAILS if whole else ((0,),)
    layouts = layouts_of(groups)
    routes = [(1, 1)] + [(1 << one, 1 << other) for one, other in zip(*bit_orders(groups))]

    keeps, sends = opening("opening", col_basis, signal, chunks, heads)
    right0, right1, middle, left0, left1, *later = prepare(
        "prepare",
        node_order,
        sum(layouts[0], []),
        sum(layouts[-1], []),
        right_coupling,
        middle_coupling,
        left_coupling,
        list(sends[1:]),
    )
    gots = {}
    for group, send in zip(heads, [sends[0]] + later):
        got = swap(send, "sub", (1, 1))
        for i in group:
            gots[i] = (got, lows[i] - lows[group[0]])

    out, after = None, right0
    waiting, pops, entered = [], 0, 0
    parked = {}
    while waiting or entered < len(chunks):
        if entered < len(chunks) and (pops >= ENTRY[entered] or not waiting):
            waiting.append((1, entered, [keeps[entered], gots[entered][0]]))
            entered += 1
            continue
        turn = TURNS.get(pops, 0)
        stage, i, blocks = waiting.pop(turn if turn < len(waiting) else 0)
        pops += 1
        wide = chunks[i]
        if stage == 1:
            results = level(f"right0_{i}", right0, blocks, gots[i][1], wide, 2, [], after)
            axis, route = "sub", (2, 2)
        elif stage == 2:
            results = level(f"right1_{i}", right1, blocks, 0, wide, 2, [], after)
            axis, route = "mid", routes[0]
        elif stage < 2 + len(routes):
            name = f"regroup{stage}_{i}"
            results, _ = regroup(name, blocks, layouts[stage - 3], stage - 2, block, after)
            axis, route = "mid", routes[stage - 2]
        elif stage == 2 + len(routes):
            results = level(f"middle_{i}", middle, blocks, 0, wide, 2, [], after)
            axis, route = "sub", (2, 2)
        elif stage == 3 + len(routes):
            group = next(group for group in tails if i in group)
            before = [parked[group[0]][-1]] if i != group[0] else []
            results = level(f"left0_{i}", left0, blocks, 0, wide, 2, before, after)
            parked[group[0]] = parked.get(group[0], [])[:-1] + list(results)
            if i != group[-1]:
                after = results[0]
                continue
            results = parked[group[0]]
            got = swap(results[-1], "sub", (1, 1))
            waiting.append((stage + 1, group[0], [results[:-1], got]))
            after = results[-2]
            continue
        else:
            name = f"last_{i}"
            out = last(name, left1, row_basis, *blocks, out, lows[i], columns, after)
            continue
        after = results[0]
        waiting.append((stage + 1, i, [results[0], swap(results[1], axis, route)]))
    return out


def solution(mesh):
    return jax.shard_map(
        local,
        mesh=mesh,
        in_specs=(
            P(("mid", "sub"), None),
            P(("mid", "sub"), None),
            P(("mid", "sub"), None, None, None),
            P(("mid", "sub"), None, None),
            P(("mid", "sub"), None, None, None),
            P(("mid", "sub"), None),
            P(),
        ),
        out_specs=P(("mid", "sub"), None),
        check_vma=False,
    )
```

time: 54.1 us -> 54.5 us (level)
  waiting for transfers between devices: 7.06 us -> 14.1 us
  starting transfers between devices: 36.8 us -> 30 us
    ppermute x24 -> x21, waiting for transfers between devices: 7.06 us -> 14.1 us  [swap(): lax.ppermute(block, axis, [(i, i ^ distances[i & 1]) for i in range(count)])]
    ppermute x24 -> x21, starting transfers between devices: 36.8 us -> 30 us  [swap(): lax.ppermute(block, axis, [(i, i ^ distances[i & 1]) for i in range(count)])]
    pallas_call x20 -> x23, Pallas kernels: 9.87 us -> 9.93 us  [call(): pl.pallas_call(body, name=name, in_specs=specs + [PLACE] * len(extra), ou...]
  transfers between devices with their start and end apart: 24 -> 21, of which waited for: 6 -> 9; matrix products, arithmetic and copies ran while one was open for 0% -> 0% of each run, Pallas kernels for 11% -> 11%
where the time goes in v13:
time: 54.5 us; the launch traced here: 54.3 us
  starting transfers between devices  30 us (55%)
  waiting for transfers between devices  14.1 us (26%)
  Pallas kernels  9.93 us (18%)
    ppermute x21, starting transfers between devices, swap(): lax.ppermute(block, axis, [(i, i ^ distances[i & 1]) for i in range(count)])  30 us
    ppermute x21, waiting for transfers between devices, swap(): lax.ppermute(block, axis, [(i, i ^ distances[i & 1]) for i in range(count)])  14.1 us
    pallas_call x23, Pallas kernels, call(): pl.pallas_call(body, name=name, in_specs=specs + [PLACE] * len(extra), ou...  9.93 us
  transfers between devices with their start and end apart: 21, of which 9 were waited for; matrix products, arithmetic and copies ran while one was open for 0% of the time, Pallas kernels for 11%

profile of v13, /device:TPU:0, one launch (start us, length us, event | category | flops | bytes accessed | tf_op | source)
XLA Modules:
  0.0 54.3 jit_solution(9912675523876687113)
XLA Ops:
  0.0 2.5 %opening.1 = (bf16[128,384]{1,0:T(8,128)(2,1)S(1)}, bf16[128,384]{1,0:T(8,128)(2,1)S(1)}, bf16[128,384]{1,0:T(8,128)(2,1)S(1)}, bf16[128,384]{1,0:T(8,128)(2,1)S...) custom-call(bf16[768,256]{1,0:T(8,128)(2,1)} %refs_0_.2, bf16[768,1152]{1,0:T(8,128)(2,1)} %refs_1_.5), custom_call_target="tpu_custom_call" | custom-call | tf_op jit(solution)/shard_map/opening/pallas_call | solution.py:62
  2.5 3.1 %collective-permute-start.1 = (bf16[128,384]{1,0:T(8,128)(2,1)S(1)}, bf16[128,384]{1,0:T(8,128)(2,1)S(1)}, u32[]{:S(2)}, u32[]{:S(2)}) collective-permute-start(bf16[128,384]{1,0:T(8,128)(2,1)S(1)} %get-tuple-element.64), channel_id=1, source_target_pairs={{0,1},{1,0},{2,3},{3,2},{4,5},{5,4},{6,7},{7,6},{8,9},{9,8},{10,11... | collective-permute-start | bytes 294920 | tf_op jit(solution)/shard_map/ppermute | solution.py:37
  5.6 0.9 %prepare.1 = (bf16[256,256]{1,0:T(8,128)(2,1)S(1)}, bf16[256,256]{1,0:T(8,128)(2,1)S(1)}, bf16[256,256]{1,0:T(8,128)(2,1)S(1)}, bf16[256,256]{1,0:T(8,128)(2,1)S...) custom-call(s32[8]{0:T(128)S(1)} %copy-done.4, ...), custom_call_target="tpu_custom_call" | custom-call | tf_op jit(solution)/shard_map/prepare/pallas_call | solution.py:62
  6.6 2.1 %collective-permute-done.1.refs_2_ = bf16[128,384]{1,0:T(8,128)(2,1)S(1)} collective-permute-done((bf16[128,384]{1,0:T(8,128)(2,1)S(1)}, bf16[128,384]{1,0:T(8,128)(2,1)S(1)}, u32[]{:S(2)}, u32[]{:S(2)}) %collective-permute-start.1) | collective-permute-done | bytes 98336 | tf_op jit(solution)/shard_map/ppermute | solution.py:37
  9.0 2.7 %collective-permute-start.2 = (bf16[128,384]{1,0:T(8,128)(2,1)S(1)}, bf16[128,384]{1,0:T(8,128)(2,1)S(1)}, u32[]{:S(2)}, u32[]{:S(2)}) collective-permute-start(bf16[128,384]{1,0:T(8,128)(2,1)S(1)} %get-tuple-element.66), channel_id=1, source_target_pairs={{0,2},{1,3},{2,0},{3,1},{4,6},{5,7},{6,4},{7,5},{8,10},{9,11},{10,... | collective-permute-start | bytes 294920 | tf_op jit(solution)/shard_map/ppermute | solution.py:37
  11.7 2.5 %collective-permute-start = (bf16[128,384]{1,0:T(8,128)(2,1)S(1)}, bf16[128,384]{1,0:T(8,128)(2,1)S(1)}, u32[]{:S(2)}, u32[]{:S(2)}) collective-permute-start(bf16[128,384]{1,0:T(8,128)(2,1)S(1)} %get-tuple-element.62), channel_id=1, source_target_pairs={{0,1},{1,0},{2,3},{3,2},{4,5},{5,4},{6,7},{7,6},{8,9},{9,8},{10,11... | collective-permute-start | bytes 294920 | tf_op jit(solution)/shard_map/ppermute | solution.py:37
  15.4 1.3 %collective-permute-done.refs_2_ = bf16[128,384]{1,0:T(8,128)(2,1)S(1)} collective-permute-done((bf16[128,384]{1,0:T(8,128)(2,1)S(1)}, bf16[128,384]{1,0:T(8,128)(2,1)S(1)}, u32[]{:S(2)}, u32[]{:S(2)}) %collective-permute-start) | collective-permute-done | bytes 98336 | tf_op jit(solution)/shard_map/ppermute | solution.py:37
  17.0 2.4 %collective-permute-start.4 = (bf16[128,384]{1,0:T(8,128)(2,1)S(1)}, bf16[128,384]{1,0:T(8,128)(2,1)S(1)}, u32[]{:S(2)}, u32[]{:S(2)}) collective-permute-start(bf16[128,384]{1,0:T(8,128)(2,1)S(1)} %get-tuple-element.72), channel_id=1, source_target_pairs={{0,2},{1,3},{2,0},{3,1},{4,6},{5,7},{6,4},{7,5},{8,10},{9,11},{10,... | collective-permute-start | bytes 294920 | tf_op jit(solution)/shard_map/ppermute | solution.py:37
  19.4 1.6 %collective-permute-done.6.refs_2_ = bf16[128,384]{1,0:T(8,128)(2,1)S(1)} collective-permute-done((bf16[128,384]{1,0:T(8,128)(2,1)S(1)}, bf16[128,384]{1,0:T(8,128)(2,1)S(1)}, u32[]{:S(2)}, u32[]{:S(2)}) %collective-permute-start.6) | collective-permute-done | bytes 98336 | tf_op jit(solution)/shard_map/ppermute | solution.py:37
  21.3 1.6 %collective-permute-start.8 = (bf16[128,384]{1,0:T(8,128)(2,1)S(1)}, bf16[128,384]{1,0:T(8,128)(2,1)S(1)}, u32[]{:S(2)}, u32[]{:S(2)}) collective-permute-start(bf16[128,384]{1,0:T(8,128)(2,1)S(1)} %get-tuple-element.79), channel_id=1, source_target_pairs={{0,16},{4,12},{8,24},{12,4},{16,0},{20,28},{24,8},{28,20},{1,17},{... | collective-permute-start | bytes 294920 | tf_op jit(solution)/shard_map/ppermute | solution.py:37
  23.4 1.6 %collective-permute-start.12 = (bf16[128,384]{1,0:T(8,128)(2,1)S(1)}, bf16[128,384]{1,0:T(8,128)(2,1)S(1)}, u32[]{:S(2)}, u32[]{:S(2)}) collective-permute-start(bf16[128,384]{1,0:T(8,128)(2,1)S(1)} %get-tuple-element.86), channel_id=1, source_target_pairs={{0,16},{4,12},{8,24},{12,4},{16,0},{20,28},{24,8},{28,20},{1,17},{... | collective-permute-start | bytes 294920 | tf_op jit(solution)/shard_map/ppermute | solution.py:37
  25.0 1.0 %collective-permute-done.8.refs_1_ = bf16[128,384]{1,0:T(8,128)(2,1)S(1)} collective-permute-done((bf16[128,384]{1,0:T(8,128)(2,1)S(1)}, bf16[128,384]{1,0:T(8,128)(2,1)S(1)}, u32[]{:S(2)}, u32[]{:S(2)}) %collective-permute-start.8) | collective-permute-done | bytes 98336 | tf_op jit(solution)/shard_map/ppermute | solution.py:37
  26.0 1.6 %collective-permute-start.11 = (bf16[128,384]{1,0:T(8,128)(2,1)S(1)}, bf16[128,384]{1,0:T(8,128)(2,1)S(1)}, u32[]{:S(2)}, u32[]{:S(2)}) collective-permute-start(bf16[128,384]{1,0:T(8,128)(2,1)S(1)} %get-tuple-element.85), channel_id=1, source_target_pairs={{0,8},{4,20},{8,0},{12,28},{16,24},{20,4},{24,16},{28,12},{1,9},{5... | collective-permute-start | bytes 294920 | tf_op jit(solution)/shard_map/ppermute | solution.py:37
  27.6 1.6 %collective-permute-start.10 = (bf16[128,384]{1,0:T(8,128)(2,1)S(1)}, bf16[128,384]{1,0:T(8,128)(2,1)S(1)}, u32[]{:S(2)}, u32[]{:S(2)}) collective-permute-start(bf16[128,384]{1,0:T(8,128)(2,1)S(1)} %get-tuple-element.84), channel_id=1, source_target_pairs={{0,16},{4,12},{8,24},{12,4},{16,0},{20,28},{24,8},{28,20},{1,17},{... | collective-permute-start | bytes 294920 | tf_op jit(solution)/shard_map/ppermute | solution.py:37
  29.8 1.9 %collective-permute-done.11.refs_2_ = bf16[128,384]{1,0:T(8,128)(2,1)S(1)} collective-permute-done((bf16[128,384]{1,0:T(8,128)(2,1)S(1)}, bf16[128,384]{1,0:T(8,128)(2,1)S(1)}, u32[]{:S(2)}, u32[]{:S(2)}) %collective-permute-start.11) | collective-permute-done | bytes 98336 | tf_op jit(solution)/shard_map/ppermute | solution.py:37
  32.0 0.8 %collective-permute-start.14 = (bf16[128,384]{1,0:T(8,128)(2,1)S(1)}, bf16[128,384]{1,0:T(8,128)(2,1)S(1)}, u32[]{:S(2)}, u32[]{:S(2)}) collective-permute-start(bf16[128,384]{1,0:T(8,128)(2,1)S(1)} %get-tuple-element.91), channel_id=1, source_target_pairs={{0,2},{1,3},{2,0},{3,1},{4,6},{5,7},{6,4},{7,5},{8,10},{9,11},{10,... | collective-permute-start | bytes 294920 | tf_op jit(solution)/shard_map/ppermute | solution.py:37
  33.1 1.1 %collective-permute-start.13 = (bf16[128,384]{1,0:T(8,128)(2,1)S(1)}, bf16[128,384]{1,0:T(8,128)(2,1)S(1)}, u32[]{:S(2)}, u32[]{:S(2)}) collective-permute-start(bf16[128,384]{1,0:T(8,128)(2,1)S(1)} %get-tuple-element.90), channel_id=1, source_target_pairs={{0,8},{4,20},{8,0},{12,28},{16,24},{20,4},{24,16},{28,12},{1,9},{5... | collective-permute-start | bytes 294920 | tf_op jit(solution)/shard_map/ppermute | solution.py:37
  34.4 2.5 %collective-permute-start.17 = (bf16[128,384]{1,0:T(8,128)(2,1)S(1)}, bf16[128,384]{1,0:T(8,128)(2,1)S(1)}, u32[]{:S(2)}, u32[]{:S(2)}) collective-permute-start(bf16[128,384]{1,0:T(8,128)(2,1)S(1)} %get-tuple-element.97), channel_id=1, source_target_pairs={{0,2},{1,3},{2,0},{3,1},{4,6},{5,7},{6,4},{7,5},{8,10},{9,11},{10,... | collective-permute-start | bytes 294920 | tf_op jit(solution)/shard_map/ppermute | solution.py:37
  36.8 4.7 %collective-permute-done.14.refs_2_ = bf16[128,384]{1,0:T(8,128)(2,1)S(1)} collective-permute-done((bf16[128,384]{1,0:T(8,128)(2,1)S(1)}, bf16[128,384]{1,0:T(8,128)(2,1)S(1)}, u32[]{:S(2)}, u32[]{:S(2)}) %collective-permute-start.14) | collective-permute-done | bytes 98336 | tf_op jit(solution)/shard_map/ppermute | solution.py:37
  42.1 4.4 %collective-permute-start.20 = (bf16[128,384]{1,0:T(8,128)(2,1)S(1)}, bf16[128,384]{1,0:T(8,128)(2,1)S(1)}, u32[]{:S(2)}, u32[]{:S(2)}) collective-permute-start(bf16[128,384]{1,0:T(8,128)(2,1)S(1)} %get-tuple-element.102), channel_id=1, source_target_pairs={{0,1},{1,0},{2,3},{3,2},{4,5},{5,4},{6,7},{7,6},{8,9},{9,8},{10,11... | collective-permute-start | bytes 294920 | tf_op jit(solution)/shard_map/ppermute | solution.py:37
  47.9 2.3 %collective-permute-start.18 = (bf16[128,384]{1,0:T(8,128)(2,1)S(1)}, bf16[128,384]{1,0:T(8,128)(2,1)S(1)}, u32[]{:S(2)}, u32[]{:S(2)}) collective-permute-start(bf16[128,384]{1,0:T(8,128)(2,1)S(1)} %get-tuple-element.99), channel_id=1, source_target_pairs={{0,1},{1,0},{2,3},{3,2},{4,5},{5,4},{6,7},{7,6},{8,9},{9,8},{10,11... | collective-permute-start | bytes 294920 | tf_op jit(solution)/shard_map/ppermute | solution.py:37
  50.2 1.3 %last_0.1.refs_4_ = bf16[768,1152]{1,0:T(8,128)(2,1)} custom-call(bf16[256,256]{1,0:T(8,128)(2,1)S(1)} %get-tuple-element.56.refs_0_, bf16[768,256]{1,0:T(8,128)(2,1)S(1)} %copy-done, bf16[128,384]{1,0:T(8,128)(2,1)S(1)} %collective-permute-done.20.refs_2_, bf16[128,384]{1,0:T(8,128)(2,1)S(1)} %get-tuple-element.94.refs_3_, ...), custom_call_target="tpu_custom_call" | custom-call | tf_op jit(solution)/shard_map/last_0/pallas_call | solution.py:62
  51.8 1.3 %last_1.1.refs_4_ = bf16[768,1152]{1,0:T(8,128)(2,1)} custom-call(bf16[256,256]{1,0:T(8,128)(2,1)S(1)} %get-tuple-element.56.refs_0_, bf16[768,256]{1,0:T(8,128)(2,1)S(1)} %copy-done, bf16[128,384]{1,0:T(8,128)(2,1)S(1)} %collective-permute-done.19.refs_2_, bf16[128,384]{1,0:T(8,128)(2,1)S(1)} %get-tuple-element.98.refs_3_.refs_4_, ...), custom_call_target="tpu_custom_call", output_to_operand_aliasing={{}: (4, {})} | custom-call | tf_op jit(solution)/shard_map/last_1/pallas_call | solution.py:62
  53.1 1.3 %last_2.1 = bf16[768,1152]{1,0:T(8,128)(2,1)} custom-call(bf16[256,256]{1,0:T(8,128)(2,1)S(1)} %get-tuple-element.56.refs_0_, bf16[768,256]{1,0:T(8,128)(2,1)S(1)} %copy-done, bf16[128,384]{1,0:T(8,128)(2,1)S(1)} %collective-permute-done.18.refs_2_, bf16[128,384]{1,0:T(8,128)(2,1)S(1)} %get-tuple-element.100.refs_5_.refs_3_, ...), custom_call_target="tpu_custom_call", output_to_operand_aliasing={{}: (4, {})} | custom-call | tf_op jit(solution)/shard_map/last_2/pallas_call | solution.py:62
  (51 shorter events, 6.3 us)
Async XLA Ops:
  0.0 5.6 %copy-start.3 = (bf16[1,256,256]{2,1,0:T(8,128)(2,1)S(1)}, bf16[1,256,256]{2,1,0:T(8,128)(2,1)}, u32[]{:S(2)}) copy-start(bf16[1,256,256]{2,1,0:T(8,128)(2,1)} %refs_2_.1) | copy-start | bytes 393220
  0.0 5.6 %copy-start.1 = (bf16[1,2,256,256]{3,2,1,0:T(8,128)(2,1)S(1)}, bf16[1,2,256,256]{3,2,1,0:T(8,128)(2,1)}, u32[]{:S(2)}) copy-start(bf16[1,2,256,256]{3,2,1,0:T(8,128)(2,1)} %refs_1_.6) | copy-start | bytes 786436
  2.5 6.2 %collective-permute-start.1 = (bf16[128,384]{1,0:T(8,128)(2,1)S(1)}, bf16[128,384]{1,0:T(8,128)(2,1)S(1)}, u32[]{:S(2)}, u32[]{:S(2)}) collective-permute-start(bf16[128,384]{1,0:T(8,128)(2,1)S(1)} %get-tuple-element.64), channel_id=1, source_target_pairs={{0,1},{1,0},{2,3},{3,2},{4,5},{5,4},{6,7},{7,6},{8,9},{9,8},{10,11... | collective-permute-start | bytes 294920 | tf_op jit(solution)/shard_map/ppermute | solution.py:37
  6.5 7.7 %collective-permute-start.3 = (bf16[128,384]{1,0:T(8,128)(2,1)S(1)}, bf16[128,384]{1,0:T(8,128)(2,1)S(1)}, u32[]{:S(2)}, u32[]{:S(2)}) collective-permute-start(bf16[128,384]{1,0:T(8,128)(2,1)S(1)} %get-tuple-element.68), channel_id=1, source_target_pairs={{0,1},{1,0},{2,3},{3,2},{4,5},{5,4},{6,7},{7,6},{8,9},{9,8},{10,11... | collective-permute-start | bytes 294920 | tf_op jit(solution)/shard_map/ppermute | solution.py:37
  9.0 6.2 %collective-permute-start.2 = (bf16[128,384]{1,0:T(8,128)(2,1)S(1)}, bf16[128,384]{1,0:T(8,128)(2,1)S(1)}, u32[]{:S(2)}, u32[]{:S(2)}) collective-permute-start(bf16[128,384]{1,0:T(8,128)(2,1)S(1)} %get-tuple-element.66), channel_id=1, source_target_pairs={{0,2},{1,3},{2,0},{3,1},{4,6},{5,7},{6,4},{7,5},{8,10},{9,11},{10,... | collective-permute-start | bytes 294920 | tf_op jit(solution)/shard_map/ppermute | solution.py:37
  11.7 5.1 %collective-permute-start = (bf16[128,384]{1,0:T(8,128)(2,1)S(1)}, bf16[128,384]{1,0:T(8,128)(2,1)S(1)}, u32[]{:S(2)}, u32[]{:S(2)}) collective-permute-start(bf16[128,384]{1,0:T(8,128)(2,1)S(1)} %get-tuple-element.62), channel_id=1, source_target_pairs={{0,1},{1,0},{2,3},{3,2},{4,5},{5,4},{6,7},{7,6},{8,9},{9,8},{10,11... | collective-permute-start | bytes 294920 | tf_op jit(solution)/shard_map/ppermute | solution.py:37
  14.4 6.6 %collective-permute-start.6 = (bf16[128,384]{1,0:T(8,128)(2,1)S(1)}, bf16[128,384]{1,0:T(8,128)(2,1)S(1)}, u32[]{:S(2)}, u32[]{:S(2)}) collective-permute-start(bf16[128,384]{1,0:T(8,128)(2,1)S(1)} %get-tuple-element.74), channel_id=1, source_target_pairs={{0,2},{1,3},{2,0},{3,1},{4,6},{5,7},{6,4},{7,5},{8,10},{9,11},{10,... | collective-permute-start | bytes 294920 | tf_op jit(solution)/shard_map/ppermute | solution.py:37
  15.4 5.9 %collective-permute-start.5 = (bf16[128,384]{1,0:T(8,128)(2,1)S(1)}, bf16[128,384]{1,0:T(8,128)(2,1)S(1)}, u32[]{:S(2)}, u32[]{:S(2)}) collective-permute-start(bf16[128,384]{1,0:T(8,128)(2,1)S(1)} %get-tuple-element.73), channel_id=1, source_target_pairs={{0,4},{4,0},{8,12},{12,8},{16,20},{20,16},{24,28},{28,24},{1,5},{5... | collective-permute-start | bytes 294920 | tf_op jit(solution)/shard_map/ppermute | solution.py:37
  17.0 5.9 %collective-permute-start.4 = (bf16[128,384]{1,0:T(8,128)(2,1)S(1)}, bf16[128,384]{1,0:T(8,128)(2,1)S(1)}, u32[]{:S(2)}, u32[]{:S(2)}) collective-permute-start(bf16[128,384]{1,0:T(8,128)(2,1)S(1)} %get-tuple-element.72), channel_id=1, source_target_pairs={{0,2},{1,3},{2,0},{3,1},{4,6},{5,7},{6,4},{7,5},{8,10},{9,11},{10,... | collective-permute-start | bytes 294920 | tf_op jit(solution)/shard_map/ppermute | solution.py:37
  21.2 2.2 %collective-permute-start.9 = (bf16[128,384]{1,0:T(8,128)(2,1)S(1)}, bf16[128,384]{1,0:T(8,128)(2,1)S(1)}, u32[]{:S(2)}, u32[]{:S(2)}) collective-permute-start(bf16[128,384]{1,0:T(8,128)(2,1)S(1)} %get-tuple-element.80), channel_id=1, source_target_pairs={{0,4},{4,0},{8,12},{12,8},{16,20},{20,16},{24,28},{28,24},{1,5},{5... | collective-permute-start | bytes 294920 | tf_op jit(solution)/shard_map/ppermute | solution.py:37
  21.3 4.7 %collective-permute-start.8 = (bf16[128,384]{1,0:T(8,128)(2,1)S(1)}, bf16[128,384]{1,0:T(8,128)(2,1)S(1)}, u32[]{:S(2)}, u32[]{:S(2)}) collective-permute-start(bf16[128,384]{1,0:T(8,128)(2,1)S(1)} %get-tuple-element.79), channel_id=1, source_target_pairs={{0,16},{4,12},{8,24},{12,4},{16,0},{20,28},{24,8},{28,20},{1,17},{... | collective-permute-start | bytes 294920 | tf_op jit(solution)/shard_map/ppermute | solution.py:37
  23.1 4.5 %collective-permute-start.7 = (bf16[128,384]{1,0:T(8,128)(2,1)S(1)}, bf16[128,384]{1,0:T(8,128)(2,1)S(1)}, u32[]{:S(2)}, u32[]{:S(2)}) collective-permute-start(bf16[128,384]{1,0:T(8,128)(2,1)S(1)} %get-tuple-element.78), channel_id=1, source_target_pairs={{0,4},{4,0},{8,12},{12,8},{16,20},{20,16},{24,28},{28,24},{1,5},{5... | collective-permute-start | bytes 294920 | tf_op jit(solution)/shard_map/ppermute | solution.py:37
  23.4 5.8 %collective-permute-start.12 = (bf16[128,384]{1,0:T(8,128)(2,1)S(1)}, bf16[128,384]{1,0:T(8,128)(2,1)S(1)}, u32[]{:S(2)}, u32[]{:S(2)}) collective-permute-start(bf16[128,384]{1,0:T(8,128)(2,1)S(1)} %get-tuple-element.86), channel_id=1, source_target_pairs={{0,16},{4,12},{8,24},{12,4},{16,0},{20,28},{24,8},{28,20},{1,17},{... | collective-permute-start | bytes 294920 | tf_op jit(solution)/shard_map/ppermute | solution.py:37
  26.0 24.2 %copy-start = (bf16[768,256]{1,0:T(8,128)(2,1)S(1)}, bf16[768,256]{1,0:T(8,128)(2,1)}, u32[]{:S(2)}) copy-start(bf16[768,256]{1,0:T(8,128)(2,1)} %refs_1_.9) | copy-start | bytes 1179652
  26.0 5.7 %collective-permute-start.11 = (bf16[128,384]{1,0:T(8,128)(2,1)S(1)}, bf16[128,384]{1,0:T(8,128)(2,1)S(1)}, u32[]{:S(2)}, u32[]{:S(2)}) collective-permute-start(bf16[128,384]{1,0:T(8,128)(2,1)S(1)} %get-tuple-element.85), channel_id=1, source_target_pairs={{0,8},{4,20},{8,0},{12,28},{16,24},{20,4},{24,16},{28,12},{1,9},{5... | collective-permute-start | bytes 294920 | tf_op jit(solution)/shard_map/ppermute | solution.py:37
  27.6 5.4 %collective-permute-start.10 = (bf16[128,384]{1,0:T(8,128)(2,1)S(1)}, bf16[128,384]{1,0:T(8,128)(2,1)S(1)}, u32[]{:S(2)}, u32[]{:S(2)}) collective-permute-start(bf16[128,384]{1,0:T(8,128)(2,1)S(1)} %get-tuple-element.84), channel_id=1, source_target_pairs={{0,16},{4,12},{8,24},{12,4},{16,0},{20,28},{24,8},{28,20},{1,17},{... | collective-permute-start | bytes 294920 | tf_op jit(solution)/shard_map/ppermute | solution.py:37
  29.2 4.9 %collective-permute-start.15 = (bf16[128,384]{1,0:T(8,128)(2,1)S(1)}, bf16[128,384]{1,0:T(8,128)(2,1)S(1)}, u32[]{:S(2)}, u32[]{:S(2)}) collective-permute-start(bf16[128,384]{1,0:T(8,128)(2,1)S(1)} %get-tuple-element.92), channel_id=1, source_target_pairs={{0,8},{4,20},{8,0},{12,28},{16,24},{20,4},{24,16},{28,12},{1,9},{5... | collective-permute-start | bytes 294920 | tf_op jit(solution)/shard_map/ppermute | solution.py:37
  32.0 9.6 %collective-permute-start.14 = (bf16[128,384]{1,0:T(8,128)(2,1)S(1)}, bf16[128,384]{1,0:T(8,128)(2,1)S(1)}, u32[]{:S(2)}, u32[]{:S(2)}) collective-permute-start(bf16[128,384]{1,0:T(8,128)(2,1)S(1)} %get-tuple-element.91), channel_id=1, source_target_pairs={{0,2},{1,3},{2,0},{3,1},{4,6},{5,7},{6,4},{7,5},{8,10},{9,11},{10,... | collective-permute-start | bytes 294920 | tf_op jit(solution)/shard_map/ppermute | solution.py:37
  33.1 8.7 %collective-permute-start.13 = (bf16[128,384]{1,0:T(8,128)(2,1)S(1)}, bf16[128,384]{1,0:T(8,128)(2,1)S(1)}, u32[]{:S(2)}, u32[]{:S(2)}) collective-permute-start(bf16[128,384]{1,0:T(8,128)(2,1)S(1)} %get-tuple-element.90), channel_id=1, source_target_pairs={{0,8},{4,20},{8,0},{12,28},{16,24},{20,4},{24,16},{28,12},{1,9},{5... | collective-permute-start | bytes 294920 | tf_op jit(solution)/shard_map/ppermute | solution.py:37
  34.4 12.2 %collective-permute-start.17 = (bf16[128,384]{1,0:T(8,128)(2,1)S(1)}, bf16[128,384]{1,0:T(8,128)(2,1)S(1)}, u32[]{:S(2)}, u32[]{:S(2)}) collective-permute-start(bf16[128,384]{1,0:T(8,128)(2,1)S(1)} %get-tuple-element.97), channel_id=1, source_target_pairs={{0,2},{1,3},{2,0},{3,1},{4,6},{5,7},{6,4},{7,5},{8,10},{9,11},{10,... | collective-permute-start | bytes 294920 | tf_op jit(solution)/shard_map/ppermute | solution.py:37
  42.0 5.6 %collective-permute-start.16 = (bf16[128,384]{1,0:T(8,128)(2,1)S(1)}, bf16[128,384]{1,0:T(8,128)(2,1)S(1)}, u32[]{:S(2)}, u32[]{:S(2)}) collective-permute-start(bf16[128,384]{1,0:T(8,128)(2,1)S(1)} %get-tuple-element.96), channel_id=1, source_target_pairs={{0,2},{1,3},{2,0},{3,1},{4,6},{5,7},{6,4},{7,5},{8,10},{9,11},{10,... | collective-permute-start | bytes 294920 | tf_op jit(solution)/shard_map/ppermute | solution.py:37
  42.1 8.1 %collective-permute-start.20 = (bf16[128,384]{1,0:T(8,128)(2,1)S(1)}, bf16[128,384]{1,0:T(8,128)(2,1)S(1)}, u32[]{:S(2)}, u32[]{:S(2)}) collective-permute-start(bf16[128,384]{1,0:T(8,128)(2,1)S(1)} %get-tuple-element.102), channel_id=1, source_target_pairs={{0,1},{1,0},{2,3},{3,2},{4,5},{5,4},{6,7},{7,6},{8,9},{9,8},{10,11... | collective-permute-start | bytes 294920 | tf_op jit(solution)/shard_map/ppermute | solution.py:37
  46.8 5.0 %collective-permute-start.19 = (bf16[128,384]{1,0:T(8,128)(2,1)S(1)}, bf16[128,384]{1,0:T(8,128)(2,1)S(1)}, u32[]{:S(2)}, u32[]{:S(2)}) collective-permute-start(bf16[128,384]{1,0:T(8,128)(2,1)S(1)} %get-tuple-element.101), channel_id=1, source_target_pairs={{0,1},{1,0},{2,3},{3,2},{4,5},{5,4},{6,7},{7,6},{8,9},{9,8},{10,11... | collective-permute-start | bytes 294920 | tf_op jit(solution)/shard_map/ppermute | solution.py:37
  47.9 5.2 %collective-permute-start.18 = (bf16[128,384]{1,0:T(8,128)(2,1)S(1)}, bf16[128,384]{1,0:T(8,128)(2,1)S(1)}, u32[]{:S(2)}, u32[]{:S(2)}) collective-permute-start(bf16[128,384]{1,0:T(8,128)(2,1)S(1)} %get-tuple-element.99), channel_id=1, source_target_pairs={{0,1},{1,0},{2,3},{3,2},{4,5},{5,4},{6,7},{7,6},{8,9},{9,8},{10,11... | collective-permute-start | bytes 294920 | tf_op jit(solution)/shard_map/ppermute | solution.py:37
  (2 other events, 11.2 us)

commit v14 on v13

--- a/solution.py
+++ b/solution.py
@@ -8,9 +8,9 @@
 LANES = 128
 SHARES = (3, 3, 3)
 HEADS = ((0,), (1,), (2,))
-TAILS = ((0,), (1,), (2,))
 ENTRY = (0, 0, 1)
-TURNS = {}
+WAITS = {1: 0}
+TURNS = {6: 1}
 SPANS = {}
 ROWS = 16
 SCOPED = 8 * 2**20
@@ -32,9 +32,9 @@
     return [high - low for low, high in zip(edges[:-1], edges[1:])]
 
 
-def swap(block, axis, distances):
+def swap(block, axis, distance):
     count = lax.axis_size(axis)
-    return lax.ppermute(block, axis, [(i, i ^ distances[i & 1]) for i in range(count)])
+    return lax.ppermute(block, axis, [(i, i ^ distance) for i in range(count)])
 
 
 def swapped(matrix, axis, flag):
@@ -69,15 +69,10 @@
     )(*operands, *extra)
 
 
-def prepare(name, node_order, places_out, places_in, right, middle, left, held):
+def prepare(name, node_order, slots_out, slots_in, right, middle, left, held):
     width = middle.shape[-1]
     groups = node_order.shape[0]
     block = width // groups
-
-    orders = bit_orders(groups)
-
-    def slot(place, core):
-        return jnp.where(core == 1, slot_number(place, orders[1]), slot_number(place, orders[0]))
 
     def kernel(node_order, right, middle, left, *refs):
         right0, right1, middle0, left0, left1, *passed = refs[len(held) :]
@@ -88,17 +83,16 @@
         right0[...] = swapped(swapped(right[0, 0], 1, bit0), 0, bit1)
         place = lax.broadcasted_iota(jnp.int32, (width, 1), 0)
         source = place % block
-        for i, p in enumerate(places_out):
-            piece = node_order[slot(p, group & 1 ^ p & 1) ^ group] * block
+        for i, slot in enumerate(slots_out):
+            piece = node_order[slot ^ group] * block
             source += jnp.where(place // block == i, piece, 0)
         across = lax.broadcasted_iota(jnp.int32, (width, width), 1)
         pick = jnp.where(across == source, 1.0, 0.0).astype(BF16)
         right1[...] = matmul(pick, swapped(right[0, 1], 1, bit1)).astype(BF16)
         place = lax.broadcasted_iota(jnp.int32, (1, width), 1)
         source = place % block
-        for i, p in enumerate(places_in):
-            piece = (slot(p, group & 1) ^ group) * block
-            source += jnp.where(place // block == i, piece, 0)
+        for i, slot in enumerate(slots_in):
+            source += jnp.where(place // block == i, (slot ^ group) * block, 0)
         down = lax.broadcasted_iota(jnp.int32, (width, width), 0)
         pick = jnp.where(down == source, 1.0, 0.0).astype(BF16)
         middle0[...] = swapped(matmul(middle[0], pick).astype(BF16), 0, bit1)
@@ -173,61 +167,64 @@
     return outs[: len(widths)], outs[len(widths) :]
 
 
-def level(name, weight, blocks, low, wide, count, before, after):
+def level(name, weight, blocks, low, wide, count, held, after):
     width = weight.shape[0]
     depth = width // count
-    ahead = sum(block.shape[1] for block in before)
+    given = len(blocks) + len(held)
 
     def kernel(weight, *refs):
-        ins, outs = refs[: len(blocks)], refs[len(blocks) + len(before) :]
+        ins, outs = refs[: len(blocks)], refs[given:]
         here = [slice(low, low + wide) if ref.shape[1] > wide else slice(None) for ref in ins]
         stacked = jnp.concatenate([ref[:, part] for ref, part in zip(ins, here)], axis=0)
         total = matmul(weight[...], stacked)
-        for i, out in enumerate(outs):
-            value = total[i * depth : (i + 1) * depth].astype(BF16)
-            if before and i == count - 1:
-                out[:, :ahead] = refs[len(blocks)][...]
-                out[:, ahead:] = value
-            else:
-                out[...] = value
-
-    widths = [wide] * (count - 1) + [ahead + wide]
+        for i, out in enumerate(outs[:count]):
+            out[...] = total[i * depth : (i + 1) * depth].astype(BF16)
+        for ref, out in zip(refs[len(blocks) : given], outs[count:]):
+            out[...] = ref[...]
+
+    shapes = [(depth, wide)] * count + [block.shape for block in held]
     return call(
         kernel,
         name,
-        [jax.ShapeDtypeStruct((depth, columns), BF16) for columns in widths],
-        [WHOLE] * (1 + len(blocks) + len(before)),
-        [weight] + blocks + before,
+        [jax.ShapeDtypeStruct(shape, BF16) for shape in shapes],
+        [WHOLE] * (1 + given),
+        [weight] + blocks + held,
         after,
-        out_specs=[WHOLE] * count,
-        cost_estimate=span(name),
-    )
-
-
-def bit_orders(groups):
-    bits = list(range(1, groups.bit_length() - 1))
-    return [bits[::-1], bits]
-
-
-def slot_number(place, order):
-    return place & 1 | sum((place >> 1 + t & 1) << bit for t, bit in enumerate(order))
-
-
-def by_bit(places, bit):
-    return [[p for p in places if p >> bit & 1 == value] for value in range(2)]
-
-
-def layouts_of(groups):
-    layouts = [by_bit(range(groups), 0)]
-    for bit in range(1, groups.bit_length() - 1):
-        layouts.append(by_bit(sum(layouts[-1], []), bit))
+        out_specs=[WHOLE] * len(shapes),
+        cost_estimate=span(name),
+    )
+
+
+def digits(groups):
+    bits = groups.bit_length() - 1
+    found, shift = [(0, 2)], 1
+    while shift < bits:
+        count = 2 if shift + 2 <= bits else 1
+        found.append((shift, 1 << count))
+        shift += count
+    return found
+
+
+def layouts_of(groups, steps):
+    layouts = [by_digit(range(groups), steps[0])]
+    for step in steps[1:]:
+        layouts.append(by_digit(sum(layouts[-1], []), step))
     return layouts
 
 
-def regroup(name, blocks, layout, bit, block, after):
+def values_of(radix):
+    return [0] + sorted(range(1, radix), key=lambda value: -value.bit_count())
+
+
+def by_digit(slots, digit):
+    shift, radix = digit
+    return [[r for r in slots if r >> shift & radix - 1 == value] for value in values_of(radix)]
+
+
+def regroup(name, blocks, layout, digit, block, after):
     columns = blocks[0].shape[1]
     place = {r: (i, j) for i, held in enumerate(layout) for j, r in enumerate(held)}
-    wanted = by_bit(sum(layout, []), bit)
+    wanted = by_digit(sum(layout, []), digit)
 
     def sort(values):
         parts = [[values[place[r][0]][place[r][1] * block :][:block] for r in held] for held in wanted]
@@ -298,9 +295,8 @@
     lows = [sum(chunks[:i]) for i in range(len(chunks))]
     whole = len(chunks) == len(SHARES)
     heads = HEADS if whole else ((0,),)
-    tails = TAILS if whole else ((0,),)
-    layouts = layouts_of(groups)
-    routes = [(1, 1)] + [(1 << one, 1 << other) for one, other in zip(*bit_orders(groups))]
+    steps = digits(groups)
+    layouts = layouts_of(groups, steps)
 
     keeps, sends = opening("opening", col_basis, signal, chunks, heads)
     right0, right1, middle, left0, left1, *later = prepare(
@@ -315,13 +311,13 @@
     )
     gots = {}
     for group, send in zip(heads, [sends[0]] + later):
-        got = swap(send, "sub", (1, 1))
+        got = swap(send, "sub", 1)
         for i in group:
             gots[i] = (got, lows[i] - lows[group[0]])
 
     out, after = None, right0
     waiting, pops, entered = [], 0, 0
-    parked = {}
+    held = []
     while waiting or entered < len(chunks):
         if entered < len(chunks) and (pops >= ENTRY[entered] or not waiting):
             waiting.append((1, entered, [keeps[entered], gots[entered][0]]))
@@ -331,38 +327,44 @@
         stage, i, blocks = waiting.pop(turn if turn < len(waiting) else 0)
         pops += 1
         wide = chunks[i]
+        released = []
         if stage == 1:
             results = level(f"right0_{i}", right0, blocks, gots[i][1], wide, 2, [], after)
-            axis, route = "sub", (2, 2)
-        elif stage == 2:
-            results = level(f"right1_{i}", right1, blocks, 0, wide, 2, [], after)
-            axis, route = "mid", routes[0]
-        elif stage < 2 + len(routes):
-            name = f"regroup{stage}_{i}"
-            results, _ = regroup(name, blocks, layouts[stage - 3], stage - 2, block, after)
-            axis, route = "mid", routes[stage - 2]
-        elif stage == 2 + len(routes):
-            results = level(f"middle_{i}", middle, blocks, 0, wide, 2, [], after)
-            axis, route = "sub", (2, 2)
-        elif stage == 3 + len(routes):
-            group = next(group for group in tails if i in group)
-            before = [parked[group[0]][-1]] if i != group[0] else []
-            results = level(f"left0_{i}", left0, blocks, 0, wide, 2, before, after)
-            parked[group[0]] = parked.get(group[0], [])[:-1] + list(results)
-            if i != group[-1]:
+            axis, shift, radix = "sub", 1, 2
+            if i in WAITS and whole:
+                held.append((i, results))
                 after = results[0]
                 continue
-            results = parked[group[0]]
-            got = swap(results[-1], "sub", (1, 1))
-            waiting.append((stage + 1, group[0], [results[:-1], got]))
-            after = results[-2]
-            continue
+        elif stage == 2:
+            count = steps[0][1]
+            free = [(j, kept) for j, kept in held if WAITS[j] == i]
+            sends = [kept[1] for _, kept in free]
+            results = level(f"right1_{i}", right1, blocks, 0, wide, count, sends, after)
+            axis, shift, radix = "mid", *steps[0]
+            for (j, kept), send in zip(free, results[count:]):
+                released.append((2, j, [kept[0], swap(send, "sub", 2)]))
+            results = results[:count]
+        elif stage < 2 + len(steps):
+            step = steps[stage - 2]
+            results, _ = regroup(
+                f"regroup{stage}_{i}", blocks, layouts[stage - 3], step, block, after
+            )
+            axis, shift, radix = "mid", *step
+        elif stage == 2 + len(steps):
+            results = level(f"middle_{i}", middle, blocks, 0, wide, 2, [], after)
+            axis, shift, radix = "sub", 1, 2
+        elif stage == 3 + len(steps):
+            results = level(f"left0_{i}", left0, blocks, 0, wide, 2, [], after)
+            axis, shift, radix = "sub", 0, 2
         else:
             name = f"last_{i}"
-            out = last(name, left1, row_basis, *blocks, out, lows[i], columns, after)
+            out = last(name, left1, row_basis, blocks[:1], blocks[1], out, lows[i], columns, after)
             continue
         after = results[0]
-        waiting.append((stage + 1, i, [results[0], swap(results[1], axis, route)]))
+        routes = [value << shift for value in values_of(radix)[1:]]
+        moved = [swap(send, axis, route) for send, route in zip(results[1:], routes)]
+        waiting.append((stage + 1, i, [results[0]] + moved))
+        waiting += released
     return out
 
 

time: 54.5 us -> 56 us (1.028)
  waiting for transfers between devices: 14.1 us -> 17.2 us
  starting transfers between devices: 30 us -> 28.5 us
    ppermute x21 -> x24, waiting for transfers between devices: 14.1 us -> 17.2 us  [swap(): return lax.ppermute(block, axis, [(i, i ^ distance) for i in range(count)])]
    ppermute x21 -> x24, starting transfers between devices: 30 us -> 28.5 us  [swap(): return lax.ppermute(block, axis, [(i, i ^ distance) for i in range(count)])]
    pallas_call x23 -> x20, Pallas kernels: 9.93 us -> 9.87 us  [call(): pl.pallas_call(body, name=name, in_specs=specs + [PLACE] * len(extra), ou...]
  transfers between devices with their start and end apart: 21 -> 24, of which waited for: 9 -> 12; matrix products, arithmetic and copies ran while one was open for 0% -> 0% of each run, Pallas kernels for 11% -> 11%
where the time goes in v14:
time: 56 us; the launch traced here: 55.8 us
  starting transfers between devices  28.5 us (51%)
  waiting for transfers between devices  17.2 us (31%)
  Pallas kernels  9.87 us (18%)
    ppermute x24, starting transfers between devices, swap(): return lax.ppermute(block, axis, [(i, i ^ distance) for i in range(count)])  28.5 us
    ppermute x24, waiting for transfers between devices, swap(): return lax.ppermute(block, axis, [(i, i ^ distance) for i in range(count)])  17.2 us
    pallas_call x20, Pallas kernels, call(): pl.pallas_call(body, name=name, in_specs=specs + [PLACE] * len(extra), ou...  9.87 us
  transfers between devices with their start and end apart: 24, of which 12 were waited for; matrix products, arithmetic and copies ran while one was open for 0% of the time, Pallas kernels for 11%

profile of v14, /device:TPU:0, one launch (start us, length us, event | category | flops | bytes accessed | tf_op | source)
XLA Modules:
  0.0 55.8 jit_solution(6252155515041617530)
XLA Ops:
  0.0 2.5 %opening.1 = (bf16[128,384]{1,0:T(8,128)(2,1)S(1)}, bf16[128,384]{1,0:T(8,128)(2,1)S(1)}, bf16[128,384]{1,0:T(8,128)(2,1)S(1)}, bf16[128,384]{1,0:T(8,128)(2,1)S...) custom-call(bf16[768,256]{1,0:T(8,128)(2,1)} %refs_0_.2, bf16[768,1152]{1,0:T(8,128)(2,1)} %refs_1_.5), custom_call_target="tpu_custom_call" | custom-call | tf_op jit(solution)/shard_map/opening/pallas_call | solution.py:62
  2.5 3.1 %collective-permute-start.1 = (bf16[128,384]{1,0:T(8,128)(2,1)S(1)}, bf16[128,384]{1,0:T(8,128)(2,1)S(1)}, u32[]{:S(2)}, u32[]{:S(2)}) collective-permute-start(bf16[128,384]{1,0:T(8,128)(2,1)S(1)} %get-tuple-element.65), channel_id=1, source_target_pairs={{0,1},{1,0},{2,3},{3,2},{4,5},{5,4},{6,7},{7,6},{8,9},{9,8},{10,11... | collective-permute-start | bytes 294920 | tf_op jit(solution)/shard_map/ppermute | solution.py:37
  6.6 2.1 %collective-permute-done.1.refs_2_ = bf16[128,384]{1,0:T(8,128)(2,1)S(1)} collective-permute-done((bf16[128,384]{1,0:T(8,128)(2,1)S(1)}, bf16[128,384]{1,0:T(8,128)(2,1)S(1)}, u32[]{:S(2)}, u32[]{:S(2)}) %collective-permute-start.1) | collective-permute-done | bytes 98336 | tf_op jit(solution)/shard_map/ppermute | solution.py:37
  9.0 2.7 %collective-permute-start.2 = (bf16[128,384]{1,0:T(8,128)(2,1)S(1)}, bf16[128,384]{1,0:T(8,128)(2,1)S(1)}, u32[]{:S(2)}, u32[]{:S(2)}) collective-permute-start(bf16[128,384]{1,0:T(8,128)(2,1)S(1)} %get-tuple-element.67), channel_id=1, source_target_pairs={{0,2},{1,3},{2,0},{3,1},{4,6},{5,7},{6,4},{7,5},{8,10},{9,11},{10,... | collective-permute-start | bytes 294920 | tf_op jit(solution)/shard_map/ppermute | solution.py:37
  11.7 2.5 %collective-permute-start = (bf16[128,384]{1,0:T(8,128)(2,1)S(1)}, bf16[128,384]{1,0:T(8,128)(2,1)S(1)}, u32[]{:S(2)}, u32[]{:S(2)}) collective-permute-start(bf16[128,384]{1,0:T(8,128)(2,1)S(1)} %get-tuple-element.63), channel_id=1, source_target_pairs={{0,1},{1,0},{2,3},{3,2},{4,5},{5,4},{6,7},{7,6},{8,9},{9,8},{10,11... | collective-permute-start | bytes 294920 | tf_op jit(solution)/shard_map/ppermute | solution.py:37
  15.2 2.4 %collective-permute-start.9 = (bf16[128,384]{1,0:T(8,128)(2,1)S(1)}, bf16[128,384]{1,0:T(8,128)(2,1)S(1)}, u32[]{:S(2)}, u32[]{:S(2)}) collective-permute-start(bf16[128,384]{1,0:T(8,128)(2,1)S(1)} %get-tuple-element.80), channel_id=1, source_target_pairs={{0,2},{1,3},{2,0},{3,1},{4,6},{5,7},{6,4},{7,5},{8,10},{9,11},{10,... | collective-permute-start | bytes 294920 | tf_op jit(solution)/shard_map/ppermute | solution.py:37
  18.5 2.6 %collective-permute-start.6 = (bf16[64,384]{1,0:T(8,128)(2,1)S(1)}, bf16[64,384]{1,0:T(8,128)(2,1)S(1)}, u32[]{:S(2)}, u32[]{:S(2)}) collective-permute-start(bf16[64,384]{1,0:T(8,128)(2,1)S(1)} %get-tuple-element.77), channel_id=1, source_target_pairs={{0,24},{4,28},{8,16},{12,20},{16,8},{20,12},{24,0},{28,4},{1,25},{... | collective-permute-start | bytes 147464 | tf_op jit(solution)/shard_map/ppermute | solution.py:37
  22.1 1.6 %collective-permute-done.9.refs_2_ = bf16[128,384]{1,0:T(8,128)(2,1)S(1)} collective-permute-done((bf16[128,384]{1,0:T(8,128)(2,1)S(1)}, bf16[128,384]{1,0:T(8,128)(2,1)S(1)}, u32[]{:S(2)}, u32[]{:S(2)}) %collective-permute-start.9) | collective-permute-done | bytes 98336 | tf_op jit(solution)/shard_map/ppermute | solution.py:37
  24.0 1.2 %collective-permute-done.7.refs_3_ = bf16[64,384]{1,0:T(8,128)(2,1)S(1)} collective-permute-done((bf16[64,384]{1,0:T(8,128)(2,1)S(1)}, bf16[64,384]{1,0:T(8,128)(2,1)S(1)}, u32[]{:S(2)}, u32[]{:S(2)}) %collective-permute-start.7) | collective-permute-done | bytes 49184 | tf_op jit(solution)/shard_map/ppermute | solution.py:37
  25.9 2.3 %collective-permute-start.11 = (bf16[128,384]{1,0:T(8,128)(2,1)S(1)}, bf16[128,384]{1,0:T(8,128)(2,1)S(1)}, u32[]{:S(2)}, u32[]{:S(2)}) collective-permute-start(bf16[128,384]{1,0:T(8,128)(2,1)S(1)} %get-tuple-element.85), channel_id=1, source_target_pairs={{0,2},{1,3},{2,0},{3,1},{4,6},{5,7},{6,4},{7,5},{8,10},{9,11},{10,... | collective-permute-start | bytes 294920 | tf_op jit(solution)/shard_map/ppermute | solution.py:37
  28.6 1.9 %collective-permute-start.16 = (bf16[64,384]{1,0:T(8,128)(2,1)S(1)}, bf16[64,384]{1,0:T(8,128)(2,1)S(1)}, u32[]{:S(2)}, u32[]{:S(2)}) collective-permute-start(bf16[64,384]{1,0:T(8,128)(2,1)S(1)} %get-tuple-element.93), channel_id=1, source_target_pairs={{0,24},{4,28},{8,16},{12,20},{16,8},{20,12},{24,0},{28,4},{1,25},{... | collective-permute-start | bytes 147464 | tf_op jit(solution)/shard_map/ppermute | solution.py:37
  31.1 1.1 %collective-permute-start.18 = (bf16[64,384]{1,0:T(8,128)(2,1)S(1)}, bf16[64,384]{1,0:T(8,128)(2,1)S(1)}, u32[]{:S(2)}, u32[]{:S(2)}) collective-permute-start(bf16[64,384]{1,0:T(8,128)(2,1)S(1)} %get-tuple-element.95), channel_id=1, source_target_pairs={{0,16},{4,20},{8,24},{12,28},{16,0},{20,4},{24,8},{28,12},{1,17},{... | collective-permute-start | bytes 147464 | tf_op jit(solution)/shard_map/ppermute | solution.py:37
  32.2 1.5 %collective-permute-done.11.refs_2_ = bf16[128,384]{1,0:T(8,128)(2,1)S(1)} collective-permute-done((bf16[128,384]{1,0:T(8,128)(2,1)S(1)}, bf16[128,384]{1,0:T(8,128)(2,1)S(1)}, u32[]{:S(2)}, u32[]{:S(2)}) %collective-permute-start.11) | collective-permute-done | bytes 98336 | tf_op jit(solution)/shard_map/ppermute | solution.py:37
  33.9 3.6 %collective-permute-start.13 = (bf16[64,384]{1,0:T(8,128)(2,1)S(1)}, bf16[64,384]{1,0:T(8,128)(2,1)S(1)}, u32[]{:S(2)}, u32[]{:S(2)}) collective-permute-start(bf16[64,384]{1,0:T(8,128)(2,1)S(1)} %get-tuple-element.90), channel_id=1, source_target_pairs={{0,24},{4,28},{8,16},{12,20},{16,8},{20,12},{24,0},{28,4},{1,25},{... | collective-permute-start | bytes 147464 | tf_op jit(solution)/shard_map/ppermute | solution.py:37
  38.4 1.1 %collective-permute-done.13.refs_2_ = bf16[64,384]{1,0:T(8,128)(2,1)S(1)} collective-permute-done((bf16[64,384]{1,0:T(8,128)(2,1)S(1)}, bf16[64,384]{1,0:T(8,128)(2,1)S(1)}, u32[]{:S(2)}, u32[]{:S(2)}) %collective-permute-start.13) | collective-permute-done | bytes 49184 | tf_op jit(solution)/shard_map/ppermute | solution.py:37
  39.5 2.0 %collective-permute-done.14.refs_3_ = bf16[64,384]{1,0:T(8,128)(2,1)S(1)} collective-permute-done((bf16[64,384]{1,0:T(8,128)(2,1)S(1)}, bf16[64,384]{1,0:T(8,128)(2,1)S(1)}, u32[]{:S(2)}, u32[]{:S(2)}) %collective-permute-start.14) | collective-permute-done | bytes 49184 | tf_op jit(solution)/shard_map/ppermute | solution.py:37
  42.4 1.7 %collective-permute-start.23 = (bf16[128,384]{1,0:T(8,128)(2,1)S(1)}, bf16[128,384]{1,0:T(8,128)(2,1)S(1)}, u32[]{:S(2)}, u32[]{:S(2)}) collective-permute-start(bf16[128,384]{1,0:T(8,128)(2,1)S(1)} %get-tuple-element.104), channel_id=1, source_target_pairs={{0,1},{1,0},{2,3},{3,2},{4,5},{5,4},{6,7},{7,6},{8,9},{9,8},{10,11... | collective-permute-start | bytes 294920 | tf_op jit(solution)/shard_map/ppermute | solution.py:37
  44.2 3.9 %collective-permute-done.20.refs_2_ = bf16[128,384]{1,0:T(8,128)(2,1)S(1)} collective-permute-done((bf16[128,384]{1,0:T(8,128)(2,1)S(1)}, bf16[128,384]{1,0:T(8,128)(2,1)S(1)}, u32[]{:S(2)}, u32[]{:S(2)}) %collective-permute-start.20) | collective-permute-done | bytes 98336 | tf_op jit(solution)/shard_map/ppermute | solution.py:37
  48.3 0.9 %collective-permute-done.19.refs_2_ = bf16[128,384]{1,0:T(8,128)(2,1)S(1)} collective-permute-done((bf16[128,384]{1,0:T(8,128)(2,1)S(1)}, bf16[128,384]{1,0:T(8,128)(2,1)S(1)}, u32[]{:S(2)}, u32[]{:S(2)}) %collective-permute-start.19) | collective-permute-done | bytes 98336 | tf_op jit(solution)/shard_map/ppermute | solution.py:37
  49.4 1.2 %collective-permute-start.21 = (bf16[128,384]{1,0:T(8,128)(2,1)S(1)}, bf16[128,384]{1,0:T(8,128)(2,1)S(1)}, u32[]{:S(2)}, u32[]{:S(2)}) collective-permute-start(bf16[128,384]{1,0:T(8,128)(2,1)S(1)} %get-tuple-element.101), channel_id=1, source_target_pairs={{0,1},{1,0},{2,3},{3,2},{4,5},{5,4},{6,7},{7,6},{8,9},{9,8},{10,11... | collective-permute-start | bytes 294920 | tf_op jit(solution)/shard_map/ppermute | solution.py:37
  50.6 1.3 %last_0.1.refs_4_ = bf16[768,1152]{1,0:T(8,128)(2,1)} custom-call(bf16[256,256]{1,0:T(8,128)(2,1)S(1)} %get-tuple-element.57.refs_0_, bf16[768,256]{1,0:T(8,128)(2,1)S(1)} %copy-done, bf16[128,384]{1,0:T(8,128)(2,1)S(1)} %collective-permute-done.23.refs_2_, bf16[128,384]{1,0:T(8,128)(2,1)S(1)} %get-tuple-element.88.refs_2_.refs_3_, ...), custom_call_target="tpu_custom_call" | custom-call | tf_op jit(solution)/shard_map/last_0/pallas_call | solution.py:62
  51.9 1.4 %collective-permute-done.22.refs_2_ = bf16[128,384]{1,0:T(8,128)(2,1)S(1)} collective-permute-done((bf16[128,384]{1,0:T(8,128)(2,1)S(1)}, bf16[128,384]{1,0:T(8,128)(2,1)S(1)}, u32[]{:S(2)}, u32[]{:S(2)}) %collective-permute-start.22) | collective-permute-done | bytes 98336 | tf_op jit(solution)/shard_map/ppermute | solution.py:37
  53.3 1.3 %last_1.1.refs_4_ = bf16[768,1152]{1,0:T(8,128)(2,1)} custom-call(bf16[256,256]{1,0:T(8,128)(2,1)S(1)} %get-tuple-element.57.refs_0_, bf16[768,256]{1,0:T(8,128)(2,1)S(1)} %copy-done, bf16[128,384]{1,0:T(8,128)(2,1)S(1)} %collective-permute-done.22.refs_2_, bf16[128,384]{1,0:T(8,128)(2,1)S(1)} %get-tuple-element.100.refs_3_, ...), custom_call_target="tpu_custom_call", output_to_operand_aliasing={{}: (4, {})} | custom-call | tf_op jit(solution)/shard_map/last_1/pallas_call | solution.py:62
  54.6 1.3 %last_2.1 = bf16[768,1152]{1,0:T(8,128)(2,1)} custom-call(bf16[256,256]{1,0:T(8,128)(2,1)S(1)} %get-tuple-element.57.refs_0_, bf16[768,256]{1,0:T(8,128)(2,1)S(1)} %copy-done, bf16[128,384]{1,0:T(8,128)(2,1)S(1)} %collective-permute-done.21.refs_2_, bf16[128,384]{1,0:T(8,128)(2,1)S(1)} %get-tuple-element.102.refs_5_.refs_3_, ...), custom_call_target="tpu_custom_call", output_to_operand_aliasing={{}: (4, {})} | custom-call | tf_op jit(solution)/shard_map/last_2/pallas_call | solution.py:62
  (54 shorter events, 8.7 us)
Async XLA Ops:
  2.5 6.2 %collective-permute-start.1 = (bf16[128,384]{1,0:T(8,128)(2,1)S(1)}, bf16[128,384]{1,0:T(8,128)(2,1)S(1)}, u32[]{:S(2)}, u32[]{:S(2)}) collective-permute-start(bf16[128,384]{1,0:T(8,128)(2,1)S(1)} %get-tuple-element.65), channel_id=1, source_target_pairs={{0,1},{1,0},{2,3},{3,2},{4,5},{5,4},{6,7},{7,6},{8,9},{9,8},{10,11... | collective-permute-start | bytes 294920 | tf_op jit(solution)/shard_map/ppermute | solution.py:37
  6.5 7.7 %collective-permute-start.3 = (bf16[128,384]{1,0:T(8,128)(2,1)S(1)}, bf16[128,384]{1,0:T(8,128)(2,1)S(1)}, u32[]{:S(2)}, u32[]{:S(2)}) collective-permute-start(bf16[128,384]{1,0:T(8,128)(2,1)S(1)} %get-tuple-element.69), channel_id=1, source_target_pairs={{0,1},{1,0},{2,3},{3,2},{4,5},{5,4},{6,7},{7,6},{8,9},{9,8},{10,11... | collective-permute-start | bytes 294920 | tf_op jit(solution)/shard_map/ppermute | solution.py:37
  9.0 6.0 %collective-permute-start.2 = (bf16[128,384]{1,0:T(8,128)(2,1)S(1)}, bf16[128,384]{1,0:T(8,128)(2,1)S(1)}, u32[]{:S(2)}, u32[]{:S(2)}) collective-permute-start(bf16[128,384]{1,0:T(8,128)(2,1)S(1)} %get-tuple-element.67), channel_id=1, source_target_pairs={{0,2},{1,3},{2,0},{3,1},{4,6},{5,7},{6,4},{7,5},{8,10},{9,11},{10,... | collective-permute-start | bytes 294920 | tf_op jit(solution)/shard_map/ppermute | solution.py:37
  11.7 5.9 %collective-permute-start = (bf16[128,384]{1,0:T(8,128)(2,1)S(1)}, bf16[128,384]{1,0:T(8,128)(2,1)S(1)}, u32[]{:S(2)}, u32[]{:S(2)}) collective-permute-start(bf16[128,384]{1,0:T(8,128)(2,1)S(1)} %get-tuple-element.63), channel_id=1, source_target_pairs={{0,1},{1,0},{2,3},{3,2},{4,5},{5,4},{6,7},{7,6},{8,9},{9,8},{10,11... | collective-permute-start | bytes 294920 | tf_op jit(solution)/shard_map/ppermute | solution.py:37
  15.1 3.4 %collective-permute-start.5 = (bf16[128,384]{1,0:T(8,128)(2,1)S(1)}, bf16[128,384]{1,0:T(8,128)(2,1)S(1)}, u32[]{:S(2)}, u32[]{:S(2)}) collective-permute-start(bf16[128,384]{1,0:T(8,128)(2,1)S(1)} %get-tuple-element.75), channel_id=1, source_target_pairs={{0,4},{4,0},{8,12},{12,8},{16,20},{20,16},{24,28},{28,24},{1,5},{5... | collective-permute-start | bytes 294920 | tf_op jit(solution)/shard_map/ppermute | solution.py:37
  15.2 8.5 %collective-permute-start.9 = (bf16[128,384]{1,0:T(8,128)(2,1)S(1)}, bf16[128,384]{1,0:T(8,128)(2,1)S(1)}, u32[]{:S(2)}, u32[]{:S(2)}) collective-permute-start(bf16[128,384]{1,0:T(8,128)(2,1)S(1)} %get-tuple-element.80), channel_id=1, source_target_pairs={{0,2},{1,3},{2,0},{3,1},{4,6},{5,7},{6,4},{7,5},{8,10},{9,11},{10,... | collective-permute-start | bytes 294920 | tf_op jit(solution)/shard_map/ppermute | solution.py:37
  17.8 10.4 %collective-permute-start.4 = (bf16[128,384]{1,0:T(8,128)(2,1)S(1)}, bf16[128,384]{1,0:T(8,128)(2,1)S(1)}, u32[]{:S(2)}, u32[]{:S(2)}) collective-permute-start(bf16[128,384]{1,0:T(8,128)(2,1)S(1)} %get-tuple-element.74), channel_id=1, source_target_pairs={{0,2},{1,3},{2,0},{3,1},{4,6},{5,7},{6,4},{7,5},{8,10},{9,11},{10,... | collective-permute-start | bytes 294920 | tf_op jit(solution)/shard_map/ppermute | solution.py:37
  18.5 5.5 %collective-permute-start.6 = (bf16[64,384]{1,0:T(8,128)(2,1)S(1)}, bf16[64,384]{1,0:T(8,128)(2,1)S(1)}, u32[]{:S(2)}, u32[]{:S(2)}) collective-permute-start(bf16[64,384]{1,0:T(8,128)(2,1)S(1)} %get-tuple-element.77), channel_id=1, source_target_pairs={{0,24},{4,28},{8,16},{12,20},{16,8},{20,12},{24,0},{28,4},{1,25},{... | collective-permute-start | bytes 147464 | tf_op jit(solution)/shard_map/ppermute | solution.py:37
  21.1 4.1 %collective-permute-start.7 = (bf16[64,384]{1,0:T(8,128)(2,1)S(1)}, bf16[64,384]{1,0:T(8,128)(2,1)S(1)}, u32[]{:S(2)}, u32[]{:S(2)}) collective-permute-start(bf16[64,384]{1,0:T(8,128)(2,1)S(1)} %get-tuple-element.78), channel_id=1, source_target_pairs={{0,8},{4,12},{8,0},{12,4},{16,24},{20,28},{24,16},{28,20},{1,9},{5... | collective-permute-start | bytes 147464 | tf_op jit(solution)/shard_map/ppermute | solution.py:37
  21.6 4.1 %collective-permute-start.8 = (bf16[64,384]{1,0:T(8,128)(2,1)S(1)}, bf16[64,384]{1,0:T(8,128)(2,1)S(1)}, u32[]{:S(2)}, u32[]{:S(2)}) collective-permute-start(bf16[64,384]{1,0:T(8,128)(2,1)S(1)} %get-tuple-element.79), channel_id=1, source_target_pairs={{0,16},{4,20},{8,24},{12,28},{16,0},{20,4},{24,8},{28,12},{1,17},{... | collective-permute-start | bytes 147464 | tf_op jit(solution)/shard_map/ppermute | solution.py:37
  23.9 4.7 %collective-permute-start.12 = (bf16[128,384]{1,0:T(8,128)(2,1)S(1)}, bf16[128,384]{1,0:T(8,128)(2,1)S(1)}, u32[]{:S(2)}, u32[]{:S(2)}) collective-permute-start(bf16[128,384]{1,0:T(8,128)(2,1)S(1)} %get-tuple-element.86), channel_id=1, source_target_pairs={{0,4},{4,0},{8,12},{12,8},{16,20},{20,16},{24,28},{28,24},{1,5},{5... | collective-permute-start | bytes 294920 | tf_op jit(solution)/shard_map/ppermute | solution.py:37
  25.9 7.7 %collective-permute-start.11 = (bf16[128,384]{1,0:T(8,128)(2,1)S(1)}, bf16[128,384]{1,0:T(8,128)(2,1)S(1)}, u32[]{:S(2)}, u32[]{:S(2)}) collective-permute-start(bf16[128,384]{1,0:T(8,128)(2,1)S(1)} %get-tuple-element.85), channel_id=1, source_target_pairs={{0,2},{1,3},{2,0},{3,1},{4,6},{5,7},{6,4},{7,5},{8,10},{9,11},{10,... | collective-permute-start | bytes 294920 | tf_op jit(solution)/shard_map/ppermute | solution.py:37
  28.5 5.4 %collective-permute-start.10 = (bf16[128,384]{1,0:T(8,128)(2,1)S(1)}, bf16[128,384]{1,0:T(8,128)(2,1)S(1)}, u32[]{:S(2)}, u32[]{:S(2)}) collective-permute-start(bf16[128,384]{1,0:T(8,128)(2,1)S(1)} %get-tuple-element.84), channel_id=1, source_target_pairs={{0,4},{4,0},{8,12},{12,8},{16,20},{20,16},{24,28},{28,24},{1,5},{5... | collective-permute-start | bytes 294920 | tf_op jit(solution)/shard_map/ppermute | solution.py:37
  28.6 9.4 %collective-permute-start.16 = (bf16[64,384]{1,0:T(8,128)(2,1)S(1)}, bf16[64,384]{1,0:T(8,128)(2,1)S(1)}, u32[]{:S(2)}, u32[]{:S(2)}) collective-permute-start(bf16[64,384]{1,0:T(8,128)(2,1)S(1)} %get-tuple-element.93), channel_id=1, source_target_pairs={{0,24},{4,28},{8,16},{12,20},{16,8},{20,12},{24,0},{28,4},{1,25},{... | collective-permute-start | bytes 147464 | tf_op jit(solution)/shard_map/ppermute | solution.py:37
  30.5 7.6 %collective-permute-start.17 = (bf16[64,384]{1,0:T(8,128)(2,1)S(1)}, bf16[64,384]{1,0:T(8,128)(2,1)S(1)}, u32[]{:S(2)}, u32[]{:S(2)}) collective-permute-start(bf16[64,384]{1,0:T(8,128)(2,1)S(1)} %get-tuple-element.94), channel_id=1, source_target_pairs={{0,8},{4,12},{8,0},{12,4},{16,24},{20,28},{24,16},{28,20},{1,9},{5... | collective-permute-start | bytes 147464 | tf_op jit(solution)/shard_map/ppermute | solution.py:37
  31.1 7.0 %collective-permute-start.18 = (bf16[64,384]{1,0:T(8,128)(2,1)S(1)}, bf16[64,384]{1,0:T(8,128)(2,1)S(1)}, u32[]{:S(2)}, u32[]{:S(2)}) collective-permute-start(bf16[64,384]{1,0:T(8,128)(2,1)S(1)} %get-tuple-element.95), channel_id=1, source_target_pairs={{0,16},{4,20},{8,24},{12,28},{16,0},{20,4},{24,8},{28,12},{1,17},{... | collective-permute-start | bytes 147464 | tf_op jit(solution)/shard_map/ppermute | solution.py:37
  33.9 5.6 %collective-permute-start.13 = (bf16[64,384]{1,0:T(8,128)(2,1)S(1)}, bf16[64,384]{1,0:T(8,128)(2,1)S(1)}, u32[]{:S(2)}, u32[]{:S(2)}) collective-permute-start(bf16[64,384]{1,0:T(8,128)(2,1)S(1)} %get-tuple-element.90), channel_id=1, source_target_pairs={{0,24},{4,28},{8,16},{12,20},{16,8},{20,12},{24,0},{28,4},{1,25},{... | collective-permute-start | bytes 147464 | tf_op jit(solution)/shard_map/ppermute | solution.py:37
  37.5 4.1 %collective-permute-start.14 = (bf16[64,384]{1,0:T(8,128)(2,1)S(1)}, bf16[64,384]{1,0:T(8,128)(2,1)S(1)}, u32[]{:S(2)}, u32[]{:S(2)}) collective-permute-start(bf16[64,384]{1,0:T(8,128)(2,1)S(1)} %get-tuple-element.91), channel_id=1, source_target_pairs={{0,8},{4,12},{8,0},{12,4},{16,24},{20,28},{24,16},{28,20},{1,9},{5... | collective-permute-start | bytes 147464 | tf_op jit(solution)/shard_map/ppermute | solution.py:37
  38.0 4.1 %collective-permute-start.15 = (bf16[64,384]{1,0:T(8,128)(2,1)S(1)}, bf16[64,384]{1,0:T(8,128)(2,1)S(1)}, u32[]{:S(2)}, u32[]{:S(2)}) collective-permute-start(bf16[64,384]{1,0:T(8,128)(2,1)S(1)} %get-tuple-element.92), channel_id=1, source_target_pairs={{0,16},{4,20},{8,24},{12,28},{16,0},{20,4},{24,8},{28,12},{1,17},{... | collective-permute-start | bytes 147464 | tf_op jit(solution)/shard_map/ppermute | solution.py:37
  38.3 9.7 %collective-permute-start.20 = (bf16[128,384]{1,0:T(8,128)(2,1)S(1)}, bf16[128,384]{1,0:T(8,128)(2,1)S(1)}, u32[]{:S(2)}, u32[]{:S(2)}) collective-permute-start(bf16[128,384]{1,0:T(8,128)(2,1)S(1)} %get-tuple-element.99), channel_id=1, source_target_pairs={{0,2},{1,3},{2,0},{3,1},{4,6},{5,7},{6,4},{7,5},{8,10},{9,11},{10,... | collective-permute-start | bytes 294920 | tf_op jit(solution)/shard_map/ppermute | solution.py:37
  42.3 6.9 %collective-permute-start.19 = (bf16[128,384]{1,0:T(8,128)(2,1)S(1)}, bf16[128,384]{1,0:T(8,128)(2,1)S(1)}, u32[]{:S(2)}, u32[]{:S(2)}) collective-permute-start(bf16[128,384]{1,0:T(8,128)(2,1)S(1)} %get-tuple-element.98), channel_id=1, source_target_pairs={{0,2},{1,3},{2,0},{3,1},{4,6},{5,7},{6,4},{7,5},{8,10},{9,11},{10,... | collective-permute-start | bytes 294920 | tf_op jit(solution)/shard_map/ppermute | solution.py:37
  42.4 8.2 %collective-permute-start.23 = (bf16[128,384]{1,0:T(8,128)(2,1)S(1)}, bf16[128,384]{1,0:T(8,128)(2,1)S(1)}, u32[]{:S(2)}, u32[]{:S(2)}) collective-permute-start(bf16[128,384]{1,0:T(8,128)(2,1)S(1)} %get-tuple-element.104), channel_id=1, source_target_pairs={{0,1},{1,0},{2,3},{3,2},{4,5},{5,4},{6,7},{7,6},{8,9},{9,8},{10,11... | collective-permute-start | bytes 294920 | tf_op jit(solution)/shard_map/ppermute | solution.py:37
  48.2 5.0 %collective-permute-start.22 = (bf16[128,384]{1,0:T(8,128)(2,1)S(1)}, bf16[128,384]{1,0:T(8,128)(2,1)S(1)}, u32[]{:S(2)}, u32[]{:S(2)}) collective-permute-start(bf16[128,384]{1,0:T(8,128)(2,1)S(1)} %get-tuple-element.103), channel_id=1, source_target_pairs={{0,1},{1,0},{2,3},{3,2},{4,5},{5,4},{6,7},{7,6},{8,9},{9,8},{10,11... | collective-permute-start | bytes 294920 | tf_op jit(solution)/shard_map/ppermute | solution.py:37
  49.4 5.1 %collective-permute-start.21 = (bf16[128,384]{1,0:T(8,128)(2,1)S(1)}, bf16[128,384]{1,0:T(8,128)(2,1)S(1)}, u32[]{:S(2)}, u32[]{:S(2)}) collective-permute-start(bf16[128,384]{1,0:T(8,128)(2,1)S(1)} %get-tuple-element.101), channel_id=1, source_target_pairs={{0,1},{1,0},{2,3},{3,2},{4,5},{5,4},{6,7},{7,6},{8,9},{9,8},{10,11... | collective-permute-start | bytes 294920 | tf_op jit(solution)/shard_map/ppermute | solution.py:37
  (5 other events, 49.2 us)

commit v15 on v14

--- a/solution.py
+++ b/solution.py
@@ -10,7 +10,7 @@
 HEADS = ((0,), (1,), (2,))
 ENTRY = (0, 0, 1)
 WAITS = {1: 0}
-TURNS = {6: 1}
+TURNS = {6: 1, 7: 1, 9: 1}
 SPANS = {}
 ROWS = 16
 SCOPED = 8 * 2**20
@@ -49,7 +49,7 @@
 
 
 def span(name):
-    flops = SPANS.get(name.split("_")[0], 0)
+    flops = SPANS.get(name.split("_")[0], 6 * 10**8)
     return pl.CostEstimate(flops=flops, bytes_accessed=0, transcendentals=0)
 
 

time: 56 us -> 56.3 us (level)
  starting transfers between devices: 28.5 us -> 29.3 us
    ppermute x24, starting transfers between devices: 28.5 us -> 29.3 us  [swap(): return lax.ppermute(block, axis, [(i, i ^ distance) for i in range(count)])]
  transfers between devices with their start and end apart: 24 -> 24, of which waited for: 12 -> 13; matrix products, arithmetic and copies ran while one was open for 0% -> 0% of each run, Pallas kernels for 11% -> 10%
where the time goes in v15:
time: 56.3 us; the launch traced here: 56.1 us
  starting transfers between devices  29.3 us (52%)
  waiting for transfers between devices  16.7 us (30%)
  Pallas kernels  9.85 us (17%)
    ppermute x24, starting transfers between devices, swap(): return lax.ppermute(block, axis, [(i, i ^ distance) for i in range(count)])  29.3 us
    ppermute x24, waiting for transfers between devices, swap(): return lax.ppermute(block, axis, [(i, i ^ distance) for i in range(count)])  16.7 us
    pallas_call x20, Pallas kernels, call(): pl.pallas_call(body, name=name, in_specs=specs + [PLACE] * len(extra), ou...  9.85 us
  transfers between devices with their start and end apart: 24, of which 13 were waited for; matrix products, arithmetic and copies ran while one was open for 0% of the time, Pallas kernels for 10%

profile of v15, /device:TPU:0, one launch (start us, length us, event | category | flops | bytes accessed | tf_op | source)
XLA Modules:
  0.0 56.1 jit_solution(16469754952075579753)
XLA Ops:
  0.0 2.5 %opening.1 = (bf16[128,384]{1,0:T(8,128)(2,1)S(1)}, bf16[128,384]{1,0:T(8,128)(2,1)S(1)}, bf16[128,384]{1,0:T(8,128)(2,1)S(1)}, bf16[128,384]{1,0:T(8,128)(2,1)S...) custom-call(bf16[768,256]{1,0:T(8,128)(2,1)} %refs_0_.2, bf16[768,1152]{1,0:T(8,128)(2,1)} %refs_1_.5), custom_call_target="tpu_custom_call" | custom-call | flops 600000000 | tf_op jit(solution)/shard_map/opening/pallas_call | solution.py:62
  2.5 3.1 %collective-permute-start.1 = (bf16[128,384]{1,0:T(8,128)(2,1)S(1)}, bf16[128,384]{1,0:T(8,128)(2,1)S(1)}, u32[]{:S(2)}, u32[]{:S(2)}) collective-permute-start(bf16[128,384]{1,0:T(8,128)(2,1)S(1)} %get-tuple-element.65), channel_id=1, source_target_pairs={{0,1},{1,0},{2,3},{3,2},{4,5},{5,4},{6,7},{7,6},{8,9},{9,8},{10,11... | collective-permute-start | bytes 294920 | tf_op jit(solution)/shard_map/ppermute | solution.py:37
  5.6 0.9 %prepare.1 = (bf16[256,256]{1,0:T(8,128)(2,1)S(1)}, bf16[256,256]{1,0:T(8,128)(2,1)S(1)}, bf16[256,256]{1,0:T(8,128)(2,1)S(1)}, bf16[256,256]{1,0:T(8,128)(2,1)S...) custom-call(s32[8]{0:T(128)S(1)} %copy-done.4, ...), custom_call_target="tpu_custom_call" | custom-call | flops 600000000 | tf_op jit(solution)/shard_map/prepare/pallas_call | solution.py:62
  6.6 2.1 %collective-permute-done.1.refs_2_ = bf16[128,384]{1,0:T(8,128)(2,1)S(1)} collective-permute-done((bf16[128,384]{1,0:T(8,128)(2,1)S(1)}, bf16[128,384]{1,0:T(8,128)(2,1)S(1)}, u32[]{:S(2)}, u32[]{:S(2)}) %collective-permute-start.1) | collective-permute-done | bytes 98336 | tf_op jit(solution)/shard_map/ppermute | solution.py:37
  9.0 2.7 %collective-permute-start.2 = (bf16[128,384]{1,0:T(8,128)(2,1)S(1)}, bf16[128,384]{1,0:T(8,128)(2,1)S(1)}, u32[]{:S(2)}, u32[]{:S(2)}) collective-permute-start(bf16[128,384]{1,0:T(8,128)(2,1)S(1)} %get-tuple-element.67), channel_id=1, source_target_pairs={{0,2},{1,3},{2,0},{3,1},{4,6},{5,7},{6,4},{7,5},{8,10},{9,11},{10,... | collective-permute-start | bytes 294920 | tf_op jit(solution)/shard_map/ppermute | solution.py:37
  11.7 2.5 %collective-permute-start = (bf16[128,384]{1,0:T(8,128)(2,1)S(1)}, bf16[128,384]{1,0:T(8,128)(2,1)S(1)}, u32[]{:S(2)}, u32[]{:S(2)}) collective-permute-start(bf16[128,384]{1,0:T(8,128)(2,1)S(1)} %get-tuple-element.63), channel_id=1, source_target_pairs={{0,1},{1,0},{2,3},{3,2},{4,5},{5,4},{6,7},{7,6},{8,9},{9,8},{10,11... | collective-permute-start | bytes 294920 | tf_op jit(solution)/shard_map/ppermute | solution.py:37
  15.2 2.4 %collective-permute-start.5 = (bf16[128,384]{1,0:T(8,128)(2,1)S(1)}, bf16[128,384]{1,0:T(8,128)(2,1)S(1)}, u32[]{:S(2)}, u32[]{:S(2)}) collective-permute-start(bf16[128,384]{1,0:T(8,128)(2,1)S(1)} %get-tuple-element.75), channel_id=1, source_target_pairs={{0,2},{1,3},{2,0},{3,1},{4,6},{5,7},{6,4},{7,5},{8,10},{9,11},{10,... | collective-permute-start | bytes 294920 | tf_op jit(solution)/shard_map/ppermute | solution.py:37
  17.8 2.5 %collective-permute-start.8 = (bf16[64,384]{1,0:T(8,128)(2,1)S(1)}, bf16[64,384]{1,0:T(8,128)(2,1)S(1)}, u32[]{:S(2)}, u32[]{:S(2)}) collective-permute-start(bf16[64,384]{1,0:T(8,128)(2,1)S(1)} %get-tuple-element.80), channel_id=1, source_target_pairs={{0,24},{4,28},{8,16},{12,20},{16,8},{20,12},{24,0},{28,4},{1,25},{... | collective-permute-start | bytes 147464 | tf_op jit(solution)/shard_map/ppermute | solution.py:37
  21.4 2.0 %collective-permute-done.5.refs_2_ = bf16[128,384]{1,0:T(8,128)(2,1)S(1)} collective-permute-done((bf16[128,384]{1,0:T(8,128)(2,1)S(1)}, bf16[128,384]{1,0:T(8,128)(2,1)S(1)}, u32[]{:S(2)}, u32[]{:S(2)}) %collective-permute-start.5) | collective-permute-done | bytes 98336 | tf_op jit(solution)/shard_map/ppermute | solution.py:37
  25.2 1.8 %collective-permute-start.12 = (bf16[128,384]{1,0:T(8,128)(2,1)S(1)}, bf16[128,384]{1,0:T(8,128)(2,1)S(1)}, u32[]{:S(2)}, u32[]{:S(2)}) collective-permute-start(bf16[128,384]{1,0:T(8,128)(2,1)S(1)} %get-tuple-element.87), channel_id=1, source_target_pairs={{0,2},{1,3},{2,0},{3,1},{4,6},{5,7},{6,4},{7,5},{8,10},{9,11},{10,... | collective-permute-start | bytes 294920 | tf_op jit(solution)/shard_map/ppermute | solution.py:37
  27.1 2.6 %collective-permute-start.13 = (bf16[64,384]{1,0:T(8,128)(2,1)S(1)}, bf16[64,384]{1,0:T(8,128)(2,1)S(1)}, u32[]{:S(2)}, u32[]{:S(2)}) collective-permute-start(bf16[64,384]{1,0:T(8,128)(2,1)S(1)} %get-tuple-element.88), channel_id=1, source_target_pairs={{0,24},{4,28},{8,16},{12,20},{16,8},{20,12},{24,0},{28,4},{1,25},{... | collective-permute-start | bytes 147464 | tf_op jit(solution)/shard_map/ppermute | solution.py:37
  30.6 3.9 %collective-permute-done.4.refs_2_ = bf16[128,384]{1,0:T(8,128)(2,1)S(1)} collective-permute-done((bf16[128,384]{1,0:T(8,128)(2,1)S(1)}, bf16[128,384]{1,0:T(8,128)(2,1)S(1)}, u32[]{:S(2)}, u32[]{:S(2)}) %collective-permute-start.4) | collective-permute-done | bytes 98336 | tf_op jit(solution)/shard_map/ppermute | solution.py:37
  35.2 1.0 %collective-permute-done.12.refs_2_ = bf16[128,384]{1,0:T(8,128)(2,1)S(1)} collective-permute-done((bf16[128,384]{1,0:T(8,128)(2,1)S(1)}, bf16[128,384]{1,0:T(8,128)(2,1)S(1)}, u32[]{:S(2)}, u32[]{:S(2)}) %collective-permute-start.12) | collective-permute-done | bytes 98336 | tf_op jit(solution)/shard_map/ppermute | solution.py:37
  36.4 2.6 %collective-permute-start.16 = (bf16[64,384]{1,0:T(8,128)(2,1)S(1)}, bf16[64,384]{1,0:T(8,128)(2,1)S(1)}, u32[]{:S(2)}, u32[]{:S(2)}) collective-permute-start(bf16[64,384]{1,0:T(8,128)(2,1)S(1)} %get-tuple-element.94), channel_id=1, source_target_pairs={{0,24},{4,28},{8,16},{12,20},{16,8},{20,12},{24,0},{28,4},{1,25},{... | collective-permute-start | bytes 147464 | tf_op jit(solution)/shard_map/ppermute | solution.py:37
  40.0 2.3 %collective-permute-done.19.refs_2_ = bf16[128,384]{1,0:T(8,128)(2,1)S(1)} collective-permute-done((bf16[128,384]{1,0:T(8,128)(2,1)S(1)}, bf16[128,384]{1,0:T(8,128)(2,1)S(1)}, u32[]{:S(2)}, u32[]{:S(2)}) %collective-permute-start.19) | collective-permute-done | bytes 98336 | tf_op jit(solution)/shard_map/ppermute | solution.py:37
  42.5 0.6 %collective-permute-done.17.refs_3_ = bf16[64,384]{1,0:T(8,128)(2,1)S(1)} collective-permute-done((bf16[64,384]{1,0:T(8,128)(2,1)S(1)}, bf16[64,384]{1,0:T(8,128)(2,1)S(1)}, u32[]{:S(2)}, u32[]{:S(2)}) %collective-permute-start.17) | collective-permute-done | bytes 49184 | tf_op jit(solution)/shard_map/ppermute | solution.py:37
  43.8 2.0 %collective-permute-start.20 = (bf16[128,384]{1,0:T(8,128)(2,1)S(1)}, bf16[128,384]{1,0:T(8,128)(2,1)S(1)}, u32[]{:S(2)}, u32[]{:S(2)}) collective-permute-start(bf16[128,384]{1,0:T(8,128)(2,1)S(1)} %get-tuple-element.100), channel_id=1, source_target_pairs={{0,2},{1,3},{2,0},{3,1},{4,6},{5,7},{6,4},{7,5},{8,10},{9,11},{10,... | collective-permute-start | bytes 294920 | tf_op jit(solution)/shard_map/ppermute | solution.py:37
  46.0 1.9 %collective-permute-start.22 = (bf16[128,384]{1,0:T(8,128)(2,1)S(1)}, bf16[128,384]{1,0:T(8,128)(2,1)S(1)}, u32[]{:S(2)}, u32[]{:S(2)}) collective-permute-start(bf16[128,384]{1,0:T(8,128)(2,1)S(1)} %get-tuple-element.103), channel_id=1, source_target_pairs={{0,1},{1,0},{2,3},{3,2},{4,5},{5,4},{6,7},{7,6},{8,9},{9,8},{10,11... | collective-permute-start | bytes 294920 | tf_op jit(solution)/shard_map/ppermute | solution.py:37
  47.8 2.1 %collective-permute-done.20.refs_2_ = bf16[128,384]{1,0:T(8,128)(2,1)S(1)} collective-permute-done((bf16[128,384]{1,0:T(8,128)(2,1)S(1)}, bf16[128,384]{1,0:T(8,128)(2,1)S(1)}, u32[]{:S(2)}, u32[]{:S(2)}) %collective-permute-start.20) | collective-permute-done | bytes 98336 | tf_op jit(solution)/shard_map/ppermute | solution.py:37
  50.1 1.4 %collective-permute-start.21 = (bf16[128,384]{1,0:T(8,128)(2,1)S(1)}, bf16[128,384]{1,0:T(8,128)(2,1)S(1)}, u32[]{:S(2)}, u32[]{:S(2)}) collective-permute-start(bf16[128,384]{1,0:T(8,128)(2,1)S(1)} %get-tuple-element.101), channel_id=1, source_target_pairs={{0,1},{1,0},{2,3},{3,2},{4,5},{5,4},{6,7},{7,6},{8,9},{9,8},{10,11... | collective-permute-start | bytes 294920 | tf_op jit(solution)/shard_map/ppermute | solution.py:37
  51.8 1.3 %last_0.1.refs_4_ = bf16[768,1152]{1,0:T(8,128)(2,1)} custom-call(bf16[256,256]{1,0:T(8,128)(2,1)S(1)} %get-tuple-element.57.refs_0_, bf16[768,256]{1,0:T(8,128)(2,1)S(1)} %copy-done, bf16[128,384]{1,0:T(8,128)(2,1)S(1)} %collective-permute-done.23.refs_2_, bf16[128,384]{1,0:T(8,128)(2,1)S(1)} %get-tuple-element.92.refs_2_.refs_3_, ...), custom_call_target="tpu_custom_call" | custom-call | flops 600000000 | tf_op jit(solution)/shard_map/last_0/pallas_call | solution.py:62
  53.1 0.5 collective-permute-done.22.refs_2_
  53.6 1.3 %last_1.1.refs_4_ = bf16[768,1152]{1,0:T(8,128)(2,1)} custom-call(bf16[256,256]{1,0:T(8,128)(2,1)S(1)} %get-tuple-element.57.refs_0_, bf16[768,256]{1,0:T(8,128)(2,1)S(1)} %copy-done, bf16[128,384]{1,0:T(8,128)(2,1)S(1)} %collective-permute-done.22.refs_2_, ...), custom_call_target="tpu_custom_call", output_to_operand_aliasing={{}: (4, {})} | custom-call | flops 600000000 | tf_op jit(solution)/shard_map/last_1/pallas_call | solution.py:62
  54.9 1.3 %last_2.1 = bf16[768,1152]{1,0:T(8,128)(2,1)} custom-call(bf16[256,256]{1,0:T(8,128)(2,1)S(1)} %get-tuple-element.57.refs_0_, bf16[768,256]{1,0:T(8,128)(2,1)S(1)} %copy-done, bf16[128,384]{1,0:T(8,128)(2,1)S(1)} %collective-permute-done.21.refs_2_, bf16[128,384]{1,0:T(8,128)(2,1)S(1)} %get-tuple-element.102.refs_3_.refs_5_, ...), custom_call_target="tpu_custom_call", output_to_operand_aliasing={{}: (4, {})} | custom-call | flops 600000000 | tf_op jit(solution)/shard_map/last_2/pallas_call | solution.py:62
  (54 shorter events, 8.9 us)
Async XLA Ops:
  2.5 6.2 %collective-permute-start.1 = (bf16[128,384]{1,0:T(8,128)(2,1)S(1)}, bf16[128,384]{1,0:T(8,128)(2,1)S(1)}, u32[]{:S(2)}, u32[]{:S(2)}) collective-permute-start(bf16[128,384]{1,0:T(8,128)(2,1)S(1)} %get-tuple-element.65), channel_id=1, source_target_pairs={{0,1},{1,0},{2,3},{3,2},{4,5},{5,4},{6,7},{7,6},{8,9},{9,8},{10,11... | collective-permute-start | bytes 294920 | tf_op jit(solution)/shard_map/ppermute | solution.py:37
  6.5 7.7 %collective-permute-start.3 = (bf16[128,384]{1,0:T(8,128)(2,1)S(1)}, bf16[128,384]{1,0:T(8,128)(2,1)S(1)}, u32[]{:S(2)}, u32[]{:S(2)}) collective-permute-start(bf16[128,384]{1,0:T(8,128)(2,1)S(1)} %get-tuple-element.69), channel_id=1, source_target_pairs={{0,1},{1,0},{2,3},{3,2},{4,5},{5,4},{6,7},{7,6},{8,9},{9,8},{10,11... | collective-permute-start | bytes 294920 | tf_op jit(solution)/shard_map/ppermute | solution.py:37
  9.0 6.0 %collective-permute-start.2 = (bf16[128,384]{1,0:T(8,128)(2,1)S(1)}, bf16[128,384]{1,0:T(8,128)(2,1)S(1)}, u32[]{:S(2)}, u32[]{:S(2)}) collective-permute-start(bf16[128,384]{1,0:T(8,128)(2,1)S(1)} %get-tuple-element.67), channel_id=1, source_target_pairs={{0,2},{1,3},{2,0},{3,1},{4,6},{5,7},{6,4},{7,5},{8,10},{9,11},{10,... | collective-permute-start | bytes 294920 | tf_op jit(solution)/shard_map/ppermute | solution.py:37
  11.7 5.9 %collective-permute-start = (bf16[128,384]{1,0:T(8,128)(2,1)S(1)}, bf16[128,384]{1,0:T(8,128)(2,1)S(1)}, u32[]{:S(2)}, u32[]{:S(2)}) collective-permute-start(bf16[128,384]{1,0:T(8,128)(2,1)S(1)} %get-tuple-element.63), channel_id=1, source_target_pairs={{0,1},{1,0},{2,3},{3,2},{4,5},{5,4},{6,7},{7,6},{8,9},{9,8},{10,11... | collective-permute-start | bytes 294920 | tf_op jit(solution)/shard_map/ppermute | solution.py:37
  15.1 2.7 %collective-permute-start.6 = (bf16[128,384]{1,0:T(8,128)(2,1)S(1)}, bf16[128,384]{1,0:T(8,128)(2,1)S(1)}, u32[]{:S(2)}, u32[]{:S(2)}) collective-permute-start(bf16[128,384]{1,0:T(8,128)(2,1)S(1)} %get-tuple-element.76), channel_id=1, source_target_pairs={{0,4},{4,0},{8,12},{12,8},{16,20},{20,16},{24,28},{28,24},{1,5},{5... | collective-permute-start | bytes 294920 | tf_op jit(solution)/shard_map/ppermute | solution.py:37
  15.2 8.2 %collective-permute-start.5 = (bf16[128,384]{1,0:T(8,128)(2,1)S(1)}, bf16[128,384]{1,0:T(8,128)(2,1)S(1)}, u32[]{:S(2)}, u32[]{:S(2)}) collective-permute-start(bf16[128,384]{1,0:T(8,128)(2,1)S(1)} %get-tuple-element.75), channel_id=1, source_target_pairs={{0,2},{1,3},{2,0},{3,1},{4,6},{5,7},{6,4},{7,5},{8,10},{9,11},{10,... | collective-permute-start | bytes 294920 | tf_op jit(solution)/shard_map/ppermute | solution.py:37
  17.8 6.3 %collective-permute-start.8 = (bf16[64,384]{1,0:T(8,128)(2,1)S(1)}, bf16[64,384]{1,0:T(8,128)(2,1)S(1)}, u32[]{:S(2)}, u32[]{:S(2)}) collective-permute-start(bf16[64,384]{1,0:T(8,128)(2,1)S(1)} %get-tuple-element.80), channel_id=1, source_target_pairs={{0,24},{4,28},{8,16},{12,20},{16,8},{20,12},{24,0},{28,4},{1,25},{... | collective-permute-start | bytes 147464 | tf_op jit(solution)/shard_map/ppermute | solution.py:37
  20.4 4.1 %collective-permute-start.9 = (bf16[64,384]{1,0:T(8,128)(2,1)S(1)}, bf16[64,384]{1,0:T(8,128)(2,1)S(1)}, u32[]{:S(2)}, u32[]{:S(2)}) collective-permute-start(bf16[64,384]{1,0:T(8,128)(2,1)S(1)} %get-tuple-element.81), channel_id=1, source_target_pairs={{0,8},{4,12},{8,0},{12,4},{16,24},{20,28},{24,16},{28,20},{1,9},{5... | collective-permute-start | bytes 147464 | tf_op jit(solution)/shard_map/ppermute | solution.py:37
  20.9 4.1 %collective-permute-start.10 = (bf16[64,384]{1,0:T(8,128)(2,1)S(1)}, bf16[64,384]{1,0:T(8,128)(2,1)S(1)}, u32[]{:S(2)}, u32[]{:S(2)}) collective-permute-start(bf16[64,384]{1,0:T(8,128)(2,1)S(1)} %get-tuple-element.82), channel_id=1, source_target_pairs={{0,16},{4,20},{8,24},{12,28},{16,0},{20,4},{24,8},{28,12},{1,17},{... | collective-permute-start | bytes 147464 | tf_op jit(solution)/shard_map/ppermute | solution.py:37
  23.7 3.4 %collective-permute-start.7 = (bf16[128,384]{1,0:T(8,128)(2,1)S(1)}, bf16[128,384]{1,0:T(8,128)(2,1)S(1)}, u32[]{:S(2)}, u32[]{:S(2)}) collective-permute-start(bf16[128,384]{1,0:T(8,128)(2,1)S(1)} %get-tuple-element.79), channel_id=1, source_target_pairs={{0,4},{4,0},{8,12},{12,8},{16,20},{20,16},{24,28},{28,24},{1,5},{5... | collective-permute-start | bytes 294920 | tf_op jit(solution)/shard_map/ppermute | solution.py:37
  23.7 10.8 %collective-permute-start.4 = (bf16[128,384]{1,0:T(8,128)(2,1)S(1)}, bf16[128,384]{1,0:T(8,128)(2,1)S(1)}, u32[]{:S(2)}, u32[]{:S(2)}) collective-permute-start(bf16[128,384]{1,0:T(8,128)(2,1)S(1)} %get-tuple-element.74), channel_id=1, source_target_pairs={{0,2},{1,3},{2,0},{3,1},{4,6},{5,7},{6,4},{7,5},{8,10},{9,11},{10,... | collective-permute-start | bytes 294920 | tf_op jit(solution)/shard_map/ppermute | solution.py:37
  25.2 11.0 %collective-permute-start.12 = (bf16[128,384]{1,0:T(8,128)(2,1)S(1)}, bf16[128,384]{1,0:T(8,128)(2,1)S(1)}, u32[]{:S(2)}, u32[]{:S(2)}) collective-permute-start(bf16[128,384]{1,0:T(8,128)(2,1)S(1)} %get-tuple-element.87), channel_id=1, source_target_pairs={{0,2},{1,3},{2,0},{3,1},{4,6},{5,7},{6,4},{7,5},{8,10},{9,11},{10,... | collective-permute-start | bytes 294920 | tf_op jit(solution)/shard_map/ppermute | solution.py:37
  27.1 7.8 %collective-permute-start.13 = (bf16[64,384]{1,0:T(8,128)(2,1)S(1)}, bf16[64,384]{1,0:T(8,128)(2,1)S(1)}, u32[]{:S(2)}, u32[]{:S(2)}) collective-permute-start(bf16[64,384]{1,0:T(8,128)(2,1)S(1)} %get-tuple-element.88), channel_id=1, source_target_pairs={{0,24},{4,28},{8,16},{12,20},{16,8},{20,12},{24,0},{28,4},{1,25},{... | collective-permute-start | bytes 147464 | tf_op jit(solution)/shard_map/ppermute | solution.py:37
  29.6 5.2 %collective-permute-start.14 = (bf16[64,384]{1,0:T(8,128)(2,1)S(1)}, bf16[64,384]{1,0:T(8,128)(2,1)S(1)}, u32[]{:S(2)}, u32[]{:S(2)}) collective-permute-start(bf16[64,384]{1,0:T(8,128)(2,1)S(1)} %get-tuple-element.89), channel_id=1, source_target_pairs={{0,8},{4,12},{8,0},{12,4},{16,24},{20,28},{24,16},{28,20},{1,9},{5... | collective-permute-start | bytes 147464 | tf_op jit(solution)/shard_map/ppermute | solution.py:37
  30.2 4.7 %collective-permute-start.15 = (bf16[64,384]{1,0:T(8,128)(2,1)S(1)}, bf16[64,384]{1,0:T(8,128)(2,1)S(1)}, u32[]{:S(2)}, u32[]{:S(2)}) collective-permute-start(bf16[64,384]{1,0:T(8,128)(2,1)S(1)} %get-tuple-element.90), channel_id=1, source_target_pairs={{0,16},{4,20},{8,24},{12,28},{16,0},{20,4},{24,8},{28,12},{1,17},{... | collective-permute-start | bytes 147464 | tf_op jit(solution)/shard_map/ppermute | solution.py:37
  34.7 1.7 %collective-permute-start.11 = (bf16[128,384]{1,0:T(8,128)(2,1)S(1)}, bf16[128,384]{1,0:T(8,128)(2,1)S(1)}, u32[]{:S(2)}, u32[]{:S(2)}) collective-permute-start(bf16[128,384]{1,0:T(8,128)(2,1)S(1)} %get-tuple-element.86), channel_id=1, source_target_pairs={{0,4},{4,0},{8,12},{12,8},{16,20},{20,16},{24,28},{28,24},{1,5},{5... | collective-permute-start | bytes 294920 | tf_op jit(solution)/shard_map/ppermute | solution.py:37
  35.1 7.2 %collective-permute-start.19 = (bf16[128,384]{1,0:T(8,128)(2,1)S(1)}, bf16[128,384]{1,0:T(8,128)(2,1)S(1)}, u32[]{:S(2)}, u32[]{:S(2)}) collective-permute-start(bf16[128,384]{1,0:T(8,128)(2,1)S(1)} %get-tuple-element.97), channel_id=1, source_target_pairs={{0,2},{1,3},{2,0},{3,1},{4,6},{5,7},{6,4},{7,5},{8,10},{9,11},{10,... | collective-permute-start | bytes 294920 | tf_op jit(solution)/shard_map/ppermute | solution.py:37
  36.4 6.1 %collective-permute-start.16 = (bf16[64,384]{1,0:T(8,128)(2,1)S(1)}, bf16[64,384]{1,0:T(8,128)(2,1)S(1)}, u32[]{:S(2)}, u32[]{:S(2)}) collective-permute-start(bf16[64,384]{1,0:T(8,128)(2,1)S(1)} %get-tuple-element.94), channel_id=1, source_target_pairs={{0,24},{4,28},{8,16},{12,20},{16,8},{20,12},{24,0},{28,4},{1,25},{... | collective-permute-start | bytes 147464 | tf_op jit(solution)/shard_map/ppermute | solution.py:37
  39.0 4.1 %collective-permute-start.17 = (bf16[64,384]{1,0:T(8,128)(2,1)S(1)}, bf16[64,384]{1,0:T(8,128)(2,1)S(1)}, u32[]{:S(2)}, u32[]{:S(2)}) collective-permute-start(bf16[64,384]{1,0:T(8,128)(2,1)S(1)} %get-tuple-element.95), channel_id=1, source_target_pairs={{0,8},{4,12},{8,0},{12,4},{16,24},{20,28},{24,16},{28,20},{1,9},{5... | collective-permute-start | bytes 147464 | tf_op jit(solution)/shard_map/ppermute | solution.py:37
  39.5 4.1 %collective-permute-start.18 = (bf16[64,384]{1,0:T(8,128)(2,1)S(1)}, bf16[64,384]{1,0:T(8,128)(2,1)S(1)}, u32[]{:S(2)}, u32[]{:S(2)}) collective-permute-start(bf16[64,384]{1,0:T(8,128)(2,1)S(1)} %get-tuple-element.96), channel_id=1, source_target_pairs={{0,16},{4,20},{8,24},{12,28},{16,0},{20,4},{24,8},{28,12},{1,17},{... | collective-permute-start | bytes 147464 | tf_op jit(solution)/shard_map/ppermute | solution.py:37
  43.8 6.1 %collective-permute-start.20 = (bf16[128,384]{1,0:T(8,128)(2,1)S(1)}, bf16[128,384]{1,0:T(8,128)(2,1)S(1)}, u32[]{:S(2)}, u32[]{:S(2)}) collective-permute-start(bf16[128,384]{1,0:T(8,128)(2,1)S(1)} %get-tuple-element.100), channel_id=1, source_target_pairs={{0,2},{1,3},{2,0},{3,1},{4,6},{5,7},{6,4},{7,5},{8,10},{9,11},{10,... | collective-permute-start | bytes 294920 | tf_op jit(solution)/shard_map/ppermute | solution.py:37
  45.8 6.0 %collective-permute-start.23 = (bf16[128,384]{1,0:T(8,128)(2,1)S(1)}, bf16[128,384]{1,0:T(8,128)(2,1)S(1)}, u32[]{:S(2)}, u32[]{:S(2)}) collective-permute-start(bf16[128,384]{1,0:T(8,128)(2,1)S(1)} %get-tuple-element.104), channel_id=1, source_target_pairs={{0,1},{1,0},{2,3},{3,2},{4,5},{5,4},{6,7},{7,6},{8,9},{9,8},{10,11... | collective-permute-start | bytes 294920 | tf_op jit(solution)/shard_map/ppermute | solution.py:37
  46.0 7.7 %collective-permute-start.22 = (bf16[128,384]{1,0:T(8,128)(2,1)S(1)}, bf16[128,384]{1,0:T(8,128)(2,1)S(1)}, u32[]{:S(2)}, u32[]{:S(2)}) collective-permute-start(bf16[128,384]{1,0:T(8,128)(2,1)S(1)} %get-tuple-element.103), channel_id=1, source_target_pairs={{0,1},{1,0},{2,3},{3,2},{4,5},{5,4},{6,7},{7,6},{8,9},{9,8},{10,11... | collective-permute-start | bytes 294920 | tf_op jit(solution)/shard_map/ppermute | solution.py:37
  50.1 4.7 %collective-permute-start.21 = (bf16[128,384]{1,0:T(8,128)(2,1)S(1)}, bf16[128,384]{1,0:T(8,128)(2,1)S(1)}, u32[]{:S(2)}, u32[]{:S(2)}) collective-permute-start(bf16[128,384]{1,0:T(8,128)(2,1)S(1)} %get-tuple-element.101), channel_id=1, source_target_pairs={{0,1},{1,0},{2,3},{3,2},{4,5},{5,4},{6,7},{7,6},{8,9},{9,8},{10,11... | collective-permute-start | bytes 294920 | tf_op jit(solution)/shard_map/ppermute | solution.py:37
  (5 other events, 30.7 us)

commit v16 on v15

--- a/solution.py
+++ b/solution.py
@@ -6,11 +6,10 @@
 from jax.sharding import PartitionSpec as P
 
 LANES = 128
-SHARES = (3, 3, 3)
+SHARES = (2, 3, 4)
 HEADS = ((0,), (1,), (2,))
+TAILS = ((0, 1), (2,))
 ENTRY = (0, 0, 1)
-WAITS = {1: 0}
-TURNS = {6: 1, 7: 1, 9: 1}
 SPANS = {}
 ROWS = 16
 SCOPED = 8 * 2**20
@@ -49,7 +48,7 @@
 
 
 def span(name):
-    flops = SPANS.get(name.split("_")[0], 6 * 10**8)
+    flops = SPANS.get(name.split("_")[0], 10**9)
     return pl.CostEstimate(flops=flops, bytes_accessed=0, transcendentals=0)
 
 
@@ -167,30 +166,33 @@
     return outs[: len(widths)], outs[len(widths) :]
 
 
-def level(name, weight, blocks, low, wide, count, held, after):
+def level(name, weight, blocks, low, wide, count, before, after):
     width = weight.shape[0]
     depth = width // count
-    given = len(blocks) + len(held)
+    ahead = sum(block.shape[1] for block in before)
 
     def kernel(weight, *refs):
-        ins, outs = refs[: len(blocks)], refs[given:]
+        ins, outs = refs[: len(blocks)], refs[len(blocks) + len(before) :]
         here = [slice(low, low + wide) if ref.shape[1] > wide else slice(None) for ref in ins]
         stacked = jnp.concatenate([ref[:, part] for ref, part in zip(ins, here)], axis=0)
         total = matmul(weight[...], stacked)
-        for i, out in enumerate(outs[:count]):
-            out[...] = total[i * depth : (i + 1) * depth].astype(BF16)
-        for ref, out in zip(refs[len(blocks) : given], outs[count:]):
-            out[...] = ref[...]
-
-    shapes = [(depth, wide)] * count + [block.shape for block in held]
+        for i, out in enumerate(outs):
+            value = total[i * depth : (i + 1) * depth].astype(BF16)
+            if before and i == count - 1:
+                out[:, :ahead] = refs[len(blocks)][...]
+                out[:, ahead:] = value
+            else:
+                out[...] = value
+
+    widths = [wide] * (count - 1) + [ahead + wide]
     return call(
         kernel,
         name,
-        [jax.ShapeDtypeStruct(shape, BF16) for shape in shapes],
-        [WHOLE] * (1 + given),
-        [weight] + blocks + held,
+        [jax.ShapeDtypeStruct((depth, columns), BF16) for columns in widths],
+        [WHOLE] * (1 + len(blocks) + len(before)),
+        [weight] + blocks + before,
         after,
-        out_specs=[WHOLE] * len(shapes),
+        out_specs=[WHOLE] * count,
         cost_estimate=span(name),
     )
 
@@ -295,6 +297,7 @@
     lows = [sum(chunks[:i]) for i in range(len(chunks))]
     whole = len(chunks) == len(SHARES)
     heads = HEADS if whole else ((0,),)
+    tails = TAILS if whole else ((0,),)
     steps = digits(groups)
     layouts = layouts_of(groups, steps)
 
@@ -317,33 +320,22 @@
 
     out, after = None, right0
     waiting, pops, entered = [], 0, 0
-    held = []
+    parked = {}
     while waiting or entered < len(chunks):
         if entered < len(chunks) and (pops >= ENTRY[entered] or not waiting):
             waiting.append((1, entered, [keeps[entered], gots[entered][0]]))
             entered += 1
             continue
-        turn = TURNS.get(pops, 0)
-        stage, i, blocks = waiting.pop(turn if turn < len(waiting) else 0)
+        stage, i, blocks = waiting.pop(0)
         pops += 1
         wide = chunks[i]
-        released = []
         if stage == 1:
             results = level(f"right0_{i}", right0, blocks, gots[i][1], wide, 2, [], after)
             axis, shift, radix = "sub", 1, 2
-            if i in WAITS and whole:
-                held.append((i, results))
-                after = results[0]
-                continue
         elif stage == 2:
             count = steps[0][1]
-            free = [(j, kept) for j, kept in held if WAITS[j] == i]
-            sends = [kept[1] for _, kept in free]
-            results = level(f"right1_{i}", right1, blocks, 0, wide, count, sends, after)
+            results = level(f"right1_{i}", right1, blocks, 0, wide, count, [], after)
             axis, shift, radix = "mid", *steps[0]
-            for (j, kept), send in zip(free, results[count:]):
-                released.append((2, j, [kept[0], swap(send, "sub", 2)]))
-            results = results[:count]
         elif stage < 2 + len(steps):
             step = steps[stage - 2]
             results, _ = regroup(
@@ -354,17 +346,27 @@
             results = level(f"middle_{i}", middle, blocks, 0, wide, 2, [], after)
             axis, shift, radix = "sub", 1, 2
         elif stage == 3 + len(steps):
-            results = level(f"left0_{i}", left0, blocks, 0, wide, 2, [], after)
+            group = next(group for group in tails if i in group)
+            before = [parked[group[0]][-1]] if i != group[0] else []
+            results = level(f"left0_{i}", left0, blocks, 0, wide, 2, before, after)
             axis, shift, radix = "sub", 0, 2
+            parked[group[0]] = parked.get(group[0], [])[:-1] + list(results)
+            if i != group[-1]:
+                after = results[0]
+                continue
+            results = parked[group[0]]
+            got = swap(results[-1], axis, 1)
+            waiting.append((stage + 1, group[0], [results[:-1], got]))
+            after = results[-2]
+            continue
         else:
             name = f"last_{i}"
-            out = last(name, left1, row_basis, blocks[:1], blocks[1], out, lows[i], columns, after)
+            out = last(name, left1, row_basis, *blocks, out, lows[i], columns, after)
             continue
         after = results[0]
         routes = [value << shift for value in values_of(radix)[1:]]
         moved = [swap(send, axis, route) for send, route in zip(results[1:], routes)]
         waiting.append((stage + 1, i, [results[0]] + moved))
-        waiting += released
     return out
 
 

time: 56.3 us -> 54.5 us (0.968)
  Pallas kernels: 9.85 us -> 8.61 us
    pallas_call x20 -> x19, Pallas kernels: 9.85 us -> 8.61 us  [call(): pl.pallas_call(body, name=name, in_specs=specs + [PLACE] * len(extra), ou...]
    ppermute x24 -> x23, starting transfers between devices: 29.3 us -> 29 us  [swap(): return lax.ppermute(block, axis, [(i, i ^ distance) for i in range(count)])]
    ppermute x24 -> x23, waiting for transfers between devices: 16.7 us -> 16.5 us  [swap(): return lax.ppermute(block, axis, [(i, i ^ distance) for i in range(count)])]
  transfers between devices with their start and end apart: 24 -> 23, of which waited for: 13 -> 8; matrix products, arithmetic and copies ran while one was open for 0% -> 0% of each run, Pallas kernels for 10% -> 9%
where the time goes in v16:
time: 54.5 us; the launch traced here: 54.3 us
  starting transfers between devices  29 us (53%)
  waiting for transfers between devices  16.5 us (30%)
  Pallas kernels  8.61 us (16%)
    ppermute x23, starting transfers between devices, swap(): return lax.ppermute(block, axis, [(i, i ^ distance) for i in range(count)])  29 us
    ppermute x23, waiting for transfers between devices, swap(): return lax.ppermute(block, axis, [(i, i ^ distance) for i in range(count)])  16.5 us
    pallas_call x19, Pallas kernels, call(): pl.pallas_call(body, name=name, in_specs=specs + [PLACE] * len(extra), ou...  8.61 us
  transfers between devices with their start and end apart: 23, of which 8 were waited for; matrix products, arithmetic and copies ran while one was open for 0% of the time, Pallas kernels for 9%

profile of v16, /device:TPU:0, one launch (start us, length us, event | category | flops | bytes accessed | tf_op | source)
XLA Modules:
  0.0 54.3 jit_solution(10557129183189672874)
XLA Ops:
  0.0 2.4 %opening.1 = (bf16[128,256]{1,0:T(8,128)(2,1)S(1)}, bf16[128,384]{1,0:T(8,128)(2,1)S(1)}, bf16[128,512]{1,0:T(8,128)(2,1)S(1)}, bf16[128,256]{1,0:T(8,128)(2,1)S...) custom-call(bf16[768,256]{1,0:T(8,128)(2,1)} %refs_0_.2, bf16[768,1152]{1,0:T(8,128)(2,1)} %refs_1_.4), custom_call_target="tpu_custom_call" | custom-call | flops 1000000000 | tf_op jit(solution)/shard_map/opening/pallas_call | solution.py:61
  2.4 3.1 %collective-permute-start.1 = (bf16[128,256]{1,0:T(8,128)(2,1)S(1)}, bf16[128,256]{1,0:T(8,128)(2,1)S(1)}, u32[]{:S(2)}, u32[]{:S(2)}) collective-permute-start(bf16[128,256]{1,0:T(8,128)(2,1)S(1)} %get-tuple-element.64), channel_id=1, source_target_pairs={{0,1},{1,0},{2,3},{3,2},{4,5},{5,4},{6,7},{7,6},{8,9},{9,8},{10,11... | collective-permute-start | bytes 196616 | tf_op jit(solution)/shard_map/ppermute | solution.py:36
  5.5 0.9 %prepare.1 = (bf16[256,256]{1,0:T(8,128)(2,1)S(1)}, bf16[256,256]{1,0:T(8,128)(2,1)S(1)}, bf16[256,256]{1,0:T(8,128)(2,1)S(1)}, bf16[256,256]{1,0:T(8,128)(2,1)S...) custom-call(s32[8]{0:T(128)S(1)} %copy-done.4, ...), custom_call_target="tpu_custom_call" | custom-call | flops 1000000000 | tf_op jit(solution)/shard_map/prepare/pallas_call | solution.py:61
  6.5 2.0 %collective-permute-start = (bf16[128,512]{1,0:T(8,128)(2,1)S(1)}, bf16[128,512]{1,0:T(8,128)(2,1)S(1)}, u32[]{:S(2)}, u32[]{:S(2)}) collective-permute-start(bf16[128,512]{1,0:T(8,128)(2,1)S(1)} %get-tuple-element.62), channel_id=1, source_target_pairs={{0,1},{1,0},{2,3},{3,2},{4,5},{5,4},{6,7},{7,6},{8,9},{9,8},{10,11... | collective-permute-start | bytes 393224 | tf_op jit(solution)/shard_map/ppermute | solution.py:36
  8.7 2.7 %collective-permute-start.2 = (bf16[128,256]{1,0:T(8,128)(2,1)S(1)}, bf16[128,256]{1,0:T(8,128)(2,1)S(1)}, u32[]{:S(2)}, u32[]{:S(2)}) collective-permute-start(bf16[128,256]{1,0:T(8,128)(2,1)S(1)} %get-tuple-element.66), channel_id=1, source_target_pairs={{0,2},{1,3},{2,0},{3,1},{4,6},{5,7},{6,4},{7,5},{8,10},{9,11},{10,... | collective-permute-start | bytes 196616 | tf_op jit(solution)/shard_map/ppermute | solution.py:36
  11.4 1.5 %collective-permute-done.3.refs_2_ = bf16[128,384]{1,0:T(8,128)(2,1)S(1)} collective-permute-done((bf16[128,384]{1,0:T(8,128)(2,1)S(1)}, bf16[128,384]{1,0:T(8,128)(2,1)S(1)}, u32[]{:S(2)}, u32[]{:S(2)}) %collective-permute-start.3) | collective-permute-done | bytes 98336 | tf_op jit(solution)/shard_map/ppermute | solution.py:36
  13.1 2.0 %collective-permute-start.6 = (bf16[128,384]{1,0:T(8,128)(2,1)S(1)}, bf16[128,384]{1,0:T(8,128)(2,1)S(1)}, u32[]{:S(2)}, u32[]{:S(2)}) collective-permute-start(bf16[128,384]{1,0:T(8,128)(2,1)S(1)} %get-tuple-element.74), channel_id=1, source_target_pairs={{0,2},{1,3},{2,0},{3,1},{4,6},{5,7},{6,4},{7,5},{8,10},{9,11},{10,... | collective-permute-start | bytes 294920 | tf_op jit(solution)/shard_map/ppermute | solution.py:36
  15.4 0.6 %collective-permute-done.refs_2_ = bf16[128,512]{1,0:T(8,128)(2,1)S(1)} collective-permute-done((bf16[128,512]{1,0:T(8,128)(2,1)S(1)}, bf16[128,512]{1,0:T(8,128)(2,1)S(1)}, u32[]{:S(2)}, u32[]{:S(2)}) %collective-permute-start) | collective-permute-done | bytes 131104 | tf_op jit(solution)/shard_map/ppermute | solution.py:36
  16.2 2.2 %collective-permute-start.4 = (bf16[128,512]{1,0:T(8,128)(2,1)S(1)}, bf16[128,512]{1,0:T(8,128)(2,1)S(1)}, u32[]{:S(2)}, u32[]{:S(2)}) collective-permute-start(bf16[128,512]{1,0:T(8,128)(2,1)S(1)} %get-tuple-element.72), channel_id=1, source_target_pairs={{0,2},{1,3},{2,0},{3,1},{4,6},{5,7},{6,4},{7,5},{8,10},{9,11},{10,... | collective-permute-start | bytes 393224 | tf_op jit(solution)/shard_map/ppermute | solution.py:36
  18.4 2.1 %collective-permute-done.6.refs_2_ = bf16[128,384]{1,0:T(8,128)(2,1)S(1)} collective-permute-done((bf16[128,384]{1,0:T(8,128)(2,1)S(1)}, bf16[128,384]{1,0:T(8,128)(2,1)S(1)}, u32[]{:S(2)}, u32[]{:S(2)}) %collective-permute-start.6) | collective-permute-done | bytes 98336 | tf_op jit(solution)/shard_map/ppermute | solution.py:36
  20.8 2.5 %collective-permute-start.8 = (bf16[64,256]{1,0:T(8,128)(2,1)S(1)}, bf16[64,256]{1,0:T(8,128)(2,1)S(1)}, u32[]{:S(2)}, u32[]{:S(2)}) collective-permute-start(bf16[64,256]{1,0:T(8,128)(2,1)S(1)} %get-tuple-element.79), channel_id=1, source_target_pairs={{0,24},{4,28},{8,16},{12,20},{16,8},{20,12},{24,0},{28,4},{1,25},{... | collective-permute-start | bytes 98312 | tf_op jit(solution)/shard_map/ppermute | solution.py:36
  23.3 0.5 collective-permute-start.9
  24.4 1.4 %collective-permute-done.4.refs_2_ = bf16[128,512]{1,0:T(8,128)(2,1)S(1)} collective-permute-done((bf16[128,512]{1,0:T(8,128)(2,1)S(1)}, bf16[128,512]{1,0:T(8,128)(2,1)S(1)}, u32[]{:S(2)}, u32[]{:S(2)}) %collective-permute-start.4) | collective-permute-done | bytes 131104 | tf_op jit(solution)/shard_map/ppermute | solution.py:36
  26.1 2.5 %collective-permute-start.16 = (bf16[64,384]{1,0:T(8,128)(2,1)S(1)}, bf16[64,384]{1,0:T(8,128)(2,1)S(1)}, u32[]{:S(2)}, u32[]{:S(2)}) collective-permute-start(bf16[64,384]{1,0:T(8,128)(2,1)S(1)} %get-tuple-element.90), channel_id=1, source_target_pairs={{0,24},{4,28},{8,16},{12,20},{16,8},{20,12},{24,0},{28,4},{1,25},{... | collective-permute-start | bytes 147464 | tf_op jit(solution)/shard_map/ppermute | solution.py:36
  30.0 2.5 %collective-permute-start.12 = (bf16[64,512]{1,0:T(8,128)(2,1)S(1)}, bf16[64,512]{1,0:T(8,128)(2,1)S(1)}, u32[]{:S(2)}, u32[]{:S(2)}) collective-permute-start(bf16[64,512]{1,0:T(8,128)(2,1)S(1)} %get-tuple-element.86), channel_id=1, source_target_pairs={{0,24},{4,28},{8,16},{12,20},{16,8},{20,12},{24,0},{28,4},{1,25},{... | collective-permute-start | bytes 196616 | tf_op jit(solution)/shard_map/ppermute | solution.py:36
  32.5 0.6 %collective-permute-start.13 = (bf16[64,512]{1,0:T(8,128)(2,1)S(1)}, bf16[64,512]{1,0:T(8,128)(2,1)S(1)}, u32[]{:S(2)}, u32[]{:S(2)}) collective-permute-start(bf16[64,512]{1,0:T(8,128)(2,1)S(1)} %get-tuple-element.87), channel_id=1, source_target_pairs={{0,8},{4,12},{8,0},{12,4},{16,24},{20,28},{24,16},{28,20},{1,9},{5... | collective-permute-start | bytes 196616 | tf_op jit(solution)/shard_map/ppermute | solution.py:36
  33.1 1.5 %collective-permute-start.14 = (bf16[64,512]{1,0:T(8,128)(2,1)S(1)}, bf16[64,512]{1,0:T(8,128)(2,1)S(1)}, u32[]{:S(2)}, u32[]{:S(2)}) collective-permute-start(bf16[64,512]{1,0:T(8,128)(2,1)S(1)} %get-tuple-element.88), channel_id=1, source_target_pairs={{0,16},{4,20},{8,24},{12,28},{16,0},{20,4},{24,8},{28,12},{1,17},{... | collective-permute-start | bytes 196616 | tf_op jit(solution)/shard_map/ppermute | solution.py:36
  34.9 1.9 %collective-permute-start.20 = (bf16[128,384]{1,0:T(8,128)(2,1)S(1)}, bf16[128,384]{1,0:T(8,128)(2,1)S(1)}, u32[]{:S(2)}, u32[]{:S(2)}) collective-permute-start(bf16[128,384]{1,0:T(8,128)(2,1)S(1)} %get-tuple-element.97), channel_id=1, source_target_pairs={{0,2},{1,3},{2,0},{3,1},{4,6},{5,7},{6,4},{7,5},{8,10},{9,11},{10,... | collective-permute-start | bytes 294920 | tf_op jit(solution)/shard_map/ppermute | solution.py:36
  37.6 2.9 %collective-permute-start.19 = (bf16[128,512]{1,0:T(8,128)(2,1)S(1)}, bf16[128,512]{1,0:T(8,128)(2,1)S(1)}, u32[]{:S(2)}, u32[]{:S(2)}) collective-permute-start(bf16[128,512]{1,0:T(8,128)(2,1)S(1)} %get-tuple-element.96), channel_id=1, source_target_pairs={{0,2},{1,3},{2,0},{3,1},{4,6},{5,7},{6,4},{7,5},{8,10},{9,11},{10,... | collective-permute-start | bytes 393224 | tf_op jit(solution)/shard_map/ppermute | solution.py:36
  40.5 4.1 %collective-permute-done.20.refs_2_ = bf16[128,384]{1,0:T(8,128)(2,1)S(1)} collective-permute-done((bf16[128,384]{1,0:T(8,128)(2,1)S(1)}, bf16[128,384]{1,0:T(8,128)(2,1)S(1)}, u32[]{:S(2)}, u32[]{:S(2)}) %collective-permute-start.20) | collective-permute-done | bytes 98336 | tf_op jit(solution)/shard_map/ppermute | solution.py:36
  44.9 2.9 %collective-permute-done.19.refs_2_ = bf16[128,512]{1,0:T(8,128)(2,1)S(1)} collective-permute-done((bf16[128,512]{1,0:T(8,128)(2,1)S(1)}, bf16[128,512]{1,0:T(8,128)(2,1)S(1)}, u32[]{:S(2)}, u32[]{:S(2)}) %collective-permute-start.19) | collective-permute-done | bytes 131104 | tf_op jit(solution)/shard_map/ppermute | solution.py:36
  48.1 3.4 %collective-permute-done.22.refs_2_ = bf16[128,640]{1,0:T(8,128)(2,1)S(1)} collective-permute-done((bf16[128,640]{1,0:T(8,128)(2,1)S(1)}, bf16[128,640]{1,0:T(8,128)(2,1)S(1)}, u32[]{:S(2)}, u32[]{:S(2)}) %collective-permute-start.22) | collective-permute-done | bytes 163872 | tf_op jit(solution)/shard_map/ppermute | solution.py:36
  51.5 1.4 %last_0.1.refs_4_ = bf16[768,1152]{1,0:T(8,128)(2,1)} custom-call(bf16[256,256]{1,0:T(8,128)(2,1)S(1)} %get-tuple-element.56.refs_0_, bf16[768,256]{1,0:T(8,128)(2,1)S(1)} %copy-done, bf16[128,640]{1,0:T(8,128)(2,1)S(1)} %collective-permute-done.22.refs_2_, bf16[128,256]{1,0:T(8,128)(2,1)S(1)} %get-tuple-element.94.refs_5_.refs_3_, ...), custom_call_target="tpu_custom_call" | custom-call | flops 1000000000 | tf_op jit(solution)/shard_map/last_0/pallas_call | solution.py:61
  53.0 1.3 %last_2.1 = bf16[768,1152]{1,0:T(8,128)(2,1)} custom-call(bf16[256,256]{1,0:T(8,128)(2,1)S(1)} %get-tuple-element.56.refs_0_, bf16[768,256]{1,0:T(8,128)(2,1)S(1)} %copy-done, bf16[128,512]{1,0:T(8,128)(2,1)S(1)} %collective-permute-done.21.refs_2_, bf16[128,512]{1,0:T(8,128)(2,1)S(1)} %get-tuple-element.101.refs_5_.refs_3_, ...), custom_call_target="tpu_custom_call", output_to_operand_aliasing={{}: (4, {})} | custom-call | flops 1000000000 | tf_op jit(solution)/shard_map/last_2/pallas_call | solution.py:61
  (51 shorter events, 5.2 us)
Async XLA Ops:
  0.0 5.5 %copy-start.1 = (bf16[1,2,256,256]{3,2,1,0:T(8,128)(2,1)S(1)}, bf16[1,2,256,256]{3,2,1,0:T(8,128)(2,1)}, u32[]{:S(2)}) copy-start(bf16[1,2,256,256]{3,2,1,0:T(8,128)(2,1)} %refs_1_.5) | copy-start | bytes 786436
  2.4 6.1 %collective-permute-start.1 = (bf16[128,256]{1,0:T(8,128)(2,1)S(1)}, bf16[128,256]{1,0:T(8,128)(2,1)S(1)}, u32[]{:S(2)}, u32[]{:S(2)}) collective-permute-start(bf16[128,256]{1,0:T(8,128)(2,1)S(1)} %get-tuple-element.64), channel_id=1, source_target_pairs={{0,1},{1,0},{2,3},{3,2},{4,5},{5,4},{6,7},{7,6},{8,9},{9,8},{10,11... | collective-permute-start | bytes 196616 | tf_op jit(solution)/shard_map/ppermute | solution.py:36
  6.4 6.4 %collective-permute-start.3 = (bf16[128,384]{1,0:T(8,128)(2,1)S(1)}, bf16[128,384]{1,0:T(8,128)(2,1)S(1)}, u32[]{:S(2)}, u32[]{:S(2)}) collective-permute-start(bf16[128,384]{1,0:T(8,128)(2,1)S(1)} %get-tuple-element.68), channel_id=1, source_target_pairs={{0,1},{1,0},{2,3},{3,2},{4,5},{5,4},{6,7},{7,6},{8,9},{9,8},{10,11... | collective-permute-start | bytes 294920 | tf_op jit(solution)/shard_map/ppermute | solution.py:36
  6.5 9.5 %collective-permute-start = (bf16[128,512]{1,0:T(8,128)(2,1)S(1)}, bf16[128,512]{1,0:T(8,128)(2,1)S(1)}, u32[]{:S(2)}, u32[]{:S(2)}) collective-permute-start(bf16[128,512]{1,0:T(8,128)(2,1)S(1)} %get-tuple-element.62), channel_id=1, source_target_pairs={{0,1},{1,0},{2,3},{3,2},{4,5},{5,4},{6,7},{7,6},{8,9},{9,8},{10,11... | collective-permute-start | bytes 393224 | tf_op jit(solution)/shard_map/ppermute | solution.py:36
  8.7 6.4 %collective-permute-start.2 = (bf16[128,256]{1,0:T(8,128)(2,1)S(1)}, bf16[128,256]{1,0:T(8,128)(2,1)S(1)}, u32[]{:S(2)}, u32[]{:S(2)}) collective-permute-start(bf16[128,256]{1,0:T(8,128)(2,1)S(1)} %get-tuple-element.66), channel_id=1, source_target_pairs={{0,2},{1,3},{2,0},{3,1},{4,6},{5,7},{6,4},{7,5},{8,10},{9,11},{10,... | collective-permute-start | bytes 196616 | tf_op jit(solution)/shard_map/ppermute | solution.py:36
  13.1 7.4 %collective-permute-start.6 = (bf16[128,384]{1,0:T(8,128)(2,1)S(1)}, bf16[128,384]{1,0:T(8,128)(2,1)S(1)}, u32[]{:S(2)}, u32[]{:S(2)}) collective-permute-start(bf16[128,384]{1,0:T(8,128)(2,1)S(1)} %get-tuple-element.74), channel_id=1, source_target_pairs={{0,2},{1,3},{2,0},{3,1},{4,6},{5,7},{6,4},{7,5},{8,10},{9,11},{10,... | collective-permute-start | bytes 294920 | tf_op jit(solution)/shard_map/ppermute | solution.py:36
  15.3 5.5 %collective-permute-start.5 = (bf16[128,256]{1,0:T(8,128)(2,1)S(1)}, bf16[128,256]{1,0:T(8,128)(2,1)S(1)}, u32[]{:S(2)}, u32[]{:S(2)}) collective-permute-start(bf16[128,256]{1,0:T(8,128)(2,1)S(1)} %get-tuple-element.73), channel_id=1, source_target_pairs={{0,4},{4,0},{8,12},{12,8},{16,20},{20,16},{24,28},{28,24},{1,5},{5... | collective-permute-start | bytes 196616 | tf_op jit(solution)/shard_map/ppermute | solution.py:36
  16.2 9.5 %collective-permute-start.4 = (bf16[128,512]{1,0:T(8,128)(2,1)S(1)}, bf16[128,512]{1,0:T(8,128)(2,1)S(1)}, u32[]{:S(2)}, u32[]{:S(2)}) collective-permute-start(bf16[128,512]{1,0:T(8,128)(2,1)S(1)} %get-tuple-element.72), channel_id=1, source_target_pairs={{0,2},{1,3},{2,0},{3,1},{4,6},{5,7},{6,4},{7,5},{8,10},{9,11},{10,... | collective-permute-start | bytes 393224 | tf_op jit(solution)/shard_map/ppermute | solution.py:36
  20.7 5.4 %collective-permute-start.11 = (bf16[128,384]{1,0:T(8,128)(2,1)S(1)}, bf16[128,384]{1,0:T(8,128)(2,1)S(1)}, u32[]{:S(2)}, u32[]{:S(2)}) collective-permute-start(bf16[128,384]{1,0:T(8,128)(2,1)S(1)} %get-tuple-element.82), channel_id=1, source_target_pairs={{0,4},{4,0},{8,12},{12,8},{16,20},{20,16},{24,28},{28,24},{1,5},{5... | collective-permute-start | bytes 294920 | tf_op jit(solution)/shard_map/ppermute | solution.py:36
  20.8 7.8 %collective-permute-start.8 = (bf16[64,256]{1,0:T(8,128)(2,1)S(1)}, bf16[64,256]{1,0:T(8,128)(2,1)S(1)}, u32[]{:S(2)}, u32[]{:S(2)}) collective-permute-start(bf16[64,256]{1,0:T(8,128)(2,1)S(1)} %get-tuple-element.79), channel_id=1, source_target_pairs={{0,24},{4,28},{8,16},{12,20},{16,8},{20,12},{24,0},{28,4},{1,25},{... | collective-permute-start | bytes 98312 | tf_op jit(solution)/shard_map/ppermute | solution.py:36
  23.3 5.8 %collective-permute-start.9 = (bf16[64,256]{1,0:T(8,128)(2,1)S(1)}, bf16[64,256]{1,0:T(8,128)(2,1)S(1)}, u32[]{:S(2)}, u32[]{:S(2)}) collective-permute-start(bf16[64,256]{1,0:T(8,128)(2,1)S(1)} %get-tuple-element.80), channel_id=1, source_target_pairs={{0,8},{4,12},{8,0},{12,4},{16,24},{20,28},{24,16},{28,20},{1,9},{5... | collective-permute-start | bytes 98312 | tf_op jit(solution)/shard_map/ppermute | solution.py:36
  23.8 5.8 %collective-permute-start.10 = (bf16[64,256]{1,0:T(8,128)(2,1)S(1)}, bf16[64,256]{1,0:T(8,128)(2,1)S(1)}, u32[]{:S(2)}, u32[]{:S(2)}) collective-permute-start(bf16[64,256]{1,0:T(8,128)(2,1)S(1)} %get-tuple-element.81), channel_id=1, source_target_pairs={{0,16},{4,20},{8,24},{12,28},{16,0},{20,4},{24,8},{28,12},{1,17},{... | collective-permute-start | bytes 98312 | tf_op jit(solution)/shard_map/ppermute | solution.py:36
  26.0 4.0 %collective-permute-start.7 = (bf16[128,512]{1,0:T(8,128)(2,1)S(1)}, bf16[128,512]{1,0:T(8,128)(2,1)S(1)}, u32[]{:S(2)}, u32[]{:S(2)}) collective-permute-start(bf16[128,512]{1,0:T(8,128)(2,1)S(1)} %get-tuple-element.78), channel_id=1, source_target_pairs={{0,4},{4,0},{8,12},{12,8},{16,20},{20,16},{24,28},{28,24},{1,5},{5... | collective-permute-start | bytes 393224 | tf_op jit(solution)/shard_map/ppermute | solution.py:36
  26.1 6.4 %collective-permute-start.16 = (bf16[64,384]{1,0:T(8,128)(2,1)S(1)}, bf16[64,384]{1,0:T(8,128)(2,1)S(1)}, u32[]{:S(2)}, u32[]{:S(2)}) collective-permute-start(bf16[64,384]{1,0:T(8,128)(2,1)S(1)} %get-tuple-element.90), channel_id=1, source_target_pairs={{0,24},{4,28},{8,16},{12,20},{16,8},{20,12},{24,0},{28,4},{1,25},{... | collective-permute-start | bytes 147464 | tf_op jit(solution)/shard_map/ppermute | solution.py:36
  28.6 4.5 %collective-permute-start.17 = (bf16[64,384]{1,0:T(8,128)(2,1)S(1)}, bf16[64,384]{1,0:T(8,128)(2,1)S(1)}, u32[]{:S(2)}, u32[]{:S(2)}) collective-permute-start(bf16[64,384]{1,0:T(8,128)(2,1)S(1)} %get-tuple-element.91), channel_id=1, source_target_pairs={{0,8},{4,12},{8,0},{12,4},{16,24},{20,28},{24,16},{28,20},{1,9},{5... | collective-permute-start | bytes 147464 | tf_op jit(solution)/shard_map/ppermute | solution.py:36
  29.2 5.5 %collective-permute-start.18 = (bf16[64,384]{1,0:T(8,128)(2,1)S(1)}, bf16[64,384]{1,0:T(8,128)(2,1)S(1)}, u32[]{:S(2)}, u32[]{:S(2)}) collective-permute-start(bf16[64,384]{1,0:T(8,128)(2,1)S(1)} %get-tuple-element.92), channel_id=1, source_target_pairs={{0,16},{4,20},{8,24},{12,28},{16,0},{20,4},{24,8},{28,12},{1,17},{... | collective-permute-start | bytes 147464 | tf_op jit(solution)/shard_map/ppermute | solution.py:36
  29.9 6.9 %collective-permute-start.15 = (bf16[128,256]{1,0:T(8,128)(2,1)S(1)}, bf16[128,256]{1,0:T(8,128)(2,1)S(1)}, u32[]{:S(2)}, u32[]{:S(2)}) collective-permute-start(bf16[128,256]{1,0:T(8,128)(2,1)S(1)} %get-tuple-element.89), channel_id=1, source_target_pairs={{0,2},{1,3},{2,0},{3,1},{4,6},{5,7},{6,4},{7,5},{8,10},{9,11},{10,... | collective-permute-start | bytes 196616 | tf_op jit(solution)/shard_map/ppermute | solution.py:36
  30.0 7.0 %collective-permute-start.12 = (bf16[64,512]{1,0:T(8,128)(2,1)S(1)}, bf16[64,512]{1,0:T(8,128)(2,1)S(1)}, u32[]{:S(2)}, u32[]{:S(2)}) collective-permute-start(bf16[64,512]{1,0:T(8,128)(2,1)S(1)} %get-tuple-element.86), channel_id=1, source_target_pairs={{0,24},{4,28},{8,16},{12,20},{16,8},{20,12},{24,0},{28,4},{1,25},{... | collective-permute-start | bytes 196616 | tf_op jit(solution)/shard_map/ppermute | solution.py:36
  32.5 4.4 %collective-permute-start.13 = (bf16[64,512]{1,0:T(8,128)(2,1)S(1)}, bf16[64,512]{1,0:T(8,128)(2,1)S(1)}, u32[]{:S(2)}, u32[]{:S(2)}) collective-permute-start(bf16[64,512]{1,0:T(8,128)(2,1)S(1)} %get-tuple-element.87), channel_id=1, source_target_pairs={{0,8},{4,12},{8,0},{12,4},{16,24},{20,28},{24,16},{28,20},{1,9},{5... | collective-permute-start | bytes 196616 | tf_op jit(solution)/shard_map/ppermute | solution.py:36
  33.1 4.3 %collective-permute-start.14 = (bf16[64,512]{1,0:T(8,128)(2,1)S(1)}, bf16[64,512]{1,0:T(8,128)(2,1)S(1)}, u32[]{:S(2)}, u32[]{:S(2)}) collective-permute-start(bf16[64,512]{1,0:T(8,128)(2,1)S(1)} %get-tuple-element.88), channel_id=1, source_target_pairs={{0,16},{4,20},{8,24},{12,28},{16,0},{20,4},{24,8},{28,12},{1,17},{... | collective-permute-start | bytes 196616 | tf_op jit(solution)/shard_map/ppermute | solution.py:36
  34.9 9.7 %collective-permute-start.20 = (bf16[128,384]{1,0:T(8,128)(2,1)S(1)}, bf16[128,384]{1,0:T(8,128)(2,1)S(1)}, u32[]{:S(2)}, u32[]{:S(2)}) collective-permute-start(bf16[128,384]{1,0:T(8,128)(2,1)S(1)} %get-tuple-element.97), channel_id=1, source_target_pairs={{0,2},{1,3},{2,0},{3,1},{4,6},{5,7},{6,4},{7,5},{8,10},{9,11},{10,... | collective-permute-start | bytes 294920 | tf_op jit(solution)/shard_map/ppermute | solution.py:36
  37.6 10.1 %collective-permute-start.19 = (bf16[128,512]{1,0:T(8,128)(2,1)S(1)}, bf16[128,512]{1,0:T(8,128)(2,1)S(1)}, u32[]{:S(2)}, u32[]{:S(2)}) collective-permute-start(bf16[128,512]{1,0:T(8,128)(2,1)S(1)} %get-tuple-element.96), channel_id=1, source_target_pairs={{0,2},{1,3},{2,0},{3,1},{4,6},{5,7},{6,4},{7,5},{8,10},{9,11},{10,... | collective-permute-start | bytes 393224 | tf_op jit(solution)/shard_map/ppermute | solution.py:36
  44.8 6.7 %collective-permute-start.22 = (bf16[128,640]{1,0:T(8,128)(2,1)S(1)}, bf16[128,640]{1,0:T(8,128)(2,1)S(1)}, u32[]{:S(2)}, u32[]{:S(2)}) collective-permute-start(bf16[128,640]{1,0:T(8,128)(2,1)S(1)} %get-tuple-element.102), channel_id=1, source_target_pairs={{0,1},{1,0},{2,3},{3,2},{4,5},{5,4},{6,7},{7,6},{8,9},{9,8},{10,11... | collective-permute-start | bytes 491528 | tf_op jit(solution)/shard_map/ppermute | solution.py:36
  48.0 5.0 %collective-permute-start.21 = (bf16[128,512]{1,0:T(8,128)(2,1)S(1)}, bf16[128,512]{1,0:T(8,128)(2,1)S(1)}, u32[]{:S(2)}, u32[]{:S(2)}) collective-permute-start(bf16[128,512]{1,0:T(8,128)(2,1)S(1)} %get-tuple-element.100), channel_id=1, source_target_pairs={{0,1},{1,0},{2,3},{3,2},{4,5},{5,4},{6,7},{7,6},{8,9},{9,8},{10,11... | collective-permute-start | bytes 393224 | tf_op jit(solution)/shard_map/ppermute | solution.py:36
  (4 other events, 20.4 us)

commit v17 on v8

--- a/solution.py
+++ b/solution.py
@@ -112,7 +112,7 @@
 def opening(name, basis, signal, widths):
     rows, width = basis.shape
     half = width // 2
-    pieces = row_pieces(rows, 6)
+    pieces = row_pieces(rows, 12)
     depth = rows // pieces
     lows = [sum(widths[:i]) for i in range(len(widths))]
 
@@ -236,7 +236,7 @@
 def last(name, weight, basis, keep, got, before, low, columns, after):
     rows, width = basis.shape
     wide = keep.shape[1]
-    pieces = row_pieces(rows, 6)
+    pieces = row_pieces(rows, 4)
     depth = rows // pieces
     given = [] if before is None else [before]
 

time: 53.5 us -> 53.7 us (level)
  transfers between devices with their start and end apart: 24 -> 24, of which waited for: 12 -> 11; matrix products, arithmetic and copies ran while one was open for 0% -> 0% of each run, Pallas kernels for 11% -> 11%
where the time goes in v17:
time: 53.7 us; the launch traced here: 53.5 us
  starting transfers between devices  29.7 us (55%)
  waiting for transfers between devices  13.5 us (25%)
  Pallas kernels  10 us (19%)
    ppermute x24, starting transfers between devices, swap(): return lax.ppermute(block, axis, [(i, i ^ distance) for i in range(count)])  29.7 us
    ppermute x24, waiting for transfers between devices, swap(): return lax.ppermute(block, axis, [(i, i ^ distance) for i in range(count)])  13.5 us
    pallas_call x20, Pallas kernels, call(): pl.pallas_call(body, name=name, in_specs=specs + [PLACE] * len(extra), ou...  10 us
  transfers between devices with their start and end apart: 24, of which 11 were waited for; matrix products, arithmetic and copies ran while one was open for 0% of the time, Pallas kernels for 11%

profile of v17, /device:TPU:0, one launch (start us, length us, event | category | flops | bytes accessed | tf_op | source)
XLA Modules:
  0.0 53.5 jit_solution(15118687901004345128)
XLA Ops:
  0.0 2.7 %opening.1 = (bf16[128,384]{1,0:T(8,128)(2,1)S(1)}, bf16[128,384]{1,0:T(8,128)(2,1)S(1)}, bf16[128,384]{1,0:T(8,128)(2,1)S(1)}, bf16[128,384]{1,0:T(8,128)(2,1)S...) custom-call(bf16[768,256]{1,0:T(8,128)(2,1)} %refs_0_.3, bf16[768,1152]{1,0:T(8,128)(2,1)} %refs_1_.6), custom_call_target="tpu_custom_call" | custom-call | flops 452984832 | bytes 2162688 | tf_op jit(solution)/shard_map/opening/pallas_call | solution.py:59
  2.7 3.1 %collective-permute-start.1 = (bf16[128,384]{1,0:T(8,128)(2,1)S(1)}, bf16[128,384]{1,0:T(8,128)(2,1)S(1)}, u32[]{:S(2)}, u32[]{:S(2)}) collective-permute-start(bf16[128,384]{1,0:T(8,128)(2,1)S(1)} %get-tuple-element.60), channel_id=1, source_target_pairs={{0,1},{1,0},{2,3},{3,2},{4,5},{5,4},{6,7},{7,6},{8,9},{9,8},{10,11... | collective-permute-start | bytes 294920 | tf_op jit(solution)/shard_map/ppermute | solution.py:35
  6.8 2.6 %collective-permute-done.1.refs_2_ = bf16[128,384]{1,0:T(8,128)(2,1)S(1)} collective-permute-done((bf16[128,384]{1,0:T(8,128)(2,1)S(1)}, bf16[128,384]{1,0:T(8,128)(2,1)S(1)}, u32[]{:S(2)}, u32[]{:S(2)}) %collective-permute-start.1) | collective-permute-done | bytes 98336 | tf_op jit(solution)/shard_map/ppermute | solution.py:35
  9.6 3.1 %collective-permute-start.2 = (bf16[128,384]{1,0:T(8,128)(2,1)S(1)}, bf16[128,384]{1,0:T(8,128)(2,1)S(1)}, u32[]{:S(2)}, u32[]{:S(2)}) collective-permute-start(bf16[128,384]{1,0:T(8,128)(2,1)S(1)} %get-tuple-element.62), channel_id=1, source_target_pairs={{0,2},{1,3},{2,0},{3,1},{4,6},{5,7},{6,4},{7,5},{8,10},{9,11},{10,... | collective-permute-start | bytes 294920 | tf_op jit(solution)/shard_map/ppermute | solution.py:35
  12.6 1.7 %collective-permute-start = (bf16[128,384]{1,0:T(8,128)(2,1)S(1)}, bf16[128,384]{1,0:T(8,128)(2,1)S(1)}, u32[]{:S(2)}, u32[]{:S(2)}) collective-permute-start(bf16[128,384]{1,0:T(8,128)(2,1)S(1)} %get-tuple-element.58), channel_id=1, source_target_pairs={{0,1},{1,0},{2,3},{3,2},{4,5},{5,4},{6,7},{7,6},{8,9},{9,8},{10,11... | collective-permute-start | bytes 294920 | tf_op jit(solution)/shard_map/ppermute | solution.py:35
  14.9 2.4 %collective-permute-done.2.refs_2_ = bf16[128,384]{1,0:T(8,128)(2,1)S(1)} collective-permute-done((bf16[128,384]{1,0:T(8,128)(2,1)S(1)}, bf16[128,384]{1,0:T(8,128)(2,1)S(1)}, u32[]{:S(2)}, u32[]{:S(2)}) %collective-permute-start.2) | collective-permute-done | bytes 98336 | tf_op jit(solution)/shard_map/ppermute | solution.py:35
  17.9 1.5 %collective-permute-start.4 = (bf16[128,384]{1,0:T(8,128)(2,1)S(1)}, bf16[128,384]{1,0:T(8,128)(2,1)S(1)}, u32[]{:S(2)}, u32[]{:S(2)}) collective-permute-start(bf16[128,384]{1,0:T(8,128)(2,1)S(1)} %get-tuple-element.68), channel_id=1, source_target_pairs={{0,2},{1,3},{2,0},{3,1},{4,6},{5,7},{6,4},{7,5},{8,10},{9,11},{10,... | collective-permute-start | bytes 294920 | tf_op jit(solution)/shard_map/ppermute | solution.py:35
  19.4 1.6 %collective-permute-done.6.refs_2_ = bf16[128,384]{1,0:T(8,128)(2,1)S(1)} collective-permute-done((bf16[128,384]{1,0:T(8,128)(2,1)S(1)}, bf16[128,384]{1,0:T(8,128)(2,1)S(1)}, u32[]{:S(2)}, u32[]{:S(2)}) %collective-permute-start.6) | collective-permute-done | bytes 98336 | tf_op jit(solution)/shard_map/ppermute | solution.py:35
  21.3 1.6 %collective-permute-start.8 = (bf16[64,384]{1,0:T(8,128)(2,1)S(1)}, bf16[64,384]{1,0:T(8,128)(2,1)S(1)}, u32[]{:S(2)}, u32[]{:S(2)}) collective-permute-start(bf16[64,384]{1,0:T(8,128)(2,1)S(1)} %get-tuple-element.75), channel_id=1, source_target_pairs={{0,8},{4,12},{8,0},{12,4},{16,24},{20,28},{24,16},{28,20},{1,9},{5... | collective-permute-start | bytes 147464 | tf_op jit(solution)/shard_map/ppermute | solution.py:35
  22.9 1.5 %collective-permute-start.9 = (bf16[64,384]{1,0:T(8,128)(2,1)S(1)}, bf16[64,384]{1,0:T(8,128)(2,1)S(1)}, u32[]{:S(2)}, u32[]{:S(2)}) collective-permute-start(bf16[64,384]{1,0:T(8,128)(2,1)S(1)} %get-tuple-element.76), channel_id=1, source_target_pairs={{0,16},{4,20},{8,24},{12,28},{16,0},{20,4},{24,8},{28,12},{1,17},{... | collective-permute-start | bytes 147464 | tf_op jit(solution)/shard_map/ppermute | solution.py:35
  25.5 1.5 %collective-permute-done.9.refs_3_ = bf16[64,384]{1,0:T(8,128)(2,1)S(1)} collective-permute-done((bf16[64,384]{1,0:T(8,128)(2,1)S(1)}, bf16[64,384]{1,0:T(8,128)(2,1)S(1)}, u32[]{:S(2)}, u32[]{:S(2)}) %collective-permute-start.9) | collective-permute-done | bytes 49184 | tf_op jit(solution)/shard_map/ppermute | solution.py:35
  27.0 2.4 %collective-permute-done.10.refs_4_ = bf16[64,384]{1,0:T(8,128)(2,1)S(1)} collective-permute-done((bf16[64,384]{1,0:T(8,128)(2,1)S(1)}, bf16[64,384]{1,0:T(8,128)(2,1)S(1)}, u32[]{:S(2)}, u32[]{:S(2)}) %collective-permute-start.10) | collective-permute-done | bytes 49184 | tf_op jit(solution)/shard_map/ppermute | solution.py:35
  29.6 0.9 %collective-permute-start.15 = (bf16[128,384]{1,0:T(8,128)(2,1)S(1)}, bf16[128,384]{1,0:T(8,128)(2,1)S(1)}, u32[]{:S(2)}, u32[]{:S(2)}) collective-permute-start(bf16[128,384]{1,0:T(8,128)(2,1)S(1)} %get-tuple-element.85), channel_id=1, source_target_pairs={{0,2},{1,3},{2,0},{3,1},{4,6},{5,7},{6,4},{7,5},{8,10},{9,11},{10,... | collective-permute-start | bytes 294920 | tf_op jit(solution)/shard_map/ppermute | solution.py:35
  31.2 2.8 %collective-permute-start.18 = (bf16[64,384]{1,0:T(8,128)(2,1)S(1)}, bf16[64,384]{1,0:T(8,128)(2,1)S(1)}, u32[]{:S(2)}, u32[]{:S(2)}) collective-permute-start(bf16[64,384]{1,0:T(8,128)(2,1)S(1)} %get-tuple-element.88), channel_id=1, source_target_pairs={{0,24},{4,28},{8,16},{12,20},{16,8},{20,12},{24,0},{28,4},{1,25},{... | collective-permute-start | bytes 147464 | tf_op jit(solution)/shard_map/ppermute | solution.py:35
  36.4 1.2 %collective-permute-start.14 = (bf16[64,384]{1,0:T(8,128)(2,1)S(1)}, bf16[64,384]{1,0:T(8,128)(2,1)S(1)}, u32[]{:S(2)}, u32[]{:S(2)}) collective-permute-start(bf16[64,384]{1,0:T(8,128)(2,1)S(1)} %get-tuple-element.84), channel_id=1, source_target_pairs={{0,24},{4,28},{8,16},{12,20},{16,8},{20,12},{24,0},{28,4},{1,25},{... | collective-permute-start | bytes 147464 | tf_op jit(solution)/shard_map/ppermute | solution.py:35
  37.8 2.2 %collective-permute-start.20 = (bf16[128,384]{1,0:T(8,128)(2,1)S(1)}, bf16[128,384]{1,0:T(8,128)(2,1)S(1)}, u32[]{:S(2)}, u32[]{:S(2)}) collective-permute-start(bf16[128,384]{1,0:T(8,128)(2,1)S(1)} %get-tuple-element.93), channel_id=1, source_target_pairs={{0,2},{1,3},{2,0},{3,1},{4,6},{5,7},{6,4},{7,5},{8,10},{9,11},{10,... | collective-permute-start | bytes 294920 | tf_op jit(solution)/shard_map/ppermute | solution.py:35
  40.2 1.1 %collective-permute-done.14.refs_4_ = bf16[64,384]{1,0:T(8,128)(2,1)S(1)} collective-permute-done((bf16[64,384]{1,0:T(8,128)(2,1)S(1)}, bf16[64,384]{1,0:T(8,128)(2,1)S(1)}, u32[]{:S(2)}, u32[]{:S(2)}) %collective-permute-start.14) | collective-permute-done | bytes 49184 | tf_op jit(solution)/shard_map/ppermute | solution.py:35
  41.6 1.7 %collective-permute-start.19 = (bf16[128,384]{1,0:T(8,128)(2,1)S(1)}, bf16[128,384]{1,0:T(8,128)(2,1)S(1)}, u32[]{:S(2)}, u32[]{:S(2)}) collective-permute-start(bf16[128,384]{1,0:T(8,128)(2,1)S(1)} %get-tuple-element.92), channel_id=1, source_target_pairs={{0,2},{1,3},{2,0},{3,1},{4,6},{5,7},{6,4},{7,5},{8,10},{9,11},{10,... | collective-permute-start | bytes 294920 | tf_op jit(solution)/shard_map/ppermute | solution.py:35
  43.3 2.4 %collective-permute-start.23 = (bf16[128,384]{1,0:T(8,128)(2,1)S(1)}, bf16[128,384]{1,0:T(8,128)(2,1)S(1)}, u32[]{:S(2)}, u32[]{:S(2)}) collective-permute-start(bf16[128,384]{1,0:T(8,128)(2,1)S(1)} %get-tuple-element.98), channel_id=1, source_target_pairs={{0,1},{1,0},{2,3},{3,2},{4,5},{5,4},{6,7},{7,6},{8,9},{9,8},{10,11... | collective-permute-start | bytes 294920 | tf_op jit(solution)/shard_map/ppermute | solution.py:35
  46.2 1.2 %collective-permute-start.22 = (bf16[128,384]{1,0:T(8,128)(2,1)S(1)}, bf16[128,384]{1,0:T(8,128)(2,1)S(1)}, u32[]{:S(2)}, u32[]{:S(2)}) collective-permute-start(bf16[128,384]{1,0:T(8,128)(2,1)S(1)} %get-tuple-element.97), channel_id=1, source_target_pairs={{0,1},{1,0},{2,3},{3,2},{4,5},{5,4},{6,7},{7,6},{8,9},{9,8},{10,11... | collective-permute-start | bytes 294920 | tf_op jit(solution)/shard_map/ppermute | solution.py:35
  47.6 1.9 %collective-permute-start.21 = (bf16[128,384]{1,0:T(8,128)(2,1)S(1)}, bf16[128,384]{1,0:T(8,128)(2,1)S(1)}, u32[]{:S(2)}, u32[]{:S(2)}) collective-permute-start(bf16[128,384]{1,0:T(8,128)(2,1)S(1)} %get-tuple-element.96), channel_id=1, source_target_pairs={{0,1},{1,0},{2,3},{3,2},{4,5},{5,4},{6,7},{7,6},{8,9},{9,8},{10,11... | collective-permute-start | bytes 294920 | tf_op jit(solution)/shard_map/ppermute | solution.py:35
  49.5 1.3 %last0.1.refs_4_ = bf16[768,1152]{1,0:T(8,128)(2,1)} custom-call(bf16[256,256]{1,0:T(8,128)(2,1)S(1)} %get-tuple-element.52.refs_0_, bf16[768,256]{1,0:T(8,128)(2,1)S(1)} %copy-done, bf16[128,384]{1,0:T(8,128)(2,1)S(1)} %get-tuple-element.90.refs_5_.refs_2_, bf16[128,384]{1,0:T(8,128)(2,1)S(1)} %collective-permute-done.23.refs_3_, ...), custom_call_target="tpu_custom_call" | custom-call | flops 150994944 | bytes 589824 | tf_op jit(solution)/shard_map/last0/pallas_call | solution.py:59
  50.8 1.3 %last384.1.refs_4_ = bf16[768,1152]{1,0:T(8,128)(2,1)} custom-call(bf16[256,256]{1,0:T(8,128)(2,1)S(1)} %get-tuple-element.52.refs_0_, bf16[768,256]{1,0:T(8,128)(2,1)S(1)} %copy-done, bf16[128,384]{1,0:T(8,128)(2,1)S(1)} %get-tuple-element.94.refs_3_.refs_4_.refs_2_, ...), custom_call_target="tpu_custom_call", output_to_operand_aliasing={{}: (4, {})} | custom-call | flops 150994944 | bytes 589824 | tf_op jit(solution)/shard_map/last384/pallas_call | solution.py:59
  52.3 1.3 %last768.1 = bf16[768,1152]{1,0:T(8,128)(2,1)} custom-call(bf16[256,256]{1,0:T(8,128)(2,1)S(1)} %get-tuple-element.52.refs_0_, bf16[768,256]{1,0:T(8,128)(2,1)S(1)} %copy-done, bf16[128,384]{1,0:T(8,128)(2,1)S(1)} %get-tuple-element.95.refs_5_.refs_2_, bf16[128,384]{1,0:T(8,128)(2,1)S(1)} %collective-permute-done.21.refs_3_, ...), custom_call_target="tpu_custom_call", output_to_operand_aliasing={{}: (4, {})} | custom-call | flops 150994944 | bytes 589824 | tf_op jit(solution)/shard_map/last768/pallas_call | solution.py:59
  (54 shorter events, 8.6 us)
Async XLA Ops:
  2.7 6.6 %collective-permute-start.1 = (bf16[128,384]{1,0:T(8,128)(2,1)S(1)}, bf16[128,384]{1,0:T(8,128)(2,1)S(1)}, u32[]{:S(2)}, u32[]{:S(2)}) collective-permute-start(bf16[128,384]{1,0:T(8,128)(2,1)S(1)} %get-tuple-element.60), channel_id=1, source_target_pairs={{0,1},{1,0},{2,3},{3,2},{4,5},{5,4},{6,7},{7,6},{8,9},{9,8},{10,11... | collective-permute-start | bytes 294920 | tf_op jit(solution)/shard_map/ppermute | solution.py:35
  5.8 8.5 %collective-permute-start.3 = (bf16[128,384]{1,0:T(8,128)(2,1)S(1)}, bf16[128,384]{1,0:T(8,128)(2,1)S(1)}, u32[]{:S(2)}, u32[]{:S(2)}) collective-permute-start(bf16[128,384]{1,0:T(8,128)(2,1)S(1)} %get-tuple-element.64), channel_id=1, source_target_pairs={{0,1},{1,0},{2,3},{3,2},{4,5},{5,4},{6,7},{7,6},{8,9},{9,8},{10,11... | collective-permute-start | bytes 294920 | tf_op jit(solution)/shard_map/ppermute | solution.py:35
  9.6 7.8 %collective-permute-start.2 = (bf16[128,384]{1,0:T(8,128)(2,1)S(1)}, bf16[128,384]{1,0:T(8,128)(2,1)S(1)}, u32[]{:S(2)}, u32[]{:S(2)}) collective-permute-start(bf16[128,384]{1,0:T(8,128)(2,1)S(1)} %get-tuple-element.62), channel_id=1, source_target_pairs={{0,2},{1,3},{2,0},{3,1},{4,6},{5,7},{6,4},{7,5},{8,10},{9,11},{10,... | collective-permute-start | bytes 294920 | tf_op jit(solution)/shard_map/ppermute | solution.py:35
  12.6 5.0 %collective-permute-start = (bf16[128,384]{1,0:T(8,128)(2,1)S(1)}, bf16[128,384]{1,0:T(8,128)(2,1)S(1)}, u32[]{:S(2)}, u32[]{:S(2)}) collective-permute-start(bf16[128,384]{1,0:T(8,128)(2,1)S(1)} %get-tuple-element.58), channel_id=1, source_target_pairs={{0,1},{1,0},{2,3},{3,2},{4,5},{5,4},{6,7},{7,6},{8,9},{9,8},{10,11... | collective-permute-start | bytes 294920 | tf_op jit(solution)/shard_map/ppermute | solution.py:35
  14.5 6.4 %collective-permute-start.6 = (bf16[128,384]{1,0:T(8,128)(2,1)S(1)}, bf16[128,384]{1,0:T(8,128)(2,1)S(1)}, u32[]{:S(2)}, u32[]{:S(2)}) collective-permute-start(bf16[128,384]{1,0:T(8,128)(2,1)S(1)} %get-tuple-element.70), channel_id=1, source_target_pairs={{0,2},{1,3},{2,0},{3,1},{4,6},{5,7},{6,4},{7,5},{8,10},{9,11},{10,... | collective-permute-start | bytes 294920 | tf_op jit(solution)/shard_map/ppermute | solution.py:35
  17.6 3.7 %collective-permute-start.5 = (bf16[128,384]{1,0:T(8,128)(2,1)S(1)}, bf16[128,384]{1,0:T(8,128)(2,1)S(1)}, u32[]{:S(2)}, u32[]{:S(2)}) collective-permute-start(bf16[128,384]{1,0:T(8,128)(2,1)S(1)} %get-tuple-element.69), channel_id=1, source_target_pairs={{0,4},{4,0},{8,12},{12,8},{16,20},{20,16},{24,28},{28,24},{1,5},{5... | collective-permute-start | bytes 294920 | tf_op jit(solution)/shard_map/ppermute | solution.py:35
  17.9 7.0 %collective-permute-start.4 = (bf16[128,384]{1,0:T(8,128)(2,1)S(1)}, bf16[128,384]{1,0:T(8,128)(2,1)S(1)}, u32[]{:S(2)}, u32[]{:S(2)}) collective-permute-start(bf16[128,384]{1,0:T(8,128)(2,1)S(1)} %get-tuple-element.68), channel_id=1, source_target_pairs={{0,2},{1,3},{2,0},{3,1},{4,6},{5,7},{6,4},{7,5},{8,10},{9,11},{10,... | collective-permute-start | bytes 294920 | tf_op jit(solution)/shard_map/ppermute | solution.py:35
  21.2 4.0 %collective-permute-start.11 = (bf16[128,384]{1,0:T(8,128)(2,1)S(1)}, bf16[128,384]{1,0:T(8,128)(2,1)S(1)}, u32[]{:S(2)}, u32[]{:S(2)}) collective-permute-start(bf16[128,384]{1,0:T(8,128)(2,1)S(1)} %get-tuple-element.78), channel_id=1, source_target_pairs={{0,4},{4,0},{8,12},{12,8},{16,20},{20,16},{24,28},{28,24},{1,5},{5... | collective-permute-start | bytes 294920 | tf_op jit(solution)/shard_map/ppermute | solution.py:35
  21.3 4.2 %collective-permute-start.8 = (bf16[64,384]{1,0:T(8,128)(2,1)S(1)}, bf16[64,384]{1,0:T(8,128)(2,1)S(1)}, u32[]{:S(2)}, u32[]{:S(2)}) collective-permute-start(bf16[64,384]{1,0:T(8,128)(2,1)S(1)} %get-tuple-element.75), channel_id=1, source_target_pairs={{0,8},{4,12},{8,0},{12,4},{16,24},{20,28},{24,16},{28,20},{1,9},{5... | collective-permute-start | bytes 147464 | tf_op jit(solution)/shard_map/ppermute | solution.py:35
  22.9 4.1 %collective-permute-start.9 = (bf16[64,384]{1,0:T(8,128)(2,1)S(1)}, bf16[64,384]{1,0:T(8,128)(2,1)S(1)}, u32[]{:S(2)}, u32[]{:S(2)}) collective-permute-start(bf16[64,384]{1,0:T(8,128)(2,1)S(1)} %get-tuple-element.76), channel_id=1, source_target_pairs={{0,16},{4,20},{8,24},{12,28},{16,0},{20,4},{24,8},{28,12},{1,17},{... | collective-permute-start | bytes 147464 | tf_op jit(solution)/shard_map/ppermute | solution.py:35
  24.4 5.0 %collective-permute-start.10 = (bf16[64,384]{1,0:T(8,128)(2,1)S(1)}, bf16[64,384]{1,0:T(8,128)(2,1)S(1)}, u32[]{:S(2)}, u32[]{:S(2)}) collective-permute-start(bf16[64,384]{1,0:T(8,128)(2,1)S(1)} %get-tuple-element.77), channel_id=1, source_target_pairs={{0,24},{4,28},{8,16},{12,20},{16,8},{20,12},{24,0},{28,4},{1,25},{... | collective-permute-start | bytes 147464 | tf_op jit(solution)/shard_map/ppermute | solution.py:35
  25.1 8.9 %collective-permute-start.7 = (bf16[128,384]{1,0:T(8,128)(2,1)S(1)}, bf16[128,384]{1,0:T(8,128)(2,1)S(1)}, u32[]{:S(2)}, u32[]{:S(2)}) collective-permute-start(bf16[128,384]{1,0:T(8,128)(2,1)S(1)} %get-tuple-element.74), channel_id=1, source_target_pairs={{0,4},{4,0},{8,12},{12,8},{16,20},{20,16},{24,28},{28,24},{1,5},{5... | collective-permute-start | bytes 294920 | tf_op jit(solution)/shard_map/ppermute | solution.py:35
  29.6 10.4 %collective-permute-start.15 = (bf16[128,384]{1,0:T(8,128)(2,1)S(1)}, bf16[128,384]{1,0:T(8,128)(2,1)S(1)}, u32[]{:S(2)}, u32[]{:S(2)}) collective-permute-start(bf16[128,384]{1,0:T(8,128)(2,1)S(1)} %get-tuple-element.85), channel_id=1, source_target_pairs={{0,2},{1,3},{2,0},{3,1},{4,6},{5,7},{6,4},{7,5},{8,10},{9,11},{10,... | collective-permute-start | bytes 294920 | tf_op jit(solution)/shard_map/ppermute | solution.py:35
  30.5 4.5 %collective-permute-start.16 = (bf16[64,384]{1,0:T(8,128)(2,1)S(1)}, bf16[64,384]{1,0:T(8,128)(2,1)S(1)}, u32[]{:S(2)}, u32[]{:S(2)}) collective-permute-start(bf16[64,384]{1,0:T(8,128)(2,1)S(1)} %get-tuple-element.86), channel_id=1, source_target_pairs={{0,8},{4,12},{8,0},{12,4},{16,24},{20,28},{24,16},{28,20},{1,9},{5... | collective-permute-start | bytes 147464 | tf_op jit(solution)/shard_map/ppermute | solution.py:35
  31.0 5.4 %collective-permute-start.17 = (bf16[64,384]{1,0:T(8,128)(2,1)S(1)}, bf16[64,384]{1,0:T(8,128)(2,1)S(1)}, u32[]{:S(2)}, u32[]{:S(2)}) collective-permute-start(bf16[64,384]{1,0:T(8,128)(2,1)S(1)} %get-tuple-element.87), channel_id=1, source_target_pairs={{0,16},{4,20},{8,24},{12,28},{16,0},{20,4},{24,8},{28,12},{1,17},{... | collective-permute-start | bytes 147464 | tf_op jit(solution)/shard_map/ppermute | solution.py:35
  31.2 6.4 %collective-permute-start.18 = (bf16[64,384]{1,0:T(8,128)(2,1)S(1)}, bf16[64,384]{1,0:T(8,128)(2,1)S(1)}, u32[]{:S(2)}, u32[]{:S(2)}) collective-permute-start(bf16[64,384]{1,0:T(8,128)(2,1)S(1)} %get-tuple-element.88), channel_id=1, source_target_pairs={{0,24},{4,28},{8,16},{12,20},{16,8},{20,12},{24,0},{28,4},{1,25},{... | collective-permute-start | bytes 147464 | tf_op jit(solution)/shard_map/ppermute | solution.py:35
  34.0 6.2 %collective-permute-start.12 = (bf16[64,384]{1,0:T(8,128)(2,1)S(1)}, bf16[64,384]{1,0:T(8,128)(2,1)S(1)}, u32[]{:S(2)}, u32[]{:S(2)}) collective-permute-start(bf16[64,384]{1,0:T(8,128)(2,1)S(1)} %get-tuple-element.82), channel_id=1, source_target_pairs={{0,8},{4,12},{8,0},{12,4},{16,24},{20,28},{24,16},{28,20},{1,9},{5... | collective-permute-start | bytes 147464 | tf_op jit(solution)/shard_map/ppermute | solution.py:35
  35.0 5.2 %collective-permute-start.13 = (bf16[64,384]{1,0:T(8,128)(2,1)S(1)}, bf16[64,384]{1,0:T(8,128)(2,1)S(1)}, u32[]{:S(2)}, u32[]{:S(2)}) collective-permute-start(bf16[64,384]{1,0:T(8,128)(2,1)S(1)} %get-tuple-element.83), channel_id=1, source_target_pairs={{0,16},{4,20},{8,24},{12,28},{16,0},{20,4},{24,8},{28,12},{1,17},{... | collective-permute-start | bytes 147464 | tf_op jit(solution)/shard_map/ppermute | solution.py:35
  36.4 5.0 %collective-permute-start.14 = (bf16[64,384]{1,0:T(8,128)(2,1)S(1)}, bf16[64,384]{1,0:T(8,128)(2,1)S(1)}, u32[]{:S(2)}, u32[]{:S(2)}) collective-permute-start(bf16[64,384]{1,0:T(8,128)(2,1)S(1)} %get-tuple-element.84), channel_id=1, source_target_pairs={{0,24},{4,28},{8,16},{12,20},{16,8},{20,12},{24,0},{28,4},{1,25},{... | collective-permute-start | bytes 147464 | tf_op jit(solution)/shard_map/ppermute | solution.py:35
  37.8 8.1 %collective-permute-start.20 = (bf16[128,384]{1,0:T(8,128)(2,1)S(1)}, bf16[128,384]{1,0:T(8,128)(2,1)S(1)}, u32[]{:S(2)}, u32[]{:S(2)}) collective-permute-start(bf16[128,384]{1,0:T(8,128)(2,1)S(1)} %get-tuple-element.93), channel_id=1, source_target_pairs={{0,2},{1,3},{2,0},{3,1},{4,6},{5,7},{6,4},{7,5},{8,10},{9,11},{10,... | collective-permute-start | bytes 294920 | tf_op jit(solution)/shard_map/ppermute | solution.py:35
  41.6 5.8 %collective-permute-start.19 = (bf16[128,384]{1,0:T(8,128)(2,1)S(1)}, bf16[128,384]{1,0:T(8,128)(2,1)S(1)}, u32[]{:S(2)}, u32[]{:S(2)}) collective-permute-start(bf16[128,384]{1,0:T(8,128)(2,1)S(1)} %get-tuple-element.92), channel_id=1, source_target_pairs={{0,2},{1,3},{2,0},{3,1},{4,6},{5,7},{6,4},{7,5},{8,10},{9,11},{10,... | collective-permute-start | bytes 294920 | tf_op jit(solution)/shard_map/ppermute | solution.py:35
  43.3 6.2 %collective-permute-start.23 = (bf16[128,384]{1,0:T(8,128)(2,1)S(1)}, bf16[128,384]{1,0:T(8,128)(2,1)S(1)}, u32[]{:S(2)}, u32[]{:S(2)}) collective-permute-start(bf16[128,384]{1,0:T(8,128)(2,1)S(1)} %get-tuple-element.98), channel_id=1, source_target_pairs={{0,1},{1,0},{2,3},{3,2},{4,5},{5,4},{6,7},{7,6},{8,9},{9,8},{10,11... | collective-permute-start | bytes 294920 | tf_op jit(solution)/shard_map/ppermute | solution.py:35
  46.2 4.7 %collective-permute-start.22 = (bf16[128,384]{1,0:T(8,128)(2,1)S(1)}, bf16[128,384]{1,0:T(8,128)(2,1)S(1)}, u32[]{:S(2)}, u32[]{:S(2)}) collective-permute-start(bf16[128,384]{1,0:T(8,128)(2,1)S(1)} %get-tuple-element.97), channel_id=1, source_target_pairs={{0,1},{1,0},{2,3},{3,2},{4,5},{5,4},{6,7},{7,6},{8,9},{9,8},{10,11... | collective-permute-start | bytes 294920 | tf_op jit(solution)/shard_map/ppermute | solution.py:35
  47.6 4.7 %collective-permute-start.21 = (bf16[128,384]{1,0:T(8,128)(2,1)S(1)}, bf16[128,384]{1,0:T(8,128)(2,1)S(1)}, u32[]{:S(2)}, u32[]{:S(2)}) collective-permute-start(bf16[128,384]{1,0:T(8,128)(2,1)S(1)} %get-tuple-element.96), channel_id=1, source_target_pairs={{0,1},{1,0},{2,3},{3,2},{4,5},{5,4},{6,7},{7,6},{8,9},{9,8},{10,11... | collective-permute-start | bytes 294920 | tf_op jit(solution)/shard_map/ppermute | solution.py:35
  (5 other events, 51.9 us)

commit v18 on v16

--- a/solution.py
+++ b/solution.py
@@ -6,7 +6,7 @@
 from jax.sharding import PartitionSpec as P
 
 LANES = 128
-SHARES = (2, 3, 4)
+SHARES = (3, 3, 3)
 HEADS = ((0,), (1,), (2,))
 TAILS = ((0, 1), (2,))
 ENTRY = (0, 0, 1)
@@ -48,7 +48,7 @@
 
 
 def span(name):
-    flops = SPANS.get(name.split("_")[0], 10**9)
+    flops = SPANS.get(name.split("_")[0], 0)
     return pl.CostEstimate(flops=flops, bytes_accessed=0, transcendentals=0)
 
 
@@ -118,7 +118,7 @@
 def opening(name, basis, signal, widths, groups):
     rows, width = basis.shape
     half = width // 2
-    pieces = row_pieces(rows, 6)
+    pieces = row_pieces(rows, 2)
     depth = rows // pieces
     lows = [sum(widths[:i]) for i in range(len(widths))]
     all_widths = widths + [sum(widths[i] for i in group) for group in groups]

time: 54.5 us -> 59.3 us (1.088)
  starting transfers between devices: 29 us -> 32.6 us
  waiting for transfers between devices: 16.5 us -> 17.6 us
    ppermute x23, starting transfers between devices: 29 us -> 32.6 us  [swap(): return lax.ppermute(block, axis, [(i, i ^ distance) for i in range(count)])]
    ppermute x23, waiting for transfers between devices: 16.5 us -> 17.6 us  [swap(): return lax.ppermute(block, axis, [(i, i ^ distance) for i in range(count)])]
  transfers between devices with their start and end apart: 23 -> 23, of which waited for: 8 -> 9; matrix products, arithmetic and copies ran while one was open for 0% -> 0% of each run, Pallas kernels for 9% -> 8%
where the time goes in v18:
time: 59.3 us; the launch traced here: 59.2 us
  starting transfers between devices  32.6 us (55%)
  waiting for transfers between devices  17.6 us (30%)
  Pallas kernels  8.77 us (15%)
    ppermute x23, starting transfers between devices, swap(): return lax.ppermute(block, axis, [(i, i ^ distance) for i in range(count)])  32.6 us
    ppermute x23, waiting for transfers between devices, swap(): return lax.ppermute(block, axis, [(i, i ^ distance) for i in range(count)])  17.6 us
    pallas_call x19, Pallas kernels, call(): pl.pallas_call(body, name=name, in_specs=specs + [PLACE] * len(extra), ou...  8.77 us
  transfers between devices with their start and end apart: 23, of which 9 were waited for; matrix products, arithmetic and copies ran while one was open for 0% of the time, Pallas kernels for 8%

profile of v18, /device:TPU:0, one launch (start us, length us, event | category | flops | bytes accessed | tf_op | source)
XLA Modules:
  0.0 59.2 jit_solution(16995485746152897992)
XLA Ops:
  0.0 2.4 %opening.1 = (bf16[128,384]{1,0:T(8,128)(2,1)S(1)}, bf16[128,384]{1,0:T(8,128)(2,1)S(1)}, bf16[128,384]{1,0:T(8,128)(2,1)S(1)}, bf16[128,384]{1,0:T(8,128)(2,1)S...) custom-call(bf16[768,256]{1,0:T(8,128)(2,1)} %refs_0_.2, bf16[768,1152]{1,0:T(8,128)(2,1)} %refs_1_.4), custom_call_target="tpu_custom_call" | custom-call | tf_op jit(solution)/shard_map/opening/pallas_call | solution.py:61
  2.4 3.1 %collective-permute-start.1 = (bf16[128,384]{1,0:T(8,128)(2,1)S(1)}, bf16[128,384]{1,0:T(8,128)(2,1)S(1)}, u32[]{:S(2)}, u32[]{:S(2)}) collective-permute-start(bf16[128,384]{1,0:T(8,128)(2,1)S(1)} %get-tuple-element.64), channel_id=1, source_target_pairs={{0,1},{1,0},{2,3},{3,2},{4,5},{5,4},{6,7},{7,6},{8,9},{9,8},{10,11... | collective-permute-start | bytes 294920 | tf_op jit(solution)/shard_map/ppermute | solution.py:36
  5.5 0.9 %prepare.1 = (bf16[256,256]{1,0:T(8,128)(2,1)S(1)}, bf16[256,256]{1,0:T(8,128)(2,1)S(1)}, bf16[256,256]{1,0:T(8,128)(2,1)S(1)}, bf16[256,256]{1,0:T(8,128)(2,1)S...) custom-call(s32[8]{0:T(128)S(1)} %copy-done.4, ...), custom_call_target="tpu_custom_call" | custom-call | tf_op jit(solution)/shard_map/prepare/pallas_call | solution.py:61
  6.5 2.1 %collective-permute-done.1.refs_2_ = bf16[128,384]{1,0:T(8,128)(2,1)S(1)} collective-permute-done((bf16[128,384]{1,0:T(8,128)(2,1)S(1)}, bf16[128,384]{1,0:T(8,128)(2,1)S(1)}, u32[]{:S(2)}, u32[]{:S(2)}) %collective-permute-start.1) | collective-permute-done | bytes 98336 | tf_op jit(solution)/shard_map/ppermute | solution.py:36
  8.9 2.7 %collective-permute-start.2 = (bf16[128,384]{1,0:T(8,128)(2,1)S(1)}, bf16[128,384]{1,0:T(8,128)(2,1)S(1)}, u32[]{:S(2)}, u32[]{:S(2)}) collective-permute-start(bf16[128,384]{1,0:T(8,128)(2,1)S(1)} %get-tuple-element.66), channel_id=1, source_target_pairs={{0,2},{1,3},{2,0},{3,1},{4,6},{5,7},{6,4},{7,5},{8,10},{9,11},{10,... | collective-permute-start | bytes 294920 | tf_op jit(solution)/shard_map/ppermute | solution.py:36
  11.6 2.5 %collective-permute-start = (bf16[128,384]{1,0:T(8,128)(2,1)S(1)}, bf16[128,384]{1,0:T(8,128)(2,1)S(1)}, u32[]{:S(2)}, u32[]{:S(2)}) collective-permute-start(bf16[128,384]{1,0:T(8,128)(2,1)S(1)} %get-tuple-element.62), channel_id=1, source_target_pairs={{0,1},{1,0},{2,3},{3,2},{4,5},{5,4},{6,7},{7,6},{8,9},{9,8},{10,11... | collective-permute-start | bytes 294920 | tf_op jit(solution)/shard_map/ppermute | solution.py:36
  15.3 1.3 %collective-permute-done.refs_2_ = bf16[128,384]{1,0:T(8,128)(2,1)S(1)} collective-permute-done((bf16[128,384]{1,0:T(8,128)(2,1)S(1)}, bf16[128,384]{1,0:T(8,128)(2,1)S(1)}, u32[]{:S(2)}, u32[]{:S(2)}) %collective-permute-start) | collective-permute-done | bytes 98336 | tf_op jit(solution)/shard_map/ppermute | solution.py:36
  16.9 2.4 %collective-permute-start.4 = (bf16[128,384]{1,0:T(8,128)(2,1)S(1)}, bf16[128,384]{1,0:T(8,128)(2,1)S(1)}, u32[]{:S(2)}, u32[]{:S(2)}) collective-permute-start(bf16[128,384]{1,0:T(8,128)(2,1)S(1)} %get-tuple-element.72), channel_id=1, source_target_pairs={{0,2},{1,3},{2,0},{3,1},{4,6},{5,7},{6,4},{7,5},{8,10},{9,11},{10,... | collective-permute-start | bytes 294920 | tf_op jit(solution)/shard_map/ppermute | solution.py:36
  19.3 1.6 %collective-permute-done.6.refs_2_ = bf16[128,384]{1,0:T(8,128)(2,1)S(1)} collective-permute-done((bf16[128,384]{1,0:T(8,128)(2,1)S(1)}, bf16[128,384]{1,0:T(8,128)(2,1)S(1)}, u32[]{:S(2)}, u32[]{:S(2)}) %collective-permute-start.6) | collective-permute-done | bytes 98336 | tf_op jit(solution)/shard_map/ppermute | solution.py:36
  21.2 2.5 %collective-permute-start.8 = (bf16[64,384]{1,0:T(8,128)(2,1)S(1)}, bf16[64,384]{1,0:T(8,128)(2,1)S(1)}, u32[]{:S(2)}, u32[]{:S(2)}) collective-permute-start(bf16[64,384]{1,0:T(8,128)(2,1)S(1)} %get-tuple-element.79), channel_id=1, source_target_pairs={{0,24},{4,28},{8,16},{12,20},{16,8},{20,12},{24,0},{28,4},{1,25},{... | collective-permute-start | bytes 147464 | tf_op jit(solution)/shard_map/ppermute | solution.py:36
  24.8 1.2 %collective-permute-start.10 = (bf16[64,384]{1,0:T(8,128)(2,1)S(1)}, bf16[64,384]{1,0:T(8,128)(2,1)S(1)}, u32[]{:S(2)}, u32[]{:S(2)}) collective-permute-start(bf16[64,384]{1,0:T(8,128)(2,1)S(1)} %get-tuple-element.81), channel_id=1, source_target_pairs={{0,16},{4,20},{8,24},{12,28},{16,0},{20,4},{24,8},{28,12},{1,17},{... | collective-permute-start | bytes 147464 | tf_op jit(solution)/shard_map/ppermute | solution.py:36
  26.0 1.8 %collective-permute-start.16 = (bf16[64,384]{1,0:T(8,128)(2,1)S(1)}, bf16[64,384]{1,0:T(8,128)(2,1)S(1)}, u32[]{:S(2)}, u32[]{:S(2)}) collective-permute-start(bf16[64,384]{1,0:T(8,128)(2,1)S(1)} %get-tuple-element.90), channel_id=1, source_target_pairs={{0,24},{4,28},{8,16},{12,20},{16,8},{20,12},{24,0},{28,4},{1,25},{... | collective-permute-start | bytes 147464 | tf_op jit(solution)/shard_map/ppermute | solution.py:36
  28.4 1.2 %collective-permute-start.18 = (bf16[64,384]{1,0:T(8,128)(2,1)S(1)}, bf16[64,384]{1,0:T(8,128)(2,1)S(1)}, u32[]{:S(2)}, u32[]{:S(2)}) collective-permute-start(bf16[64,384]{1,0:T(8,128)(2,1)S(1)} %get-tuple-element.92), channel_id=1, source_target_pairs={{0,16},{4,20},{8,24},{12,28},{16,0},{20,4},{24,8},{28,12},{1,17},{... | collective-permute-start | bytes 147464 | tf_op jit(solution)/shard_map/ppermute | solution.py:36
  29.8 2.3 %collective-permute-start.15 = (bf16[128,384]{1,0:T(8,128)(2,1)S(1)}, bf16[128,384]{1,0:T(8,128)(2,1)S(1)}, u32[]{:S(2)}, u32[]{:S(2)}) collective-permute-start(bf16[128,384]{1,0:T(8,128)(2,1)S(1)} %get-tuple-element.89), channel_id=1, source_target_pairs={{0,2},{1,3},{2,0},{3,1},{4,6},{5,7},{6,4},{7,5},{8,10},{9,11},{10,... | collective-permute-start | bytes 294920 | tf_op jit(solution)/shard_map/ppermute | solution.py:36
  32.7 2.0 %collective-permute-start.20 = (bf16[128,384]{1,0:T(8,128)(2,1)S(1)}, bf16[128,384]{1,0:T(8,128)(2,1)S(1)}, u32[]{:S(2)}, u32[]{:S(2)}) collective-permute-start(bf16[128,384]{1,0:T(8,128)(2,1)S(1)} %get-tuple-element.97), channel_id=1, source_target_pairs={{0,2},{1,3},{2,0},{3,1},{4,6},{5,7},{6,4},{7,5},{8,10},{9,11},{10,... | collective-permute-start | bytes 294920 | tf_op jit(solution)/shard_map/ppermute | solution.py:36
  34.7 1.5 %collective-permute-start.12 = (bf16[64,384]{1,0:T(8,128)(2,1)S(1)}, bf16[64,384]{1,0:T(8,128)(2,1)S(1)}, u32[]{:S(2)}, u32[]{:S(2)}) collective-permute-start(bf16[64,384]{1,0:T(8,128)(2,1)S(1)} %get-tuple-element.86), channel_id=1, source_target_pairs={{0,24},{4,28},{8,16},{12,20},{16,8},{20,12},{24,0},{28,4},{1,25},{... | collective-permute-start | bytes 147464 | tf_op jit(solution)/shard_map/ppermute | solution.py:36
  36.2 1.5 %collective-permute-start.13 = (bf16[64,384]{1,0:T(8,128)(2,1)S(1)}, bf16[64,384]{1,0:T(8,128)(2,1)S(1)}, u32[]{:S(2)}, u32[]{:S(2)}) collective-permute-start(bf16[64,384]{1,0:T(8,128)(2,1)S(1)} %get-tuple-element.87), channel_id=1, source_target_pairs={{0,8},{4,12},{8,0},{12,4},{16,24},{20,28},{24,16},{28,20},{1,9},{5... | collective-permute-start | bytes 147464 | tf_op jit(solution)/shard_map/ppermute | solution.py:36
  38.4 1.3 %collective-permute-done.12.refs_2_ = bf16[64,384]{1,0:T(8,128)(2,1)S(1)} collective-permute-done((bf16[64,384]{1,0:T(8,128)(2,1)S(1)}, bf16[64,384]{1,0:T(8,128)(2,1)S(1)}, u32[]{:S(2)}, u32[]{:S(2)}) %collective-permute-start.12) | collective-permute-done | bytes 49184 | tf_op jit(solution)/shard_map/ppermute | solution.py:36
  40.3 1.5 %collective-permute-done.14.refs_4_ = bf16[64,384]{1,0:T(8,128)(2,1)S(1)} collective-permute-done((bf16[64,384]{1,0:T(8,128)(2,1)S(1)}, bf16[64,384]{1,0:T(8,128)(2,1)S(1)}, u32[]{:S(2)}, u32[]{:S(2)}) %collective-permute-start.14) | collective-permute-done | bytes 49184 | tf_op jit(solution)/shard_map/ppermute | solution.py:36
  42.3 4.6 %collective-permute-start.22 = (bf16[128,768]{1,0:T(8,128)(2,1)S(1)}, bf16[128,768]{1,0:T(8,128)(2,1)S(1)}, u32[]{:S(2)}, u32[]{:S(2)}) collective-permute-start(bf16[128,768]{1,0:T(8,128)(2,1)S(1)} %get-tuple-element.102), channel_id=1, source_target_pairs={{0,1},{1,0},{2,3},{3,2},{4,5},{5,4},{6,7},{7,6},{8,9},{9,8},{10,11... | collective-permute-start | bytes 589832 | tf_op jit(solution)/shard_map/ppermute | solution.py:36
  47.2 5.9 %collective-permute-done.19.refs_2_ = bf16[128,384]{1,0:T(8,128)(2,1)S(1)} collective-permute-done((bf16[128,384]{1,0:T(8,128)(2,1)S(1)}, bf16[128,384]{1,0:T(8,128)(2,1)S(1)}, u32[]{:S(2)}, u32[]{:S(2)}) %collective-permute-start.19) | collective-permute-done | bytes 98336 | tf_op jit(solution)/shard_map/ppermute | solution.py:36
  53.4 1.5 %last_0.1.refs_4_ = bf16[768,1152]{1,0:T(8,128)(2,1)} custom-call(bf16[256,256]{1,0:T(8,128)(2,1)S(1)} %get-tuple-element.56.refs_0_, bf16[768,256]{1,0:T(8,128)(2,1)S(1)} %copy-done, bf16[128,768]{1,0:T(8,128)(2,1)S(1)} %collective-permute-done.22.refs_2_, bf16[128,384]{1,0:T(8,128)(2,1)S(1)} %get-tuple-element.94.refs_5_.refs_3_, ...), custom_call_target="tpu_custom_call" | custom-call | tf_op jit(solution)/shard_map/last_0/pallas_call | solution.py:61
  54.9 3.1 %collective-permute-done.21.refs_2_ = bf16[128,384]{1,0:T(8,128)(2,1)S(1)} collective-permute-done((bf16[128,384]{1,0:T(8,128)(2,1)S(1)}, bf16[128,384]{1,0:T(8,128)(2,1)S(1)}, u32[]{:S(2)}, u32[]{:S(2)}) %collective-permute-start.21) | collective-permute-done | bytes 98336 | tf_op jit(solution)/shard_map/ppermute | solution.py:36
  57.9 1.3 %last_2.1 = bf16[768,1152]{1,0:T(8,128)(2,1)} custom-call(bf16[256,256]{1,0:T(8,128)(2,1)S(1)} %get-tuple-element.56.refs_0_, bf16[768,256]{1,0:T(8,128)(2,1)S(1)} %copy-done, bf16[128,384]{1,0:T(8,128)(2,1)S(1)} %collective-permute-done.21.refs_2_, bf16[128,384]{1,0:T(8,128)(2,1)S(1)} %get-tuple-element.101.refs_5_.refs_3_, ...), custom_call_target="tpu_custom_call", output_to_operand_aliasing={{}: (4, {})} | custom-call | tf_op jit(solution)/shard_map/last_2/pallas_call | solution.py:61
  (51 shorter events, 6.8 us)
Async XLA Ops:
  2.4 6.2 %collective-permute-start.1 = (bf16[128,384]{1,0:T(8,128)(2,1)S(1)}, bf16[128,384]{1,0:T(8,128)(2,1)S(1)}, u32[]{:S(2)}, u32[]{:S(2)}) collective-permute-start(bf16[128,384]{1,0:T(8,128)(2,1)S(1)} %get-tuple-element.64), channel_id=1, source_target_pairs={{0,1},{1,0},{2,3},{3,2},{4,5},{5,4},{6,7},{7,6},{8,9},{9,8},{10,11... | collective-permute-start | bytes 294920 | tf_op jit(solution)/shard_map/ppermute | solution.py:36
  6.4 7.7 %collective-permute-start.3 = (bf16[128,384]{1,0:T(8,128)(2,1)S(1)}, bf16[128,384]{1,0:T(8,128)(2,1)S(1)}, u32[]{:S(2)}, u32[]{:S(2)}) collective-permute-start(bf16[128,384]{1,0:T(8,128)(2,1)S(1)} %get-tuple-element.68), channel_id=1, source_target_pairs={{0,1},{1,0},{2,3},{3,2},{4,5},{5,4},{6,7},{7,6},{8,9},{9,8},{10,11... | collective-permute-start | bytes 294920 | tf_op jit(solution)/shard_map/ppermute | solution.py:36
  8.9 6.2 %collective-permute-start.2 = (bf16[128,384]{1,0:T(8,128)(2,1)S(1)}, bf16[128,384]{1,0:T(8,128)(2,1)S(1)}, u32[]{:S(2)}, u32[]{:S(2)}) collective-permute-start(bf16[128,384]{1,0:T(8,128)(2,1)S(1)} %get-tuple-element.66), channel_id=1, source_target_pairs={{0,2},{1,3},{2,0},{3,1},{4,6},{5,7},{6,4},{7,5},{8,10},{9,11},{10,... | collective-permute-start | bytes 294920 | tf_op jit(solution)/shard_map/ppermute | solution.py:36
  11.6 5.1 %collective-permute-start = (bf16[128,384]{1,0:T(8,128)(2,1)S(1)}, bf16[128,384]{1,0:T(8,128)(2,1)S(1)}, u32[]{:S(2)}, u32[]{:S(2)}) collective-permute-start(bf16[128,384]{1,0:T(8,128)(2,1)S(1)} %get-tuple-element.62), channel_id=1, source_target_pairs={{0,1},{1,0},{2,3},{3,2},{4,5},{5,4},{6,7},{7,6},{8,9},{9,8},{10,11... | collective-permute-start | bytes 294920 | tf_op jit(solution)/shard_map/ppermute | solution.py:36
  14.3 6.6 %collective-permute-start.6 = (bf16[128,384]{1,0:T(8,128)(2,1)S(1)}, bf16[128,384]{1,0:T(8,128)(2,1)S(1)}, u32[]{:S(2)}, u32[]{:S(2)}) collective-permute-start(bf16[128,384]{1,0:T(8,128)(2,1)S(1)} %get-tuple-element.74), channel_id=1, source_target_pairs={{0,2},{1,3},{2,0},{3,1},{4,6},{5,7},{6,4},{7,5},{8,10},{9,11},{10,... | collective-permute-start | bytes 294920 | tf_op jit(solution)/shard_map/ppermute | solution.py:36
  15.3 5.9 %collective-permute-start.5 = (bf16[128,384]{1,0:T(8,128)(2,1)S(1)}, bf16[128,384]{1,0:T(8,128)(2,1)S(1)}, u32[]{:S(2)}, u32[]{:S(2)}) collective-permute-start(bf16[128,384]{1,0:T(8,128)(2,1)S(1)} %get-tuple-element.73), channel_id=1, source_target_pairs={{0,4},{4,0},{8,12},{12,8},{16,20},{20,16},{24,28},{28,24},{1,5},{5... | collective-permute-start | bytes 294920 | tf_op jit(solution)/shard_map/ppermute | solution.py:36
  16.9 6.8 %collective-permute-start.4 = (bf16[128,384]{1,0:T(8,128)(2,1)S(1)}, bf16[128,384]{1,0:T(8,128)(2,1)S(1)}, u32[]{:S(2)}, u32[]{:S(2)}) collective-permute-start(bf16[128,384]{1,0:T(8,128)(2,1)S(1)} %get-tuple-element.72), channel_id=1, source_target_pairs={{0,2},{1,3},{2,0},{3,1},{4,6},{5,7},{6,4},{7,5},{8,10},{9,11},{10,... | collective-permute-start | bytes 294920 | tf_op jit(solution)/shard_map/ppermute | solution.py:36
  21.1 4.9 %collective-permute-start.11 = (bf16[128,384]{1,0:T(8,128)(2,1)S(1)}, bf16[128,384]{1,0:T(8,128)(2,1)S(1)}, u32[]{:S(2)}, u32[]{:S(2)}) collective-permute-start(bf16[128,384]{1,0:T(8,128)(2,1)S(1)} %get-tuple-element.82), channel_id=1, source_target_pairs={{0,4},{4,0},{8,12},{12,8},{16,20},{20,16},{24,28},{28,24},{1,5},{5... | collective-permute-start | bytes 294920 | tf_op jit(solution)/shard_map/ppermute | solution.py:36
  21.2 6.6 %collective-permute-start.8 = (bf16[64,384]{1,0:T(8,128)(2,1)S(1)}, bf16[64,384]{1,0:T(8,128)(2,1)S(1)}, u32[]{:S(2)}, u32[]{:S(2)}) collective-permute-start(bf16[64,384]{1,0:T(8,128)(2,1)S(1)} %get-tuple-element.79), channel_id=1, source_target_pairs={{0,24},{4,28},{8,16},{12,20},{16,8},{20,12},{24,0},{28,4},{1,25},{... | collective-permute-start | bytes 147464 | tf_op jit(solution)/shard_map/ppermute | solution.py:36
  23.7 29.6 %copy-start = (bf16[768,256]{1,0:T(8,128)(2,1)S(1)}, bf16[768,256]{1,0:T(8,128)(2,1)}, u32[]{:S(2)}) copy-start(bf16[768,256]{1,0:T(8,128)(2,1)} %refs_1_.7) | copy-start | bytes 1179652
  24.0 8.2 %collective-permute-start.7 = (bf16[128,384]{1,0:T(8,128)(2,1)S(1)}, bf16[128,384]{1,0:T(8,128)(2,1)S(1)}, u32[]{:S(2)}, u32[]{:S(2)}) collective-permute-start(bf16[128,384]{1,0:T(8,128)(2,1)S(1)} %get-tuple-element.78), channel_id=1, source_target_pairs={{0,4},{4,0},{8,12},{12,8},{16,20},{20,16},{24,28},{28,24},{1,5},{5... | collective-permute-start | bytes 294920 | tf_op jit(solution)/shard_map/ppermute | solution.py:36
  24.2 4.1 %collective-permute-start.9 = (bf16[64,384]{1,0:T(8,128)(2,1)S(1)}, bf16[64,384]{1,0:T(8,128)(2,1)S(1)}, u32[]{:S(2)}, u32[]{:S(2)}) collective-permute-start(bf16[64,384]{1,0:T(8,128)(2,1)S(1)} %get-tuple-element.80), channel_id=1, source_target_pairs={{0,8},{4,12},{8,0},{12,4},{16,24},{20,28},{24,16},{28,20},{1,9},{5... | collective-permute-start | bytes 147464 | tf_op jit(solution)/shard_map/ppermute | solution.py:36
  24.8 4.8 %collective-permute-start.10 = (bf16[64,384]{1,0:T(8,128)(2,1)S(1)}, bf16[64,384]{1,0:T(8,128)(2,1)S(1)}, u32[]{:S(2)}, u32[]{:S(2)}) collective-permute-start(bf16[64,384]{1,0:T(8,128)(2,1)S(1)} %get-tuple-element.81), channel_id=1, source_target_pairs={{0,16},{4,20},{8,24},{12,28},{16,0},{20,4},{24,8},{28,12},{1,17},{... | collective-permute-start | bytes 147464 | tf_op jit(solution)/shard_map/ppermute | solution.py:36
  26.0 6.1 %collective-permute-start.16 = (bf16[64,384]{1,0:T(8,128)(2,1)S(1)}, bf16[64,384]{1,0:T(8,128)(2,1)S(1)}, u32[]{:S(2)}, u32[]{:S(2)}) collective-permute-start(bf16[64,384]{1,0:T(8,128)(2,1)S(1)} %get-tuple-element.90), channel_id=1, source_target_pairs={{0,24},{4,28},{8,16},{12,20},{16,8},{20,12},{24,0},{28,4},{1,25},{... | collective-permute-start | bytes 147464 | tf_op jit(solution)/shard_map/ppermute | solution.py:36
  27.8 4.4 %collective-permute-start.17 = (bf16[64,384]{1,0:T(8,128)(2,1)S(1)}, bf16[64,384]{1,0:T(8,128)(2,1)S(1)}, u32[]{:S(2)}, u32[]{:S(2)}) collective-permute-start(bf16[64,384]{1,0:T(8,128)(2,1)S(1)} %get-tuple-element.91), channel_id=1, source_target_pairs={{0,8},{4,12},{8,0},{12,4},{16,24},{20,28},{24,16},{28,20},{1,9},{5... | collective-permute-start | bytes 147464 | tf_op jit(solution)/shard_map/ppermute | solution.py:36
  28.4 4.1 %collective-permute-start.18 = (bf16[64,384]{1,0:T(8,128)(2,1)S(1)}, bf16[64,384]{1,0:T(8,128)(2,1)S(1)}, u32[]{:S(2)}, u32[]{:S(2)}) collective-permute-start(bf16[64,384]{1,0:T(8,128)(2,1)S(1)} %get-tuple-element.92), channel_id=1, source_target_pairs={{0,16},{4,20},{8,24},{12,28},{16,0},{20,4},{24,8},{28,12},{1,17},{... | collective-permute-start | bytes 147464 | tf_op jit(solution)/shard_map/ppermute | solution.py:36
  29.8 8.4 %collective-permute-start.15 = (bf16[128,384]{1,0:T(8,128)(2,1)S(1)}, bf16[128,384]{1,0:T(8,128)(2,1)S(1)}, u32[]{:S(2)}, u32[]{:S(2)}) collective-permute-start(bf16[128,384]{1,0:T(8,128)(2,1)S(1)} %get-tuple-element.89), channel_id=1, source_target_pairs={{0,2},{1,3},{2,0},{3,1},{4,6},{5,7},{6,4},{7,5},{8,10},{9,11},{10,... | collective-permute-start | bytes 294920 | tf_op jit(solution)/shard_map/ppermute | solution.py:36
  32.7 9.3 %collective-permute-start.20 = (bf16[128,384]{1,0:T(8,128)(2,1)S(1)}, bf16[128,384]{1,0:T(8,128)(2,1)S(1)}, u32[]{:S(2)}, u32[]{:S(2)}) collective-permute-start(bf16[128,384]{1,0:T(8,128)(2,1)S(1)} %get-tuple-element.97), channel_id=1, source_target_pairs={{0,2},{1,3},{2,0},{3,1},{4,6},{5,7},{6,4},{7,5},{8,10},{9,11},{10,... | collective-permute-start | bytes 294920 | tf_op jit(solution)/shard_map/ppermute | solution.py:36
  34.7 5.0 %collective-permute-start.12 = (bf16[64,384]{1,0:T(8,128)(2,1)S(1)}, bf16[64,384]{1,0:T(8,128)(2,1)S(1)}, u32[]{:S(2)}, u32[]{:S(2)}) collective-permute-start(bf16[64,384]{1,0:T(8,128)(2,1)S(1)} %get-tuple-element.86), channel_id=1, source_target_pairs={{0,24},{4,28},{8,16},{12,20},{16,8},{20,12},{24,0},{28,4},{1,25},{... | collective-permute-start | bytes 147464 | tf_op jit(solution)/shard_map/ppermute | solution.py:36
  36.2 4.1 %collective-permute-start.13 = (bf16[64,384]{1,0:T(8,128)(2,1)S(1)}, bf16[64,384]{1,0:T(8,128)(2,1)S(1)}, u32[]{:S(2)}, u32[]{:S(2)}) collective-permute-start(bf16[64,384]{1,0:T(8,128)(2,1)S(1)} %get-tuple-element.87), channel_id=1, source_target_pairs={{0,8},{4,12},{8,0},{12,4},{16,24},{20,28},{24,16},{28,20},{1,9},{5... | collective-permute-start | bytes 147464 | tf_op jit(solution)/shard_map/ppermute | solution.py:36
  37.7 4.1 %collective-permute-start.14 = (bf16[64,384]{1,0:T(8,128)(2,1)S(1)}, bf16[64,384]{1,0:T(8,128)(2,1)S(1)}, u32[]{:S(2)}, u32[]{:S(2)}) collective-permute-start(bf16[64,384]{1,0:T(8,128)(2,1)S(1)} %get-tuple-element.88), channel_id=1, source_target_pairs={{0,16},{4,20},{8,24},{12,28},{16,0},{20,4},{24,8},{28,12},{1,17},{... | collective-permute-start | bytes 147464 | tf_op jit(solution)/shard_map/ppermute | solution.py:36
  42.3 11.1 %collective-permute-start.22 = (bf16[128,768]{1,0:T(8,128)(2,1)S(1)}, bf16[128,768]{1,0:T(8,128)(2,1)S(1)}, u32[]{:S(2)}, u32[]{:S(2)}) collective-permute-start(bf16[128,768]{1,0:T(8,128)(2,1)S(1)} %get-tuple-element.102), channel_id=1, source_target_pairs={{0,1},{1,0},{2,3},{3,2},{4,5},{5,4},{6,7},{7,6},{8,9},{9,8},{10,11... | collective-permute-start | bytes 589832 | tf_op jit(solution)/shard_map/ppermute | solution.py:36
  46.9 6.2 %collective-permute-start.19 = (bf16[128,384]{1,0:T(8,128)(2,1)S(1)}, bf16[128,384]{1,0:T(8,128)(2,1)S(1)}, u32[]{:S(2)}, u32[]{:S(2)}) collective-permute-start(bf16[128,384]{1,0:T(8,128)(2,1)S(1)} %get-tuple-element.96), channel_id=1, source_target_pairs={{0,2},{1,3},{2,0},{3,1},{4,6},{5,7},{6,4},{7,5},{8,10},{9,11},{10,... | collective-permute-start | bytes 294920 | tf_op jit(solution)/shard_map/ppermute | solution.py:36
  53.3 4.7 %collective-permute-start.21 = (bf16[128,384]{1,0:T(8,128)(2,1)S(1)}, bf16[128,384]{1,0:T(8,128)(2,1)S(1)}, u32[]{:S(2)}, u32[]{:S(2)}) collective-permute-start(bf16[128,384]{1,0:T(8,128)(2,1)S(1)} %get-tuple-element.100), channel_id=1, source_target_pairs={{0,1},{1,0},{2,3},{3,2},{4,5},{5,4},{6,7},{7,6},{8,9},{9,8},{10,11... | collective-permute-start | bytes 294920 | tf_op jit(solution)/shard_map/ppermute | solution.py:36
  (4 other events, 22.1 us)

commit v19 on v18

--- a/solution.py
+++ b/solution.py
@@ -6,9 +6,9 @@
 from jax.sharding import PartitionSpec as P
 
 LANES = 128
-SHARES = (3, 3, 3)
+SHARES = (2, 3, 4)
 HEADS = ((0,), (1,), (2,))
-TAILS = ((0, 1), (2,))
+TAILS = ((0,), (1,), (2,))
 ENTRY = (0, 0, 1)
 SPANS = {}
 ROWS = 16
@@ -48,7 +48,7 @@
 
 
 def span(name):
-    flops = SPANS.get(name.split("_")[0], 0)
+    flops = SPANS.get(name.split("_")[0], 10 * 10**8)
     return pl.CostEstimate(flops=flops, bytes_accessed=0, transcendentals=0)
 
 

time: 59.3 us -> 54.4 us (0.917)
  waiting for transfers between devices: 17.6 us -> 13.9 us
  starting transfers between devices: 32.6 us -> 29.9 us
  Pallas kernels: 8.77 us -> 9.52 us
  local copies, waits for them, and re-layouts: 0.02 us -> 0.66 us
    ppermute x23 -> x24, waiting for transfers between devices: 17.6 us -> 13.9 us  [swap(): return lax.ppermute(block, axis, [(i, i ^ distance) for i in range(count)])]
    ppermute x23 -> x24, starting transfers between devices: 32.6 us -> 29.9 us  [swap(): return lax.ppermute(block, axis, [(i, i ^ distance) for i in range(count)])]
    pallas_call x19 -> x20, Pallas kernels: 8.77 us -> 9.52 us  [call(): pl.pallas_call(body, name=name, in_specs=specs + [PLACE] * len(extra), ou...]
    unnamed x10, local copies, waits for them, and re-layouts: 0.02 us -> 0.66 us
  transfers between devices with their start and end apart: 23 -> 24, of which waited for: 9 -> 9; matrix products, arithmetic and copies ran while one was open for 0% -> 0% of each run, Pallas kernels for 8% -> 11%
where the time goes in v19:
time: 54.4 us; the launch traced here: 54.3 us
  starting transfers between devices  29.9 us (55%)
  waiting for transfers between devices  13.9 us (26%)
  Pallas kernels  9.52 us (18%)
  local copies, waits for them, and re-layouts  0.66 us (1%)
    ppermute x24, starting transfers between devices, swap(): return lax.ppermute(block, axis, [(i, i ^ distance) for i in range(count)])  29.9 us
    ppermute x24, waiting for transfers between devices, swap(): return lax.ppermute(block, axis, [(i, i ^ distance) for i in range(count)])  13.9 us
    pallas_call x20, Pallas kernels, call(): pl.pallas_call(body, name=name, in_specs=specs + [PLACE] * len(extra), ou...  9.52 us
  transfers between devices with their start and end apart: 24, of which 9 were waited for; matrix products, arithmetic and copies ran while one was open for 0% of the time, Pallas kernels for 11%

profile of v19, /device:TPU:0, one launch (start us, length us, event | category | flops | bytes accessed | tf_op | source)
XLA Modules:
  0.0 54.3 jit_solution(11508034195447716733)
XLA Ops:
  0.0 2.3 %opening.1 = (bf16[128,256]{1,0:T(8,128)(2,1)S(1)}, bf16[128,384]{1,0:T(8,128)(2,1)S(1)}, bf16[128,512]{1,0:T(8,128)(2,1)S(1)}, bf16[128,256]{1,0:T(8,128)(2,1)S...) custom-call(bf16[768,256]{1,0:T(8,128)(2,1)} %refs_0_.2, bf16[768,1152]{1,0:T(8,128)(2,1)} %refs_1_.5), custom_call_target="tpu_custom_call" | custom-call | flops 1000000000 | tf_op jit(solution)/shard_map/opening/pallas_call | solution.py:61
  2.3 3.1 %collective-permute-start.1 = (bf16[128,256]{1,0:T(8,128)(2,1)S(1)}, bf16[128,256]{1,0:T(8,128)(2,1)S(1)}, u32[]{:S(2)}, u32[]{:S(2)}) collective-permute-start(bf16[128,256]{1,0:T(8,128)(2,1)S(1)} %get-tuple-element.64), channel_id=1, source_target_pairs={{0,1},{1,0},{2,3},{3,2},{4,5},{5,4},{6,7},{7,6},{8,9},{9,8},{10,11... | collective-permute-start | bytes 196616 | tf_op jit(solution)/shard_map/ppermute | solution.py:36
  5.5 0.9 %prepare.1 = (bf16[256,256]{1,0:T(8,128)(2,1)S(1)}, bf16[256,256]{1,0:T(8,128)(2,1)S(1)}, bf16[256,256]{1,0:T(8,128)(2,1)S(1)}, bf16[256,256]{1,0:T(8,128)(2,1)S...) custom-call(s32[8]{0:T(128)S(1)} %copy-done.4, ...), custom_call_target="tpu_custom_call" | custom-call | flops 1000000000 | tf_op jit(solution)/shard_map/prepare/pallas_call | solution.py:61
  6.4 2.0 %collective-permute-start = (bf16[128,512]{1,0:T(8,128)(2,1)S(1)}, bf16[128,512]{1,0:T(8,128)(2,1)S(1)}, u32[]{:S(2)}, u32[]{:S(2)}) collective-permute-start(bf16[128,512]{1,0:T(8,128)(2,1)S(1)} %get-tuple-element.62), channel_id=1, source_target_pairs={{0,1},{1,0},{2,3},{3,2},{4,5},{5,4},{6,7},{7,6},{8,9},{9,8},{10,11... | collective-permute-start | bytes 393224 | tf_op jit(solution)/shard_map/ppermute | solution.py:36
  8.6 2.7 %collective-permute-start.2 = (bf16[128,256]{1,0:T(8,128)(2,1)S(1)}, bf16[128,256]{1,0:T(8,128)(2,1)S(1)}, u32[]{:S(2)}, u32[]{:S(2)}) collective-permute-start(bf16[128,256]{1,0:T(8,128)(2,1)S(1)} %get-tuple-element.66), channel_id=1, source_target_pairs={{0,2},{1,3},{2,0},{3,1},{4,6},{5,7},{6,4},{7,5},{8,10},{9,11},{10,... | collective-permute-start | bytes 196616 | tf_op jit(solution)/shard_map/ppermute | solution.py:36
  11.3 1.5 %collective-permute-done.3.refs_2_ = bf16[128,384]{1,0:T(8,128)(2,1)S(1)} collective-permute-done((bf16[128,384]{1,0:T(8,128)(2,1)S(1)}, bf16[128,384]{1,0:T(8,128)(2,1)S(1)}, u32[]{:S(2)}, u32[]{:S(2)}) %collective-permute-start.3) | collective-permute-done | bytes 98336 | tf_op jit(solution)/shard_map/ppermute | solution.py:36
  13.0 2.0 %collective-permute-start.6 = (bf16[128,384]{1,0:T(8,128)(2,1)S(1)}, bf16[128,384]{1,0:T(8,128)(2,1)S(1)}, u32[]{:S(2)}, u32[]{:S(2)}) collective-permute-start(bf16[128,384]{1,0:T(8,128)(2,1)S(1)} %get-tuple-element.74), channel_id=1, source_target_pairs={{0,2},{1,3},{2,0},{3,1},{4,6},{5,7},{6,4},{7,5},{8,10},{9,11},{10,... | collective-permute-start | bytes 294920 | tf_op jit(solution)/shard_map/ppermute | solution.py:36
  16.1 2.2 %collective-permute-start.4 = (bf16[128,512]{1,0:T(8,128)(2,1)S(1)}, bf16[128,512]{1,0:T(8,128)(2,1)S(1)}, u32[]{:S(2)}, u32[]{:S(2)}) collective-permute-start(bf16[128,512]{1,0:T(8,128)(2,1)S(1)} %get-tuple-element.72), channel_id=1, source_target_pairs={{0,2},{1,3},{2,0},{3,1},{4,6},{5,7},{6,4},{7,5},{8,10},{9,11},{10,... | collective-permute-start | bytes 393224 | tf_op jit(solution)/shard_map/ppermute | solution.py:36
  18.3 2.1 %collective-permute-done.6.refs_2_ = bf16[128,384]{1,0:T(8,128)(2,1)S(1)} collective-permute-done((bf16[128,384]{1,0:T(8,128)(2,1)S(1)}, bf16[128,384]{1,0:T(8,128)(2,1)S(1)}, u32[]{:S(2)}, u32[]{:S(2)}) %collective-permute-start.6) | collective-permute-done | bytes 98336 | tf_op jit(solution)/shard_map/ppermute | solution.py:36
  20.7 2.5 %collective-permute-start.8 = (bf16[64,256]{1,0:T(8,128)(2,1)S(1)}, bf16[64,256]{1,0:T(8,128)(2,1)S(1)}, u32[]{:S(2)}, u32[]{:S(2)}) collective-permute-start(bf16[64,256]{1,0:T(8,128)(2,1)S(1)} %get-tuple-element.79), channel_id=1, source_target_pairs={{0,24},{4,28},{8,16},{12,20},{16,8},{20,12},{24,0},{28,4},{1,25},{... | collective-permute-start | bytes 98312 | tf_op jit(solution)/shard_map/ppermute | solution.py:36
  24.3 1.4 %collective-permute-done.4.refs_2_ = bf16[128,512]{1,0:T(8,128)(2,1)S(1)} collective-permute-done((bf16[128,512]{1,0:T(8,128)(2,1)S(1)}, bf16[128,512]{1,0:T(8,128)(2,1)S(1)}, u32[]{:S(2)}, u32[]{:S(2)}) %collective-permute-start.4) | collective-permute-done | bytes 131104 | tf_op jit(solution)/shard_map/ppermute | solution.py:36
  26.0 2.5 %collective-permute-start.16 = (bf16[64,384]{1,0:T(8,128)(2,1)S(1)}, bf16[64,384]{1,0:T(8,128)(2,1)S(1)}, u32[]{:S(2)}, u32[]{:S(2)}) collective-permute-start(bf16[64,384]{1,0:T(8,128)(2,1)S(1)} %get-tuple-element.90), channel_id=1, source_target_pairs={{0,24},{4,28},{8,16},{12,20},{16,8},{20,12},{24,0},{28,4},{1,25},{... | collective-permute-start | bytes 147464 | tf_op jit(solution)/shard_map/ppermute | solution.py:36
  29.9 2.5 %collective-permute-start.12 = (bf16[64,512]{1,0:T(8,128)(2,1)S(1)}, bf16[64,512]{1,0:T(8,128)(2,1)S(1)}, u32[]{:S(2)}, u32[]{:S(2)}) collective-permute-start(bf16[64,512]{1,0:T(8,128)(2,1)S(1)} %get-tuple-element.86), channel_id=1, source_target_pairs={{0,24},{4,28},{8,16},{12,20},{16,8},{20,12},{24,0},{28,4},{1,25},{... | collective-permute-start | bytes 196616 | tf_op jit(solution)/shard_map/ppermute | solution.py:36
  33.0 1.5 %collective-permute-start.14 = (bf16[64,512]{1,0:T(8,128)(2,1)S(1)}, bf16[64,512]{1,0:T(8,128)(2,1)S(1)}, u32[]{:S(2)}, u32[]{:S(2)}) collective-permute-start(bf16[64,512]{1,0:T(8,128)(2,1)S(1)} %get-tuple-element.88), channel_id=1, source_target_pairs={{0,16},{4,20},{8,24},{12,28},{16,0},{20,4},{24,8},{28,12},{1,17},{... | collective-permute-start | bytes 196616 | tf_op jit(solution)/shard_map/ppermute | solution.py:36
  34.8 1.9 %collective-permute-start.20 = (bf16[128,384]{1,0:T(8,128)(2,1)S(1)}, bf16[128,384]{1,0:T(8,128)(2,1)S(1)}, u32[]{:S(2)}, u32[]{:S(2)}) collective-permute-start(bf16[128,384]{1,0:T(8,128)(2,1)S(1)} %get-tuple-element.97), channel_id=1, source_target_pairs={{0,2},{1,3},{2,0},{3,1},{4,6},{5,7},{6,4},{7,5},{8,10},{9,11},{10,... | collective-permute-start | bytes 294920 | tf_op jit(solution)/shard_map/ppermute | solution.py:36
  37.5 2.9 %collective-permute-start.19 = (bf16[128,512]{1,0:T(8,128)(2,1)S(1)}, bf16[128,512]{1,0:T(8,128)(2,1)S(1)}, u32[]{:S(2)}, u32[]{:S(2)}) collective-permute-start(bf16[128,512]{1,0:T(8,128)(2,1)S(1)} %get-tuple-element.96), channel_id=1, source_target_pairs={{0,2},{1,3},{2,0},{3,1},{4,6},{5,7},{6,4},{7,5},{8,10},{9,11},{10,... | collective-permute-start | bytes 393224 | tf_op jit(solution)/shard_map/ppermute | solution.py:36
  40.4 0.9 %collective-permute-start.23 = (bf16[128,256]{1,0:T(8,128)(2,1)S(1)}, bf16[128,256]{1,0:T(8,128)(2,1)S(1)}, u32[]{:S(2)}, u32[]{:S(2)}) collective-permute-start(bf16[128,256]{1,0:T(8,128)(2,1)S(1)} %get-tuple-element.102), channel_id=1, source_target_pairs={{0,1},{1,0},{2,3},{3,2},{4,5},{5,4},{6,7},{7,6},{8,9},{9,8},{10,11... | collective-permute-start | bytes 196616 | tf_op jit(solution)/shard_map/ppermute | solution.py:36
  41.3 3.2 %collective-permute-done.20.refs_2_ = bf16[128,384]{1,0:T(8,128)(2,1)S(1)} collective-permute-done((bf16[128,384]{1,0:T(8,128)(2,1)S(1)}, bf16[128,384]{1,0:T(8,128)(2,1)S(1)}, u32[]{:S(2)}, u32[]{:S(2)}) %collective-permute-start.20) | collective-permute-done | bytes 98336 | tf_op jit(solution)/shard_map/ppermute | solution.py:36
  44.8 2.8 %collective-permute-done.19.refs_2_ = bf16[128,512]{1,0:T(8,128)(2,1)S(1)} collective-permute-done((bf16[128,512]{1,0:T(8,128)(2,1)S(1)}, bf16[128,512]{1,0:T(8,128)(2,1)S(1)}, u32[]{:S(2)}, u32[]{:S(2)}) %collective-permute-start.19) | collective-permute-done | bytes 131104 | tf_op jit(solution)/shard_map/ppermute | solution.py:36
  48.0 0.6 %copy-done = bf16[768,256]{1,0:T(8,128)(2,1)S(1)} copy-done((bf16[768,256]{1,0:T(8,128)(2,1)S(1)}, bf16[768,256]{1,0:T(8,128)(2,1)}, u32[]{:S(2)}) %copy-start) | copy-done | bytes 393240
  48.7 1.2 %last_0.1.refs_4_ = bf16[768,1152]{1,0:T(8,128)(2,1)} custom-call(bf16[256,256]{1,0:T(8,128)(2,1)S(1)} %get-tuple-element.56.refs_0_, bf16[768,256]{1,0:T(8,128)(2,1)S(1)} %copy-done, bf16[128,256]{1,0:T(8,128)(2,1)S(1)} %collective-permute-done.23.refs_2_, bf16[128,256]{1,0:T(8,128)(2,1)S(1)} %get-tuple-element.94.refs_5_.refs_3_, ...), custom_call_target="tpu_custom_call" | custom-call | flops 1000000000 | tf_op jit(solution)/shard_map/last_0/pallas_call | solution.py:61
  50.5 1.3 %last_1.1.refs_4_ = bf16[768,1152]{1,0:T(8,128)(2,1)} custom-call(bf16[256,256]{1,0:T(8,128)(2,1)S(1)} %get-tuple-element.56.refs_0_, bf16[768,256]{1,0:T(8,128)(2,1)S(1)} %copy-done, bf16[128,384]{1,0:T(8,128)(2,1)S(1)} %collective-permute-done.22.refs_2_, bf16[128,384]{1,0:T(8,128)(2,1)S(1)} %get-tuple-element.98.refs_3_.refs_4_, ...), custom_call_target="tpu_custom_call", output_to_operand_aliasing={{}: (4, {})} | custom-call | flops 1000000000 | tf_op jit(solution)/shard_map/last_1/pallas_call | solution.py:61
  51.7 1.2 %collective-permute-done.21.refs_2_ = bf16[128,512]{1,0:T(8,128)(2,1)S(1)} collective-permute-done((bf16[128,512]{1,0:T(8,128)(2,1)S(1)}, bf16[128,512]{1,0:T(8,128)(2,1)S(1)}, u32[]{:S(2)}, u32[]{:S(2)}) %collective-permute-start.21) | collective-permute-done | bytes 131104 | tf_op jit(solution)/shard_map/ppermute | solution.py:36
  52.9 1.3 %last_2.1 = bf16[768,1152]{1,0:T(8,128)(2,1)} custom-call(bf16[256,256]{1,0:T(8,128)(2,1)S(1)} %get-tuple-element.56.refs_0_, bf16[768,256]{1,0:T(8,128)(2,1)S(1)} %copy-done, bf16[128,512]{1,0:T(8,128)(2,1)S(1)} %collective-permute-done.21.refs_2_, bf16[128,512]{1,0:T(8,128)(2,1)S(1)} %get-tuple-element.100.refs_5_.refs_3_, ...), custom_call_target="tpu_custom_call", output_to_operand_aliasing={{}: (4, {})} | custom-call | flops 1000000000 | tf_op jit(solution)/shard_map/last_2/pallas_call | solution.py:61
  (54 shorter events, 7.6 us)
Async XLA Ops:
  2.3 6.1 %collective-permute-start.1 = (bf16[128,256]{1,0:T(8,128)(2,1)S(1)}, bf16[128,256]{1,0:T(8,128)(2,1)S(1)}, u32[]{:S(2)}, u32[]{:S(2)}) collective-permute-start(bf16[128,256]{1,0:T(8,128)(2,1)S(1)} %get-tuple-element.64), channel_id=1, source_target_pairs={{0,1},{1,0},{2,3},{3,2},{4,5},{5,4},{6,7},{7,6},{8,9},{9,8},{10,11... | collective-permute-start | bytes 196616 | tf_op jit(solution)/shard_map/ppermute | solution.py:36
  6.3 6.4 %collective-permute-start.3 = (bf16[128,384]{1,0:T(8,128)(2,1)S(1)}, bf16[128,384]{1,0:T(8,128)(2,1)S(1)}, u32[]{:S(2)}, u32[]{:S(2)}) collective-permute-start(bf16[128,384]{1,0:T(8,128)(2,1)S(1)} %get-tuple-element.68), channel_id=1, source_target_pairs={{0,1},{1,0},{2,3},{3,2},{4,5},{5,4},{6,7},{7,6},{8,9},{9,8},{10,11... | collective-permute-start | bytes 294920 | tf_op jit(solution)/shard_map/ppermute | solution.py:36
  6.4 9.5 %collective-permute-start = (bf16[128,512]{1,0:T(8,128)(2,1)S(1)}, bf16[128,512]{1,0:T(8,128)(2,1)S(1)}, u32[]{:S(2)}, u32[]{:S(2)}) collective-permute-start(bf16[128,512]{1,0:T(8,128)(2,1)S(1)} %get-tuple-element.62), channel_id=1, source_target_pairs={{0,1},{1,0},{2,3},{3,2},{4,5},{5,4},{6,7},{7,6},{8,9},{9,8},{10,11... | collective-permute-start | bytes 393224 | tf_op jit(solution)/shard_map/ppermute | solution.py:36
  8.6 6.4 %collective-permute-start.2 = (bf16[128,256]{1,0:T(8,128)(2,1)S(1)}, bf16[128,256]{1,0:T(8,128)(2,1)S(1)}, u32[]{:S(2)}, u32[]{:S(2)}) collective-permute-start(bf16[128,256]{1,0:T(8,128)(2,1)S(1)} %get-tuple-element.66), channel_id=1, source_target_pairs={{0,2},{1,3},{2,0},{3,1},{4,6},{5,7},{6,4},{7,5},{8,10},{9,11},{10,... | collective-permute-start | bytes 196616 | tf_op jit(solution)/shard_map/ppermute | solution.py:36
  13.0 7.4 %collective-permute-start.6 = (bf16[128,384]{1,0:T(8,128)(2,1)S(1)}, bf16[128,384]{1,0:T(8,128)(2,1)S(1)}, u32[]{:S(2)}, u32[]{:S(2)}) collective-permute-start(bf16[128,384]{1,0:T(8,128)(2,1)S(1)} %get-tuple-element.74), channel_id=1, source_target_pairs={{0,2},{1,3},{2,0},{3,1},{4,6},{5,7},{6,4},{7,5},{8,10},{9,11},{10,... | collective-permute-start | bytes 294920 | tf_op jit(solution)/shard_map/ppermute | solution.py:36
  15.2 5.5 %collective-permute-start.5 = (bf16[128,256]{1,0:T(8,128)(2,1)S(1)}, bf16[128,256]{1,0:T(8,128)(2,1)S(1)}, u32[]{:S(2)}, u32[]{:S(2)}) collective-permute-start(bf16[128,256]{1,0:T(8,128)(2,1)S(1)} %get-tuple-element.73), channel_id=1, source_target_pairs={{0,4},{4,0},{8,12},{12,8},{16,20},{20,16},{24,28},{28,24},{1,5},{5... | collective-permute-start | bytes 196616 | tf_op jit(solution)/shard_map/ppermute | solution.py:36
  16.1 9.5 %collective-permute-start.4 = (bf16[128,512]{1,0:T(8,128)(2,1)S(1)}, bf16[128,512]{1,0:T(8,128)(2,1)S(1)}, u32[]{:S(2)}, u32[]{:S(2)}) collective-permute-start(bf16[128,512]{1,0:T(8,128)(2,1)S(1)} %get-tuple-element.72), channel_id=1, source_target_pairs={{0,2},{1,3},{2,0},{3,1},{4,6},{5,7},{6,4},{7,5},{8,10},{9,11},{10,... | collective-permute-start | bytes 393224 | tf_op jit(solution)/shard_map/ppermute | solution.py:36
  20.6 5.4 %collective-permute-start.11 = (bf16[128,384]{1,0:T(8,128)(2,1)S(1)}, bf16[128,384]{1,0:T(8,128)(2,1)S(1)}, u32[]{:S(2)}, u32[]{:S(2)}) collective-permute-start(bf16[128,384]{1,0:T(8,128)(2,1)S(1)} %get-tuple-element.82), channel_id=1, source_target_pairs={{0,4},{4,0},{8,12},{12,8},{16,20},{20,16},{24,28},{28,24},{1,5},{5... | collective-permute-start | bytes 294920 | tf_op jit(solution)/shard_map/ppermute | solution.py:36
  20.7 7.8 %collective-permute-start.8 = (bf16[64,256]{1,0:T(8,128)(2,1)S(1)}, bf16[64,256]{1,0:T(8,128)(2,1)S(1)}, u32[]{:S(2)}, u32[]{:S(2)}) collective-permute-start(bf16[64,256]{1,0:T(8,128)(2,1)S(1)} %get-tuple-element.79), channel_id=1, source_target_pairs={{0,24},{4,28},{8,16},{12,20},{16,8},{20,12},{24,0},{28,4},{1,25},{... | collective-permute-start | bytes 98312 | tf_op jit(solution)/shard_map/ppermute | solution.py:36
  23.2 5.8 %collective-permute-start.9 = (bf16[64,256]{1,0:T(8,128)(2,1)S(1)}, bf16[64,256]{1,0:T(8,128)(2,1)S(1)}, u32[]{:S(2)}, u32[]{:S(2)}) collective-permute-start(bf16[64,256]{1,0:T(8,128)(2,1)S(1)} %get-tuple-element.80), channel_id=1, source_target_pairs={{0,8},{4,12},{8,0},{12,4},{16,24},{20,28},{24,16},{28,20},{1,9},{5... | collective-permute-start | bytes 98312 | tf_op jit(solution)/shard_map/ppermute | solution.py:36
  23.8 5.8 %collective-permute-start.10 = (bf16[64,256]{1,0:T(8,128)(2,1)S(1)}, bf16[64,256]{1,0:T(8,128)(2,1)S(1)}, u32[]{:S(2)}, u32[]{:S(2)}) collective-permute-start(bf16[64,256]{1,0:T(8,128)(2,1)S(1)} %get-tuple-element.81), channel_id=1, source_target_pairs={{0,16},{4,20},{8,24},{12,28},{16,0},{20,4},{24,8},{28,12},{1,17},{... | collective-permute-start | bytes 98312 | tf_op jit(solution)/shard_map/ppermute | solution.py:36
  25.9 4.0 %collective-permute-start.7 = (bf16[128,512]{1,0:T(8,128)(2,1)S(1)}, bf16[128,512]{1,0:T(8,128)(2,1)S(1)}, u32[]{:S(2)}, u32[]{:S(2)}) collective-permute-start(bf16[128,512]{1,0:T(8,128)(2,1)S(1)} %get-tuple-element.78), channel_id=1, source_target_pairs={{0,4},{4,0},{8,12},{12,8},{16,20},{20,16},{24,28},{28,24},{1,5},{5... | collective-permute-start | bytes 393224 | tf_op jit(solution)/shard_map/ppermute | solution.py:36
  26.0 6.4 %collective-permute-start.16 = (bf16[64,384]{1,0:T(8,128)(2,1)S(1)}, bf16[64,384]{1,0:T(8,128)(2,1)S(1)}, u32[]{:S(2)}, u32[]{:S(2)}) collective-permute-start(bf16[64,384]{1,0:T(8,128)(2,1)S(1)} %get-tuple-element.90), channel_id=1, source_target_pairs={{0,24},{4,28},{8,16},{12,20},{16,8},{20,12},{24,0},{28,4},{1,25},{... | collective-permute-start | bytes 147464 | tf_op jit(solution)/shard_map/ppermute | solution.py:36
  28.5 4.5 %collective-permute-start.17 = (bf16[64,384]{1,0:T(8,128)(2,1)S(1)}, bf16[64,384]{1,0:T(8,128)(2,1)S(1)}, u32[]{:S(2)}, u32[]{:S(2)}) collective-permute-start(bf16[64,384]{1,0:T(8,128)(2,1)S(1)} %get-tuple-element.91), channel_id=1, source_target_pairs={{0,8},{4,12},{8,0},{12,4},{16,24},{20,28},{24,16},{28,20},{1,9},{5... | collective-permute-start | bytes 147464 | tf_op jit(solution)/shard_map/ppermute | solution.py:36
  29.1 5.5 %collective-permute-start.18 = (bf16[64,384]{1,0:T(8,128)(2,1)S(1)}, bf16[64,384]{1,0:T(8,128)(2,1)S(1)}, u32[]{:S(2)}, u32[]{:S(2)}) collective-permute-start(bf16[64,384]{1,0:T(8,128)(2,1)S(1)} %get-tuple-element.92), channel_id=1, source_target_pairs={{0,16},{4,20},{8,24},{12,28},{16,0},{20,4},{24,8},{28,12},{1,17},{... | collective-permute-start | bytes 147464 | tf_op jit(solution)/shard_map/ppermute | solution.py:36
  29.8 6.9 %collective-permute-start.15 = (bf16[128,256]{1,0:T(8,128)(2,1)S(1)}, bf16[128,256]{1,0:T(8,128)(2,1)S(1)}, u32[]{:S(2)}, u32[]{:S(2)}) collective-permute-start(bf16[128,256]{1,0:T(8,128)(2,1)S(1)} %get-tuple-element.89), channel_id=1, source_target_pairs={{0,2},{1,3},{2,0},{3,1},{4,6},{5,7},{6,4},{7,5},{8,10},{9,11},{10,... | collective-permute-start | bytes 196616 | tf_op jit(solution)/shard_map/ppermute | solution.py:36
  29.9 7.0 %collective-permute-start.12 = (bf16[64,512]{1,0:T(8,128)(2,1)S(1)}, bf16[64,512]{1,0:T(8,128)(2,1)S(1)}, u32[]{:S(2)}, u32[]{:S(2)}) collective-permute-start(bf16[64,512]{1,0:T(8,128)(2,1)S(1)} %get-tuple-element.86), channel_id=1, source_target_pairs={{0,24},{4,28},{8,16},{12,20},{16,8},{20,12},{24,0},{28,4},{1,25},{... | collective-permute-start | bytes 196616 | tf_op jit(solution)/shard_map/ppermute | solution.py:36
  32.4 4.5 %collective-permute-start.13 = (bf16[64,512]{1,0:T(8,128)(2,1)S(1)}, bf16[64,512]{1,0:T(8,128)(2,1)S(1)}, u32[]{:S(2)}, u32[]{:S(2)}) collective-permute-start(bf16[64,512]{1,0:T(8,128)(2,1)S(1)} %get-tuple-element.87), channel_id=1, source_target_pairs={{0,8},{4,12},{8,0},{12,4},{16,24},{20,28},{24,16},{28,20},{1,9},{5... | collective-permute-start | bytes 196616 | tf_op jit(solution)/shard_map/ppermute | solution.py:36
  33.0 4.3 %collective-permute-start.14 = (bf16[64,512]{1,0:T(8,128)(2,1)S(1)}, bf16[64,512]{1,0:T(8,128)(2,1)S(1)}, u32[]{:S(2)}, u32[]{:S(2)}) collective-permute-start(bf16[64,512]{1,0:T(8,128)(2,1)S(1)} %get-tuple-element.88), channel_id=1, source_target_pairs={{0,16},{4,20},{8,24},{12,28},{16,0},{20,4},{24,8},{28,12},{1,17},{... | collective-permute-start | bytes 196616 | tf_op jit(solution)/shard_map/ppermute | solution.py:36
  34.8 9.8 %collective-permute-start.20 = (bf16[128,384]{1,0:T(8,128)(2,1)S(1)}, bf16[128,384]{1,0:T(8,128)(2,1)S(1)}, u32[]{:S(2)}, u32[]{:S(2)}) collective-permute-start(bf16[128,384]{1,0:T(8,128)(2,1)S(1)} %get-tuple-element.97), channel_id=1, source_target_pairs={{0,2},{1,3},{2,0},{3,1},{4,6},{5,7},{6,4},{7,5},{8,10},{9,11},{10,... | collective-permute-start | bytes 294920 | tf_op jit(solution)/shard_map/ppermute | solution.py:36
  37.5 10.2 %collective-permute-start.19 = (bf16[128,512]{1,0:T(8,128)(2,1)S(1)}, bf16[128,512]{1,0:T(8,128)(2,1)S(1)}, u32[]{:S(2)}, u32[]{:S(2)}) collective-permute-start(bf16[128,512]{1,0:T(8,128)(2,1)S(1)} %get-tuple-element.96), channel_id=1, source_target_pairs={{0,2},{1,3},{2,0},{3,1},{4,6},{5,7},{6,4},{7,5},{8,10},{9,11},{10,... | collective-permute-start | bytes 393224 | tf_op jit(solution)/shard_map/ppermute | solution.py:36
  40.4 7.6 %collective-permute-start.23 = (bf16[128,256]{1,0:T(8,128)(2,1)S(1)}, bf16[128,256]{1,0:T(8,128)(2,1)S(1)}, u32[]{:S(2)}, u32[]{:S(2)}) collective-permute-start(bf16[128,256]{1,0:T(8,128)(2,1)S(1)} %get-tuple-element.102), channel_id=1, source_target_pairs={{0,1},{1,0},{2,3},{3,2},{4,5},{5,4},{6,7},{7,6},{8,9},{9,8},{10,11... | collective-permute-start | bytes 196616 | tf_op jit(solution)/shard_map/ppermute | solution.py:36
  44.7 5.7 %collective-permute-start.22 = (bf16[128,384]{1,0:T(8,128)(2,1)S(1)}, bf16[128,384]{1,0:T(8,128)(2,1)S(1)}, u32[]{:S(2)}, u32[]{:S(2)}) collective-permute-start(bf16[128,384]{1,0:T(8,128)(2,1)S(1)} %get-tuple-element.101), channel_id=1, source_target_pairs={{0,1},{1,0},{2,3},{3,2},{4,5},{5,4},{6,7},{7,6},{8,9},{9,8},{10,11... | collective-permute-start | bytes 294920 | tf_op jit(solution)/shard_map/ppermute | solution.py:36
  47.9 5.0 %collective-permute-start.21 = (bf16[128,512]{1,0:T(8,128)(2,1)S(1)}, bf16[128,512]{1,0:T(8,128)(2,1)S(1)}, u32[]{:S(2)}, u32[]{:S(2)}) collective-permute-start(bf16[128,512]{1,0:T(8,128)(2,1)S(1)} %get-tuple-element.99), channel_id=1, source_target_pairs={{0,1},{1,0},{2,3},{3,2},{4,5},{5,4},{6,7},{7,6},{8,9},{9,8},{10,11... | collective-permute-start | bytes 393224 | tf_op jit(solution)/shard_map/ppermute | solution.py:36
  (5 other events, 22.8 us)

commit v20 on v8

--- a/solution.py
+++ b/solution.py
@@ -112,7 +112,7 @@
 def opening(name, basis, signal, widths):
     rows, width = basis.shape
     half = width // 2
-    pieces = row_pieces(rows, 6)
+    pieces = row_pieces(rows, 2)
     depth = rows // pieces
     lows = [sum(widths[:i]) for i in range(len(widths))]
 

time: 53.5 us -> 53.4 us (level)
  no operation moved by 1% of the time
where the time goes in v20:
time: 53.4 us; the launch traced here: 53.2 us
  starting transfers between devices  29.7 us (56%)
  waiting for transfers between devices  13.6 us (25%)
  Pallas kernels  9.72 us (18%)
    ppermute x24, starting transfers between devices, swap(): return lax.ppermute(block, axis, [(i, i ^ distance) for i in range(count)])  29.7 us
    ppermute x24, waiting for transfers between devices, swap(): return lax.ppermute(block, axis, [(i, i ^ distance) for i in range(count)])  13.6 us
    pallas_call x20, Pallas kernels, call(): pl.pallas_call(body, name=name, in_specs=specs + [PLACE] * len(extra), ou...  9.72 us
  transfers between devices with their start and end apart: 24, of which 12 were waited for; matrix products, arithmetic and copies ran while one was open for 0% of the time, Pallas kernels for 11%

profile of v20, /device:TPU:0, one launch (start us, length us, event | category | flops | bytes accessed | tf_op | source)
XLA Modules:
  0.0 53.2 jit_solution(15593820272045066234)
XLA Ops:
  0.0 2.4 %opening.1 = (bf16[128,384]{1,0:T(8,128)(2,1)S(1)}, bf16[128,384]{1,0:T(8,128)(2,1)S(1)}, bf16[128,384]{1,0:T(8,128)(2,1)S(1)}, bf16[128,384]{1,0:T(8,128)(2,1)S...) custom-call(bf16[768,256]{1,0:T(8,128)(2,1)} %refs_0_.3, bf16[768,1152]{1,0:T(8,128)(2,1)} %refs_1_.6), custom_call_target="tpu_custom_call" | custom-call | flops 452984832 | bytes 2162688 | tf_op jit(solution)/shard_map/opening/pallas_call | solution.py:59
  2.4 3.1 %collective-permute-start.1 = (bf16[128,384]{1,0:T(8,128)(2,1)S(1)}, bf16[128,384]{1,0:T(8,128)(2,1)S(1)}, u32[]{:S(2)}, u32[]{:S(2)}) collective-permute-start(bf16[128,384]{1,0:T(8,128)(2,1)S(1)} %get-tuple-element.60), channel_id=1, source_target_pairs={{0,1},{1,0},{2,3},{3,2},{4,5},{5,4},{6,7},{7,6},{8,9},{9,8},{10,11... | collective-permute-start | bytes 294920 | tf_op jit(solution)/shard_map/ppermute | solution.py:35
  6.5 2.5 %collective-permute-done.1.refs_2_ = bf16[128,384]{1,0:T(8,128)(2,1)S(1)} collective-permute-done((bf16[128,384]{1,0:T(8,128)(2,1)S(1)}, bf16[128,384]{1,0:T(8,128)(2,1)S(1)}, u32[]{:S(2)}, u32[]{:S(2)}) %collective-permute-start.1) | collective-permute-done | bytes 98336 | tf_op jit(solution)/shard_map/ppermute | solution.py:35
  9.2 3.1 %collective-permute-start.2 = (bf16[128,384]{1,0:T(8,128)(2,1)S(1)}, bf16[128,384]{1,0:T(8,128)(2,1)S(1)}, u32[]{:S(2)}, u32[]{:S(2)}) collective-permute-start(bf16[128,384]{1,0:T(8,128)(2,1)S(1)} %get-tuple-element.62), channel_id=1, source_target_pairs={{0,2},{1,3},{2,0},{3,1},{4,6},{5,7},{6,4},{7,5},{8,10},{9,11},{10,... | collective-permute-start | bytes 294920 | tf_op jit(solution)/shard_map/ppermute | solution.py:35
  12.3 1.7 %collective-permute-start = (bf16[128,384]{1,0:T(8,128)(2,1)S(1)}, bf16[128,384]{1,0:T(8,128)(2,1)S(1)}, u32[]{:S(2)}, u32[]{:S(2)}) collective-permute-start(bf16[128,384]{1,0:T(8,128)(2,1)S(1)} %get-tuple-element.58), channel_id=1, source_target_pairs={{0,1},{1,0},{2,3},{3,2},{4,5},{5,4},{6,7},{7,6},{8,9},{9,8},{10,11... | collective-permute-start | bytes 294920 | tf_op jit(solution)/shard_map/ppermute | solution.py:35
  14.6 2.4 %collective-permute-done.2.refs_2_ = bf16[128,384]{1,0:T(8,128)(2,1)S(1)} collective-permute-done((bf16[128,384]{1,0:T(8,128)(2,1)S(1)}, bf16[128,384]{1,0:T(8,128)(2,1)S(1)}, u32[]{:S(2)}, u32[]{:S(2)}) %collective-permute-start.2) | collective-permute-done | bytes 98336 | tf_op jit(solution)/shard_map/ppermute | solution.py:35
  17.6 1.5 %collective-permute-start.4 = (bf16[128,384]{1,0:T(8,128)(2,1)S(1)}, bf16[128,384]{1,0:T(8,128)(2,1)S(1)}, u32[]{:S(2)}, u32[]{:S(2)}) collective-permute-start(bf16[128,384]{1,0:T(8,128)(2,1)S(1)} %get-tuple-element.68), channel_id=1, source_target_pairs={{0,2},{1,3},{2,0},{3,1},{4,6},{5,7},{6,4},{7,5},{8,10},{9,11},{10,... | collective-permute-start | bytes 294920 | tf_op jit(solution)/shard_map/ppermute | solution.py:35
  19.1 1.6 %collective-permute-done.6.refs_2_ = bf16[128,384]{1,0:T(8,128)(2,1)S(1)} collective-permute-done((bf16[128,384]{1,0:T(8,128)(2,1)S(1)}, bf16[128,384]{1,0:T(8,128)(2,1)S(1)}, u32[]{:S(2)}, u32[]{:S(2)}) %collective-permute-start.6) | collective-permute-done | bytes 98336 | tf_op jit(solution)/shard_map/ppermute | solution.py:35
  21.0 1.6 %collective-permute-start.8 = (bf16[64,384]{1,0:T(8,128)(2,1)S(1)}, bf16[64,384]{1,0:T(8,128)(2,1)S(1)}, u32[]{:S(2)}, u32[]{:S(2)}) collective-permute-start(bf16[64,384]{1,0:T(8,128)(2,1)S(1)} %get-tuple-element.75), channel_id=1, source_target_pairs={{0,8},{4,12},{8,0},{12,4},{16,24},{20,28},{24,16},{28,20},{1,9},{5... | collective-permute-start | bytes 147464 | tf_op jit(solution)/shard_map/ppermute | solution.py:35
  22.6 1.5 %collective-permute-start.9 = (bf16[64,384]{1,0:T(8,128)(2,1)S(1)}, bf16[64,384]{1,0:T(8,128)(2,1)S(1)}, u32[]{:S(2)}, u32[]{:S(2)}) collective-permute-start(bf16[64,384]{1,0:T(8,128)(2,1)S(1)} %get-tuple-element.76), channel_id=1, source_target_pairs={{0,16},{4,20},{8,24},{12,28},{16,0},{20,4},{24,8},{28,12},{1,17},{... | collective-permute-start | bytes 147464 | tf_op jit(solution)/shard_map/ppermute | solution.py:35
  25.2 1.4 %collective-permute-done.9.refs_3_ = bf16[64,384]{1,0:T(8,128)(2,1)S(1)} collective-permute-done((bf16[64,384]{1,0:T(8,128)(2,1)S(1)}, bf16[64,384]{1,0:T(8,128)(2,1)S(1)}, u32[]{:S(2)}, u32[]{:S(2)}) %collective-permute-start.9) | collective-permute-done | bytes 49184 | tf_op jit(solution)/shard_map/ppermute | solution.py:35
  26.7 2.4 %collective-permute-done.10.refs_4_ = bf16[64,384]{1,0:T(8,128)(2,1)S(1)} collective-permute-done((bf16[64,384]{1,0:T(8,128)(2,1)S(1)}, bf16[64,384]{1,0:T(8,128)(2,1)S(1)}, u32[]{:S(2)}, u32[]{:S(2)}) %collective-permute-start.10) | collective-permute-done | bytes 49184 | tf_op jit(solution)/shard_map/ppermute | solution.py:35
  29.3 0.9 %collective-permute-start.15 = (bf16[128,384]{1,0:T(8,128)(2,1)S(1)}, bf16[128,384]{1,0:T(8,128)(2,1)S(1)}, u32[]{:S(2)}, u32[]{:S(2)}) collective-permute-start(bf16[128,384]{1,0:T(8,128)(2,1)S(1)} %get-tuple-element.85), channel_id=1, source_target_pairs={{0,2},{1,3},{2,0},{3,1},{4,6},{5,7},{6,4},{7,5},{8,10},{9,11},{10,... | collective-permute-start | bytes 294920 | tf_op jit(solution)/shard_map/ppermute | solution.py:35
  30.9 2.8 %collective-permute-start.18 = (bf16[64,384]{1,0:T(8,128)(2,1)S(1)}, bf16[64,384]{1,0:T(8,128)(2,1)S(1)}, u32[]{:S(2)}, u32[]{:S(2)}) collective-permute-start(bf16[64,384]{1,0:T(8,128)(2,1)S(1)} %get-tuple-element.88), channel_id=1, source_target_pairs={{0,24},{4,28},{8,16},{12,20},{16,8},{20,12},{24,0},{28,4},{1,25},{... | collective-permute-start | bytes 147464 | tf_op jit(solution)/shard_map/ppermute | solution.py:35
  36.1 1.2 %collective-permute-start.14 = (bf16[64,384]{1,0:T(8,128)(2,1)S(1)}, bf16[64,384]{1,0:T(8,128)(2,1)S(1)}, u32[]{:S(2)}, u32[]{:S(2)}) collective-permute-start(bf16[64,384]{1,0:T(8,128)(2,1)S(1)} %get-tuple-element.84), channel_id=1, source_target_pairs={{0,24},{4,28},{8,16},{12,20},{16,8},{20,12},{24,0},{28,4},{1,25},{... | collective-permute-start | bytes 147464 | tf_op jit(solution)/shard_map/ppermute | solution.py:35
  37.5 2.2 %collective-permute-start.20 = (bf16[128,384]{1,0:T(8,128)(2,1)S(1)}, bf16[128,384]{1,0:T(8,128)(2,1)S(1)}, u32[]{:S(2)}, u32[]{:S(2)}) collective-permute-start(bf16[128,384]{1,0:T(8,128)(2,1)S(1)} %get-tuple-element.93), channel_id=1, source_target_pairs={{0,2},{1,3},{2,0},{3,1},{4,6},{5,7},{6,4},{7,5},{8,10},{9,11},{10,... | collective-permute-start | bytes 294920 | tf_op jit(solution)/shard_map/ppermute | solution.py:35
  39.9 1.1 %collective-permute-done.14.refs_4_ = bf16[64,384]{1,0:T(8,128)(2,1)S(1)} collective-permute-done((bf16[64,384]{1,0:T(8,128)(2,1)S(1)}, bf16[64,384]{1,0:T(8,128)(2,1)S(1)}, u32[]{:S(2)}, u32[]{:S(2)}) %collective-permute-start.14) | collective-permute-done | bytes 49184 | tf_op jit(solution)/shard_map/ppermute | solution.py:35
  41.3 1.7 %collective-permute-start.19 = (bf16[128,384]{1,0:T(8,128)(2,1)S(1)}, bf16[128,384]{1,0:T(8,128)(2,1)S(1)}, u32[]{:S(2)}, u32[]{:S(2)}) collective-permute-start(bf16[128,384]{1,0:T(8,128)(2,1)S(1)} %get-tuple-element.92), channel_id=1, source_target_pairs={{0,2},{1,3},{2,0},{3,1},{4,6},{5,7},{6,4},{7,5},{8,10},{9,11},{10,... | collective-permute-start | bytes 294920 | tf_op jit(solution)/shard_map/ppermute | solution.py:35
  43.0 2.4 %collective-permute-start.23 = (bf16[128,384]{1,0:T(8,128)(2,1)S(1)}, bf16[128,384]{1,0:T(8,128)(2,1)S(1)}, u32[]{:S(2)}, u32[]{:S(2)}) collective-permute-start(bf16[128,384]{1,0:T(8,128)(2,1)S(1)} %get-tuple-element.98), channel_id=1, source_target_pairs={{0,1},{1,0},{2,3},{3,2},{4,5},{5,4},{6,7},{7,6},{8,9},{9,8},{10,11... | collective-permute-start | bytes 294920 | tf_op jit(solution)/shard_map/ppermute | solution.py:35
  45.9 1.2 %collective-permute-start.22 = (bf16[128,384]{1,0:T(8,128)(2,1)S(1)}, bf16[128,384]{1,0:T(8,128)(2,1)S(1)}, u32[]{:S(2)}, u32[]{:S(2)}) collective-permute-start(bf16[128,384]{1,0:T(8,128)(2,1)S(1)} %get-tuple-element.97), channel_id=1, source_target_pairs={{0,1},{1,0},{2,3},{3,2},{4,5},{5,4},{6,7},{7,6},{8,9},{9,8},{10,11... | collective-permute-start | bytes 294920 | tf_op jit(solution)/shard_map/ppermute | solution.py:35
  47.3 1.9 %collective-permute-start.21 = (bf16[128,384]{1,0:T(8,128)(2,1)S(1)}, bf16[128,384]{1,0:T(8,128)(2,1)S(1)}, u32[]{:S(2)}, u32[]{:S(2)}) collective-permute-start(bf16[128,384]{1,0:T(8,128)(2,1)S(1)} %get-tuple-element.96), channel_id=1, source_target_pairs={{0,1},{1,0},{2,3},{3,2},{4,5},{5,4},{6,7},{7,6},{8,9},{9,8},{10,11... | collective-permute-start | bytes 294920 | tf_op jit(solution)/shard_map/ppermute | solution.py:35
  49.2 1.2 %last0.1.refs_4_ = bf16[768,1152]{1,0:T(8,128)(2,1)} custom-call(bf16[256,256]{1,0:T(8,128)(2,1)S(1)} %get-tuple-element.52.refs_0_, bf16[768,256]{1,0:T(8,128)(2,1)S(1)} %copy-done, bf16[128,384]{1,0:T(8,128)(2,1)S(1)} %get-tuple-element.90.refs_5_.refs_2_, bf16[128,384]{1,0:T(8,128)(2,1)S(1)} %collective-permute-done.23.refs_3_, ...), custom_call_target="tpu_custom_call" | custom-call | flops 150994944 | bytes 589824 | tf_op jit(solution)/shard_map/last0/pallas_call | solution.py:59
  50.5 1.2 %last384.1.refs_4_ = bf16[768,1152]{1,0:T(8,128)(2,1)} custom-call(bf16[256,256]{1,0:T(8,128)(2,1)S(1)} %get-tuple-element.52.refs_0_, bf16[768,256]{1,0:T(8,128)(2,1)S(1)} %copy-done, bf16[128,384]{1,0:T(8,128)(2,1)S(1)} %get-tuple-element.94.refs_3_.refs_4_.refs_2_, ...), custom_call_target="tpu_custom_call", output_to_operand_aliasing={{}: (4, {})} | custom-call | flops 150994944 | bytes 589824 | tf_op jit(solution)/shard_map/last384/pallas_call | solution.py:59
  52.0 1.3 %last768.1 = bf16[768,1152]{1,0:T(8,128)(2,1)} custom-call(bf16[256,256]{1,0:T(8,128)(2,1)S(1)} %get-tuple-element.52.refs_0_, bf16[768,256]{1,0:T(8,128)(2,1)S(1)} %copy-done, bf16[128,384]{1,0:T(8,128)(2,1)S(1)} %get-tuple-element.95.refs_5_.refs_2_, bf16[128,384]{1,0:T(8,128)(2,1)S(1)} %collective-permute-done.21.refs_3_, ...), custom_call_target="tpu_custom_call", output_to_operand_aliasing={{}: (4, {})} | custom-call | flops 150994944 | bytes 589824 | tf_op jit(solution)/shard_map/last768/pallas_call | solution.py:59
  (54 shorter events, 8.6 us)
Async XLA Ops:
  2.4 6.6 %collective-permute-start.1 = (bf16[128,384]{1,0:T(8,128)(2,1)S(1)}, bf16[128,384]{1,0:T(8,128)(2,1)S(1)}, u32[]{:S(2)}, u32[]{:S(2)}) collective-permute-start(bf16[128,384]{1,0:T(8,128)(2,1)S(1)} %get-tuple-element.60), channel_id=1, source_target_pairs={{0,1},{1,0},{2,3},{3,2},{4,5},{5,4},{6,7},{7,6},{8,9},{9,8},{10,11... | collective-permute-start | bytes 294920 | tf_op jit(solution)/shard_map/ppermute | solution.py:35
  5.5 8.5 %collective-permute-start.3 = (bf16[128,384]{1,0:T(8,128)(2,1)S(1)}, bf16[128,384]{1,0:T(8,128)(2,1)S(1)}, u32[]{:S(2)}, u32[]{:S(2)}) collective-permute-start(bf16[128,384]{1,0:T(8,128)(2,1)S(1)} %get-tuple-element.64), channel_id=1, source_target_pairs={{0,1},{1,0},{2,3},{3,2},{4,5},{5,4},{6,7},{7,6},{8,9},{9,8},{10,11... | collective-permute-start | bytes 294920 | tf_op jit(solution)/shard_map/ppermute | solution.py:35
  9.2 7.8 %collective-permute-start.2 = (bf16[128,384]{1,0:T(8,128)(2,1)S(1)}, bf16[128,384]{1,0:T(8,128)(2,1)S(1)}, u32[]{:S(2)}, u32[]{:S(2)}) collective-permute-start(bf16[128,384]{1,0:T(8,128)(2,1)S(1)} %get-tuple-element.62), channel_id=1, source_target_pairs={{0,2},{1,3},{2,0},{3,1},{4,6},{5,7},{6,4},{7,5},{8,10},{9,11},{10,... | collective-permute-start | bytes 294920 | tf_op jit(solution)/shard_map/ppermute | solution.py:35
  12.3 5.0 %collective-permute-start = (bf16[128,384]{1,0:T(8,128)(2,1)S(1)}, bf16[128,384]{1,0:T(8,128)(2,1)S(1)}, u32[]{:S(2)}, u32[]{:S(2)}) collective-permute-start(bf16[128,384]{1,0:T(8,128)(2,1)S(1)} %get-tuple-element.58), channel_id=1, source_target_pairs={{0,1},{1,0},{2,3},{3,2},{4,5},{5,4},{6,7},{7,6},{8,9},{9,8},{10,11... | collective-permute-start | bytes 294920 | tf_op jit(solution)/shard_map/ppermute | solution.py:35
  14.2 6.4 %collective-permute-start.6 = (bf16[128,384]{1,0:T(8,128)(2,1)S(1)}, bf16[128,384]{1,0:T(8,128)(2,1)S(1)}, u32[]{:S(2)}, u32[]{:S(2)}) collective-permute-start(bf16[128,384]{1,0:T(8,128)(2,1)S(1)} %get-tuple-element.70), channel_id=1, source_target_pairs={{0,2},{1,3},{2,0},{3,1},{4,6},{5,7},{6,4},{7,5},{8,10},{9,11},{10,... | collective-permute-start | bytes 294920 | tf_op jit(solution)/shard_map/ppermute | solution.py:35
  17.3 3.7 %collective-permute-start.5 = (bf16[128,384]{1,0:T(8,128)(2,1)S(1)}, bf16[128,384]{1,0:T(8,128)(2,1)S(1)}, u32[]{:S(2)}, u32[]{:S(2)}) collective-permute-start(bf16[128,384]{1,0:T(8,128)(2,1)S(1)} %get-tuple-element.69), channel_id=1, source_target_pairs={{0,4},{4,0},{8,12},{12,8},{16,20},{20,16},{24,28},{28,24},{1,5},{5... | collective-permute-start | bytes 294920 | tf_op jit(solution)/shard_map/ppermute | solution.py:35
  17.6 7.0 %collective-permute-start.4 = (bf16[128,384]{1,0:T(8,128)(2,1)S(1)}, bf16[128,384]{1,0:T(8,128)(2,1)S(1)}, u32[]{:S(2)}, u32[]{:S(2)}) collective-permute-start(bf16[128,384]{1,0:T(8,128)(2,1)S(1)} %get-tuple-element.68), channel_id=1, source_target_pairs={{0,2},{1,3},{2,0},{3,1},{4,6},{5,7},{6,4},{7,5},{8,10},{9,11},{10,... | collective-permute-start | bytes 294920 | tf_op jit(solution)/shard_map/ppermute | solution.py:35
  20.9 4.0 %collective-permute-start.11 = (bf16[128,384]{1,0:T(8,128)(2,1)S(1)}, bf16[128,384]{1,0:T(8,128)(2,1)S(1)}, u32[]{:S(2)}, u32[]{:S(2)}) collective-permute-start(bf16[128,384]{1,0:T(8,128)(2,1)S(1)} %get-tuple-element.78), channel_id=1, source_target_pairs={{0,4},{4,0},{8,12},{12,8},{16,20},{20,16},{24,28},{28,24},{1,5},{5... | collective-permute-start | bytes 294920 | tf_op jit(solution)/shard_map/ppermute | solution.py:35
  21.0 4.2 %collective-permute-start.8 = (bf16[64,384]{1,0:T(8,128)(2,1)S(1)}, bf16[64,384]{1,0:T(8,128)(2,1)S(1)}, u32[]{:S(2)}, u32[]{:S(2)}) collective-permute-start(bf16[64,384]{1,0:T(8,128)(2,1)S(1)} %get-tuple-element.75), channel_id=1, source_target_pairs={{0,8},{4,12},{8,0},{12,4},{16,24},{20,28},{24,16},{28,20},{1,9},{5... | collective-permute-start | bytes 147464 | tf_op jit(solution)/shard_map/ppermute | solution.py:35
  22.6 4.1 %collective-permute-start.9 = (bf16[64,384]{1,0:T(8,128)(2,1)S(1)}, bf16[64,384]{1,0:T(8,128)(2,1)S(1)}, u32[]{:S(2)}, u32[]{:S(2)}) collective-permute-start(bf16[64,384]{1,0:T(8,128)(2,1)S(1)} %get-tuple-element.76), channel_id=1, source_target_pairs={{0,16},{4,20},{8,24},{12,28},{16,0},{20,4},{24,8},{28,12},{1,17},{... | collective-permute-start | bytes 147464 | tf_op jit(solution)/shard_map/ppermute | solution.py:35
  24.1 5.0 %collective-permute-start.10 = (bf16[64,384]{1,0:T(8,128)(2,1)S(1)}, bf16[64,384]{1,0:T(8,128)(2,1)S(1)}, u32[]{:S(2)}, u32[]{:S(2)}) collective-permute-start(bf16[64,384]{1,0:T(8,128)(2,1)S(1)} %get-tuple-element.77), channel_id=1, source_target_pairs={{0,24},{4,28},{8,16},{12,20},{16,8},{20,12},{24,0},{28,4},{1,25},{... | collective-permute-start | bytes 147464 | tf_op jit(solution)/shard_map/ppermute | solution.py:35
  24.8 8.9 %collective-permute-start.7 = (bf16[128,384]{1,0:T(8,128)(2,1)S(1)}, bf16[128,384]{1,0:T(8,128)(2,1)S(1)}, u32[]{:S(2)}, u32[]{:S(2)}) collective-permute-start(bf16[128,384]{1,0:T(8,128)(2,1)S(1)} %get-tuple-element.74), channel_id=1, source_target_pairs={{0,4},{4,0},{8,12},{12,8},{16,20},{20,16},{24,28},{28,24},{1,5},{5... | collective-permute-start | bytes 294920 | tf_op jit(solution)/shard_map/ppermute | solution.py:35
  29.3 10.4 %collective-permute-start.15 = (bf16[128,384]{1,0:T(8,128)(2,1)S(1)}, bf16[128,384]{1,0:T(8,128)(2,1)S(1)}, u32[]{:S(2)}, u32[]{:S(2)}) collective-permute-start(bf16[128,384]{1,0:T(8,128)(2,1)S(1)} %get-tuple-element.85), channel_id=1, source_target_pairs={{0,2},{1,3},{2,0},{3,1},{4,6},{5,7},{6,4},{7,5},{8,10},{9,11},{10,... | collective-permute-start | bytes 294920 | tf_op jit(solution)/shard_map/ppermute | solution.py:35
  30.2 4.5 %collective-permute-start.16 = (bf16[64,384]{1,0:T(8,128)(2,1)S(1)}, bf16[64,384]{1,0:T(8,128)(2,1)S(1)}, u32[]{:S(2)}, u32[]{:S(2)}) collective-permute-start(bf16[64,384]{1,0:T(8,128)(2,1)S(1)} %get-tuple-element.86), channel_id=1, source_target_pairs={{0,8},{4,12},{8,0},{12,4},{16,24},{20,28},{24,16},{28,20},{1,9},{5... | collective-permute-start | bytes 147464 | tf_op jit(solution)/shard_map/ppermute | solution.py:35
  30.7 5.4 %collective-permute-start.17 = (bf16[64,384]{1,0:T(8,128)(2,1)S(1)}, bf16[64,384]{1,0:T(8,128)(2,1)S(1)}, u32[]{:S(2)}, u32[]{:S(2)}) collective-permute-start(bf16[64,384]{1,0:T(8,128)(2,1)S(1)} %get-tuple-element.87), channel_id=1, source_target_pairs={{0,16},{4,20},{8,24},{12,28},{16,0},{20,4},{24,8},{28,12},{1,17},{... | collective-permute-start | bytes 147464 | tf_op jit(solution)/shard_map/ppermute | solution.py:35
  30.9 6.4 %collective-permute-start.18 = (bf16[64,384]{1,0:T(8,128)(2,1)S(1)}, bf16[64,384]{1,0:T(8,128)(2,1)S(1)}, u32[]{:S(2)}, u32[]{:S(2)}) collective-permute-start(bf16[64,384]{1,0:T(8,128)(2,1)S(1)} %get-tuple-element.88), channel_id=1, source_target_pairs={{0,24},{4,28},{8,16},{12,20},{16,8},{20,12},{24,0},{28,4},{1,25},{... | collective-permute-start | bytes 147464 | tf_op jit(solution)/shard_map/ppermute | solution.py:35
  33.7 6.2 %collective-permute-start.12 = (bf16[64,384]{1,0:T(8,128)(2,1)S(1)}, bf16[64,384]{1,0:T(8,128)(2,1)S(1)}, u32[]{:S(2)}, u32[]{:S(2)}) collective-permute-start(bf16[64,384]{1,0:T(8,128)(2,1)S(1)} %get-tuple-element.82), channel_id=1, source_target_pairs={{0,8},{4,12},{8,0},{12,4},{16,24},{20,28},{24,16},{28,20},{1,9},{5... | collective-permute-start | bytes 147464 | tf_op jit(solution)/shard_map/ppermute | solution.py:35
  34.7 5.2 %collective-permute-start.13 = (bf16[64,384]{1,0:T(8,128)(2,1)S(1)}, bf16[64,384]{1,0:T(8,128)(2,1)S(1)}, u32[]{:S(2)}, u32[]{:S(2)}) collective-permute-start(bf16[64,384]{1,0:T(8,128)(2,1)S(1)} %get-tuple-element.83), channel_id=1, source_target_pairs={{0,16},{4,20},{8,24},{12,28},{16,0},{20,4},{24,8},{28,12},{1,17},{... | collective-permute-start | bytes 147464 | tf_op jit(solution)/shard_map/ppermute | solution.py:35
  36.1 5.0 %collective-permute-start.14 = (bf16[64,384]{1,0:T(8,128)(2,1)S(1)}, bf16[64,384]{1,0:T(8,128)(2,1)S(1)}, u32[]{:S(2)}, u32[]{:S(2)}) collective-permute-start(bf16[64,384]{1,0:T(8,128)(2,1)S(1)} %get-tuple-element.84), channel_id=1, source_target_pairs={{0,24},{4,28},{8,16},{12,20},{16,8},{20,12},{24,0},{28,4},{1,25},{... | collective-permute-start | bytes 147464 | tf_op jit(solution)/shard_map/ppermute | solution.py:35
  37.5 8.2 %collective-permute-start.20 = (bf16[128,384]{1,0:T(8,128)(2,1)S(1)}, bf16[128,384]{1,0:T(8,128)(2,1)S(1)}, u32[]{:S(2)}, u32[]{:S(2)}) collective-permute-start(bf16[128,384]{1,0:T(8,128)(2,1)S(1)} %get-tuple-element.93), channel_id=1, source_target_pairs={{0,2},{1,3},{2,0},{3,1},{4,6},{5,7},{6,4},{7,5},{8,10},{9,11},{10,... | collective-permute-start | bytes 294920 | tf_op jit(solution)/shard_map/ppermute | solution.py:35
  41.3 5.8 %collective-permute-start.19 = (bf16[128,384]{1,0:T(8,128)(2,1)S(1)}, bf16[128,384]{1,0:T(8,128)(2,1)S(1)}, u32[]{:S(2)}, u32[]{:S(2)}) collective-permute-start(bf16[128,384]{1,0:T(8,128)(2,1)S(1)} %get-tuple-element.92), channel_id=1, source_target_pairs={{0,2},{1,3},{2,0},{3,1},{4,6},{5,7},{6,4},{7,5},{8,10},{9,11},{10,... | collective-permute-start | bytes 294920 | tf_op jit(solution)/shard_map/ppermute | solution.py:35
  43.0 6.2 %collective-permute-start.23 = (bf16[128,384]{1,0:T(8,128)(2,1)S(1)}, bf16[128,384]{1,0:T(8,128)(2,1)S(1)}, u32[]{:S(2)}, u32[]{:S(2)}) collective-permute-start(bf16[128,384]{1,0:T(8,128)(2,1)S(1)} %get-tuple-element.98), channel_id=1, source_target_pairs={{0,1},{1,0},{2,3},{3,2},{4,5},{5,4},{6,7},{7,6},{8,9},{9,8},{10,11... | collective-permute-start | bytes 294920 | tf_op jit(solution)/shard_map/ppermute | solution.py:35
  45.9 4.7 %collective-permute-start.22 = (bf16[128,384]{1,0:T(8,128)(2,1)S(1)}, bf16[128,384]{1,0:T(8,128)(2,1)S(1)}, u32[]{:S(2)}, u32[]{:S(2)}) collective-permute-start(bf16[128,384]{1,0:T(8,128)(2,1)S(1)} %get-tuple-element.97), channel_id=1, source_target_pairs={{0,1},{1,0},{2,3},{3,2},{4,5},{5,4},{6,7},{7,6},{8,9},{9,8},{10,11... | collective-permute-start | bytes 294920 | tf_op jit(solution)/shard_map/ppermute | solution.py:35
  47.3 4.7 %collective-permute-start.21 = (bf16[128,384]{1,0:T(8,128)(2,1)S(1)}, bf16[128,384]{1,0:T(8,128)(2,1)S(1)}, u32[]{:S(2)}, u32[]{:S(2)}) collective-permute-start(bf16[128,384]{1,0:T(8,128)(2,1)S(1)} %get-tuple-element.96), channel_id=1, source_target_pairs={{0,1},{1,0},{2,3},{3,2},{4,5},{5,4},{6,7},{7,6},{8,9},{9,8},{10,11... | collective-permute-start | bytes 294920 | tf_op jit(solution)/shard_map/ppermute | solution.py:35
  (5 other events, 50.7 us)
